TPU v7x, 32 devices: a whole 2x2x4 slice. The times are simulated.
32 devices in a mesh: group: 4 (over y, core), ingroup: 4 (over z), dp: 2 (over x).
Axes of the slice: x: 2, y: 2, z: 4, core: 2. Of those that a mesh axis runs over, the one named last changes fastest.
Arguments:
- tokens: bfloat16 [256, 3584], P(('group', 'ingroup'), 'dp'), may hold values from -6 to 6
- cotangent: bfloat16 [256, 3584], P(('group', 'ingroup'), 'dp'), may hold values from -6 to 6
- expert_ids: int32 [256, 8], P(('group', 'ingroup')), may hold values from 0 to 15, as said below
- gate_fixed: int32 [256, 8], P(('group', 'ingroup')), may hold values from 6554 to 65535
- w_gate: bfloat16 [16, 3584, 1024], P(('group', 'ingroup'), 'dp'), may hold values from -0.09375 to 0.09375
- w_up: bfloat16 [16, 3584, 1024], P(('group', 'ingroup'), 'dp'), may hold values from -0.09375 to 0.09375
- w_down: bfloat16 [16, 1024, 3584], P(('group', 'ingroup'), None, 'dp'), may hold values from -0.1875 to 0.1875
Outputs:
- mixed: bfloat16 [256, 3584], P(('group', 'ingroup'), 'dp')
- token_grad: bfloat16 [256, 3584], P(('group', 'ingroup'), 'dp')
Inputs may be any that keep to these rules, and one draw needn't show every extreme that they name: `expert_ids`: expert e belongs to group e // 4. Each token chooses 4 different groups and names two experts in each, 8 different experts in all. One group, drawn from the seed, is chosen by every token. In each aligned block of 16 tokens at most 8 tokens name one expert, and the experts of one group are named by counts that differ by at most one.
All inputs are finite; a program needn't handle non-finite values.
Results may differ from a plain program's by a relative error of at most 0.0064.
Values may be sent and summed in bfloat16 or wider, within the bound.
No kernel may reach another device: no remote copies, remote signals or barrier semaphores. Data moves between devices by JAX's collectives and lax.ppermute only.
A program may use at most 64 MiB of HBM per device.

v0:
```python
import jax
import jax.numpy as jnp
from jax import lax
from jax.sharding import PartitionSpec as P


def contract_last(left, right):
    return lax.dot_general(
        left, right, (((1,), (1,)), ((), ())), preferred_element_type=jnp.float32
    )


def expert_pass(rows_x, rows_d, gate_weight, up_weight, down_weight):
    gate_part = jnp.dot(rows_x, gate_weight, preferred_element_type=jnp.float32)
    up_part = jnp.dot(rows_x, up_weight, preferred_element_type=jnp.float32)
    back_part = contract_last(rows_d, down_weight)
    gate_share, up_share, back_share = (
        lax.psum_scatter(gate_part, "dp", scatter_dimension=1, tiled=True),
        lax.psum_scatter(up_part, "dp", scatter_dimension=1, tiled=True),
        lax.psum_scatter(back_part, "dp", scatter_dimension=1, tiled=True),
    )
    sigmoid_share = jax.nn.sigmoid(gate_share)
    hidden_share = (gate_share * sigmoid_share * up_share).astype(jnp.bfloat16)
    d_gate_share = (
        back_share * up_share * sigmoid_share * (1.0 + gate_share * (1.0 - sigmoid_share))
    ).astype(jnp.bfloat16)
    d_up_share = (back_share * gate_share * sigmoid_share).astype(jnp.bfloat16)
    hidden, d_gate, d_up = (
        lax.all_gather(hidden_share, "dp", axis=1, tiled=True),
        lax.all_gather(d_gate_share, "dp", axis=1, tiled=True),
        lax.all_gather(d_up_share, "dp", axis=1, tiled=True),
    )
    out_rows = jnp.dot(hidden, down_weight, preferred_element_type=jnp.float32).astype(jnp.bfloat16)
    grad_rows = (contract_last(d_gate, gate_weight) + contract_last(d_up, up_weight)).astype(
        jnp.bfloat16
    )
    return (out_rows, grad_rows)


def on_device(tokens, cotangent, expert_ids, gate_fixed, w_gate, w_up, w_down):
    group_count = lax.axis_size("group")
    inner_count = lax.axis_size("ingroup")
    token_count, features = tokens.shape
    topk_count = expert_ids.shape[1]
    expert_count = group_count * inner_count
    capacity = 2 * token_count // inner_count
    slot_total = expert_count * capacity
    weights = gate_fixed.astype(jnp.float32) / 65536.0
    is_named = (expert_ids[:, :, None] == jnp.arange(expert_count, dtype=jnp.int32)).astype(
        jnp.int32
    )
    per_token = jnp.sum(is_named, axis=1)
    before = jnp.cumsum(per_token, axis=0) - per_token
    slot_rank = jnp.take_along_axis(before, expert_ids, axis=1)
    zero_half = jnp.zeros((), jnp.bfloat16)
    flat_slot = (expert_ids * capacity + slot_rank).reshape(-1)
    token_index = jnp.repeat(jnp.arange(token_count, dtype=jnp.int32), topk_count)
    source_row = jnp.zeros((slot_total,), jnp.int32).at[flat_slot].set(token_index)
    filled = jnp.zeros((slot_total,), jnp.bool_).at[flat_slot].set(True)
    slot_weight = jnp.zeros((slot_total,), jnp.float32).at[flat_slot].set(weights.reshape(-1))
    send_x = jnp.where(filled[:, None], tokens[source_row], zero_half)
    send_d = jnp.where(
        filled[:, None],
        slot_weight[:, None] * cotangent[source_row].astype(jnp.float32),
        jnp.float32(0.0),
    ).astype(jnp.bfloat16)
    send_shape = (group_count, inner_count, capacity * features)
    recv_x, recv_d = (
        lax.all_to_all(
            lax.all_to_all(
                send_x.reshape(send_shape), "group", split_axis=0, concat_axis=0, tiled=True
            ),
            "ingroup",
            split_axis=1,
            concat_axis=1,
            tiled=True,
        ),
        lax.all_to_all(
            lax.all_to_all(
                send_d.reshape(send_shape), "group", split_axis=0, concat_axis=0, tiled=True
            ),
            "ingroup",
            split_axis=1,
            concat_axis=1,
            tiled=True,
        ),
    )
    out_rows, grad_rows = expert_pass(
        recv_x.reshape(-1, features), recv_d.reshape(-1, features), w_gate[0], w_up[0], w_down[0]
    )
    back_y, back_dx = (
        lax.all_to_all(
            lax.all_to_all(
                out_rows.reshape(send_shape), "group", split_axis=0, concat_axis=0, tiled=True
            ),
            "ingroup",
            split_axis=1,
            concat_axis=1,
            tiled=True,
        ),
        lax.all_to_all(
            lax.all_to_all(
                grad_rows.reshape(send_shape), "group", split_axis=0, concat_axis=0, tiled=True
            ),
            "ingroup",
            split_axis=1,
            concat_axis=1,
            tiled=True,
        ),
    )
    pick_shape = (token_count, topk_count, features)
    y_pick = back_y.reshape(slot_total, features)[flat_slot].reshape(pick_shape).astype(jnp.float32)
    dx_pick = (
        back_dx.reshape(slot_total, features)[flat_slot].reshape(pick_shape).astype(jnp.float32)
    )
    mixed = jnp.sum(weights[:, :, None] * y_pick, axis=1).astype(jnp.bfloat16)
    token_grad = jnp.sum(dx_pick, axis=1).astype(jnp.bfloat16)
    return (mixed, token_grad)


def solution(mesh):
    placed = (
        P(("group", "ingroup"), "dp"),
        P(("group", "ingroup"), "dp"),
        P(("group", "ingroup"), None),
        P(("group", "ingroup"), None),
        P(("group", "ingroup"), "dp", None),
        P(("group", "ingroup"), "dp", None),
        P(("group", "ingroup"), None, "dp"),
    )
    return jax.shard_map(
        on_device,
        mesh=mesh,
        in_specs=placed,
        out_specs=(P(("group", "ingroup"), "dp"), P(("group", "ingroup"), "dp")),
        check_vma=False,
    )
```

profile of v0, /device:TPU:0, one launch (start us, length us, event | category | flops | bytes accessed | tf_op | source)
XLA Modules:
  0.0 198.4 jit_solution(15872329328329568973)
XLA Ops:
  17.8 4.2 %all-to-all-start.4 = ((bf16[4,4,14336]{2,1,0:T(4,128)(2,1)}), bf16[4,4,14336]{2,1,0:T(4,128)(2,1)S(1)}, u32[]{:S(2)}, u32[]{:S(2)}) async-start(bf16[4,4,14336]{2,1,0:T(4,128)(2,1)} %select_convert_fusion), calls=%async_computation.6 | async-start | bytes 917504 | tf_op jit(solution)/shard_map/all_to_all | solution.py:79
  23.4 6.9 %all-to-all-done.4 = bf16[4,4,14336]{2,1,0:T(4,128)(2,1)S(1)} async-done(((bf16[4,4,14336]{2,1,0:T(4,128)(2,1)}), bf16[4,4,14336]{2,1,0:T(4,128)(2,1)S(1)}, u32[]{:S(2)}, u32[]{:S(2)}) %all-to-all-start.4) | async-done | bytes 458784 | tf_op jit(solution)/shard_map/all_to_all | solution.py:79
  31.4 5.5 %all-to-all-start.5 = ((bf16[4,4,14336]{2,0,1:T(4,128)(2,1)}), bf16[4,4,14336]{2,0,1:T(4,128)(2,1)S(1)}, u32[]{:S(2)}, u32[]{:S(2)}) async-start(bf16[4,4,14336]{2,0,1:T(4,128)(2,1)} %copy.75), calls=%async_computation.7 | async-start | bytes 917504 | tf_op jit(solution)/shard_map/all_to_all | solution.py:78
  38.0 11.8 %all-to-all-done.5 = bf16[4,4,14336]{2,0,1:T(4,128)(2,1)S(1)} async-done(((bf16[4,4,14336]{2,0,1:T(4,128)(2,1)}), bf16[4,4,14336]{2,0,1:T(4,128)(2,1)S(1)}, u32[]{:S(2)}, u32[]{:S(2)}) %all-to-all-start.5) | async-done | bytes 458784 | tf_op jit(solution)/shard_map/all_to_all | solution.py:78
  49.8 3.5 %all-to-all-start = ((bf16[4,4,14336]{2,1,0:T(4,128)(2,1)}), bf16[4,4,14336]{2,1,0:T(4,128)(2,1)S(1)}, u32[]{:S(2)}, u32[]{:S(2)}) async-start(bf16[4,4,14336]{2,1,0:T(4,128)(2,1)} %broadcast_select_fusion), calls=%async_computation | async-start | bytes 917504 | tf_op jit(solution)/shard_map/all_to_all | solution.py:70
  54.0 4.1 %fusion = f32[128,1024]{1,0:T(8,128)} fusion(bf16[128,1792]{1,0:T(8,128)(2,1)S(1)} %reshape.99, bf16[1,1024,1792]{2,1,0:T(8,128)(2,1)} %param.13), kind=kOutput, calls=%fused_computation.8 | convolution fusion | flops 469762048 | bytes 4653056 | tf_op jit(solution)/shard_map/dot_general | solution.py:8
  58.2 3.1 %all-to-all-done = bf16[4,4,14336]{2,1,0:T(4,128)(2,1)S(1)} async-done(((bf16[4,4,14336]{2,1,0:T(4,128)(2,1)}), bf16[4,4,14336]{2,1,0:T(4,128)(2,1)S(1)}, u32[]{:S(2)}, u32[]{:S(2)}) %all-to-all-start) | async-done | bytes 458784 | tf_op jit(solution)/shard_map/all_to_all | solution.py:70
  61.7 15.5 %all_to_all.40 = bf16[4,4,14336]{2,0,1:T(4,128)(2,1)S(1)} all-to-all(bf16[4,4,14336]{2,0,1:T(4,128)(2,1)S(1)} %copy.70), channel_id=1, replica_groups=mesh['group'=4,'ingroup'=4,'dp'=2] {'ingroup'}, dimensions={1} | all-to-all | bytes 917504 | tf_op jit(solution)/shard_map/all_to_all | solution.py:69
  78.0 3.5 %fusion.10 = f32[128,1024]{1,0:T(8,128)} fusion(bf16[128,1792]{1,0:T(8,128)(2,1)S(1)} %reshape.95, bf16[1,1792,1024]{2,1,0:T(8,128)(2,1)} %param.11), kind=kOutput, calls=%fused_computation.18 | convolution fusion | flops 469762048 | bytes 4653056 | tf_op jit(solution)/shard_map/dot_general | solution.py:14
  81.6 3.5 %fusion.6 = f32[128,1024]{1,0:T(8,128)} fusion(bf16[128,1792]{1,0:T(8,128)(2,1)S(1)} %reshape.95, bf16[1,1792,1024]{2,1,0:T(8,128)(2,1)} %param.12), kind=kOutput, calls=%fused_computation.14 | convolution fusion | flops 469762048 | bytes 4653056 | tf_op jit(solution)/shard_map/dot_general | solution.py:15
  85.1 9.3 %reduce-scatter.4.cloned.1.call-done = f32[128,512]{1,0:T(8,128)} async-done(((f32[128,1024]{1,0:T(8,128)}), f32[128,512]{1,0:T(8,128)}) %reduce-scatter.4.cloned.1.call-update) | async-done | bytes 262160 | tf_op jit(solution)/shard_map/reduce_scatter | solution.py:18
  94.4 16.8 %reduce-scatter.6.cloned.1.call-done = f32[128,512]{1,0:T(8,128)} async-done(((f32[128,1024]{1,0:T(8,128)}), f32[128,512]{1,0:T(8,128)}) %reduce-scatter.6.cloned.1.call-update) | async-done | bytes 262160 | tf_op jit(solution)/shard_map/reduce_scatter | solution.py:19
  112.7 5.9 %all_gather.11 = bf16[128,1024]{1,0:T(8,128)(2,1)S(1)} all-gather(bf16[128,512]{1,0:T(8,128)(2,1)S(1)} %get-tuple-element.4), channel_id=1, replica_groups=mesh['group'=4,'ingroup'=4,'dp'=2] {'dp'}, dimensions={1}, use_global_device_ids=true | all-gather | bytes 393216 | tf_op jit(solution)/shard_map/all_gather | solution.py:31
  118.6 3.4 %fusion.4 = f32[128,1792]{1,0:T(8,128)S(1)} fusion(bf16[128,1024]{1,0:T(8,128)(2,1)S(1)} %all_gather.11, bf16[1,1792,1024]{2,1,0:T(8,128)(2,1)} %param.12), kind=kOutput, calls=%fused_computation.12 | convolution fusion | flops 469762048 | bytes 4849664 | tf_op jit(solution)/shard_map/dot_general | solution.py:8
  122.0 5.8 %all_gather.10 = bf16[128,1024]{1,0:T(8,128)(2,1)S(1)} all-gather(bf16[128,512]{1,0:T(8,128)(2,1)S(1)} %get-tuple-element.2), channel_id=1, replica_groups=mesh['group'=4,'ingroup'=4,'dp'=2] {'dp'}, dimensions={1}, use_global_device_ids=true | all-gather | bytes 393216 | tf_op jit(solution)/shard_map/all_gather | solution.py:30
  130.3 3.5 %all-to-all-start.6 = ((bf16[4,4,14336]{2,1,0:T(4,128)(2,1)}), bf16[4,4,14336]{2,1,0:T(4,128)(2,1)S(1)}, u32[]{:S(2)}, u32[]{:S(2)}) async-start(bf16[4,4,14336]{2,1,0:T(4,128)(2,1)} %reshape.100), calls=%async_computation.9 | async-start | bytes 917504 | tf_op jit(solution)/shard_map/all_to_all | solution.py:102
  133.7 6.5 %all_gather.9 = bf16[128,1024]{1,0:T(8,128)(2,1)S(1)} all-gather(bf16[128,512]{1,0:T(8,128)(2,1)S(1)} %get-tuple-element.3), channel_id=1, replica_groups=mesh['group'=4,'ingroup'=4,'dp'=2] {'dp'}, dimensions={1}, use_global_device_ids=true | all-gather | bytes 393216 | tf_op jit(solution)/shard_map/all_gather | solution.py:29
  140.3 2.7 %fusion.15 = bf16[128,1792]{1,0:T(8,128)(2,1)S(1)} fusion(bf16[128,1024]{1,0:T(8,128)(2,1)S(1)} %all_gather.9, bf16[1,1024,1792]{2,1,0:T(8,128)(2,1)} %param.13), kind=kOutput, calls=%fused_computation.21 | convolution fusion | flops 469991424 | bytes 4390912 | tf_op jit(solution)/shard_map/dot_general | solution.py:33
  144.1 3.5 %all-to-all-start.2 = ((bf16[4,4,14336]{2,1,0:T(4,128)(2,1)}), bf16[4,4,14336]{2,1,0:T(4,128)(2,1)S(1)}, u32[]{:S(2)}, u32[]{:S(2)}) async-start(bf16[4,4,14336]{2,1,0:T(4,128)(2,1)} %reshape.96), calls=%async_computation.4 | async-start | bytes 917504 | tf_op jit(solution)/shard_map/all_to_all | solution.py:93
  148.7 7.0 %all-to-all-done.2 = bf16[4,4,14336]{2,1,0:T(4,128)(2,1)S(1)} async-done(((bf16[4,4,14336]{2,1,0:T(4,128)(2,1)}), bf16[4,4,14336]{2,1,0:T(4,128)(2,1)S(1)}, u32[]{:S(2)}, u32[]{:S(2)}) %all-to-all-start.2) | async-done | bytes 458784 | tf_op jit(solution)/shard_map/all_to_all | solution.py:93
  155.7 4.6 %all-to-all-start.7 = ((bf16[4,4,14336]{2,0,1:T(4,128)(2,1)}), bf16[4,4,14336]{2,0,1:T(4,128)(2,1)S(1)}, u32[]{:S(2)}, u32[]{:S(2)}) async-start(bf16[4,4,14336]{2,0,1:T(4,128)(2,1)} %copy.77), calls=%async_computation.10 | async-start | bytes 917504 | tf_op jit(solution)/shard_map/all_to_all | solution.py:101
  161.4 11.8 %all-to-all-done.7 = bf16[4,4,14336]{2,0,1:T(4,128)(2,1)S(1)} async-done(((bf16[4,4,14336]{2,0,1:T(4,128)(2,1)}), bf16[4,4,14336]{2,0,1:T(4,128)(2,1)S(1)}, u32[]{:S(2)}, u32[]{:S(2)}) %all-to-all-start.7) | async-done | bytes 458784 | tf_op jit(solution)/shard_map/all_to_all | solution.py:101
  173.1 3.5 %all-to-all-start.3 = ((bf16[4,4,14336]{2,0,1:T(4,128)(2,1)}), bf16[4,4,14336]{2,0,1:T(4,128)(2,1)S(1)}, u32[]{:S(2)}, u32[]{:S(2)}) async-start(bf16[4,4,14336]{2,0,1:T(4,128)(2,1)} %copy.72), calls=%async_computation.5 | async-start | bytes 917504 | tf_op jit(solution)/shard_map/all_to_all | solution.py:92
  179.2 10.0 %all-to-all-done.3 = bf16[4,4,14336]{2,0,1:T(4,128)(2,1)S(1)} async-done(((bf16[4,4,14336]{2,0,1:T(4,128)(2,1)}), bf16[4,4,14336]{2,0,1:T(4,128)(2,1)S(1)}, u32[]{:S(2)}, u32[]{:S(2)}) %all-to-all-start.3) | async-done | bytes 458784 | tf_op jit(solution)/shard_map/all_to_all | solution.py:92
  (76 shorter events, 28.5 us)
Async XLA Ops:
  7.2 6.4 %copy-start = (bf16[16,1792]{1,0:T(8,128)(2,1)S(1)}, bf16[16,1792]{1,0:T(8,128)(2,1)}, u32[]{:S(2)}) copy-start(bf16[16,1792]{1,0:T(8,128)(2,1)} %param.8) | copy-start | bytes 172036
  9.0 1.5 copy-start.3
  9.0 1.6 copy-start.4
  14.5 7.6 %copy-start.1 = (bf16[16,1792]{1,0:T(8,128)(2,1)S(1)}, bf16[16,1792]{1,0:T(8,128)(2,1)}, u32[]{:S(2)}) copy-start(bf16[16,1792]{1,0:T(8,128)(2,1)} %param.7) | copy-start | bytes 172036
  17.8 12.4 %all-to-all-start.4 = ((bf16[4,4,14336]{2,1,0:T(4,128)(2,1)}), bf16[4,4,14336]{2,1,0:T(4,128)(2,1)S(1)}, u32[]{:S(2)}, u32[]{:S(2)}) async-start(bf16[4,4,14336]{2,1,0:T(4,128)(2,1)} %select_convert_fusion), calls=%async_computation.6 | async-start | bytes 917504 | tf_op jit(solution)/shard_map/all_to_all | solution.py:79
  31.4 18.4 %all-to-all-start.5 = ((bf16[4,4,14336]{2,0,1:T(4,128)(2,1)}), bf16[4,4,14336]{2,0,1:T(4,128)(2,1)S(1)}, u32[]{:S(2)}, u32[]{:S(2)}) async-start(bf16[4,4,14336]{2,0,1:T(4,128)(2,1)} %copy.75), calls=%async_computation.7 | async-start | bytes 917504 | tf_op jit(solution)/shard_map/all_to_all | solution.py:78
  49.8 11.6 %all-to-all-start = ((bf16[4,4,14336]{2,1,0:T(4,128)(2,1)}), bf16[4,4,14336]{2,1,0:T(4,128)(2,1)S(1)}, u32[]{:S(2)}, u32[]{:S(2)}) async-start(bf16[4,4,14336]{2,1,0:T(4,128)(2,1)} %broadcast_select_fusion), calls=%async_computation | async-start | bytes 917504 | tf_op jit(solution)/shard_map/all_to_all | solution.py:70
  53.2 31.9 %reduce-scatter.8.cloned.1.call-start = ((), (), s32[]{:S(2)}) async-start(), calls=%async_computation.13 | async-start | bytes 786432 | tf_op jit(solution)/shard_map/reduce_scatter | solution.py:20
  58.2 36.3 %reduce-scatter.4.cloned.1.call-start = ((), (), s32[]{:S(2)}) async-start(), calls=%async_computation.11 | async-start | bytes 786432 | tf_op jit(solution)/shard_map/reduce_scatter | solution.py:18
  81.5 29.8 %reduce-scatter.6.cloned.1.call-start = ((), (), s32[]{:S(2)}) async-start(), calls=%async_computation.12 | async-start | bytes 786432 | tf_op jit(solution)/shard_map/reduce_scatter | solution.py:19
  111.3 16.5 %copy-start.2 = (bf16[1,1792,1024]{2,1,0:T(8,128)(2,1)S(1)}, bf16[1,1792,1024]{2,1,0:T(8,128)(2,1)}, u32[]{:S(2)}) copy-start(bf16[1,1792,1024]{2,1,0:T(8,128)(2,1)} %param.11) | copy-start | bytes 11010052
  130.3 13.8 %all-to-all-start.6 = ((bf16[4,4,14336]{2,1,0:T(4,128)(2,1)}), bf16[4,4,14336]{2,1,0:T(4,128)(2,1)S(1)}, u32[]{:S(2)}, u32[]{:S(2)}) async-start(bf16[4,4,14336]{2,1,0:T(4,128)(2,1)} %reshape.100), calls=%async_computation.9 | async-start | bytes 917504 | tf_op jit(solution)/shard_map/all_to_all | solution.py:102
  144.1 11.6 %all-to-all-start.2 = ((bf16[4,4,14336]{2,1,0:T(4,128)(2,1)}), bf16[4,4,14336]{2,1,0:T(4,128)(2,1)S(1)}, u32[]{:S(2)}, u32[]{:S(2)}) async-start(bf16[4,4,14336]{2,1,0:T(4,128)(2,1)} %reshape.96), calls=%async_computation.4 | async-start | bytes 917504 | tf_op jit(solution)/shard_map/all_to_all | solution.py:93
  155.7 17.5 %all-to-all-start.7 = ((bf16[4,4,14336]{2,0,1:T(4,128)(2,1)}), bf16[4,4,14336]{2,0,1:T(4,128)(2,1)S(1)}, u32[]{:S(2)}, u32[]{:S(2)}) async-start(bf16[4,4,14336]{2,0,1:T(4,128)(2,1)} %copy.77), calls=%async_computation.10 | async-start | bytes 917504 | tf_op jit(solution)/shard_map/all_to_all | solution.py:101
  173.1 16.0 %all-to-all-start.3 = ((bf16[4,4,14336]{2,0,1:T(4,128)(2,1)}), bf16[4,4,14336]{2,0,1:T(4,128)(2,1)S(1)}, u32[]{:S(2)}, u32[]{:S(2)}) async-start(bf16[4,4,14336]{2,0,1:T(4,128)(2,1)} %copy.72), calls=%async_computation.5 | async-start | bytes 917504 | tf_op jit(solution)/shard_map/all_to_all | solution.py:92
Sparse Core Ops, SparseCore 0:
  58.3 14.0 reduce-scatter.7
  81.6 12.7 reduce-scatter.3
  96.7 14.5 reduce-scatter.5
where the time goes:
time: 199 us; the launch traced here: 198 us
  waiting for transfers between devices  76.6 us (38%)
  blocking collectives  33.8 us (17%)
  starting transfers between devices  28.3 us (14%)
  local copies, waits for them, and re-layouts  20.3 us (10%)
  matrix products  18.6 us (9%)
  between operations  14.1 us (7%)
  other arithmetic  6.66 us (3%)
    reduce_scatter x1, waiting for transfers between devices, expert_pass(): lax.psum_scatter(up_part, 'dp', scatter_dimension=1, tiled=True)  16.8 us
    all_to_all x1, blocking collectives, on_device(): lax.all_to_all(lax.all_to_all(send_x.reshape(send_shape), 'group', split_...  15.5 us
    all_to_all x1, waiting for transfers between devices, on_device(): lax.all_to_all(lax.all_to_all(grad_rows.reshape(send_shape), 'group', spl...  11.8 us
    all_to_all x1, waiting for transfers between devices, on_device(): lax.all_to_all(lax.all_to_all(send_d.reshape(send_shape), 'group', split_...  11.8 us
    all_to_all x1, waiting for transfers between devices, on_device(): lax.all_to_all(lax.all_to_all(out_rows.reshape(send_shape), 'group', spli...  9.96 us
    reduce_scatter x1, waiting for transfers between devices, expert_pass(): lax.psum_scatter(gate_part, 'dp', scatter_dimension=1, tiled=True)  9.28 us
    dot_general x3, matrix products, contract_last(): lax.dot_general(left, right, (((1,), (1,)), ((), ())), preferred_element_...  8.84 us
    all_to_all x1, waiting for transfers between devices, on_device(): lax.all_to_all(out_rows.reshape(send_shape), 'group', split_axis=0, conca...  6.98 us
  transfers between devices with their start and end apart: 10, of which 8 were waited for; matrix products, arithmetic and copies ran while one was open for 12% of the time, Pallas kernels for 0%

commit v1 on v0

v1 whole, which is shorter than its diff:
```python
import jax
import jax.numpy as jnp
from jax import lax
from jax.sharding import PartitionSpec as P

PLANE = ("group", "ingroup")


def dot(left, right, left_dim=1, right_dim=0):
    return lax.dot_general(
        left,
        right,
        (((left_dim,), (right_dim,)), ((), ())),
        preferred_element_type=jnp.float32,
    )


def dp_total(part):
    count = lax.axis_size("dp")
    sent = part.astype(jnp.bfloat16)
    total = part
    for step in range(1, count):
        pairs = [(i, (i + step) % count) for i in range(count)]
        total = total + lax.ppermute(sent, "dp", pairs).astype(jnp.float32)
    return total


def on_device(tokens, cotangent, expert_ids, gate_fixed, w_gate, w_up, w_down):
    group_count = lax.axis_size("group")
    inner_count = lax.axis_size("ingroup")
    block, features = tokens.shape
    expert_count = group_count * inner_count
    capacity = 2 * block // inner_count
    slots = expert_count * capacity
    total = expert_count * block

    routing = gate_fixed * expert_count + expert_ids
    routing = lax.all_gather(routing, PLANE, axis=0, tiled=True)
    all_x = lax.all_gather(tokens, PLANE, axis=0, tiled=True)
    all_d = lax.all_gather(cotangent, PLANE, axis=0, tiled=True)

    me = lax.axis_index(PLANE)
    match = (routing % expert_count) == me
    named = jnp.any(match, axis=1)
    gate = jnp.sum(jnp.where(match, routing // expert_count, 0), axis=1)
    index = jnp.arange(total, dtype=jnp.int32)
    earlier = ((index[:, None] // block) == (index[None, :] // block)) & (
        index[:, None] > index[None, :]
    )
    named_cols = jnp.broadcast_to(named[:, None], (total, slots)).astype(jnp.bfloat16)
    rank = dot(earlier.astype(jnp.bfloat16), named_cols).astype(jnp.int32)
    slot = rank + (index // block * capacity)[:, None]
    place = ((slot == jnp.arange(slots, dtype=jnp.int32)) & named[:, None]).astype(jnp.bfloat16)
    halves = jnp.stack([gate // 256, gate % 256], axis=1).astype(jnp.bfloat16)
    row_halves = dot(place, halves, 0, 0)
    scale = (row_halves[:, :1] * 256.0 + row_halves[:, 1:]) / 65536.0

    rows_x = dot(place, all_x, 0, 0).astype(jnp.bfloat16)
    rows_d = dot(place, all_d, 0, 0).astype(jnp.bfloat16)
    gate_pre = dp_total(dot(rows_x, w_gate[0]))
    up_pre = dp_total(dot(rows_x, w_up[0]))
    d_hidden = dp_total(dot(rows_d, w_down[0], 1, 1)) * scale
    sigmoid = jax.nn.sigmoid(gate_pre)
    hidden = (gate_pre * sigmoid * up_pre).astype(jnp.bfloat16)
    d_gate = (d_hidden * up_pre * sigmoid * (1.0 + gate_pre * (1.0 - sigmoid))).astype(jnp.bfloat16)
    d_up = (d_hidden * gate_pre * sigmoid).astype(jnp.bfloat16)
    out_rows = (dot(hidden, w_down[0]) * scale).astype(jnp.bfloat16)
    grad_rows = (dot(d_gate, w_gate[0], 1, 1) + dot(d_up, w_up[0], 1, 1)).astype(jnp.bfloat16)
    mixed = lax.psum_scatter(
        dot(place, out_rows).astype(jnp.bfloat16), PLANE, scatter_dimension=0, tiled=True
    )
    grad = lax.psum_scatter(
        dot(place, grad_rows).astype(jnp.bfloat16), PLANE, scatter_dimension=0, tiled=True
    )
    return mixed, grad


def solution(mesh):
    rows = P(PLANE, "dp")
    placed = (
        rows,
        rows,
        P(PLANE, None),
        P(PLANE, None),
        P(PLANE, "dp", None),
        P(PLANE, "dp", None),
        P(PLANE, None, "dp"),
    )
    return jax.shard_map(
        on_device, mesh=mesh, in_specs=placed, out_specs=(rows, rows), check_vma=False
    )
```

time: 199 us -> 270 us (1.36)
  blocking collectives: 33.8 us -> 115 us
  waiting for transfers between devices: 76.6 us -> 116 us
  starting transfers between devices: 28.3 us -> 3.56 us
  local copies, waits for them, and re-layouts: 20.3 us -> 0.11 us
  other arithmetic: 6.66 us -> 0.79 us
    all_gather x3, blocking collectives: 18.3 us -> 115 us  [the longest x1 41.9 us: on_device(): all_d = lax.all_gather(cotangent, PLANE, axis=0, tiled=True)]
    reduce_scatter x3 -> x2, waiting for transfers between devices: 26.1 us -> 112 us  [the longest x1 60.6 us: on_device(): lax.psum_scatter(dot(place, out_rows).astype(jnp.bfloat16), PLANE, scatte...]
    all_to_all x7 -> x0, waiting for transfers between devices: 50.4 us -> none  [the longest x1 11.8 us: on_device(): lax.all_to_all(lax.all_to_all(grad_rows.reshape(send_shape), 'group', spl...]
    all_to_all x7 -> x0, starting transfers between devices: 28.2 us -> none  [the longest x1 5.52 us: on_device(): lax.all_to_all(lax.all_to_all(send_d.reshape(send_shape), 'group', split_...]
    all_to_all x1 -> x0, blocking collectives: 15.5 us -> none  [on_device(): lax.all_to_all(lax.all_to_all(send_x.reshape(send_shape), 'group', split_...]
    gather x10 -> x0, local copies, waits for them, and re-layouts: 5.65 us -> none  [the longest x5 1.58 us: on_device(): slot_rank = jnp.take_along_axis(before, expert_ids, axis=1)]
    all_to_all x8 -> x0, local copies, waits for them, and re-layouts: 5.17 us -> none  [the longest x1 1.13 us: on_device(): lax.all_to_all(send_d.reshape(send_shape), 'group', split_axis=0, concat_...]
    reshape x9 -> x0, local copies, waits for them, and re-layouts: 3.86 us -> none  [the longest x1 1.11 us: on_device(): out_rows.reshape(send_shape)]
  transfers between devices with their start and end apart: 10 -> 5, of which waited for: 8 -> 4; matrix products, arithmetic and copies ran while one was open for 12% -> 5% of each run, Pallas kernels for 0% -> 0%
where the time goes in v1:
time: 270 us
  waiting for transfers between devices  116 us (43%)
  blocking collectives  115 us (43%)
  matrix products  21.3 us (8%)
  between operations  14.1 us (5%)
  starting transfers between devices  3.56 us (1%)
    reduce_scatter x1, waiting for transfers between devices, on_device(): lax.psum_scatter(dot(place, out_rows).astype(jnp.bfloat16), PLANE, scatte...  60.6 us
    reduce_scatter x1, waiting for transfers between devices, on_device(): lax.psum_scatter(dot(place, grad_rows).astype(jnp.bfloat16), PLANE, scatt...  51.8 us
    all_gather x1, blocking collectives, on_device(): all_d = lax.all_gather(cotangent, PLANE, axis=0, tiled=True)  41.9 us
    all_gather x1, blocking collectives, on_device(): all_x = lax.all_gather(tokens, PLANE, axis=0, tiled=True)  38.2 us
    all_gather x1, blocking collectives, on_device(): routing = lax.all_gather(routing, PLANE, axis=0, tiled=True)  34.4 us
    dot_general x9, matrix products, dot(): lax.dot_general(left, right, (((left_dim,), (right_dim,)), ((), ())), pre...  21.3 us
  transfers between devices with their start and end apart: 5, of which 4 were waited for; matrix products, arithmetic and copies ran while one was open for 5% of the time, Pallas kernels for 0%

profile of v1, /device:TPU:0, one launch (start us, length us, event | category | flops | bytes accessed | tf_op | source)
XLA Modules:
  0.0 270.1 jit_solution(3984503619322240361)
XLA Ops:
  7.2 0.0 reduce-scatter.5.cloned.1.call-start
  7.2 0.7 add_bitcast_fusion
  7.9 34.4 %all-gather = s32[16,16,8]{1,2,0:T(8,128)S(1)} all-gather(s32[1,16,8]{1,2,0:T(8,128)S(1)} %add_bitcast_fusion), channel_id=1, replica_groups=mesh['group'=4,'ingroup'=4,'dp'=2] {'group','ingroup'}, dimensions={0}, use_global_device_ids=true | all-gather | bytes 8704 | tf_op jit(solution)/shard_map/all_gather | solution.py:38
  42.3 0.1 reshape.155
  42.4 38.2 %all_gather.10 = bf16[256,1792]{1,0:T(8,128)(2,1)S(1)} all-gather(bf16[16,1792]{1,0:T(8,128)(2,1)} %param.7), channel_id=1, replica_groups=mesh['group'=4,'ingroup'=4,'dp'=2] {'group','ingroup'}, dimensions={0}, use_global_device_ids=true | all-gather | bytes 974848 | tf_op jit(solution)/shard_map/all_gather | solution.py:39
  80.7 0.3 fusion.30
  81.0 0.3 convolution_convert_fusion.3
  81.3 3.4 %fusion.65 = (bf16[128,1024]{1,0:T(8,128)(2,1)}, f32[128,1024]{1,0:T(8,128)S(1)}) fusion(bf16[128,1792]{1,0:T(8,128)(2,1)S(1)} %convolution_convert_fusion.3, bf16[1,1792,1024]{2,1,0:T(8,128)(2,1)} %param.11), kind=kOutput, calls=%fused_computation.77 | convolution fusion | flops 469893120 | bytes 4915200 | tf_op jit(solution)/shard_map/dot_general | solution.py:10
  84.7 1.5 collective-permute-start
  86.3 41.9 %all_gather.11 = bf16[256,1792]{1,0:T(8,128)(2,1)S(1)} all-gather(bf16[16,1792]{1,0:T(8,128)(2,1)S(1)} %copy-done.1), channel_id=1, replica_groups=mesh['group'=4,'ingroup'=4,'dp'=2] {'group','ingroup'}, dimensions={0}, use_global_device_ids=true | all-gather | bytes 974848 | tf_op jit(solution)/shard_map/all_gather | solution.py:40
  128.2 4.0 %fusion.66 = (bf16[128,1024]{1,0:T(8,128)(2,1)}, f32[128,1024]{1,0:T(8,128)S(1)}) fusion(bf16[1,1024,1792]{2,1,0:T(8,128)(2,1)} %param.13, pred[256,128]{1,0:T(32,128)(4,1)S(1)} %fusion.30, bf16[256,1792]{1,0:T(8,128)(2,1)S(1)} %all_gather.11), kind=kOutput, calls=%fused_computation.78 | convolution fusion | flops 587563008 | bytes 5406720 | tf_op jit(solution)/shard_map/dot_general | solution.py:10
  132.2 0.0 collective-permute-start.2
  132.3 2.8 %fusion.64 = (bf16[128,1024]{1,0:T(8,128)(2,1)S(1)}, f32[128,1024]{1,0:T(8,128)S(1)}) fusion(bf16[128,1792]{1,0:T(8,128)(2,1)S(1)} %convolution_convert_fusion.3, bf16[1,1792,1024]{2,1,0:T(8,128)(2,1)} %param.12), kind=kOutput, calls=%fused_computation.76 | convolution fusion | flops 469893120 | bytes 4915200 | tf_op jit(solution)/shard_map/dot_general | solution.py:10
  135.1 1.9 collective-permute-start.1
  137.0 0.1 fusion.52
  137.2 1.9 collective-permute-done.2
  139.1 1.5 fusion.4
  140.6 1.3 collective-permute-done.1
  142.0 4.9 %convolution_convert_fusion = bf16[256,1792]{1,0:T(8,128)(2,1)} fusion(pred[256,128]{1,0:T(32,128)(4,1)S(1)} %fusion.30, f32[128,1792]{1,0:T(8,128)S(1)} %fusion.4, bf16[1,1792,1024]{2,1,0:T(8,128)(2,1)} %param.11, f32[128,1024]{1,0:T(8,128)S(1)} %get-tuple-element.7, bf16[128,1024]{1,0:T(8,128)(2,1)S(1)} %collective-permute-done.1, ...), kind=kOutput, calls=%fused_computation.12 | convolution fusion | flops 590348288 | bytes 7897600 | tf_op jit(solution)/shard_map/dot_general | solution.py:10
  146.8 0.0 reduce-scatter.5.cloned.1.call-update
  146.8 0.0 reduce-scatter.3.cloned.1.call-start
  146.9 3.9 %convolution_convert_fusion.1 = bf16[256,1792]{1,0:T(8,128)(2,1)} fusion(pred[256,128]{1,0:T(32,128)(4,1)S(1)} %fusion.30, bf16[1,1024,1792]{2,1,0:T(8,128)(2,1)} %param.13, f32[128]{0:T(128)S(1)} %multiply_bitcast_fusion, f32[128,1024]{1,0:T(8,128)S(1)} %get-tuple-element.7, bf16[128,1024]{1,0:T(8,128)(2,1)S(1)} %collective-permute-done.1, ...), kind=kOutput, calls=%fused_computation.13 | convolution fusion | flops 589430784 | bytes 6193664 | tf_op jit(solution)/shard_map/dot_general | solution.py:10
  150.9 51.8 %reduce-scatter.5.cloned.1.call-done = bf16[16,1792]{1,0:T(8,128)(2,1)} async-done(((bf16[256,1792]{1,0:T(8,128)(2,1)}), bf16[16,1792]{1,0:T(8,128)(2,1)}) %reduce-scatter.5.cloned.1.call-update) | async-done | bytes 57360 | tf_op jit(solution)/shard_map/reduce_scatter | solution.py:72
  202.7 60.6 %reduce-scatter.3.cloned.1.call-done = bf16[16,1792]{1,0:T(8,128)(2,1)} async-done(((bf16[256,1792]{1,0:T(8,128)(2,1)}), bf16[16,1792]{1,0:T(8,128)(2,1)}) %reduce-scatter.3.cloned.1.call-update) | async-done | bytes 57360 | tf_op jit(solution)/shard_map/reduce_scatter | solution.py:69
  (13 shorter events, 0.1 us)
Async XLA Ops:
  7.2 195.5 %reduce-scatter.5.cloned.1.call-start = ((), (), s32[]{:S(2)}) async-start(), calls=%async_computation.3 | async-start | bytes 974848 | tf_op jit(solution)/shard_map/reduce_scatter | solution.py:72
  80.7 5.6 %copy-start.1 = (bf16[16,1792]{1,0:T(8,128)(2,1)S(1)}, bf16[16,1792]{1,0:T(8,128)(2,1)}, u32[]{:S(2)}) copy-start(bf16[16,1792]{1,0:T(8,128)(2,1)} %param.8) | copy-start | bytes 172036
  84.7 52.5 %collective-permute-start = (bf16[128,1024]{1,0:T(8,128)(2,1)}, bf16[128,1024]{1,0:T(8,128)(2,1)S(1)}, u32[]{:S(2)}, u32[]{:S(2)}) collective-permute-start(bf16[128,1024]{1,0:T(8,128)(2,1)} %get-tuple-element.8), channel_id=1, source_target_pairs={{0,1},{1,0},{2,3},{3,2},{4,5},{5,4},{6,7},{7,6},{8,9},{9,8},{10,11... | collective-permute-start | bytes 786440 | tf_op jit(solution)/shard_map/ppermute | solution.py:24
  132.2 6.9 %copy-start = (bf16[1,1792,1024]{2,1,0:T(8,128)(2,1)S(1)}, bf16[1,1792,1024]{2,1,0:T(8,128)(2,1)}, u32[]{:S(2)}) copy-start(bf16[1,1792,1024]{2,1,0:T(8,128)(2,1)} %param.12) | copy-start | bytes 11010052
  132.2 6.9 %collective-permute-start.2 = (bf16[128,1024]{1,0:T(8,128)(2,1)}, bf16[128,1024]{1,0:T(8,128)(2,1)S(1)}, u32[]{:S(2)}, u32[]{:S(2)}) collective-permute-start(bf16[128,1024]{1,0:T(8,128)(2,1)} %get-tuple-element.10), channel_id=1, source_target_pairs={{0,1},{1,0},{2,3},{3,2},{4,5},{5,4},{6,7},{7,6},{8,9},{9,8},{10,11... | collective-permute-start | bytes 786440 | tf_op jit(solution)/shard_map/ppermute | solution.py:24
  135.1 6.8 %collective-permute-start.1 = (bf16[128,1024]{1,0:T(8,128)(2,1)S(1)}, bf16[128,1024]{1,0:T(8,128)(2,1)S(1)}, u32[]{:S(2)}, u32[]{:S(2)}) collective-permute-start(bf16[128,1024]{1,0:T(8,128)(2,1)S(1)} %get-tuple-element.6), channel_id=1, source_target_pairs={{0,1},{1,0},{2,3},{3,2},{4,5},{5,4},{6,7},{7,6},{8,9},{9,8},{10,11... | collective-permute-start | bytes 786440 | tf_op jit(solution)/shard_map/ppermute | solution.py:24
  146.8 116.4 %reduce-scatter.3.cloned.1.call-start = ((), (), s32[]{:S(2)}) async-start(), calls=%async_computation.2 | async-start | bytes 974848 | tf_op jit(solution)/shard_map/reduce_scatter | solution.py:69
Sparse Core Ops, SparseCore 0:
  147.0 55.6 reduce-scatter.4
  207.2 55.9 reduce-scatter.2

commit v2 on v1

v2 whole, which is shorter than its diff:
```python
import functools

import jax
import jax.numpy as jnp
from jax import lax
from jax.experimental import pallas as pl
from jax.experimental.pallas import tpu as pltpu
from jax.sharding import PartitionSpec as P

PLANE = ("group", "ingroup")
LANES = 128
CHUNK = 256
BF16 = jnp.bfloat16
F32 = jnp.float32


def dot(left, right, left_dim=1, right_dim=0):
    return lax.dot_general(
        left, right, (((left_dim,), (right_dim,)), ((), ())), preferred_element_type=F32
    )


def call(body, outs, args, flops=0, limit=16):
    shapes = [jax.ShapeDtypeStruct(shape, dtype) for shape, dtype in outs]
    moved = sum(a.size * a.dtype.itemsize for a in args)
    moved += sum(s.size * s.dtype.itemsize for s in shapes)
    specs = [
        pl.BlockSpec(memory_space=pltpu.SMEM if a.shape == (1,) else pltpu.VMEM) for a in args
    ]
    return pl.pallas_call(
        body,
        out_shape=shapes,
        in_specs=specs,
        out_specs=[pl.BlockSpec(memory_space=pltpu.VMEM)] * len(shapes),
        compiler_params=pltpu.CompilerParams(vmem_limit_bytes=limit << 20),
        cost_estimate=pl.CostEstimate(flops=flops, bytes_accessed=moved, transcendentals=0),
    )(*args)


def swap(value, axis, offset):
    return lax.ppermute(value, axis, [(i, i ^ offset) for i in range(lax.axis_size(axis))])


def bits_of(axis):
    bits, bit = [], lax.axis_size(axis) // 2
    while bit:
        bits.append(bit)
        bit //= 2
    return bits


def payload_body(wide, tokens, ids, gate, out):
    topk, block = ids.shape
    features = tokens.shape[1]
    rows = jnp.concatenate(
        [
            ids[...].astype(F32),
            (gate[...] >> 8).astype(F32),
            (gate[...] & 255).astype(F32),
            jnp.zeros((LANES - 3 * topk, block), F32),
        ],
        axis=0,
    ).astype(BF16)
    eye = lax.broadcasted_iota(jnp.int32, (block, block), 0) == lax.broadcasted_iota(
        jnp.int32, (block, block), 1
    )
    if wide != features:
        out[...] = jnp.zeros_like(out)
    out[:, :features] = tokens[...]
    out[:, wide:] = dot(jnp.where(eye, 1.0, 0.0).astype(BF16), rows, 1, 1).astype(BF16)


def pack_body(count, *refs):
    parts, out = refs[:count], refs[-1]
    at = 0
    for part in parts:
        out[at : at + part.shape[0]] = part[...]
        at += part.shape[0]


def pack_with_body(left, right, other, out, other_out):
    out[: left.shape[0]] = left[...]
    out[left.shape[0] :] = right[...]
    other_out[...] = other[...]


def pack(parts):
    rows = sum(p.shape[0] for p in parts)
    shape = (rows, parts[0].shape[1])
    return call(functools.partial(pack_body, len(parts)), [(shape, parts[0].dtype)], parts)[0]


def spread(own, follower=None):
    inner, outer = bits_of("ingroup"), bits_of("group")
    current = own
    for bit in inner[:-1]:
        received = swap(current, "ingroup", bit)
        if follower is not None and current is own:
            shape = (2 * own.shape[0], own.shape[1])
            current, follower = call(
                pack_with_body,
                [(shape, own.dtype), (follower.shape, follower.dtype)],
                [current, received, follower],
            )
        else:
            current = pack([current, received])
    beside = swap(current, "ingroup", inner[-1])
    across = swap(current, "group", outer[0])
    last = swap(beside, "group", outer[0])
    held = [current, beside, across, last]
    for bit in outer[1:]:
        held = held + [swap(pack(held[:-1]), "group", bit), swap(held[-1], "group", bit)]
    return held, follower


def route_body(wide, topk, block, capacity, count, me, *refs):
    parts, (weight, place_out, scale_out, rows_out, part_out, sent_out) = (
        refs[:count],
        refs[count:],
    )
    features = weight.shape[0]
    total, slots = place_out.shape
    routing = jnp.concatenate([p[:, wide : wide + LANES] for p in parts], axis=0)
    lane = lax.broadcasted_iota(jnp.int32, (total, LANES), 1)
    match = (routing.astype(F32) == me[0].astype(F32)) & (lane < topk)
    source = lax.broadcasted_iota(jnp.int32, (LANES, LANES), 0)
    target = lax.broadcasted_iota(jnp.int32, (LANES, LANES), 1)

    def gate_half(offset):
        moved = dot(routing, jnp.where(source == target + offset, 1.0, 0.0).astype(BF16))
        own = jnp.where(match, moved, 0.0).astype(BF16)
        return dot(own, jnp.ones((LANES, LANES), BF16)).astype(BF16)

    named = dot(jnp.where(match, 1.0, 0.0).astype(BF16), jnp.ones((LANES, slots), BF16))
    chunk = min(total, CHUNK)
    row = lax.broadcasted_iota(jnp.int32, (chunk, chunk), 0)
    col = lax.broadcasted_iota(jnp.int32, (chunk, chunk), 1)
    earlier = jnp.where((row // block == col // block) & (row > col), 1.0, 0.0).astype(BF16)
    named_half = named.astype(BF16)
    rank = jnp.concatenate(
        [dot(earlier, named_half[i : i + chunk]) for i in range(0, total, chunk)], axis=0
    )
    start = lax.broadcasted_iota(jnp.int32, (total, slots), 0) // block * capacity
    slot = lax.broadcasted_iota(jnp.int32, (total, slots), 1) - start
    place = jnp.where((named > 0.5) & (rank == slot.astype(F32)), 1.0, 0.0).astype(BF16)
    place_out[...] = place
    high = dot(place, gate_half(topk), 0, 0)
    low = dot(place, gate_half(2 * topk), 0, 0)
    scale_out[...] = (high * 256.0 + low) / 65536.0
    values = jnp.concatenate([p[:, :features] for p in parts], axis=0)
    rows = dot(place, values, 0, 0).astype(BF16)
    rows_out[...] = rows
    part = dot(rows, weight[...])
    part_out[...] = part
    sent_out[...] = part.astype(BF16)


def up_body(rows, weight, part_out, sent_out):
    part = dot(rows[...], weight[...])
    part_out[...] = part
    sent_out[...] = part.astype(BF16)


def back_body(count, *refs):
    parts, (place, weight, part_out, sent_out) = refs[:count], refs[count:]
    values = jnp.concatenate([p[...] for p in parts], axis=0)
    rows = dot(place[...], values, 0, 0).astype(BF16)
    part = dot(rows, weight[...], 1, 1)
    part_out[...] = part
    sent_out[...] = part.astype(BF16)


def summed(own, received):
    total = own[...]
    for r in received:
        total = total + r[...].astype(F32)
    return total


def place_rows(place, rows, near_out, far_out):
    half = near_out.shape[0]
    near_out[...] = dot(place[:half], rows)
    far_out[...] = dot(place[half:], rows).astype(BF16)


def out_body(peers, *refs):
    gate, up = refs[0], refs[1]
    gate_in, up_in = refs[2 : 2 + peers], refs[2 + peers : 2 + 2 * peers]
    scale, place, weight, near_out, far_out = refs[2 + 2 * peers :]
    gate_pre, up_pre = summed(gate, gate_in), summed(up, up_in)
    hidden = (gate_pre / (1.0 + jnp.exp(-gate_pre)) * up_pre).astype(BF16)
    rows = (dot(hidden, weight[...]) * scale[:, :1]).astype(BF16)
    place_rows(place, rows, near_out, far_out)


def grad_body(peers, *refs):
    gate, up, back = refs[:3]
    gate_in, up_in, back_in = (refs[3 + i * peers : 3 + (i + 1) * peers] for i in range(3))
    scale, place, gate_weight, up_weight, near_out, far_out = refs[3 + 3 * peers :]
    gate_pre, up_pre = summed(gate, gate_in), summed(up, up_in)
    d_hidden = summed(back, back_in) * scale[:, :1]
    sigmoid = 1.0 / (1.0 + jnp.exp(-gate_pre))
    d_gate = (d_hidden * up_pre * sigmoid * (1.0 + gate_pre * (1.0 - sigmoid))).astype(BF16)
    d_up = (d_hidden * gate_pre * sigmoid).astype(BF16)
    rows = (dot(d_gate, gate_weight[...], 1, 1) + dot(d_up, up_weight[...], 1, 1)).astype(BF16)
    place_rows(place, rows, near_out, far_out)


def fold_body(count, cuts, keep, *refs):
    total = keep[...]
    for received in refs[:count]:
        total = total + received[...].astype(F32)
    for (start, stop, dtype), out in zip(cuts, refs[count:]):
        out[...] = total[start:stop].astype(dtype)


def fold(keep, received, cuts):
    outs = [((stop - start, keep.shape[1]), dtype) for start, stop, dtype in cuts]
    return call(
        functools.partial(fold_body, len(received), cuts), outs, [keep] + list(received)
    )


def collect(near, far):
    inner, outer = bits_of("ingroup"), bits_of("group")
    for bit in reversed(outer[2:]):
        half = near.shape[0] // 2
        near, far = fold(
            near, [swap(far, "group", bit)], [(0, half, F32), (half, 2 * half, BF16)]
        )
    half = near.shape[0] // 2
    quarter = half // 2
    received = swap(far, "group", outer[1])
    first, second, keep_far, keep_near = fold(
        near,
        [received],
        [
            (half + quarter, 2 * half, BF16),
            (half, half + quarter, BF16),
            (quarter, half, F32),
            (0, quarter, F32),
        ],
    )
    across = swap(first, "group", outer[0])
    last = swap(second, "group", outer[0])
    (far,) = fold(keep_far, [across], [(0, quarter, BF16)])
    near, received = keep_near, [last, swap(far, "ingroup", inner[-1])]
    for bit in reversed(inner[:-1]):
        half = near.shape[0] // 2
        near, far = fold(near, received, [(0, half, F32), (half, 2 * half, BF16)])
        received = [swap(far, "ingroup", bit)]
    return fold(near, received, [(0, near.shape[0], BF16)])[0]


def from_peers(sent):
    count = lax.axis_size("dp")
    return [
        lax.ppermute(sent, "dp", [(i, (i + step) % count) for i in range(count)])
        for step in range(1, count)
    ]


def on_device(tokens, cotangent, expert_ids, gate_fixed, w_gate, w_up, w_down):
    experts = lax.axis_size("group") * lax.axis_size("ingroup")
    block, features = tokens.shape
    topk = expert_ids.shape[1]
    hidden = w_gate.shape[2]
    capacity = 2 * block // lax.axis_size("ingroup")
    slots, total = experts * capacity, experts * block
    wide = -(-features // LANES) * LANES
    peers = lax.axis_size("dp") - 1
    w_gate, w_up, w_down = w_gate[0], w_up[0], w_down[0]
    product = 2 * slots * features * hidden

    (own,) = call(
        functools.partial(payload_body, wide),
        [((block, wide + LANES), BF16)],
        [tokens, expert_ids.T, gate_fixed.T],
    )
    x_parts, cotangent = spread(own, cotangent)
    d_parts, _ = spread(cotangent)
    me = lax.axis_index(PLANE).astype(jnp.int32).reshape(1)
    sums = [((slots, hidden), F32), ((slots, hidden), BF16)]
    place, scale, rows, gate, gate_sent = call(
        functools.partial(route_body, wide, topk, block, capacity, len(x_parts)),
        [((total, slots), BF16), ((slots, LANES), F32), ((slots, features), BF16)] + sums,
        [me] + x_parts + [w_gate],
        product,
    )
    gate_in = from_peers(gate_sent)
    up, up_sent = call(up_body, sums, [rows, w_up], product)
    up_in = from_peers(up_sent)
    back, back_sent = call(
        functools.partial(back_body, len(d_parts)), sums, d_parts + [place, w_down], product
    )
    back_in = from_peers(back_sent)
    halves = [((total // 2, features), F32), ((total // 2, features), BF16)]
    mixed = collect(
        *call(
            functools.partial(out_body, peers),
            halves,
            [gate, up] + gate_in + up_in + [scale, place, w_down],
            product,
        )
    )
    grad = collect(
        *call(
            functools.partial(grad_body, peers),
            halves,
            [gate, up, back] + gate_in + up_in + back_in + [scale, place, w_gate, w_up],
            2 * product,
            24,
        )
    )
    return mixed, grad


def solution(mesh):
    rows = P(PLANE, "dp")
    placed = (
        rows,
        rows,
        P(PLANE, None),
        P(PLANE, None),
        P(PLANE, "dp", None),
        P(PLANE, "dp", None),
        P(PLANE, None, "dp"),
    )
    return jax.shard_map(
        on_device, mesh=mesh, in_specs=placed, out_specs=(rows, rows), check_vma=False
    )
```

time: 270 us -> 83.2 us (0.31)
  blocking collectives: 115 us -> 0 us
  waiting for transfers between devices: 116 us -> 37.5 us
  starting transfers between devices: 3.56 us -> 28 us
  matrix products: 21.3 us -> 0 us
  between operations: 14.1 us -> 0.82 us
  Pallas kernels: 0 us -> 9.46 us
  local copies, waits for them, and re-layouts: 0.11 us -> 7.09 us
    all_gather x3 -> x0, blocking collectives: 115 us -> none  [the longest x1 41.9 us: on_device(): all_d = lax.all_gather(cotangent, PLANE, axis=0, tiled=True)]
    reduce_scatter x2 -> x0, waiting for transfers between devices: 112 us -> none  [the longest x1 60.6 us: on_device(): lax.psum_scatter(dot(place, out_rows).astype(jnp.bfloat16), PLANE, scatte...]
    ppermute x3 -> x25, waiting for transfers between devices: 3.29 us -> 37.5 us  [the longest x22 23.5 us: swap(): lax.ppermute(value, axis, [(i, i ^ offset) for i in range(lax.axis_size(a...]
    ppermute x3 -> x25, starting transfers between devices: 3.48 us -> 28 us  [the longest x22 24.3 us: swap(): lax.ppermute(value, axis, [(i, i ^ offset) for i in range(lax.axis_size(a...]
    dot_general x9 -> x0, matrix products: 21.3 us -> none  [dot(): lax.dot_general(left, right, (((left_dim,), (right_dim,)), ((), ())), pre...]
    pallas_call x0 -> x18, Pallas kernels: none -> 9.46 us  [call(): pl.pallas_call(body, out_shape=shapes, in_specs=specs, out_specs=[pl.Bloc...]
    unnamed x5 -> x18, local copies, waits for them, and re-layouts: 0.09 us -> 7.09 us
  transfers between devices with their start and end apart: 5 -> 25, of which waited for: 4 -> 17; matrix products, arithmetic and copies ran while one was open for 5% -> 0% of each run, Pallas kernels for 0% -> 10%
where the time goes in v2:
time: 83.2 us; the launch traced here: 82.8 us
  waiting for transfers between devices  37.5 us (45%)
  starting transfers between devices  28 us (34%)
  Pallas kernels  9.46 us (11%)
  local copies, waits for them, and re-layouts  7.09 us (9%)
    ppermute x22, starting transfers between devices, swap(): lax.ppermute(value, axis, [(i, i ^ offset) for i in range(lax.axis_size(a...  24.3 us
    ppermute x22, waiting for transfers between devices, swap(): lax.ppermute(value, axis, [(i, i ^ offset) for i in range(lax.axis_size(a...  23.5 us
    ppermute x3, waiting for transfers between devices, from_peers(): lax.ppermute(sent, 'dp', [(i, (i + step) % count) for i in range(count)])  13.9 us
    pallas_call x18, Pallas kernels, call(): pl.pallas_call(body, out_shape=shapes, in_specs=specs, out_specs=[pl.Bloc...  9.46 us
    unnamed x18, local copies, waits for them, and re-layouts  7.09 us
    ppermute x3, starting transfers between devices, from_peers(): lax.ppermute(sent, 'dp', [(i, (i + step) % count) for i in range(count)])  3.67 us
  transfers between devices with their start and end apart: 25, of which 17 were waited for; matrix products, arithmetic and copies ran while one was open for 0% of the time, Pallas kernels for 10%

profile of v2, /device:TPU:0, one launch (start us, length us, event | category | flops | bytes accessed | tf_op | source)
XLA Modules:
  0.0 82.8 jit_solution(12099839091837556288)
XLA Ops:
  2.9 4.0 %collective-permute-start = (bf16[16,1920]{1,0:T(8,128)(2,1)S(1)}, bf16[16,1920]{1,0:T(8,128)(2,1)S(1)}, u32[]{:S(2)}, u32[]{:S(2)}) collective-permute-start(bf16[16,1920]{1,0:T(8,128)(2,1)S(1)} %shard_map.86.left), channel_id=1, source_target_pairs={{0,4},{2,6},{4,0},{6,2},{1,5},{3,7},{5,1},{7,3},{8,12},{10,14},{12... | collective-permute-start | bytes 184328 | tf_op jit(solution)/shard_map/ppermute | solution.py:41
  7.0 2.9 %collective-permute-done.right = bf16[16,1920]{1,0:T(8,128)(2,1)S(1)} collective-permute-done((bf16[16,1920]{1,0:T(8,128)(2,1)S(1)}, bf16[16,1920]{1,0:T(8,128)(2,1)S(1)}, u32[]{:S(2)}, u32[]{:S(2)}) %collective-permute-start) | collective-permute-done | bytes 61472 | tf_op jit(solution)/shard_map/ppermute | solution.py:41
  10.7 1.3 %collective-permute-start.1 = (bf16[32,1920]{1,0:T(8,128)(2,1)S(1)}, bf16[32,1920]{1,0:T(8,128)(2,1)S(1)}, u32[]{:S(2)}, u32[]{:S(2)}) collective-permute-start(bf16[32,1920]{1,0:T(8,128)(2,1)S(1)} %get-tuple-element.29.refs_0_), channel_id=1, source_target_pairs={{0,2},{2,0},{4,6},{6,4},{1,3},{3,1},{5,7},{7,5},{8,10},{10,8},{12,... | collective-permute-start | bytes 368648 | tf_op jit(solution)/shard_map/ppermute | solution.py:41
  12.0 1.5 %collective-permute-start.2 = (bf16[32,1920]{1,0:T(8,128)(2,1)S(1)}, bf16[32,1920]{1,0:T(8,128)(2,1)S(1)}, u32[]{:S(2)}, u32[]{:S(2)}) collective-permute-start(bf16[32,1920]{1,0:T(8,128)(2,1)S(1)} %get-tuple-element.29.refs_0_), channel_id=1, source_target_pairs={{0,16},{8,24},{16,0},{24,8},{1,17},{9,25},{17,1},{25,9},{2,18},{10... | collective-permute-start | bytes 368648 | tf_op jit(solution)/shard_map/ppermute | solution.py:41
  13.5 3.3 %collective-permute-start.13 = (bf16[16,1792]{1,0:T(8,128)(2,1)S(1)}, bf16[16,1792]{1,0:T(8,128)(2,1)S(1)}, u32[]{:S(2)}, u32[]{:S(2)}) collective-permute-start(bf16[16,1792]{1,0:T(8,128)(2,1)S(1)} %get-tuple-element.45.refs_0_), channel_id=1, source_target_pairs={{0,4},{2,6},{4,0},{6,2},{1,5},{3,7},{5,1},{7,3},{8,12},{10,14},{12... | collective-permute-start | bytes 172040 | tf_op jit(solution)/shard_map/ppermute | solution.py:41
  16.8 2.2 %collective-permute-done.13.refs_1_ = bf16[16,1792]{1,0:T(8,128)(2,1)S(1)} collective-permute-done((bf16[16,1792]{1,0:T(8,128)(2,1)S(1)}, bf16[16,1792]{1,0:T(8,128)(2,1)S(1)}, u32[]{:S(2)}, u32[]{:S(2)}) %collective-permute-start.13) | collective-permute-done | bytes 57376 | tf_op jit(solution)/shard_map/ppermute | solution.py:41
  19.0 1.3 %collective-permute-start.14 = (bf16[32,1792]{1,0:T(8,128)(2,1)S(1)}, bf16[32,1792]{1,0:T(8,128)(2,1)S(1)}, u32[]{:S(2)}, u32[]{:S(2)}) collective-permute-start(bf16[32,1792]{1,0:T(8,128)(2,1)S(1)} %shard_map.96.refs_0_), channel_id=1, source_target_pairs={{0,2},{2,0},{4,6},{6,4},{1,3},{3,1},{5,7},{7,5},{8,10},{10,8},{12,... | collective-permute-start | bytes 344072 | tf_op jit(solution)/shard_map/ppermute | solution.py:41
  21.4 2.5 %collective-permute-done.14.refs_1_ = bf16[32,1792]{1,0:T(8,128)(2,1)S(1)} collective-permute-done((bf16[32,1792]{1,0:T(8,128)(2,1)S(1)}, bf16[32,1792]{1,0:T(8,128)(2,1)S(1)}, u32[]{:S(2)}, u32[]{:S(2)}) %collective-permute-start.14) | collective-permute-done | bytes 114720 | tf_op jit(solution)/shard_map/ppermute | solution.py:41
  27.3 4.1 %collective-permute-done.3.refs_3_ = bf16[32,1920]{1,0:T(8,128)(2,1)S(1)} collective-permute-done((bf16[32,1920]{1,0:T(8,128)(2,1)S(1)}, bf16[32,1920]{1,0:T(8,128)(2,1)S(1)}, u32[]{:S(2)}, u32[]{:S(2)}) %collective-permute-start.3) | collective-permute-done | bytes 122912 | tf_op jit(solution)/shard_map/ppermute | solution.py:41
  31.4 2.0 %collective-permute-done.16.refs_3_ = bf16[32,1792]{1,0:T(8,128)(2,1)S(1)} collective-permute-done((bf16[32,1792]{1,0:T(8,128)(2,1)S(1)}, bf16[32,1792]{1,0:T(8,128)(2,1)S(1)}, u32[]{:S(2)}, u32[]{:S(2)}) %collective-permute-start.16) | collective-permute-done | bytes 114720 | tf_op jit(solution)/shard_map/ppermute | solution.py:41
  33.4 2.0 %copy-done.1 = bf16[1,1792,1024]{2,1,0:T(8,128)(2,1)S(1)} copy-done((bf16[1,1792,1024]{2,1,0:T(8,128)(2,1)S(1)}, bf16[1,1792,1024]{2,1,0:T(8,128)(2,1)}, u32[]{:S(2)}) %copy-start.1) | copy-done | bytes 3670040
  35.5 1.3 %shard_map.89 = (bf16[256,128]{1,0:T(8,128)(2,1)S(1)}, f32[128,128]{1,0:T(8,128)S(1)}, bf16[128,1792]{1,0:T(8,128)(2,1)S(1)}, f32[128,1024]{1,0:T(8,128)S(1)}, bf16[128,1024]{1,0:T(8,128)(2,1)S(1)}) custom-call(s32[1]{0:T(128)} %bitcast.me, bf16[32,1920]{1,0:T(8,128)(2,1)S(1)} %get-tuple-element.29.refs_0_, ...), custom_call_target="tpu_custom_call" | custom-call | flops 469762048 | bytes 6029316 | tf_op jit(solution)/shard_map/pallas_call | solution.py:30
  36.8 2.0 %copy-done.3 = bf16[1,1792,1024]{2,1,0:T(8,128)(2,1)S(1)} copy-done((bf16[1,1792,1024]{2,1,0:T(8,128)(2,1)S(1)}, bf16[1,1792,1024]{2,1,0:T(8,128)(2,1)}, u32[]{:S(2)}) %copy-start.3) | copy-done | bytes 3670040
  39.5 1.6 %collective-permute-start.7 = (bf16[128,1024]{1,0:T(8,128)(2,1)S(1)}, bf16[128,1024]{1,0:T(8,128)(2,1)S(1)}, u32[]{:S(2)}, u32[]{:S(2)}) collective-permute-start(bf16[128,1024]{1,0:T(8,128)(2,1)S(1)} %get-tuple-element.34), channel_id=1, source_target_pairs={{0,1},{1,0},{2,3},{3,2},{4,5},{5,4},{6,7},{7,6},{8,9},{9,8},{10,11... | collective-permute-start | bytes 786440 | tf_op jit(solution)/shard_map/ppermute | solution.py:258
  42.9 1.6 %collective-permute-start.19 = (bf16[128,1024]{1,0:T(8,128)(2,1)S(1)}, bf16[128,1024]{1,0:T(8,128)(2,1)S(1)}, u32[]{:S(2)}, u32[]{:S(2)}) collective-permute-start(bf16[128,1024]{1,0:T(8,128)(2,1)S(1)} %get-tuple-element.47), channel_id=1, source_target_pairs={{0,1},{1,0},{2,3},{3,2},{4,5},{5,4},{6,7},{7,6},{8,9},{9,8},{10,11... | collective-permute-start | bytes 786440 | tf_op jit(solution)/shard_map/ppermute | solution.py:258
  44.5 4.2 %collective-permute-done.7.refs_3_.refs_4_ = bf16[128,1024]{1,0:T(8,128)(2,1)S(1)} collective-permute-done((bf16[128,1024]{1,0:T(8,128)(2,1)S(1)}, bf16[128,1024]{1,0:T(8,128)(2,1)S(1)}, u32[]{:S(2)}, u32[]{:S(2)}) %collective-permute-start.7) | collective-permute-done | bytes 262176 | tf_op jit(solution)/shard_map/ppermute | solution.py:258
  48.7 5.6 %collective-permute-done.6.refs_2_.refs_3_ = bf16[128,1024]{1,0:T(8,128)(2,1)S(1)} collective-permute-done((bf16[128,1024]{1,0:T(8,128)(2,1)S(1)}, bf16[128,1024]{1,0:T(8,128)(2,1)S(1)}, u32[]{:S(2)}, u32[]{:S(2)}) %collective-permute-start.6) | collective-permute-done | bytes 262176 | tf_op jit(solution)/shard_map/ppermute | solution.py:258
  55.4 4.2 %collective-permute-done.19.refs_5_ = bf16[128,1024]{1,0:T(8,128)(2,1)S(1)} collective-permute-done((bf16[128,1024]{1,0:T(8,128)(2,1)S(1)}, bf16[128,1024]{1,0:T(8,128)(2,1)S(1)}, u32[]{:S(2)}, u32[]{:S(2)}) %collective-permute-start.19) | collective-permute-done | bytes 262176 | tf_op jit(solution)/shard_map/ppermute | solution.py:258
  59.6 3.4 %shard_map.99 = (f32[128,1792]{1,0:T(8,128)S(1)}, bf16[128,1792]{1,0:T(8,128)(2,1)S(1)}) custom-call(f32[128,1024]{1,0:T(8,128)S(1)} %get-tuple-element.30.refs_0_, f32[128,1024]{1,0:T(8,128)S(1)} %get-tuple-element.32.refs_1_, f32[128,1024]{1,0:T(8,128)S(1)} %get-tuple-element.46.refs_2_, bf16[128,1024]{1,0:T(8,128)(2,1)S(1)} %collective-permute-done.6.refs_2_.refs_3_, ...), custom_call_target="tpu_custom_call" | custom-call | flops 939524096 | bytes 11206656 | tf_op jit(solution)/shard_map/pallas_call | solution.py:30
  67.0 2.1 %collective-permute-done.10.refs_0_ = bf16[32,1792]{1,0:T(8,128)(2,1)S(1)} collective-permute-done((bf16[32,1792]{1,0:T(8,128)(2,1)S(1)}, bf16[32,1792]{1,0:T(8,128)(2,1)S(1)}, u32[]{:S(2)}, u32[]{:S(2)}) %collective-permute-start.10) | collective-permute-done | bytes 114720 | tf_op jit(solution)/shard_map/ppermute | solution.py:41
  72.5 1.6 %collective-permute-done.9.refs_0_ = bf16[32,1792]{1,0:T(8,128)(2,1)S(1)} collective-permute-done((bf16[32,1792]{1,0:T(8,128)(2,1)S(1)}, bf16[32,1792]{1,0:T(8,128)(2,1)S(1)}, u32[]{:S(2)}, u32[]{:S(2)}) %collective-permute-start.9) | collective-permute-done | bytes 114720 | tf_op jit(solution)/shard_map/ppermute | solution.py:41
  74.6 1.7 %collective-permute-start.12 = (bf16[16,1792]{1,0:T(8,128)(2,1)S(1)}, bf16[16,1792]{1,0:T(8,128)(2,1)S(1)}, u32[]{:S(2)}, u32[]{:S(2)}) collective-permute-start(bf16[16,1792]{1,0:T(8,128)(2,1)S(1)} %get-tuple-element.44), channel_id=1, source_target_pairs={{0,4},{2,6},{4,0},{6,2},{1,5},{3,7},{5,1},{7,3},{8,12},{10,14},{12... | collective-permute-start | bytes 172040 | tf_op jit(solution)/shard_map/ppermute | solution.py:41
  76.6 2.2 %collective-permute-start.24 = (bf16[16,1792]{1,0:T(8,128)(2,1)S(1)}, bf16[16,1792]{1,0:T(8,128)(2,1)S(1)}, u32[]{:S(2)}, u32[]{:S(2)}) collective-permute-start(bf16[16,1792]{1,0:T(8,128)(2,1)S(1)} %get-tuple-element.55), channel_id=1, source_target_pairs={{0,4},{2,6},{4,0},{6,2},{1,5},{3,7},{5,1},{7,3},{8,12},{10,14},{12... | collective-permute-start | bytes 172040 | tf_op jit(solution)/shard_map/ppermute | solution.py:41
  78.8 2.5 %collective-permute-done.12.refs_0_ = bf16[16,1792]{1,0:T(8,128)(2,1)S(1)} collective-permute-done((bf16[16,1792]{1,0:T(8,128)(2,1)S(1)}, bf16[16,1792]{1,0:T(8,128)(2,1)S(1)}, u32[]{:S(2)}, u32[]{:S(2)}) %collective-permute-start.12) | collective-permute-done | bytes 57376 | tf_op jit(solution)/shard_map/ppermute | solution.py:41
  (62 shorter events, 20.8 us)
Async XLA Ops:
  2.9 6.9 %collective-permute-start = (bf16[16,1920]{1,0:T(8,128)(2,1)S(1)}, bf16[16,1920]{1,0:T(8,128)(2,1)S(1)}, u32[]{:S(2)}, u32[]{:S(2)}) collective-permute-start(bf16[16,1920]{1,0:T(8,128)(2,1)S(1)} %shard_map.86.left), channel_id=1, source_target_pairs={{0,4},{2,6},{4,0},{6,2},{1,5},{3,7},{5,1},{7,3},{8,12},{10,14},{12... | collective-permute-start | bytes 184328 | tf_op jit(solution)/shard_map/ppermute | solution.py:41
  10.7 10.6 %collective-permute-start.1 = (bf16[32,1920]{1,0:T(8,128)(2,1)S(1)}, bf16[32,1920]{1,0:T(8,128)(2,1)S(1)}, u32[]{:S(2)}, u32[]{:S(2)}) collective-permute-start(bf16[32,1920]{1,0:T(8,128)(2,1)S(1)} %get-tuple-element.29.refs_0_), channel_id=1, source_target_pairs={{0,2},{2,0},{4,6},{6,4},{1,3},{3,1},{5,7},{7,5},{8,10},{10,8},{12,... | collective-permute-start | bytes 368648 | tf_op jit(solution)/shard_map/ppermute | solution.py:41
  12.0 9.3 %collective-permute-start.2 = (bf16[32,1920]{1,0:T(8,128)(2,1)S(1)}, bf16[32,1920]{1,0:T(8,128)(2,1)S(1)}, u32[]{:S(2)}, u32[]{:S(2)}) collective-permute-start(bf16[32,1920]{1,0:T(8,128)(2,1)S(1)} %get-tuple-element.29.refs_0_), channel_id=1, source_target_pairs={{0,16},{8,24},{16,0},{24,8},{1,17},{9,25},{17,1},{25,9},{2,18},{10... | collective-permute-start | bytes 368648 | tf_op jit(solution)/shard_map/ppermute | solution.py:41
  13.5 5.5 %collective-permute-start.13 = (bf16[16,1792]{1,0:T(8,128)(2,1)S(1)}, bf16[16,1792]{1,0:T(8,128)(2,1)S(1)}, u32[]{:S(2)}, u32[]{:S(2)}) collective-permute-start(bf16[16,1792]{1,0:T(8,128)(2,1)S(1)} %get-tuple-element.45.refs_0_), channel_id=1, source_target_pairs={{0,4},{2,6},{4,0},{6,2},{1,5},{3,7},{5,1},{7,3},{8,12},{10,14},{12... | collective-permute-start | bytes 172040 | tf_op jit(solution)/shard_map/ppermute | solution.py:41
  19.0 4.9 %collective-permute-start.14 = (bf16[32,1792]{1,0:T(8,128)(2,1)S(1)}, bf16[32,1792]{1,0:T(8,128)(2,1)S(1)}, u32[]{:S(2)}, u32[]{:S(2)}) collective-permute-start(bf16[32,1792]{1,0:T(8,128)(2,1)S(1)} %shard_map.96.refs_0_), channel_id=1, source_target_pairs={{0,2},{2,0},{4,6},{6,4},{1,3},{3,1},{5,7},{7,5},{8,10},{10,8},{12,... | collective-permute-start | bytes 344072 | tf_op jit(solution)/shard_map/ppermute | solution.py:41
  20.3 4.8 %collective-permute-start.15 = (bf16[32,1792]{1,0:T(8,128)(2,1)S(1)}, bf16[32,1792]{1,0:T(8,128)(2,1)S(1)}, u32[]{:S(2)}, u32[]{:S(2)}) collective-permute-start(bf16[32,1792]{1,0:T(8,128)(2,1)S(1)} %shard_map.96.refs_0_), channel_id=1, source_target_pairs={{0,16},{8,24},{16,0},{24,8},{1,17},{9,25},{17,1},{25,9},{2,18},{10... | collective-permute-start | bytes 344072 | tf_op jit(solution)/shard_map/ppermute | solution.py:41
  21.3 12.1 %collective-permute-start.4 = (bf16[96,1920]{1,0:T(8,128)(2,1)S(1)}, bf16[96,1920]{1,0:T(8,128)(2,1)S(1)}, u32[]{:S(2)}, u32[]{:S(2)}) collective-permute-start(bf16[96,1920]{1,0:T(8,128)(2,1)S(1)} %shard_map.88), channel_id=1, source_target_pairs={{0,8},{8,0},{16,24},{24,16},{1,9},{9,1},{17,25},{25,17},{2,10},{10... | collective-permute-start | bytes 1105928 | tf_op jit(solution)/shard_map/ppermute | solution.py:41
  25.1 16.5 %collective-permute-start.17 = (bf16[96,1792]{1,0:T(8,128)(2,1)S(1)}, bf16[96,1792]{1,0:T(8,128)(2,1)S(1)}, u32[]{:S(2)}, u32[]{:S(2)}) collective-permute-start(bf16[96,1792]{1,0:T(8,128)(2,1)S(1)} %shard_map.97), channel_id=1, source_target_pairs={{0,8},{8,0},{16,24},{24,16},{1,9},{9,1},{17,25},{25,17},{2,10},{10... | collective-permute-start | bytes 1032200 | tf_op jit(solution)/shard_map/ppermute | solution.py:41
  25.2 6.2 %collective-permute-start.3 = (bf16[32,1920]{1,0:T(8,128)(2,1)S(1)}, bf16[32,1920]{1,0:T(8,128)(2,1)S(1)}, u32[]{:S(2)}, u32[]{:S(2)}) collective-permute-start(bf16[32,1920]{1,0:T(8,128)(2,1)S(1)} %collective-permute-done.1.refs_1_), channel_id=1, source_target_pairs={{0,16},{8,24},{16,0},{24,8},{1,17},{9,25},{17,1},{25,9},{2,18},{10... | collective-permute-start | bytes 368648 | tf_op jit(solution)/shard_map/ppermute | solution.py:41
  26.2 7.2 %collective-permute-start.16 = (bf16[32,1792]{1,0:T(8,128)(2,1)S(1)}, bf16[32,1792]{1,0:T(8,128)(2,1)S(1)}, u32[]{:S(2)}, u32[]{:S(2)}) collective-permute-start(bf16[32,1792]{1,0:T(8,128)(2,1)S(1)} %collective-permute-done.14.refs_1_), channel_id=1, source_target_pairs={{0,16},{8,24},{16,0},{24,8},{1,17},{9,25},{17,1},{25,9},{2,18},{10... | collective-permute-start | bytes 344072 | tf_op jit(solution)/shard_map/ppermute | solution.py:41
  31.4 2.0 %collective-permute-start.5 = (bf16[32,1920]{1,0:T(8,128)(2,1)S(1)}, bf16[32,1920]{1,0:T(8,128)(2,1)S(1)}, u32[]{:S(2)}, u32[]{:S(2)}) collective-permute-start(bf16[32,1920]{1,0:T(8,128)(2,1)S(1)} %collective-permute-done.3.refs_3_), channel_id=1, source_target_pairs={{0,8},{8,0},{16,24},{24,16},{1,9},{9,1},{17,25},{25,17},{2,10},{10... | collective-permute-start | bytes 368648 | tf_op jit(solution)/shard_map/ppermute | solution.py:41
  33.4 8.2 %collective-permute-start.18 = (bf16[32,1792]{1,0:T(8,128)(2,1)S(1)}, bf16[32,1792]{1,0:T(8,128)(2,1)S(1)}, u32[]{:S(2)}, u32[]{:S(2)}) collective-permute-start(bf16[32,1792]{1,0:T(8,128)(2,1)S(1)} %collective-permute-done.16.refs_3_), channel_id=1, source_target_pairs={{0,8},{8,0},{16,24},{24,16},{1,9},{9,1},{17,25},{25,17},{2,10},{10... | collective-permute-start | bytes 344072 | tf_op jit(solution)/shard_map/ppermute | solution.py:41
  39.5 9.2 %collective-permute-start.7 = (bf16[128,1024]{1,0:T(8,128)(2,1)S(1)}, bf16[128,1024]{1,0:T(8,128)(2,1)S(1)}, u32[]{:S(2)}, u32[]{:S(2)}) collective-permute-start(bf16[128,1024]{1,0:T(8,128)(2,1)S(1)} %get-tuple-element.34), channel_id=1, source_target_pairs={{0,1},{1,0},{2,3},{3,2},{4,5},{5,4},{6,7},{7,6},{8,9},{9,8},{10,11... | collective-permute-start | bytes 786440 | tf_op jit(solution)/shard_map/ppermute | solution.py:258
  41.1 13.2 %collective-permute-start.6 = (bf16[128,1024]{1,0:T(8,128)(2,1)S(1)}, bf16[128,1024]{1,0:T(8,128)(2,1)S(1)}, u32[]{:S(2)}, u32[]{:S(2)}) collective-permute-start(bf16[128,1024]{1,0:T(8,128)(2,1)S(1)} %get-tuple-element.33), channel_id=1, source_target_pairs={{0,1},{1,0},{2,3},{3,2},{4,5},{5,4},{6,7},{7,6},{8,9},{9,8},{10,11... | collective-permute-start | bytes 786440 | tf_op jit(solution)/shard_map/ppermute | solution.py:258
  42.9 16.6 %collective-permute-start.19 = (bf16[128,1024]{1,0:T(8,128)(2,1)S(1)}, bf16[128,1024]{1,0:T(8,128)(2,1)S(1)}, u32[]{:S(2)}, u32[]{:S(2)}) collective-permute-start(bf16[128,1024]{1,0:T(8,128)(2,1)S(1)} %get-tuple-element.47), channel_id=1, source_target_pairs={{0,1},{1,0},{2,3},{3,2},{4,5},{5,4},{6,7},{7,6},{8,9},{9,8},{10,11... | collective-permute-start | bytes 786440 | tf_op jit(solution)/shard_map/ppermute | solution.py:258
  55.3 7.7 %collective-permute-start.8 = (bf16[128,1792]{1,0:T(8,128)(2,1)S(1)}, bf16[128,1792]{1,0:T(8,128)(2,1)S(1)}, u32[]{:S(2)}, u32[]{:S(2)}) collective-permute-start(bf16[128,1792]{1,0:T(8,128)(2,1)S(1)} %get-tuple-element.38), channel_id=1, source_target_pairs={{0,8},{8,0},{16,24},{24,16},{1,9},{9,1},{17,25},{25,17},{2,10},{10... | collective-permute-start | bytes 1376264 | tf_op jit(solution)/shard_map/ppermute | solution.py:41
  63.1 6.0 %collective-permute-start.10 = (bf16[32,1792]{1,0:T(8,128)(2,1)S(1)}, bf16[32,1792]{1,0:T(8,128)(2,1)S(1)}, u32[]{:S(2)}, u32[]{:S(2)}) collective-permute-start(bf16[32,1792]{1,0:T(8,128)(2,1)S(1)} %get-tuple-element.42), channel_id=1, source_target_pairs={{0,16},{8,24},{16,0},{24,8},{1,17},{9,25},{17,1},{25,9},{2,18},{10... | collective-permute-start | bytes 344072 | tf_op jit(solution)/shard_map/ppermute | solution.py:41
  64.9 6.7 %collective-permute-start.22 = (bf16[32,1792]{1,0:T(8,128)(2,1)S(1)}, bf16[32,1792]{1,0:T(8,128)(2,1)S(1)}, u32[]{:S(2)}, u32[]{:S(2)}) collective-permute-start(bf16[32,1792]{1,0:T(8,128)(2,1)S(1)} %get-tuple-element.53), channel_id=1, source_target_pairs={{0,16},{8,24},{16,0},{24,8},{1,17},{9,25},{17,1},{25,9},{2,18},{10... | collective-permute-start | bytes 344072 | tf_op jit(solution)/shard_map/ppermute | solution.py:41
  65.9 8.1 %collective-permute-start.9 = (bf16[32,1792]{1,0:T(8,128)(2,1)S(1)}, bf16[32,1792]{1,0:T(8,128)(2,1)S(1)}, u32[]{:S(2)}, u32[]{:S(2)}) collective-permute-start(bf16[32,1792]{1,0:T(8,128)(2,1)S(1)} %get-tuple-element.40), channel_id=1, source_target_pairs={{0,16},{8,24},{16,0},{24,8},{1,17},{9,25},{17,1},{25,9},{2,18},{10... | collective-permute-start | bytes 344072 | tf_op jit(solution)/shard_map/ppermute | solution.py:41
  69.2 5.3 %collective-permute-start.11 = (bf16[32,1792]{1,0:T(8,128)(2,1)S(1)}, bf16[32,1792]{1,0:T(8,128)(2,1)S(1)}, u32[]{:S(2)}, u32[]{:S(2)}) collective-permute-start(bf16[32,1792]{1,0:T(8,128)(2,1)S(1)} %shard_map.93), channel_id=1, source_target_pairs={{0,2},{2,0},{4,6},{6,4},{1,3},{3,1},{5,7},{7,5},{8,10},{10,8},{12,... | collective-permute-start | bytes 344072 | tf_op jit(solution)/shard_map/ppermute | solution.py:41
  70.0 6.3 %collective-permute-start.21 = (bf16[32,1792]{1,0:T(8,128)(2,1)S(1)}, bf16[32,1792]{1,0:T(8,128)(2,1)S(1)}, u32[]{:S(2)}, u32[]{:S(2)}) collective-permute-start(bf16[32,1792]{1,0:T(8,128)(2,1)S(1)} %get-tuple-element.51), channel_id=1, source_target_pairs={{0,16},{8,24},{16,0},{24,8},{1,17},{9,25},{17,1},{25,9},{2,18},{10... | collective-permute-start | bytes 344072 | tf_op jit(solution)/shard_map/ppermute | solution.py:41
  71.6 4.9 %collective-permute-start.23 = (bf16[32,1792]{1,0:T(8,128)(2,1)S(1)}, bf16[32,1792]{1,0:T(8,128)(2,1)S(1)}, u32[]{:S(2)}, u32[]{:S(2)}) collective-permute-start(bf16[32,1792]{1,0:T(8,128)(2,1)S(1)} %shard_map.101), channel_id=1, source_target_pairs={{0,2},{2,0},{4,6},{6,4},{1,3},{3,1},{5,7},{7,5},{8,10},{10,8},{12,... | collective-permute-start | bytes 344072 | tf_op jit(solution)/shard_map/ppermute | solution.py:41
  74.6 6.7 %collective-permute-start.12 = (bf16[16,1792]{1,0:T(8,128)(2,1)S(1)}, bf16[16,1792]{1,0:T(8,128)(2,1)S(1)}, u32[]{:S(2)}, u32[]{:S(2)}) collective-permute-start(bf16[16,1792]{1,0:T(8,128)(2,1)S(1)} %get-tuple-element.44), channel_id=1, source_target_pairs={{0,4},{2,6},{4,0},{6,2},{1,5},{3,7},{5,1},{7,3},{8,12},{10,14},{12... | collective-permute-start | bytes 172040 | tf_op jit(solution)/shard_map/ppermute | solution.py:41
  76.6 5.6 %collective-permute-start.24 = (bf16[16,1792]{1,0:T(8,128)(2,1)S(1)}, bf16[16,1792]{1,0:T(8,128)(2,1)S(1)}, u32[]{:S(2)}, u32[]{:S(2)}) collective-permute-start(bf16[16,1792]{1,0:T(8,128)(2,1)S(1)} %get-tuple-element.55), channel_id=1, source_target_pairs={{0,4},{2,6},{4,0},{6,2},{1,5},{3,7},{5,1},{7,3},{8,12},{10,14},{12... | collective-permute-start | bytes 172040 | tf_op jit(solution)/shard_map/ppermute | solution.py:41
  (10 other events, 49.7 us)

commit v3 on v2

--- a/solution.py
+++ b/solution.py
@@ -20,21 +20,36 @@
     )
 
 
-def call(body, outs, args, flops=0, limit=16):
+def call(name, body, outs, args, flops=0, limit=16, hbm=(), passed=(), scratch=(), weight=1):
     shapes = [jax.ShapeDtypeStruct(shape, dtype) for shape, dtype in outs]
     moved = sum(a.size * a.dtype.itemsize for a in args)
     moved += sum(s.size * s.dtype.itemsize for s in shapes)
     specs = [
-        pl.BlockSpec(memory_space=pltpu.SMEM if a.shape == (1,) else pltpu.VMEM) for a in args
+        pl.BlockSpec(
+            memory_space=pltpu.HBM if i in hbm else pltpu.SMEM if a.shape == (1,) else pltpu.VMEM
+        )
+        for i, a in enumerate(args)
     ]
-    return pl.pallas_call(
-        body,
-        out_shape=shapes,
-        in_specs=specs,
-        out_specs=[pl.BlockSpec(memory_space=pltpu.VMEM)] * len(shapes),
+    inputs, results = len(args), len(shapes)
+
+    def run(*refs):
+        ins, rest = refs[:inputs], refs[inputs + len(passed) :]
+        body(*ins, *rest[:results], *rest[results + len(passed) :])
+
+    free = pl.BlockSpec(memory_space=pl.ANY)
+    kernel = pl.pallas_call(
+        run,
+        out_shape=shapes + [jax.ShapeDtypeStruct(p.shape, p.dtype) for p in passed],
+        in_specs=specs + [free] * len(passed),
+        out_specs=[pl.BlockSpec(memory_space=pltpu.VMEM)] * results + [free] * len(passed),
+        input_output_aliases={inputs + i: results + i for i in range(len(passed))},
+        scratch_shapes=list(scratch),
         compiler_params=pltpu.CompilerParams(vmem_limit_bytes=limit << 20),
-        cost_estimate=pl.CostEstimate(flops=flops, bytes_accessed=moved, transcendentals=0),
-    )(*args)
+        name=name,
+        cost_estimate=pl.CostEstimate(flops=flops, bytes_accessed=moved * weight, transcendentals=0),
+    )
+    with jax.named_scope(name):
+        return kernel(*args, *passed)
 
 
 def swap(value, axis, offset):
@@ -49,9 +64,8 @@
     return bits
 
 
-def payload_body(wide, tokens, ids, gate, out):
+def routing_body(ids, gate, out):
     topk, block = ids.shape
-    features = tokens.shape[1]
     rows = jnp.concatenate(
         [
             ids[...].astype(F32),
@@ -64,10 +78,18 @@
     eye = lax.broadcasted_iota(jnp.int32, (block, block), 0) == lax.broadcasted_iota(
         jnp.int32, (block, block), 1
     )
+    out[...] = dot(jnp.where(eye, 1.0, 0.0).astype(BF16), rows, 1, 1).astype(BF16)
+
+
+def merge_body(near_x, far_x, near_route, far_route, out):
+    block, features = near_x.shape
+    wide = out.shape[1] - LANES
     if wide != features:
         out[...] = jnp.zeros_like(out)
-    out[:, :features] = tokens[...]
-    out[:, wide:] = dot(jnp.where(eye, 1.0, 0.0).astype(BF16), rows, 1, 1).astype(BF16)
+    out[:block, :features] = near_x[...]
+    out[block:, :features] = far_x[...]
+    out[:block, wide:] = near_route[...]
+    out[block:, wide:] = far_route[...]
 
 
 def pack_body(count, *refs):
@@ -78,39 +100,55 @@
         at += part.shape[0]
 
 
-def pack_with_body(left, right, other, out, other_out):
-    out[: left.shape[0]] = left[...]
-    out[left.shape[0] :] = right[...]
-    other_out[...] = other[...]
-
-
-def pack(parts):
-    rows = sum(p.shape[0] for p in parts)
-    shape = (rows, parts[0].shape[1])
-    return call(functools.partial(pack_body, len(parts)), [(shape, parts[0].dtype)], parts)[0]
-
-
-def spread(own, follower=None):
+def pack(parts, after=()):
+    shape = (sum(p.shape[0] for p in parts), parts[0].shape[1])
+    return call(
+        "pack",
+        functools.partial(pack_body, len(parts)),
+        [(shape, parts[0].dtype)],
+        list(parts) + list(after),
+        weight=1,
+    )[0]
+
+
+def copy_body(source, after, out):
+    out[...] = source[...]
+
+
+def copied(source, after):
+    return call("copied", copy_body, [(source.shape, source.dtype)], [source, after], weight=40)[0]
+
+
+def spread(tokens, route, cotangent):
     inner, outer = bits_of("ingroup"), bits_of("group")
-    current = own
+    block, features = tokens.shape
+    wide = -(-features // LANES) * LANES
+    first, second = None, copied(cotangent, route)
+    first, second = call(
+        "merge",
+        merge_body,
+        [((2 * block, wide + LANES), BF16)],
+        [tokens, swap(tokens, "ingroup", inner[0]), route, swap(route, "ingroup", inner[0])],
+        passed=[second],
+    )
+    for bit in inner[1:-1]:
+        first = pack([first, swap(first, "ingroup", bit)])
+    beside = swap(first, "ingroup", inner[-1])
+    across = swap(first, "group", outer[0])
+    last = swap(beside, "group", outer[0])
     for bit in inner[:-1]:
-        received = swap(current, "ingroup", bit)
-        if follower is not None and current is own:
-            shape = (2 * own.shape[0], own.shape[1])
-            current, follower = call(
-                pack_with_body,
-                [(shape, own.dtype), (follower.shape, follower.dtype)],
-                [current, received, follower],
-            )
-        else:
-            current = pack([current, received])
-    beside = swap(current, "ingroup", inner[-1])
-    across = swap(current, "group", outer[0])
+        second = pack([second, swap(second, "ingroup", bit)])
+    first = pack([first, beside, across, last], after=[second])
+    beside = swap(second, "ingroup", inner[-1])
+    across = swap(second, "group", outer[0])
     last = swap(beside, "group", outer[0])
-    held = [current, beside, across, last]
-    for bit in outer[1:]:
-        held = held + [swap(pack(held[:-1]), "group", bit), swap(held[-1], "group", bit)]
-    return held, follower
+    for bit in outer[1:-1]:
+        first = pack([first, swap(first, "group", bit)])
+    second = pack([second, beside, across, last])
+    for bit in outer[1:-1]:
+        second = pack([second, swap(second, "group", bit)])
+    first = [first, swap(first, "group", outer[-1])]
+    return first, [second, swap(second, "group", outer[-1])]
 
 
 def route_body(wide, topk, block, capacity, count, me, *refs):
@@ -186,22 +224,31 @@
 def out_body(peers, *refs):
     gate, up = refs[0], refs[1]
     gate_in, up_in = refs[2 : 2 + peers], refs[2 + peers : 2 + 2 * peers]
-    scale, place, weight, near_out, far_out = refs[2 + 2 * peers :]
+    scale, place, weight, _, near_out, far_out = refs[2 + 2 * peers :]
     gate_pre, up_pre = summed(gate, gate_in), summed(up, up_in)
     hidden = (gate_pre / (1.0 + jnp.exp(-gate_pre)) * up_pre).astype(BF16)
     rows = (dot(hidden, weight[...]) * scale[:, :1]).astype(BF16)
     place_rows(place, rows, near_out, far_out)
 
 
+def factor_body(peers, *refs):
+    gate, up = refs[0], refs[1]
+    gate_in, up_in = refs[2 : 2 + peers], refs[2 + peers : 2 + 2 * peers]
+    scale, gate_out, up_out = refs[2 + 2 * peers :]
+    gate_pre, up_pre = summed(gate, gate_in), summed(up, up_in)
+    sigmoid = 1.0 / (1.0 + jnp.exp(-gate_pre))
+    scaled = sigmoid * scale[:, :1]
+    gate_out[...] = up_pre * scaled * (1.0 + gate_pre * (1.0 - sigmoid))
+    up_out[...] = gate_pre * scaled
+
+
 def grad_body(peers, *refs):
-    gate, up, back = refs[:3]
-    gate_in, up_in, back_in = (refs[3 + i * peers : 3 + (i + 1) * peers] for i in range(3))
-    scale, place, gate_weight, up_weight, near_out, far_out = refs[3 + 3 * peers :]
-    gate_pre, up_pre = summed(gate, gate_in), summed(up, up_in)
-    d_hidden = summed(back, back_in) * scale[:, :1]
-    sigmoid = 1.0 / (1.0 + jnp.exp(-gate_pre))
-    d_gate = (d_hidden * up_pre * sigmoid * (1.0 + gate_pre * (1.0 - sigmoid))).astype(BF16)
-    d_up = (d_hidden * gate_pre * sigmoid).astype(BF16)
+    gate_factor, up_factor, back = refs[:3]
+    back_in = refs[3 : 3 + peers]
+    place, gate_weight, up_weight, near_out, far_out = refs[3 + peers :]
+    d_hidden = summed(back, back_in)
+    d_gate = (d_hidden * gate_factor[...]).astype(BF16)
+    d_up = (d_hidden * up_factor[...]).astype(BF16)
     rows = (dot(d_gate, gate_weight[...], 1, 1) + dot(d_up, up_weight[...], 1, 1)).astype(BF16)
     place_rows(place, rows, near_out, far_out)
 
@@ -217,7 +264,7 @@
 def fold(keep, received, cuts):
     outs = [((stop - start, keep.shape[1]), dtype) for start, stop, dtype in cuts]
     return call(
-        functools.partial(fold_body, len(received), cuts), outs, [keep] + list(received)
+        "fold", functools.partial(fold_body, len(received), cuts), outs, [keep] + list(received)
     )
 
 
@@ -252,6 +299,23 @@
     return fold(near, received, [(0, near.shape[0], BF16)])[0]
 
 
+def collect_start(near, far):
+    half = near.shape[0] // 2
+    received = swap(far, "group", bits_of("group")[-1])
+    return fold(near, [received], [(0, half, F32), (half, 2 * half, BF16)])
+
+
+def collect_rest(near, far):
+    steps = [("ingroup", b) for b in bits_of("ingroup")]
+    steps += [("group", b) for b in bits_of("group")[:-1]]
+    while steps:
+        received = swap(far, *steps.pop())
+        half = near.shape[0] // 2
+        if not steps:
+            return fold(near, [received], [(0, near.shape[0], BF16)])[0]
+        near, far = fold(near, [received], [(0, half, F32), (half, 2 * half, BF16)])
+
+
 def from_peers(sent):
     count = lax.axis_size("dp")
     return [
@@ -272,47 +336,48 @@
     w_gate, w_up, w_down = w_gate[0], w_up[0], w_down[0]
     product = 2 * slots * features * hidden
 
-    (own,) = call(
-        functools.partial(payload_body, wide),
-        [((block, wide + LANES), BF16)],
-        [tokens, expert_ids.T, gate_fixed.T],
-    )
-    x_parts, cotangent = spread(own, cotangent)
-    d_parts, _ = spread(cotangent)
+    (route,) = call("routing", routing_body, [((block, LANES), BF16)], [expert_ids.T, gate_fixed.T])
+    x_parts, d_parts = spread(tokens, route, cotangent)
     me = lax.axis_index(PLANE).astype(jnp.int32).reshape(1)
     sums = [((slots, hidden), F32), ((slots, hidden), BF16)]
     place, scale, rows, gate, gate_sent = call(
+        "gate",
         functools.partial(route_body, wide, topk, block, capacity, len(x_parts)),
         [((total, slots), BF16), ((slots, LANES), F32), ((slots, features), BF16)] + sums,
         [me] + x_parts + [w_gate],
         product,
     )
     gate_in = from_peers(gate_sent)
-    up, up_sent = call(up_body, sums, [rows, w_up], product)
+    up, up_sent = call("up", up_body, sums, [rows, w_up], product)
     up_in = from_peers(up_sent)
     back, back_sent = call(
-        functools.partial(back_body, len(d_parts)), sums, d_parts + [place, w_down], product
+        "back", functools.partial(back_body, len(d_parts)), sums, d_parts + [place, w_down], product
     )
     back_in = from_peers(back_sent)
     halves = [((total // 2, features), F32), ((total // 2, features), BF16)]
-    mixed = collect(
+    near, far = collect_start(
         *call(
-            functools.partial(out_body, peers),
+            "out", functools.partial(out_body, peers),
             halves,
-            [gate, up] + gate_in + up_in + [scale, place, w_down],
+            [gate, up] + gate_in + up_in + [scale, place, w_down, back_sent],
             product,
         )
     )
+    factors = call(
+        "factor", functools.partial(factor_body, peers),
+        [((slots, hidden), F32)] * 2,
+        [gate, up] + gate_in + up_in + [scale],
+    )
     grad = collect(
         *call(
-            functools.partial(grad_body, peers),
+            "grad", functools.partial(grad_body, peers),
             halves,
-            [gate, up, back] + gate_in + up_in + back_in + [scale, place, w_gate, w_up],
+            list(factors) + [back] + back_in + [place, w_gate, w_up],
             2 * product,
             24,
         )
     )
-    return mixed, grad
+    return collect_rest(near, far), grad
 
 
 def solution(mesh):

time: 83.2 us -> 81.4 us (0.978)
  waiting for transfers between devices: 37.5 us -> 40.3 us
  starting transfers between devices: 28 us -> 25.3 us
  local copies, waits for them, and re-layouts: 7.09 us -> 5.06 us
    ppermute x22 -> x20, waiting for transfers between devices: 23.5 us -> 27.6 us  [swap(): lax.ppermute(value, axis, [(i, i ^ offset) for i in range(lax.axis_size(a...]
    ppermute x22 -> x20, starting transfers between devices: 24.3 us -> 21.5 us  [swap(): lax.ppermute(value, axis, [(i, i ^ offset) for i in range(lax.axis_size(a...]
    unnamed x18 -> x16, local copies, waits for them, and re-layouts: 7.09 us -> 5.06 us
    ppermute x3, waiting for transfers between devices: 13.9 us -> 12.7 us  [from_peers(): lax.ppermute(sent, 'dp', [(i, (i + step) % count) for i in range(count)])]
    pallas_call x18 -> x20, Pallas kernels: 9.46 us -> 9.61 us  [call(): return kernel(*args, *passed)]
  transfers between devices with their start and end apart: 25 -> 23, of which waited for: 17 -> 16; matrix products, arithmetic and copies ran while one was open for 0% -> 0% of each run, Pallas kernels for 10% -> 11%
where the time goes in v3:
time: 81.4 us; the launch traced here: 81.1 us
  waiting for transfers between devices  40.3 us (50%)
  starting transfers between devices  25.3 us (31%)
  Pallas kernels  9.61 us (12%)
  local copies, waits for them, and re-layouts  5.06 us (6%)
    ppermute x20, waiting for transfers between devices, swap(): lax.ppermute(value, axis, [(i, i ^ offset) for i in range(lax.axis_size(a...  27.6 us
    ppermute x20, starting transfers between devices, swap(): lax.ppermute(value, axis, [(i, i ^ offset) for i in range(lax.axis_size(a...  21.5 us
    ppermute x3, waiting for transfers between devices, from_peers(): lax.ppermute(sent, 'dp', [(i, (i + step) % count) for i in range(count)])  12.7 us
    pallas_call x20, Pallas kernels, call(): return kernel(*args, *passed)  9.61 us
    unnamed x16, local copies, waits for them, and re-layouts  5.06 us
    ppermute x3, starting transfers between devices, from_peers(): lax.ppermute(sent, 'dp', [(i, (i + step) % count) for i in range(count)])  3.79 us
  transfers between devices with their start and end apart: 23, of which 16 were waited for; matrix products, arithmetic and copies ran while one was open for 0% of the time, Pallas kernels for 11%

profile of v3, /device:TPU:0, one launch (start us, length us, event | category | flops | bytes accessed | tf_op | source)
XLA Modules:
  0.0 81.1 jit_solution(16680288554075842346)
XLA Ops:
  0.6 4.1 %collective-permute-start = (bf16[16,1792]{1,0:T(8,128)(2,1)}, bf16[16,1792]{1,0:T(8,128)(2,1)S(1)}, u32[]{:S(2)}, u32[]{:S(2)}) collective-permute-start(bf16[16,1792]{1,0:T(8,128)(2,1)} %refs_0_.3), channel_id=1, source_target_pairs={{0,4},{2,6},{4,0},{6,2},{1,5},{3,7},{5,1},{7,3},{8,12},{10,14},{12... | collective-permute-start | bytes 172040 | tf_op jit(solution)/shard_map/ppermute | solution.py:56
  7.1 3.7 %collective-permute-done.1.refs_3_ = bf16[16,128]{1,0:T(8,128)(2,1)S(1)} collective-permute-done((bf16[16,128]{1,0:T(8,128)(2,1)S(1)}, bf16[16,128]{1,0:T(8,128)(2,1)S(1)}, u32[]{:S(2)}, u32[]{:S(2)}) %collective-permute-start.1) | collective-permute-done | bytes 4128 | tf_op jit(solution)/shard_map/ppermute | solution.py:56
  11.6 1.6 %collective-permute-start.2 = (bf16[32,1920]{1,0:T(8,128)(2,1)S(1)}, bf16[32,1920]{1,0:T(8,128)(2,1)S(1)}, u32[]{:S(2)}, u32[]{:S(2)}) collective-permute-start(bf16[32,1920]{1,0:T(8,128)(2,1)S(1)} %get-tuple-element.31.refs_0_), channel_id=1, source_target_pairs={{0,2},{2,0},{4,6},{6,4},{1,3},{3,1},{5,7},{7,5},{8,10},{10,8},{12,... | collective-permute-start | bytes 368648 | tf_op jit(solution)/shard_map/ppermute | solution.py:56
  13.6 1.5 %collective-permute-start.3 = (bf16[32,1920]{1,0:T(8,128)(2,1)S(1)}, bf16[32,1920]{1,0:T(8,128)(2,1)S(1)}, u32[]{:S(2)}, u32[]{:S(2)}) collective-permute-start(bf16[32,1920]{1,0:T(8,128)(2,1)S(1)} %get-tuple-element.31.refs_0_), channel_id=1, source_target_pairs={{0,16},{8,24},{16,0},{24,8},{1,17},{9,25},{17,1},{25,9},{2,18},{10... | collective-permute-start | bytes 368648 | tf_op jit(solution)/shard_map/ppermute | solution.py:56
  15.1 1.9 %collective-permute-done.2.refs_1_ = bf16[32,1920]{1,0:T(8,128)(2,1)S(1)} collective-permute-done((bf16[32,1920]{1,0:T(8,128)(2,1)S(1)}, bf16[32,1920]{1,0:T(8,128)(2,1)S(1)}, u32[]{:S(2)}, u32[]{:S(2)}) %collective-permute-start.2) | collective-permute-done | bytes 122912 | tf_op jit(solution)/shard_map/ppermute | solution.py:56
  17.0 1.6 %collective-permute-start.4 = (bf16[32,1920]{1,0:T(8,128)(2,1)S(1)}, bf16[32,1920]{1,0:T(8,128)(2,1)S(1)}, u32[]{:S(2)}, u32[]{:S(2)}) collective-permute-start(bf16[32,1920]{1,0:T(8,128)(2,1)S(1)} %collective-permute-done.2.refs_1_), channel_id=1, source_target_pairs={{0,16},{8,24},{16,0},{24,8},{1,17},{9,25},{17,1},{25,9},{2,18},{10... | collective-permute-start | bytes 368648 | tf_op jit(solution)/shard_map/ppermute | solution.py:56
  19.7 2.1 %collective-permute-done.4.refs_3_ = bf16[32,1920]{1,0:T(8,128)(2,1)S(1)} collective-permute-done((bf16[32,1920]{1,0:T(8,128)(2,1)S(1)}, bf16[32,1920]{1,0:T(8,128)(2,1)S(1)}, u32[]{:S(2)}, u32[]{:S(2)}) %collective-permute-start.4) | collective-permute-done | bytes 122912 | tf_op jit(solution)/shard_map/ppermute | solution.py:56
  22.0 1.7 %collective-permute-start.10 = (bf16[32,1792]{1,0:T(8,128)(2,1)S(1)}, bf16[32,1792]{1,0:T(8,128)(2,1)S(1)}, u32[]{:S(2)}, u32[]{:S(2)}) collective-permute-start(bf16[32,1792]{1,0:T(8,128)(2,1)S(1)} %pack.3.refs_4_.refs_0_), channel_id=1, source_target_pairs={{0,16},{8,24},{16,0},{24,8},{1,17},{9,25},{17,1},{25,9},{2,18},{10... | collective-permute-start | bytes 344072 | tf_op jit(solution)/shard_map/ppermute | solution.py:56
  23.7 1.5 %collective-permute-start.11 = (bf16[32,1792]{1,0:T(8,128)(2,1)S(1)}, bf16[32,1792]{1,0:T(8,128)(2,1)S(1)}, u32[]{:S(2)}, u32[]{:S(2)}) collective-permute-start(bf16[32,1792]{1,0:T(8,128)(2,1)S(1)} %collective-permute-done.9.refs_1_), channel_id=1, source_target_pairs={{0,16},{8,24},{16,0},{24,8},{1,17},{9,25},{17,1},{25,9},{2,18},{10... | collective-permute-start | bytes 344072 | tf_op jit(solution)/shard_map/ppermute | solution.py:56
  25.2 2.8 %collective-permute-done.10.refs_2_ = bf16[32,1792]{1,0:T(8,128)(2,1)S(1)} collective-permute-done((bf16[32,1792]{1,0:T(8,128)(2,1)S(1)}, bf16[32,1792]{1,0:T(8,128)(2,1)S(1)}, u32[]{:S(2)}, u32[]{:S(2)}) %collective-permute-start.10) | collective-permute-done | bytes 114720 | tf_op jit(solution)/shard_map/ppermute | solution.py:56
  28.0 2.0 %collective-permute-done.11.refs_3_ = bf16[32,1792]{1,0:T(8,128)(2,1)S(1)} collective-permute-done((bf16[32,1792]{1,0:T(8,128)(2,1)S(1)}, bf16[32,1792]{1,0:T(8,128)(2,1)S(1)}, u32[]{:S(2)}, u32[]{:S(2)}) %collective-permute-start.11) | collective-permute-done | bytes 114720 | tf_op jit(solution)/shard_map/ppermute | solution.py:56
  30.1 2.0 %copy-done = bf16[1,1792,1024]{2,1,0:T(8,128)(2,1)S(1)} copy-done((bf16[1,1792,1024]{2,1,0:T(8,128)(2,1)S(1)}, bf16[1,1792,1024]{2,1,0:T(8,128)(2,1)}, u32[]{:S(2)}) %copy-start) | copy-done | bytes 3670040
  32.1 1.3 %gate.1 = (bf16[256,128]{1,0:T(8,128)(2,1)S(1)}, f32[128,128]{1,0:T(8,128)S(1)}, bf16[128,1792]{1,0:T(8,128)(2,1)S(1)}, f32[128,1024]{1,0:T(8,128)S(1)}, bf16[128,1024]{1,0:T(8,128)(2,1)S(1)}) custom-call(s32[1]{0:T(128)} %bitcast.refs_0_, bf16[128,1920]{1,0:T(8,128)(2,1)S(1)} %pack.4.refs_1_, bf16[128,1920]{1,0:T(8,128)(2,1)S(1)} %collective-permute-done.6.refs_2_, ...), custom_call_target="tpu_custom_call" | custom-call | flops 469762048 | bytes 6029316 | tf_op jit(solution)/shard_map/gate/gate/pallas_call | solution.py:52
  33.5 1.6 %collective-permute-start.7 = (bf16[128,1024]{1,0:T(8,128)(2,1)S(1)}, bf16[128,1024]{1,0:T(8,128)(2,1)S(1)}, u32[]{:S(2)}, u32[]{:S(2)}) collective-permute-start(bf16[128,1024]{1,0:T(8,128)(2,1)S(1)} %get-tuple-element.36), channel_id=1, source_target_pairs={{0,1},{1,0},{2,3},{3,2},{4,5},{5,4},{6,7},{7,6},{8,9},{9,8},{10,11... | collective-permute-start | bytes 786440 | tf_op jit(solution)/shard_map/ppermute | solution.py:322
  37.8 1.4 %collective-permute-start.17 = (bf16[128,1024]{1,0:T(8,128)(2,1)S(1)}, bf16[128,1024]{1,0:T(8,128)(2,1)S(1)}, u32[]{:S(2)}, u32[]{:S(2)}) collective-permute-start(bf16[128,1024]{1,0:T(8,128)(2,1)S(1)} %get-tuple-element.40.refs_7_), channel_id=1, source_target_pairs={{0,1},{1,0},{2,3},{3,2},{4,5},{5,4},{6,7},{7,6},{8,9},{9,8},{10,11... | collective-permute-start | bytes 786440 | tf_op jit(solution)/shard_map/ppermute | solution.py:322
  39.2 3.4 %collective-permute-done.7.refs_2_ = bf16[128,1024]{1,0:T(8,128)(2,1)S(1)} collective-permute-done((bf16[128,1024]{1,0:T(8,128)(2,1)S(1)}, bf16[128,1024]{1,0:T(8,128)(2,1)S(1)}, u32[]{:S(2)}, u32[]{:S(2)}) %collective-permute-start.7) | collective-permute-done | bytes 262176 | tf_op jit(solution)/shard_map/ppermute | solution.py:322
  42.7 5.6 %collective-permute-done.8.refs_3_ = bf16[128,1024]{1,0:T(8,128)(2,1)S(1)} collective-permute-done((bf16[128,1024]{1,0:T(8,128)(2,1)S(1)}, bf16[128,1024]{1,0:T(8,128)(2,1)S(1)}, u32[]{:S(2)}, u32[]{:S(2)}) %collective-permute-start.8) | collective-permute-done | bytes 262176 | tf_op jit(solution)/shard_map/ppermute | solution.py:322
  49.8 3.7 %collective-permute-done.17.refs_3_ = bf16[128,1024]{1,0:T(8,128)(2,1)S(1)} collective-permute-done((bf16[128,1024]{1,0:T(8,128)(2,1)S(1)}, bf16[128,1024]{1,0:T(8,128)(2,1)S(1)}, u32[]{:S(2)}, u32[]{:S(2)}) %collective-permute-start.17) | collective-permute-done | bytes 262176 | tf_op jit(solution)/shard_map/ppermute | solution.py:322
  53.5 3.1 %grad.1 = (f32[128,1792]{1,0:T(8,128)S(1)}, bf16[128,1792]{1,0:T(8,128)(2,1)S(1)}) custom-call(f32[128,1024]{1,0:T(8,128)S(1)} %get-tuple-element.49.refs_0_, f32[128,1024]{1,0:T(8,128)S(1)} %get-tuple-element.50.refs_1_, f32[128,1024]{1,0:T(8,128)S(1)} %get-tuple-element.51.refs_2_, bf16[128,1024]{1,0:T(8,128)(2,1)S(1)} %collective-permute-done.17.refs_3_, ...), custom_call_target="tpu_custom_call" | custom-call | flops 939524096 | bytes 10616832 | tf_op jit(solution)/shard_map/grad/grad/pallas_call | solution.py:52
  56.8 1.7 %collective-permute-start.14 = (bf16[64,1792]{1,0:T(8,128)(2,1)S(1)}, bf16[64,1792]{1,0:T(8,128)(2,1)S(1)}, u32[]{:S(2)}, u32[]{:S(2)}) collective-permute-start(bf16[64,1792]{1,0:T(8,128)(2,1)S(1)} %get-tuple-element.44), channel_id=1, source_target_pairs={{0,16},{8,24},{16,0},{24,8},{1,17},{9,25},{17,1},{25,9},{2,18},{10... | collective-permute-start | bytes 688136 | tf_op jit(solution)/shard_map/ppermute | solution.py:56
  58.6 1.7 %collective-permute-start.20 = (bf16[32,1792]{1,0:T(8,128)(2,1)S(1)}, bf16[32,1792]{1,0:T(8,128)(2,1)S(1)}, u32[]{:S(2)}, u32[]{:S(2)}) collective-permute-start(bf16[32,1792]{1,0:T(8,128)(2,1)S(1)} %get-tuple-element.57), channel_id=1, source_target_pairs={{0,16},{8,24},{16,0},{24,8},{1,17},{9,25},{17,1},{25,9},{2,18},{10... | collective-permute-start | bytes 344072 | tf_op jit(solution)/shard_map/ppermute | solution.py:56
  60.7 7.0 %collective-permute-done.20.refs_1_ = bf16[32,1792]{1,0:T(8,128)(2,1)S(1)} collective-permute-done((bf16[32,1792]{1,0:T(8,128)(2,1)S(1)}, bf16[32,1792]{1,0:T(8,128)(2,1)S(1)}, u32[]{:S(2)}, u32[]{:S(2)}) %collective-permute-start.20) | collective-permute-done | bytes 114720 | tf_op jit(solution)/shard_map/ppermute | solution.py:56
  70.0 3.4 %collective-permute-done.21.refs_2_ = bf16[32,1792]{1,0:T(8,128)(2,1)S(1)} collective-permute-done((bf16[32,1792]{1,0:T(8,128)(2,1)S(1)}, bf16[32,1792]{1,0:T(8,128)(2,1)S(1)}, u32[]{:S(2)}, u32[]{:S(2)}) %collective-permute-start.21) | collective-permute-done | bytes 114720 | tf_op jit(solution)/shard_map/ppermute | solution.py:56
  76.5 2.0 %collective-permute-done.22.refs_1_ = bf16[16,1792]{1,0:T(8,128)(2,1)S(1)} collective-permute-done((bf16[16,1792]{1,0:T(8,128)(2,1)S(1)}, bf16[16,1792]{1,0:T(8,128)(2,1)S(1)}, u32[]{:S(2)}, u32[]{:S(2)}) %collective-permute-start.22) | collective-permute-done | bytes 57376 | tf_op jit(solution)/shard_map/ppermute | solution.py:56
  (58 shorter events, 17.7 us)
Async XLA Ops:
  0.6 10.1 %collective-permute-start = (bf16[16,1792]{1,0:T(8,128)(2,1)}, bf16[16,1792]{1,0:T(8,128)(2,1)S(1)}, u32[]{:S(2)}, u32[]{:S(2)}) collective-permute-start(bf16[16,1792]{1,0:T(8,128)(2,1)} %refs_0_.3), channel_id=1, source_target_pairs={{0,4},{2,6},{4,0},{6,2},{1,5},{3,7},{5,1},{7,3},{8,12},{10,14},{12... | collective-permute-start | bytes 172040 | tf_op jit(solution)/shard_map/ppermute | solution.py:56
  6.2 4.5 %collective-permute-start.1 = (bf16[16,128]{1,0:T(8,128)(2,1)S(1)}, bf16[16,128]{1,0:T(8,128)(2,1)S(1)}, u32[]{:S(2)}, u32[]{:S(2)}) collective-permute-start(bf16[16,128]{1,0:T(8,128)(2,1)S(1)} %routing.1.refs_1_.refs_2_), channel_id=1, source_target_pairs={{0,4},{2,6},{4,0},{6,2},{1,5},{3,7},{5,1},{7,3},{8,12},{10,14},{12... | collective-permute-start | bytes 12296 | tf_op jit(solution)/shard_map/ppermute | solution.py:56
  11.6 5.4 %collective-permute-start.2 = (bf16[32,1920]{1,0:T(8,128)(2,1)S(1)}, bf16[32,1920]{1,0:T(8,128)(2,1)S(1)}, u32[]{:S(2)}, u32[]{:S(2)}) collective-permute-start(bf16[32,1920]{1,0:T(8,128)(2,1)S(1)} %get-tuple-element.31.refs_0_), channel_id=1, source_target_pairs={{0,2},{2,0},{4,6},{6,4},{1,3},{3,1},{5,7},{7,5},{8,10},{10,8},{12,... | collective-permute-start | bytes 368648 | tf_op jit(solution)/shard_map/ppermute | solution.py:56
  13.2 5.6 %collective-permute-start.5 = (bf16[16,1792]{1,0:T(8,128)(2,1)S(1)}, bf16[16,1792]{1,0:T(8,128)(2,1)S(1)}, u32[]{:S(2)}, u32[]{:S(2)}) collective-permute-start(bf16[16,1792]{1,0:T(8,128)(2,1)S(1)} %get-tuple-element.32.refs_0_), channel_id=1, source_target_pairs={{0,4},{2,6},{4,0},{6,2},{1,5},{3,7},{5,1},{7,3},{8,12},{10,14},{12... | collective-permute-start | bytes 172040 | tf_op jit(solution)/shard_map/ppermute | solution.py:56
  13.6 6.1 %collective-permute-start.3 = (bf16[32,1920]{1,0:T(8,128)(2,1)S(1)}, bf16[32,1920]{1,0:T(8,128)(2,1)S(1)}, u32[]{:S(2)}, u32[]{:S(2)}) collective-permute-start(bf16[32,1920]{1,0:T(8,128)(2,1)S(1)} %get-tuple-element.31.refs_0_), channel_id=1, source_target_pairs={{0,16},{8,24},{16,0},{24,8},{1,17},{9,25},{17,1},{25,9},{2,18},{10... | collective-permute-start | bytes 368648 | tf_op jit(solution)/shard_map/ppermute | solution.py:56
  17.0 4.9 %collective-permute-start.4 = (bf16[32,1920]{1,0:T(8,128)(2,1)S(1)}, bf16[32,1920]{1,0:T(8,128)(2,1)S(1)}, u32[]{:S(2)}, u32[]{:S(2)}) collective-permute-start(bf16[32,1920]{1,0:T(8,128)(2,1)S(1)} %collective-permute-done.2.refs_1_), channel_id=1, source_target_pairs={{0,16},{8,24},{16,0},{24,8},{1,17},{9,25},{17,1},{25,9},{2,18},{10... | collective-permute-start | bytes 368648 | tf_op jit(solution)/shard_map/ppermute | solution.py:56
  18.8 4.9 %collective-permute-start.9 = (bf16[32,1792]{1,0:T(8,128)(2,1)S(1)}, bf16[32,1792]{1,0:T(8,128)(2,1)S(1)}, u32[]{:S(2)}, u32[]{:S(2)}) collective-permute-start(bf16[32,1792]{1,0:T(8,128)(2,1)S(1)} %pack.3.refs_4_.refs_0_), channel_id=1, source_target_pairs={{0,2},{2,0},{4,6},{6,4},{1,3},{3,1},{5,7},{7,5},{8,10},{10,8},{12,... | collective-permute-start | bytes 344072 | tf_op jit(solution)/shard_map/ppermute | solution.py:56
  21.9 8.2 %collective-permute-start.6 = (bf16[128,1920]{1,0:T(8,128)(2,1)S(1)}, bf16[128,1920]{1,0:T(8,128)(2,1)S(1)}, u32[]{:S(2)}, u32[]{:S(2)}) collective-permute-start(bf16[128,1920]{1,0:T(8,128)(2,1)S(1)} %pack.4.refs_1_), channel_id=1, source_target_pairs={{0,8},{8,0},{16,24},{24,16},{1,9},{9,1},{17,25},{25,17},{2,10},{10... | collective-permute-start | bytes 1474568 | tf_op jit(solution)/shard_map/ppermute | solution.py:56
  22.0 6.0 %collective-permute-start.10 = (bf16[32,1792]{1,0:T(8,128)(2,1)S(1)}, bf16[32,1792]{1,0:T(8,128)(2,1)S(1)}, u32[]{:S(2)}, u32[]{:S(2)}) collective-permute-start(bf16[32,1792]{1,0:T(8,128)(2,1)S(1)} %pack.3.refs_4_.refs_0_), channel_id=1, source_target_pairs={{0,16},{8,24},{16,0},{24,8},{1,17},{9,25},{17,1},{25,9},{2,18},{10... | collective-permute-start | bytes 344072 | tf_op jit(solution)/shard_map/ppermute | solution.py:56
  23.7 6.3 %collective-permute-start.11 = (bf16[32,1792]{1,0:T(8,128)(2,1)S(1)}, bf16[32,1792]{1,0:T(8,128)(2,1)S(1)}, u32[]{:S(2)}, u32[]{:S(2)}) collective-permute-start(bf16[32,1792]{1,0:T(8,128)(2,1)S(1)} %collective-permute-done.9.refs_1_), channel_id=1, source_target_pairs={{0,16},{8,24},{16,0},{24,8},{1,17},{9,25},{17,1},{25,9},{2,18},{10... | collective-permute-start | bytes 344072 | tf_op jit(solution)/shard_map/ppermute | solution.py:56
  30.0 6.5 %collective-permute-start.12 = (bf16[128,1792]{1,0:T(8,128)(2,1)S(1)}, bf16[128,1792]{1,0:T(8,128)(2,1)S(1)}, u32[]{:S(2)}, u32[]{:S(2)}) collective-permute-start(bf16[128,1792]{1,0:T(8,128)(2,1)S(1)} %pack.5.refs_0_), channel_id=1, source_target_pairs={{0,8},{8,0},{16,24},{24,16},{1,9},{9,1},{17,25},{25,17},{2,10},{10... | collective-permute-start | bytes 1376264 | tf_op jit(solution)/shard_map/ppermute | solution.py:56
  33.5 9.2 %collective-permute-start.7 = (bf16[128,1024]{1,0:T(8,128)(2,1)S(1)}, bf16[128,1024]{1,0:T(8,128)(2,1)S(1)}, u32[]{:S(2)}, u32[]{:S(2)}) collective-permute-start(bf16[128,1024]{1,0:T(8,128)(2,1)S(1)} %get-tuple-element.36), channel_id=1, source_target_pairs={{0,1},{1,0},{2,3},{3,2},{4,5},{5,4},{6,7},{7,6},{8,9},{9,8},{10,11... | collective-permute-start | bytes 786440 | tf_op jit(solution)/shard_map/ppermute | solution.py:322
  35.8 12.5 %collective-permute-start.8 = (bf16[128,1024]{1,0:T(8,128)(2,1)S(1)}, bf16[128,1024]{1,0:T(8,128)(2,1)S(1)}, u32[]{:S(2)}, u32[]{:S(2)}) collective-permute-start(bf16[128,1024]{1,0:T(8,128)(2,1)S(1)} %get-tuple-element.37), channel_id=1, source_target_pairs={{0,1},{1,0},{2,3},{3,2},{4,5},{5,4},{6,7},{7,6},{8,9},{9,8},{10,11... | collective-permute-start | bytes 786440 | tf_op jit(solution)/shard_map/ppermute | solution.py:322
  37.8 15.7 %copy-start.1 = (bf16[1,1792,1024]{2,1,0:T(8,128)(2,1)S(1)}, bf16[1,1792,1024]{2,1,0:T(8,128)(2,1)}, u32[]{:S(2)}) copy-start(bf16[1,1792,1024]{2,1,0:T(8,128)(2,1)} %param.11) | copy-start | bytes 11010052
  37.8 15.7 %collective-permute-start.17 = (bf16[128,1024]{1,0:T(8,128)(2,1)S(1)}, bf16[128,1024]{1,0:T(8,128)(2,1)S(1)}, u32[]{:S(2)}, u32[]{:S(2)}) collective-permute-start(bf16[128,1024]{1,0:T(8,128)(2,1)S(1)} %get-tuple-element.40.refs_7_), channel_id=1, source_target_pairs={{0,1},{1,0},{2,3},{3,2},{4,5},{5,4},{6,7},{7,6},{8,9},{9,8},{10,11... | collective-permute-start | bytes 786440 | tf_op jit(solution)/shard_map/ppermute | solution.py:322
  49.3 7.4 %collective-permute-start.13 = (bf16[128,1792]{1,0:T(8,128)(2,1)S(1)}, bf16[128,1792]{1,0:T(8,128)(2,1)S(1)}, u32[]{:S(2)}, u32[]{:S(2)}) collective-permute-start(bf16[128,1792]{1,0:T(8,128)(2,1)S(1)} %get-tuple-element.42), channel_id=1, source_target_pairs={{0,8},{8,0},{16,24},{24,16},{1,9},{9,1},{17,25},{25,17},{2,10},{10... | collective-permute-start | bytes 1376264 | tf_op jit(solution)/shard_map/ppermute | solution.py:56
  56.6 1.9 %collective-permute-start.18 = (bf16[128,1792]{1,0:T(8,128)(2,1)S(1)}, bf16[128,1792]{1,0:T(8,128)(2,1)S(1)}, u32[]{:S(2)}, u32[]{:S(2)}) collective-permute-start(bf16[128,1792]{1,0:T(8,128)(2,1)S(1)} %get-tuple-element.53), channel_id=1, source_target_pairs={{0,8},{8,0},{16,24},{24,16},{1,9},{9,1},{17,25},{25,17},{2,10},{10... | collective-permute-start | bytes 1376264 | tf_op jit(solution)/shard_map/ppermute | solution.py:56
  56.8 12.2 %collective-permute-start.14 = (bf16[64,1792]{1,0:T(8,128)(2,1)S(1)}, bf16[64,1792]{1,0:T(8,128)(2,1)S(1)}, u32[]{:S(2)}, u32[]{:S(2)}) collective-permute-start(bf16[64,1792]{1,0:T(8,128)(2,1)S(1)} %get-tuple-element.44), channel_id=1, source_target_pairs={{0,16},{8,24},{16,0},{24,8},{1,17},{9,25},{17,1},{25,9},{2,18},{10... | collective-permute-start | bytes 688136 | tf_op jit(solution)/shard_map/ppermute | solution.py:56
  58.6 9.1 %collective-permute-start.20 = (bf16[32,1792]{1,0:T(8,128)(2,1)S(1)}, bf16[32,1792]{1,0:T(8,128)(2,1)S(1)}, u32[]{:S(2)}, u32[]{:S(2)}) collective-permute-start(bf16[32,1792]{1,0:T(8,128)(2,1)S(1)} %get-tuple-element.57), channel_id=1, source_target_pairs={{0,16},{8,24},{16,0},{24,8},{1,17},{9,25},{17,1},{25,9},{2,18},{10... | collective-permute-start | bytes 344072 | tf_op jit(solution)/shard_map/ppermute | solution.py:56
  60.2 9.7 %collective-permute-start.19 = (bf16[32,1792]{1,0:T(8,128)(2,1)S(1)}, bf16[32,1792]{1,0:T(8,128)(2,1)S(1)}, u32[]{:S(2)}, u32[]{:S(2)}) collective-permute-start(bf16[32,1792]{1,0:T(8,128)(2,1)S(1)} %get-tuple-element.55), channel_id=1, source_target_pairs={{0,16},{8,24},{16,0},{24,8},{1,17},{9,25},{17,1},{25,9},{2,18},{10... | collective-permute-start | bytes 344072 | tf_op jit(solution)/shard_map/ppermute | solution.py:56
  67.7 5.6 %collective-permute-start.21 = (bf16[32,1792]{1,0:T(8,128)(2,1)S(1)}, bf16[32,1792]{1,0:T(8,128)(2,1)S(1)}, u32[]{:S(2)}, u32[]{:S(2)}) collective-permute-start(bf16[32,1792]{1,0:T(8,128)(2,1)S(1)} %fold.13), channel_id=1, source_target_pairs={{0,2},{2,0},{4,6},{6,4},{1,3},{3,1},{5,7},{7,5},{8,10},{10,8},{12,... | collective-permute-start | bytes 344072 | tf_op jit(solution)/shard_map/ppermute | solution.py:56
  69.0 6.2 %collective-permute-start.15 = (bf16[32,1792]{1,0:T(8,128)(2,1)S(1)}, bf16[32,1792]{1,0:T(8,128)(2,1)S(1)}, u32[]{:S(2)}, u32[]{:S(2)}) collective-permute-start(bf16[32,1792]{1,0:T(8,128)(2,1)S(1)} %get-tuple-element.46), channel_id=1, source_target_pairs={{0,2},{2,0},{4,6},{6,4},{1,3},{3,1},{5,7},{7,5},{8,10},{10,8},{12,... | collective-permute-start | bytes 344072 | tf_op jit(solution)/shard_map/ppermute | solution.py:56
  73.4 5.1 %collective-permute-start.22 = (bf16[16,1792]{1,0:T(8,128)(2,1)S(1)}, bf16[16,1792]{1,0:T(8,128)(2,1)S(1)}, u32[]{:S(2)}, u32[]{:S(2)}) collective-permute-start(bf16[16,1792]{1,0:T(8,128)(2,1)S(1)} %get-tuple-element.59), channel_id=1, source_target_pairs={{0,4},{2,6},{4,0},{6,2},{1,5},{3,7},{5,1},{7,3},{8,12},{10,14},{12... | collective-permute-start | bytes 172040 | tf_op jit(solution)/shard_map/ppermute | solution.py:56
  75.3 5.2 %collective-permute-start.16 = (bf16[16,1792]{1,0:T(8,128)(2,1)S(1)}, bf16[16,1792]{1,0:T(8,128)(2,1)S(1)}, u32[]{:S(2)}, u32[]{:S(2)}) collective-permute-start(bf16[16,1792]{1,0:T(8,128)(2,1)S(1)} %get-tuple-element.48), channel_id=1, source_target_pairs={{0,4},{2,6},{4,0},{6,2},{1,5},{3,7},{5,1},{7,3},{8,12},{10,14},{12... | collective-permute-start | bytes 172040 | tf_op jit(solution)/shard_map/ppermute | solution.py:56
  (7 other events, 12.4 us)

commit v4 on v3

--- a/solution.py
+++ b/solution.py
@@ -107,7 +107,7 @@
         functools.partial(pack_body, len(parts)),
         [(shape, parts[0].dtype)],
         list(parts) + list(after),
-        weight=1,
+        flops=1 << 29,
     )[0]
 
 
@@ -116,7 +116,7 @@
 
 
 def copied(source, after):
-    return call("copied", copy_body, [(source.shape, source.dtype)], [source, after], weight=40)[0]
+    return call("copied", copy_body, [(source.shape, source.dtype)], [source, after], 1 << 31)[0]
 
 
 def spread(tokens, route, cotangent):
@@ -144,19 +144,24 @@
     last = swap(beside, "group", outer[0])
     for bit in outer[1:-1]:
         first = pack([first, swap(first, "group", bit)])
-    second = pack([second, beside, across, last])
-    for bit in outer[1:-1]:
-        second = pack([second, swap(second, "group", bit)])
     first = [first, swap(first, "group", outer[-1])]
-    return first, [second, swap(second, "group", outer[-1])]
+    return first, [second, beside, across, last]
+
+
+def spread_end(parts, after):
+    bits = bits_of("group")[1:]
+    current = pack(parts, after)
+    for bit in bits[:-1]:
+        current = pack([current, swap(current, "group", bit)])
+    return [current, swap(current, "group", bits[-1])]
 
 
 def route_body(wide, topk, block, capacity, count, me, *refs):
-    parts, (weight, place_out, scale_out, rows_out, part_out, sent_out) = (
+    parts, (gate_weight, up_weight, place_out, scale_out, part_out, sent_out) = (
         refs[:count],
         refs[count:],
     )
-    features = weight.shape[0]
+    features = gate_weight.shape[0]
     total, slots = place_out.shape
     routing = jnp.concatenate([p[:, wide : wide + LANES] for p in parts], axis=0)
     lane = lax.broadcasted_iota(jnp.int32, (total, LANES), 1)
@@ -187,16 +192,10 @@
     scale_out[...] = (high * 256.0 + low) / 65536.0
     values = jnp.concatenate([p[:, :features] for p in parts], axis=0)
     rows = dot(place, values, 0, 0).astype(BF16)
-    rows_out[...] = rows
-    part = dot(rows, weight[...])
-    part_out[...] = part
-    sent_out[...] = part.astype(BF16)
-
-
-def up_body(rows, weight, part_out, sent_out):
-    part = dot(rows[...], weight[...])
-    part_out[...] = part
-    sent_out[...] = part.astype(BF16)
+    for i, weight in enumerate((gate_weight, up_weight)):
+        part = dot(rows, weight[...])
+        part_out[i * slots : (i + 1) * slots] = part
+        sent_out[i * slots : (i + 1) * slots] = part.astype(BF16)
 
 
 def back_body(count, *refs):
@@ -215,27 +214,31 @@
     return total
 
 
-def place_rows(place, rows, near_out, far_out):
+def place_rows(place, rows, near_out, first_out, second_out):
     half = near_out.shape[0]
+    middle = half + second_out.shape[0]
+    first_out[...] = dot(place[middle:], rows).astype(BF16)
+    second_out[...] = dot(place[half:middle], rows).astype(BF16)
     near_out[...] = dot(place[:half], rows)
-    far_out[...] = dot(place[half:], rows).astype(BF16)
+
+
+def forward_sums(both, received):
+    total = summed(both, received)
+    half = total.shape[0] // 2
+    return total[:half], total[half:]
 
 
 def out_body(peers, *refs):
-    gate, up = refs[0], refs[1]
-    gate_in, up_in = refs[2 : 2 + peers], refs[2 + peers : 2 + 2 * peers]
-    scale, place, weight, _, near_out, far_out = refs[2 + 2 * peers :]
-    gate_pre, up_pre = summed(gate, gate_in), summed(up, up_in)
+    scale, place, weight, _, near_out, first_out, second_out = refs[1 + peers :]
+    gate_pre, up_pre = forward_sums(refs[0], refs[1 : 1 + peers])
     hidden = (gate_pre / (1.0 + jnp.exp(-gate_pre)) * up_pre).astype(BF16)
     rows = (dot(hidden, weight[...]) * scale[:, :1]).astype(BF16)
-    place_rows(place, rows, near_out, far_out)
+    place_rows(place, rows, near_out, first_out, second_out)
 
 
 def factor_body(peers, *refs):
-    gate, up = refs[0], refs[1]
-    gate_in, up_in = refs[2 : 2 + peers], refs[2 + peers : 2 + 2 * peers]
-    scale, gate_out, up_out = refs[2 + 2 * peers :]
-    gate_pre, up_pre = summed(gate, gate_in), summed(up, up_in)
+    scale, gate_out, up_out = refs[1 + peers :]
+    gate_pre, up_pre = forward_sums(refs[0], refs[1 : 1 + peers])
     sigmoid = 1.0 / (1.0 + jnp.exp(-gate_pre))
     scaled = sigmoid * scale[:, :1]
     gate_out[...] = up_pre * scaled * (1.0 + gate_pre * (1.0 - sigmoid))
@@ -245,75 +248,75 @@
 def grad_body(peers, *refs):
     gate_factor, up_factor, back = refs[:3]
     back_in = refs[3 : 3 + peers]
-    place, gate_weight, up_weight, near_out, far_out = refs[3 + peers :]
+    place, gate_weight, up_weight, _, near_out, first_out, second_out = refs[3 + peers :]
     d_hidden = summed(back, back_in)
     d_gate = (d_hidden * gate_factor[...]).astype(BF16)
     d_up = (d_hidden * up_factor[...]).astype(BF16)
     rows = (dot(d_gate, gate_weight[...], 1, 1) + dot(d_up, up_weight[...], 1, 1)).astype(BF16)
-    place_rows(place, rows, near_out, far_out)
-
-
-def fold_body(count, cuts, keep, *refs):
-    total = keep[...]
-    for received in refs[:count]:
-        total = total + received[...].astype(F32)
-    for (start, stop, dtype), out in zip(cuts, refs[count:]):
-        out[...] = total[start:stop].astype(dtype)
-
-
-def fold(keep, received, cuts):
-    outs = [((stop - start, keep.shape[1]), dtype) for start, stop, dtype in cuts]
+    place_rows(place, rows, near_out, first_out, second_out)
+
+
+def add_body(count, at, parts, keep, *refs):
+    rows = sum(out.shape[0] for out in refs[count:])
+    total = keep[at : at + rows].astype(F32)
+    for received, start in zip(refs[:count], parts):
+        total = total + received[start : start + rows].astype(F32)
+    start = 0
+    for out in refs[count:]:
+        out[...] = total[start : start + out.shape[0]].astype(out.dtype)
+        start += out.shape[0]
+
+
+def add(keep, at, received, outs):
     return call(
-        "fold", functools.partial(fold_body, len(received), cuts), outs, [keep] + list(received)
-    )
-
-
-def collect(near, far):
+        "add",
+        functools.partial(add_body, len(received), at, [start for _, start in received]),
+        [((rows, keep.shape[1]), dtype) for rows, dtype in outs],
+        [keep] + [r for r, _ in received],
+    )
+
+
+def collect_start(near, first, second):
+    for bit in reversed(bits_of("group")[2:]):
+        half, quarter = near.shape[0] // 2, near.shape[0] // 4
+        got_first, got_second = swap(first, "group", bit), swap(second, "group", bit)
+        (first,) = add(near, half + quarter, [(got_first, quarter)], [(quarter, BF16)])
+        (second,) = add(near, half, [(got_first, 0)], [(quarter, BF16)])
+        (near,) = add(near, 0, [(got_second, 0)], [(half, F32)])
+    bit = bits_of("group")[1]
+    return near, swap(first, "group", bit), swap(second, "group", bit)
+
+
+def collect_end(near, far, bits):
+    for bit in bits:
+        received = swap(far, "ingroup", bit)
+        half = near.shape[0] // 2
+        if bit == bits[-1]:
+            return add(near, 0, [(received, 0)], [(2 * half, BF16)])[0]
+        near, far = add(near, 0, [(received, 0)], [(half, F32), (half, BF16)])
+
+
+def collect_few(near, far, got_second):
     inner, outer = bits_of("ingroup"), bits_of("group")
-    for bit in reversed(outer[2:]):
-        half = near.shape[0] // 2
-        near, far = fold(
-            near, [swap(far, "group", bit)], [(0, half, F32), (half, 2 * half, BF16)]
-        )
     half = near.shape[0] // 2
     quarter = half // 2
-    received = swap(far, "group", outer[1])
-    first, second, keep_far, keep_near = fold(
-        near,
-        [received],
-        [
-            (half + quarter, 2 * half, BF16),
-            (half, half + quarter, BF16),
-            (quarter, half, F32),
-            (0, quarter, F32),
-        ],
-    )
-    across = swap(first, "group", outer[0])
-    last = swap(second, "group", outer[0])
-    (far,) = fold(keep_far, [across], [(0, quarter, BF16)])
-    near, received = keep_near, [last, swap(far, "ingroup", inner[-1])]
-    for bit in reversed(inner[:-1]):
-        half = near.shape[0] // 2
-        near, far = fold(near, received, [(0, half, F32), (half, 2 * half, BF16)])
-        received = [swap(far, "ingroup", bit)]
-    return fold(near, received, [(0, near.shape[0], BF16)])[0]
-
-
-def collect_start(near, far):
+    received = swap(far, "group", outer[0])
+    near, far = add(near, 0, [(got_second, 0), (received, 0)], [(quarter, F32), (quarter, BF16)])
+    return collect_end(near, far, inner[::-1])
+
+
+def collect_early(near, got_first, got_second):
+    inner, outer = bits_of("ingroup"), bits_of("group")
     half = near.shape[0] // 2
-    received = swap(far, "group", bits_of("group")[-1])
-    return fold(near, [received], [(0, half, F32), (half, 2 * half, BF16)])
-
-
-def collect_rest(near, far):
-    steps = [("ingroup", b) for b in bits_of("ingroup")]
-    steps += [("group", b) for b in bits_of("group")[:-1]]
-    while steps:
-        received = swap(far, *steps.pop())
-        half = near.shape[0] // 2
-        if not steps:
-            return fold(near, [received], [(0, near.shape[0], BF16)])[0]
-        near, far = fold(near, [received], [(0, half, F32), (half, 2 * half, BF16)])
+    quarter, eighth = half // 2, half // 4
+    low, high = add(near, half, [(got_first, 0)], [(quarter, BF16), (quarter, BF16)])
+    across, last = swap(high, "group", outer[0]), swap(low, "group", outer[0])
+    (far,) = add(near, quarter, [(got_second, quarter), (across, 0)], [(quarter, BF16)])
+    beside = swap(far, "ingroup", inner[-1])
+    near, far = add(
+        near, 0, [(got_second, 0), (last, 0), (beside, 0)], [(eighth, F32), (eighth, BF16)]
+    )
+    return collect_end(near, far, inner[-2::-1])
 
 
 def from_peers(sent):
@@ -339,45 +342,52 @@
     (route,) = call("routing", routing_body, [((block, LANES), BF16)], [expert_ids.T, gate_fixed.T])
     x_parts, d_parts = spread(tokens, route, cotangent)
     me = lax.axis_index(PLANE).astype(jnp.int32).reshape(1)
+    both, both_sent = [((2 * slots, hidden), t) for t in (F32, BF16)]
+    place, scale, both, both_sent = call(
+        "forward",
+        functools.partial(route_body, wide, topk, block, capacity, len(x_parts)),
+        [((total, slots), BF16), ((slots, LANES), F32), both, both_sent],
+        [me] + x_parts + [w_gate, w_up],
+        2 * product,
+    )
+    both_in = from_peers(both_sent)
+    d_parts = spread_end(d_parts, [both_sent])
     sums = [((slots, hidden), F32), ((slots, hidden), BF16)]
-    place, scale, rows, gate, gate_sent = call(
-        "gate",
-        functools.partial(route_body, wide, topk, block, capacity, len(x_parts)),
-        [((total, slots), BF16), ((slots, LANES), F32), ((slots, features), BF16)] + sums,
-        [me] + x_parts + [w_gate],
-        product,
-    )
-    gate_in = from_peers(gate_sent)
-    up, up_sent = call("up", up_body, sums, [rows, w_up], product)
-    up_in = from_peers(up_sent)
     back, back_sent = call(
         "back", functools.partial(back_body, len(d_parts)), sums, d_parts + [place, w_down], product
     )
     back_in = from_peers(back_sent)
-    halves = [((total // 2, features), F32), ((total // 2, features), BF16)]
-    near, far = collect_start(
+    placed = [((total // 2, features), F32)] + [((total // 4, features), BF16)] * 2
+    near, got_first, got_second = collect_start(
         *call(
-            "out", functools.partial(out_body, peers),
-            halves,
-            [gate, up] + gate_in + up_in + [scale, place, w_down, back_sent],
+            "out",
+            functools.partial(out_body, peers),
+            placed,
+            [both] + both_in + [scale, place, w_down, back_sent],
             product,
         )
     )
+    half = near.shape[0] // 2
+    (far,) = add(near, half, [(got_first, 0)], [(half, BF16)])
     factors = call(
-        "factor", functools.partial(factor_body, peers),
+        "factor",
+        functools.partial(factor_body, peers),
         [((slots, hidden), F32)] * 2,
-        [gate, up] + gate_in + up_in + [scale],
-    )
-    grad = collect(
-        *call(
-            "grad", functools.partial(grad_body, peers),
-            halves,
-            list(factors) + [back] + back_in + [place, w_gate, w_up],
-            2 * product,
-            24,
+        [both] + both_in + [scale],
+    )
+    grad = collect_early(
+        *collect_start(
+            *call(
+                "grad",
+                functools.partial(grad_body, peers),
+                placed,
+                list(factors) + [back] + back_in + [place, w_gate, w_up, far],
+                2 * product,
+                24,
+            )
         )
     )
-    return collect_rest(near, far), grad
+    return collect_few(near, far, got_second), grad
 
 
 def solution(mesh):

time: 81.4 us -> 81.1 us (level)
  starting transfers between devices: 25.3 us -> 22.2 us
  waiting for transfers between devices: 40.3 us -> 41.9 us
  local copies, waits for them, and re-layouts: 5.06 us -> 6.29 us
    ppermute x20 -> x22, waiting for transfers between devices: 27.6 us -> 30.6 us  [swap(): lax.ppermute(value, axis, [(i, i ^ offset) for i in range(lax.axis_size(a...]
    ppermute x3 -> x2, starting transfers between devices: 3.79 us -> 2.16 us  [from_peers(): lax.ppermute(sent, 'dp', [(i, (i + step) % count) for i in range(count)])]
    ppermute x3 -> x2, waiting for transfers between devices: 12.7 us -> 11.2 us  [from_peers(): lax.ppermute(sent, 'dp', [(i, (i + step) % count) for i in range(count)])]
    ppermute x20 -> x22, starting transfers between devices: 21.5 us -> 20.1 us  [swap(): lax.ppermute(value, axis, [(i, i ^ offset) for i in range(lax.axis_size(a...]
    unnamed x16 -> x18, local copies, waits for them, and re-layouts: 5.06 us -> 6.29 us
    pallas_call x20 -> x19, Pallas kernels: 9.61 us -> 9.65 us  [call(): return kernel(*args, *passed)]
  transfers between devices with their start and end apart: 23 -> 24, of which waited for: 16 -> 14; matrix products, arithmetic and copies ran while one was open for 0% -> 0% of each run, Pallas kernels for 11% -> 7%
where the time goes in v4:
time: 81.1 us; the launch traced here: 80.8 us
  waiting for transfers between devices  41.9 us (52%)
  starting transfers between devices  22.2 us (27%)
  Pallas kernels  9.65 us (12%)
  local copies, waits for them, and re-layouts  6.29 us (8%)
    ppermute x22, waiting for transfers between devices, swap(): lax.ppermute(value, axis, [(i, i ^ offset) for i in range(lax.axis_size(a...  30.6 us
    ppermute x22, starting transfers between devices, swap(): lax.ppermute(value, axis, [(i, i ^ offset) for i in range(lax.axis_size(a...  20.1 us
    ppermute x2, waiting for transfers between devices, from_peers(): lax.ppermute(sent, 'dp', [(i, (i + step) % count) for i in range(count)])  11.2 us
    pallas_call x19, Pallas kernels, call(): return kernel(*args, *passed)  9.65 us
    unnamed x18, local copies, waits for them, and re-layouts  6.29 us
    ppermute x2, starting transfers between devices, from_peers(): lax.ppermute(sent, 'dp', [(i, (i + step) % count) for i in range(count)])  2.16 us
  transfers between devices with their start and end apart: 24, of which 14 were waited for; matrix products, arithmetic and copies ran while one was open for 0% of the time, Pallas kernels for 7%

profile of v4, /device:TPU:0, one launch (start us, length us, event | category | flops | bytes accessed | tf_op | source)
XLA Modules:
  0.0 80.8 jit_solution(688752367192220361)
XLA Ops:
  0.6 4.1 %collective-permute-start = (bf16[16,1792]{1,0:T(8,128)(2,1)}, bf16[16,1792]{1,0:T(8,128)(2,1)S(1)}, u32[]{:S(2)}, u32[]{:S(2)}) collective-permute-start(bf16[16,1792]{1,0:T(8,128)(2,1)} %refs_0_.3), channel_id=1, source_target_pairs={{0,4},{2,6},{4,0},{6,2},{1,5},{3,7},{5,1},{7,3},{8,12},{10,14},{12... | collective-permute-start | bytes 172040 | tf_op jit(solution)/shard_map/ppermute | solution.py:56
  7.1 3.7 %collective-permute-done.1.refs_3_ = bf16[16,128]{1,0:T(8,128)(2,1)S(1)} collective-permute-done((bf16[16,128]{1,0:T(8,128)(2,1)S(1)}, bf16[16,128]{1,0:T(8,128)(2,1)S(1)}, u32[]{:S(2)}, u32[]{:S(2)}) %collective-permute-start.1) | collective-permute-done | bytes 4128 | tf_op jit(solution)/shard_map/ppermute | solution.py:56
  10.8 1.6 %collective-permute-start.2 = (bf16[32,1920]{1,0:T(8,128)(2,1)S(1)}, bf16[32,1920]{1,0:T(8,128)(2,1)S(1)}, u32[]{:S(2)}, u32[]{:S(2)}) collective-permute-start(bf16[32,1920]{1,0:T(8,128)(2,1)S(1)} %get-tuple-element.26.refs_0_), channel_id=1, source_target_pairs={{0,2},{2,0},{4,6},{6,4},{1,3},{3,1},{5,7},{7,5},{8,10},{10,8},{12,... | collective-permute-start | bytes 368648 | tf_op jit(solution)/shard_map/ppermute | solution.py:56
  12.4 1.5 %collective-permute-start.3 = (bf16[32,1920]{1,0:T(8,128)(2,1)S(1)}, bf16[32,1920]{1,0:T(8,128)(2,1)S(1)}, u32[]{:S(2)}, u32[]{:S(2)}) collective-permute-start(bf16[32,1920]{1,0:T(8,128)(2,1)S(1)} %get-tuple-element.26.refs_0_), channel_id=1, source_target_pairs={{0,16},{8,24},{16,0},{24,8},{1,17},{9,25},{17,1},{25,9},{2,18},{10... | collective-permute-start | bytes 368648 | tf_op jit(solution)/shard_map/ppermute | solution.py:56
  13.9 1.8 %collective-permute-done.2.refs_1_ = bf16[32,1920]{1,0:T(8,128)(2,1)S(1)} collective-permute-done((bf16[32,1920]{1,0:T(8,128)(2,1)S(1)}, bf16[32,1920]{1,0:T(8,128)(2,1)S(1)}, u32[]{:S(2)}, u32[]{:S(2)}) %collective-permute-start.2) | collective-permute-done | bytes 122912 | tf_op jit(solution)/shard_map/ppermute | solution.py:56
  15.7 1.5 %collective-permute-start.4 = (bf16[32,1920]{1,0:T(8,128)(2,1)S(1)}, bf16[32,1920]{1,0:T(8,128)(2,1)S(1)}, u32[]{:S(2)}, u32[]{:S(2)}) collective-permute-start(bf16[32,1920]{1,0:T(8,128)(2,1)S(1)} %collective-permute-done.2.refs_1_), channel_id=1, source_target_pairs={{0,16},{8,24},{16,0},{24,8},{1,17},{9,25},{17,1},{25,9},{2,18},{10... | collective-permute-start | bytes 368648 | tf_op jit(solution)/shard_map/ppermute | solution.py:56
  17.6 4.7 %collective-permute-done.5.refs_1_ = bf16[16,1792]{1,0:T(8,128)(2,1)S(1)} collective-permute-done((bf16[16,1792]{1,0:T(8,128)(2,1)S(1)}, bf16[16,1792]{1,0:T(8,128)(2,1)S(1)}, u32[]{:S(2)}, u32[]{:S(2)}) %collective-permute-start.5) | collective-permute-done | bytes 57376 | tf_op jit(solution)/shard_map/ppermute | solution.py:56
  22.5 2.2 %collective-permute-start.8 = (bf16[32,1792]{1,0:T(8,128)(2,1)S(1)}, bf16[32,1792]{1,0:T(8,128)(2,1)S(1)}, u32[]{:S(2)}, u32[]{:S(2)}) collective-permute-start(bf16[32,1792]{1,0:T(8,128)(2,1)S(1)} %pack.3.refs_4_.refs_0_), channel_id=1, source_target_pairs={{0,2},{2,0},{4,6},{6,4},{1,3},{3,1},{5,7},{7,5},{8,10},{10,8},{12,... | collective-permute-start | bytes 344072 | tf_op jit(solution)/shard_map/ppermute | solution.py:56
  24.7 3.7 %collective-permute-done.8.refs_1_ = bf16[32,1792]{1,0:T(8,128)(2,1)S(1)} collective-permute-done((bf16[32,1792]{1,0:T(8,128)(2,1)S(1)}, bf16[32,1792]{1,0:T(8,128)(2,1)S(1)}, u32[]{:S(2)}, u32[]{:S(2)}) %collective-permute-start.8) | collective-permute-done | bytes 114720 | tf_op jit(solution)/shard_map/ppermute | solution.py:56
  28.5 2.0 %copy-done = bf16[1,1792,1024]{2,1,0:T(8,128)(2,1)S(1)} copy-done((bf16[1,1792,1024]{2,1,0:T(8,128)(2,1)S(1)}, bf16[1,1792,1024]{2,1,0:T(8,128)(2,1)}, u32[]{:S(2)}) %copy-start) | copy-done | bytes 3670040
  30.6 2.0 %copy-done.2 = bf16[1,1792,1024]{2,1,0:T(8,128)(2,1)S(1)} copy-done((bf16[1,1792,1024]{2,1,0:T(8,128)(2,1)S(1)}, bf16[1,1792,1024]{2,1,0:T(8,128)(2,1)}, u32[]{:S(2)}) %copy-start.2) | copy-done | bytes 3670040
  32.6 1.8 %forward.1 = (bf16[256,128]{1,0:T(8,128)(2,1)S(1)}, f32[128,128]{1,0:T(8,128)S(1)}, f32[256,1024]{1,0:T(8,128)S(1)}, bf16[256,1024]{1,0:T(8,128)(2,1)S(1)}) custom-call(s32[1]{0:T(128)} %bitcast.refs_0_, bf16[128,1920]{1,0:T(8,128)(2,1)S(1)} %pack.4.refs_1_, bf16[128,1920]{1,0:T(8,128)(2,1)S(1)} %collective-permute-done.6.refs_2_, ...), custom_call_target="tpu_custom_call" | custom-call | flops 939524096 | bytes 10027012 | tf_op jit(solution)/shard_map/forward/forward/pallas_call | solution.py:52
  34.5 1.6 %collective-permute-start.7 = (bf16[256,1024]{1,0:T(8,128)(2,1)S(1)}, bf16[256,1024]{1,0:T(8,128)(2,1)S(1)}, u32[]{:S(2)}, u32[]{:S(2)}) collective-permute-start(bf16[256,1024]{1,0:T(8,128)(2,1)S(1)} %get-tuple-element.29.refs_4_), channel_id=1, source_target_pairs={{0,1},{1,0},{2,3},{3,2},{4,5},{5,4},{6,7},{7,6},{8,9},{9,8},{10,11... | collective-permute-start | bytes 1572872 | tf_op jit(solution)/shard_map/ppermute | solution.py:325
  36.1 1.8 %collective-permute-done.11.refs_1_ = bf16[128,1792]{1,0:T(8,128)(2,1)S(1)} collective-permute-done((bf16[128,1792]{1,0:T(8,128)(2,1)S(1)}, bf16[128,1792]{1,0:T(8,128)(2,1)S(1)}, u32[]{:S(2)}, u32[]{:S(2)}) %collective-permute-start.11) | collective-permute-done | bytes 458784 | tf_op jit(solution)/shard_map/ppermute | solution.py:56
  39.8 9.5 %collective-permute-done.7.refs_1_ = bf16[256,1024]{1,0:T(8,128)(2,1)S(1)} collective-permute-done((bf16[256,1024]{1,0:T(8,128)(2,1)S(1)}, bf16[256,1024]{1,0:T(8,128)(2,1)S(1)}, u32[]{:S(2)}, u32[]{:S(2)}) %collective-permute-start.7) | collective-permute-done | bytes 524320 | tf_op jit(solution)/shard_map/ppermute | solution.py:325
  52.0 1.7 %collective-permute-done.17.refs_3_ = bf16[128,1024]{1,0:T(8,128)(2,1)S(1)} collective-permute-done((bf16[128,1024]{1,0:T(8,128)(2,1)S(1)}, bf16[128,1024]{1,0:T(8,128)(2,1)S(1)}, u32[]{:S(2)}, u32[]{:S(2)}) %collective-permute-start.17) | collective-permute-done | bytes 262176 | tf_op jit(solution)/shard_map/ppermute | solution.py:325
  53.7 3.2 %grad.1 = (f32[128,1792]{1,0:T(8,128)S(1)}, bf16[64,1792]{1,0:T(8,128)(2,1)S(1)}, bf16[64,1792]{1,0:T(8,128)(2,1)S(1)}) custom-call(f32[128,1024]{1,0:T(8,128)S(1)} %get-tuple-element.40.refs_0_, f32[128,1024]{1,0:T(8,128)S(1)} %get-tuple-element.41.refs_1_, f32[128,1024]{1,0:T(8,128)S(1)} %get-tuple-element.42.refs_2_, ...), custom_call_target="tpu_custom_call" | custom-call | flops 939524096 | bytes 10846208 | tf_op jit(solution)/shard_map/grad/grad/pallas_call | solution.py:52
  57.6 1.7 %collective-permute-start.14 = (bf16[64,1792]{1,0:T(8,128)(2,1)S(1)}, bf16[64,1792]{1,0:T(8,128)(2,1)S(1)}, u32[]{:S(2)}, u32[]{:S(2)}) collective-permute-start(bf16[64,1792]{1,0:T(8,128)(2,1)S(1)} %add.12.refs_7_), channel_id=1, source_target_pairs={{0,16},{8,24},{16,0},{24,8},{1,17},{9,25},{17,1},{25,9},{2,18},{10... | collective-permute-start | bytes 688136 | tf_op jit(solution)/shard_map/ppermute | solution.py:56
  60.4 5.6 %collective-permute-done.14.refs_2_ = bf16[64,1792]{1,0:T(8,128)(2,1)S(1)} collective-permute-done((bf16[64,1792]{1,0:T(8,128)(2,1)S(1)}, bf16[64,1792]{1,0:T(8,128)(2,1)S(1)}, u32[]{:S(2)}, u32[]{:S(2)}) %collective-permute-start.14) | collective-permute-done | bytes 229408 | tf_op jit(solution)/shard_map/ppermute | solution.py:56
  66.1 1.6 %collective-permute-start.15 = (bf16[32,1792]{1,0:T(8,128)(2,1)S(1)}, bf16[32,1792]{1,0:T(8,128)(2,1)S(1)}, u32[]{:S(2)}, u32[]{:S(2)}) collective-permute-start(bf16[32,1792]{1,0:T(8,128)(2,1)S(1)} %get-tuple-element.37), channel_id=1, source_target_pairs={{0,2},{2,0},{4,6},{6,4},{1,3},{3,1},{5,7},{7,5},{8,10},{10,8},{12,... | collective-permute-start | bytes 344072 | tf_op jit(solution)/shard_map/ppermute | solution.py:56
  67.7 1.7 %collective-permute-start.20 = (bf16[32,1792]{1,0:T(8,128)(2,1)S(1)}, bf16[32,1792]{1,0:T(8,128)(2,1)S(1)}, u32[]{:S(2)}, u32[]{:S(2)}) collective-permute-start(bf16[32,1792]{1,0:T(8,128)(2,1)S(1)} %get-tuple-element.46), channel_id=1, source_target_pairs={{0,16},{8,24},{16,0},{24,8},{1,17},{9,25},{17,1},{25,9},{2,18},{10... | collective-permute-start | bytes 344072 | tf_op jit(solution)/shard_map/ppermute | solution.py:56
  70.1 1.9 %collective-permute-done.15.refs_1_ = bf16[32,1792]{1,0:T(8,128)(2,1)S(1)} collective-permute-done((bf16[32,1792]{1,0:T(8,128)(2,1)S(1)}, bf16[32,1792]{1,0:T(8,128)(2,1)S(1)}, u32[]{:S(2)}, u32[]{:S(2)}) %collective-permute-start.15) | collective-permute-done | bytes 114720 | tf_op jit(solution)/shard_map/ppermute | solution.py:56
  72.5 1.9 %collective-permute-done.22.refs_3_ = bf16[32,1792]{1,0:T(8,128)(2,1)S(1)} collective-permute-done((bf16[32,1792]{1,0:T(8,128)(2,1)S(1)}, bf16[32,1792]{1,0:T(8,128)(2,1)S(1)}, u32[]{:S(2)}, u32[]{:S(2)}) %collective-permute-start.22) | collective-permute-done | bytes 114720 | tf_op jit(solution)/shard_map/ppermute | solution.py:56
  75.3 3.4 %collective-permute-done.16.refs_1_ = bf16[16,1792]{1,0:T(8,128)(2,1)S(1)} collective-permute-done((bf16[16,1792]{1,0:T(8,128)(2,1)S(1)}, bf16[16,1792]{1,0:T(8,128)(2,1)S(1)}, u32[]{:S(2)}, u32[]{:S(2)}) %collective-permute-start.16) | collective-permute-done | bytes 57376 | tf_op jit(solution)/shard_map/ppermute | solution.py:56
  (61 shorter events, 13.5 us)
Async XLA Ops:
  0.6 10.1 %collective-permute-start = (bf16[16,1792]{1,0:T(8,128)(2,1)}, bf16[16,1792]{1,0:T(8,128)(2,1)S(1)}, u32[]{:S(2)}, u32[]{:S(2)}) collective-permute-start(bf16[16,1792]{1,0:T(8,128)(2,1)} %refs_0_.3), channel_id=1, source_target_pairs={{0,4},{2,6},{4,0},{6,2},{1,5},{3,7},{5,1},{7,3},{8,12},{10,14},{12... | collective-permute-start | bytes 172040 | tf_op jit(solution)/shard_map/ppermute | solution.py:56
  6.2 4.5 %collective-permute-start.1 = (bf16[16,128]{1,0:T(8,128)(2,1)S(1)}, bf16[16,128]{1,0:T(8,128)(2,1)S(1)}, u32[]{:S(2)}, u32[]{:S(2)}) collective-permute-start(bf16[16,128]{1,0:T(8,128)(2,1)S(1)} %routing.1.refs_1_.refs_2_), channel_id=1, source_target_pairs={{0,4},{2,6},{4,0},{6,2},{1,5},{3,7},{5,1},{7,3},{8,12},{10,14},{12... | collective-permute-start | bytes 12296 | tf_op jit(solution)/shard_map/ppermute | solution.py:56
  10.8 4.9 %collective-permute-start.2 = (bf16[32,1920]{1,0:T(8,128)(2,1)S(1)}, bf16[32,1920]{1,0:T(8,128)(2,1)S(1)}, u32[]{:S(2)}, u32[]{:S(2)}) collective-permute-start(bf16[32,1920]{1,0:T(8,128)(2,1)S(1)} %get-tuple-element.26.refs_0_), channel_id=1, source_target_pairs={{0,2},{2,0},{4,6},{6,4},{1,3},{3,1},{5,7},{7,5},{8,10},{10,8},{12,... | collective-permute-start | bytes 368648 | tf_op jit(solution)/shard_map/ppermute | solution.py:56
  12.4 9.9 %collective-permute-start.3 = (bf16[32,1920]{1,0:T(8,128)(2,1)S(1)}, bf16[32,1920]{1,0:T(8,128)(2,1)S(1)}, u32[]{:S(2)}, u32[]{:S(2)}) collective-permute-start(bf16[32,1920]{1,0:T(8,128)(2,1)S(1)} %get-tuple-element.26.refs_0_), channel_id=1, source_target_pairs={{0,16},{8,24},{16,0},{24,8},{1,17},{9,25},{17,1},{25,9},{2,18},{10... | collective-permute-start | bytes 368648 | tf_op jit(solution)/shard_map/ppermute | solution.py:56
  15.7 6.6 %collective-permute-start.4 = (bf16[32,1920]{1,0:T(8,128)(2,1)S(1)}, bf16[32,1920]{1,0:T(8,128)(2,1)S(1)}, u32[]{:S(2)}, u32[]{:S(2)}) collective-permute-start(bf16[32,1920]{1,0:T(8,128)(2,1)S(1)} %collective-permute-done.2.refs_1_), channel_id=1, source_target_pairs={{0,16},{8,24},{16,0},{24,8},{1,17},{9,25},{17,1},{25,9},{2,18},{10... | collective-permute-start | bytes 368648 | tf_op jit(solution)/shard_map/ppermute | solution.py:56
  17.2 5.1 %collective-permute-start.5 = (bf16[16,1792]{1,0:T(8,128)(2,1)S(1)}, bf16[16,1792]{1,0:T(8,128)(2,1)S(1)}, u32[]{:S(2)}, u32[]{:S(2)}) collective-permute-start(bf16[16,1792]{1,0:T(8,128)(2,1)S(1)} %get-tuple-element.27.refs_0_), channel_id=1, source_target_pairs={{0,4},{2,6},{4,0},{6,2},{1,5},{3,7},{5,1},{7,3},{8,12},{10,14},{12... | collective-permute-start | bytes 172040 | tf_op jit(solution)/shard_map/ppermute | solution.py:56
  22.4 6.2 %collective-permute-start.6 = (bf16[128,1920]{1,0:T(8,128)(2,1)S(1)}, bf16[128,1920]{1,0:T(8,128)(2,1)S(1)}, u32[]{:S(2)}, u32[]{:S(2)}) collective-permute-start(bf16[128,1920]{1,0:T(8,128)(2,1)S(1)} %pack.4.refs_1_), channel_id=1, source_target_pairs={{0,8},{8,0},{16,24},{24,16},{1,9},{9,1},{17,25},{25,17},{2,10},{10... | collective-permute-start | bytes 1474568 | tf_op jit(solution)/shard_map/ppermute | solution.py:56
  22.5 6.0 %collective-permute-start.8 = (bf16[32,1792]{1,0:T(8,128)(2,1)S(1)}, bf16[32,1792]{1,0:T(8,128)(2,1)S(1)}, u32[]{:S(2)}, u32[]{:S(2)}) collective-permute-start(bf16[32,1792]{1,0:T(8,128)(2,1)S(1)} %pack.3.refs_4_.refs_0_), channel_id=1, source_target_pairs={{0,2},{2,0},{4,6},{6,4},{1,3},{3,1},{5,7},{7,5},{8,10},{10,8},{12,... | collective-permute-start | bytes 344072 | tf_op jit(solution)/shard_map/ppermute | solution.py:56
  24.7 11.3 %collective-permute-start.9 = (bf16[32,1792]{1,0:T(8,128)(2,1)S(1)}, bf16[32,1792]{1,0:T(8,128)(2,1)S(1)}, u32[]{:S(2)}, u32[]{:S(2)}) collective-permute-start(bf16[32,1792]{1,0:T(8,128)(2,1)S(1)} %pack.3.refs_4_.refs_0_), channel_id=1, source_target_pairs={{0,16},{8,24},{16,0},{24,8},{1,17},{9,25},{17,1},{25,9},{2,18},{10... | collective-permute-start | bytes 344072 | tf_op jit(solution)/shard_map/ppermute | solution.py:56
  28.5 7.6 %collective-permute-start.10 = (bf16[32,1792]{1,0:T(8,128)(2,1)S(1)}, bf16[32,1792]{1,0:T(8,128)(2,1)S(1)}, u32[]{:S(2)}, u32[]{:S(2)}) collective-permute-start(bf16[32,1792]{1,0:T(8,128)(2,1)S(1)} %collective-permute-done.8.refs_1_), channel_id=1, source_target_pairs={{0,16},{8,24},{16,0},{24,8},{1,17},{9,25},{17,1},{25,9},{2,18},{10... | collective-permute-start | bytes 344072 | tf_op jit(solution)/shard_map/ppermute | solution.py:56
  34.5 14.9 %collective-permute-start.7 = (bf16[256,1024]{1,0:T(8,128)(2,1)S(1)}, bf16[256,1024]{1,0:T(8,128)(2,1)S(1)}, u32[]{:S(2)}, u32[]{:S(2)}) collective-permute-start(bf16[256,1024]{1,0:T(8,128)(2,1)S(1)} %get-tuple-element.29.refs_4_), channel_id=1, source_target_pairs={{0,1},{1,0},{2,3},{3,2},{4,5},{5,4},{6,7},{7,6},{8,9},{9,8},{10,11... | collective-permute-start | bytes 1572872 | tf_op jit(solution)/shard_map/ppermute | solution.py:325
  36.1 1.9 %collective-permute-start.11 = (bf16[128,1792]{1,0:T(8,128)(2,1)S(1)}, bf16[128,1792]{1,0:T(8,128)(2,1)S(1)}, u32[]{:S(2)}, u32[]{:S(2)}) collective-permute-start(bf16[128,1792]{1,0:T(8,128)(2,1)S(1)} %pack.5.refs_0_), channel_id=1, source_target_pairs={{0,8},{8,0},{16,24},{24,16},{1,9},{9,1},{17,25},{25,17},{2,10},{10... | collective-permute-start | bytes 1376264 | tf_op jit(solution)/shard_map/ppermute | solution.py:56
  39.2 14.5 %collective-permute-start.17 = (bf16[128,1024]{1,0:T(8,128)(2,1)S(1)}, bf16[128,1024]{1,0:T(8,128)(2,1)S(1)}, u32[]{:S(2)}, u32[]{:S(2)}) collective-permute-start(bf16[128,1024]{1,0:T(8,128)(2,1)S(1)} %get-tuple-element.32.refs_5_), channel_id=1, source_target_pairs={{0,1},{1,0},{2,3},{3,2},{4,5},{5,4},{6,7},{7,6},{8,9},{9,8},{10,11... | collective-permute-start | bytes 786440 | tf_op jit(solution)/shard_map/ppermute | solution.py:325
  50.4 1.6 %collective-permute-start.13 = (bf16[64,1792]{1,0:T(8,128)(2,1)S(1)}, bf16[64,1792]{1,0:T(8,128)(2,1)S(1)}, u32[]{:S(2)}, u32[]{:S(2)}) collective-permute-start(bf16[64,1792]{1,0:T(8,128)(2,1)S(1)} %get-tuple-element.35), channel_id=1, source_target_pairs={{0,8},{8,0},{16,24},{24,16},{1,9},{9,1},{17,25},{25,17},{2,10},{10... | collective-permute-start | bytes 688136 | tf_op jit(solution)/shard_map/ppermute | solution.py:56
  57.0 2.3 %collective-permute-start.19 = (bf16[64,1792]{1,0:T(8,128)(2,1)S(1)}, bf16[64,1792]{1,0:T(8,128)(2,1)S(1)}, u32[]{:S(2)}, u32[]{:S(2)}) collective-permute-start(bf16[64,1792]{1,0:T(8,128)(2,1)S(1)} %get-tuple-element.45), channel_id=1, source_target_pairs={{0,8},{8,0},{16,24},{24,16},{1,9},{9,1},{17,25},{25,17},{2,10},{10... | collective-permute-start | bytes 688136 | tf_op jit(solution)/shard_map/ppermute | solution.py:56
  57.1 3.3 %collective-permute-start.12 = (bf16[64,1792]{1,0:T(8,128)(2,1)S(1)}, bf16[64,1792]{1,0:T(8,128)(2,1)S(1)}, u32[]{:S(2)}, u32[]{:S(2)}) collective-permute-start(bf16[64,1792]{1,0:T(8,128)(2,1)S(1)} %get-tuple-element.34), channel_id=1, source_target_pairs={{0,8},{8,0},{16,24},{24,16},{1,9},{9,1},{17,25},{25,17},{2,10},{10... | collective-permute-start | bytes 688136 | tf_op jit(solution)/shard_map/ppermute | solution.py:56
  57.6 8.5 %collective-permute-start.14 = (bf16[64,1792]{1,0:T(8,128)(2,1)S(1)}, bf16[64,1792]{1,0:T(8,128)(2,1)S(1)}, u32[]{:S(2)}, u32[]{:S(2)}) collective-permute-start(bf16[64,1792]{1,0:T(8,128)(2,1)S(1)} %add.12.refs_7_), channel_id=1, source_target_pairs={{0,16},{8,24},{16,0},{24,8},{1,17},{9,25},{17,1},{25,9},{2,18},{10... | collective-permute-start | bytes 688136 | tf_op jit(solution)/shard_map/ppermute | solution.py:56
  59.3 10.2 %collective-permute-start.18 = (bf16[64,1792]{1,0:T(8,128)(2,1)S(1)}, bf16[64,1792]{1,0:T(8,128)(2,1)S(1)}, u32[]{:S(2)}, u32[]{:S(2)}) collective-permute-start(bf16[64,1792]{1,0:T(8,128)(2,1)S(1)} %get-tuple-element.44), channel_id=1, source_target_pairs={{0,8},{8,0},{16,24},{24,16},{1,9},{9,1},{17,25},{25,17},{2,10},{10... | collective-permute-start | bytes 688136 | tf_op jit(solution)/shard_map/ppermute | solution.py:56
  59.4 10.1 %collective-permute-start.21 = (bf16[32,1792]{1,0:T(8,128)(2,1)S(1)}, bf16[32,1792]{1,0:T(8,128)(2,1)S(1)}, u32[]{:S(2)}, u32[]{:S(2)}) collective-permute-start(bf16[32,1792]{1,0:T(8,128)(2,1)S(1)} %get-tuple-element.47), channel_id=1, source_target_pairs={{0,16},{8,24},{16,0},{24,8},{1,17},{9,25},{17,1},{25,9},{2,18},{10... | collective-permute-start | bytes 344072 | tf_op jit(solution)/shard_map/ppermute | solution.py:56
  66.1 5.8 %collective-permute-start.15 = (bf16[32,1792]{1,0:T(8,128)(2,1)S(1)}, bf16[32,1792]{1,0:T(8,128)(2,1)S(1)}, u32[]{:S(2)}, u32[]{:S(2)}) collective-permute-start(bf16[32,1792]{1,0:T(8,128)(2,1)S(1)} %get-tuple-element.37), channel_id=1, source_target_pairs={{0,2},{2,0},{4,6},{6,4},{1,3},{3,1},{5,7},{7,5},{8,10},{10,8},{12,... | collective-permute-start | bytes 344072 | tf_op jit(solution)/shard_map/ppermute | solution.py:56
  67.7 4.8 %collective-permute-start.20 = (bf16[32,1792]{1,0:T(8,128)(2,1)S(1)}, bf16[32,1792]{1,0:T(8,128)(2,1)S(1)}, u32[]{:S(2)}, u32[]{:S(2)}) collective-permute-start(bf16[32,1792]{1,0:T(8,128)(2,1)S(1)} %get-tuple-element.46), channel_id=1, source_target_pairs={{0,16},{8,24},{16,0},{24,8},{1,17},{9,25},{17,1},{25,9},{2,18},{10... | collective-permute-start | bytes 344072 | tf_op jit(solution)/shard_map/ppermute | solution.py:56
  69.5 4.9 %collective-permute-start.22 = (bf16[32,1792]{1,0:T(8,128)(2,1)S(1)}, bf16[32,1792]{1,0:T(8,128)(2,1)S(1)}, u32[]{:S(2)}, u32[]{:S(2)}) collective-permute-start(bf16[32,1792]{1,0:T(8,128)(2,1)S(1)} %add.17), channel_id=1, source_target_pairs={{0,2},{2,0},{4,6},{6,4},{1,3},{3,1},{5,7},{7,5},{8,10},{10,8},{12,... | collective-permute-start | bytes 344072 | tf_op jit(solution)/shard_map/ppermute | solution.py:56
  72.0 6.8 %collective-permute-start.16 = (bf16[16,1792]{1,0:T(8,128)(2,1)S(1)}, bf16[16,1792]{1,0:T(8,128)(2,1)S(1)}, u32[]{:S(2)}, u32[]{:S(2)}) collective-permute-start(bf16[16,1792]{1,0:T(8,128)(2,1)S(1)} %get-tuple-element.39), channel_id=1, source_target_pairs={{0,4},{2,6},{4,0},{6,2},{1,5},{3,7},{5,1},{7,3},{8,12},{10,14},{12... | collective-permute-start | bytes 172040 | tf_op jit(solution)/shard_map/ppermute | solution.py:56
  74.4 5.8 %collective-permute-start.23 = (bf16[16,1792]{1,0:T(8,128)(2,1)S(1)}, bf16[16,1792]{1,0:T(8,128)(2,1)S(1)}, u32[]{:S(2)}, u32[]{:S(2)}) collective-permute-start(bf16[16,1792]{1,0:T(8,128)(2,1)S(1)} %get-tuple-element.49), channel_id=1, source_target_pairs={{0,4},{2,6},{4,0},{6,2},{1,5},{3,7},{5,1},{7,3},{8,12},{10,14},{12... | collective-permute-start | bytes 172040 | tf_op jit(solution)/shard_map/ppermute | solution.py:56
  (9 other events, 24.9 us)

commit v5 on v4

--- a/solution.py
+++ b/solution.py
@@ -10,6 +10,7 @@
 PLANE = ("group", "ingroup")
 LANES = 128
 CHUNK = 256
+PIECES = 4
 BF16 = jnp.bfloat16
 F32 = jnp.float32
 
@@ -140,16 +141,14 @@
         second = pack([second, swap(second, "ingroup", bit)])
     first = pack([first, beside, across, last], after=[second])
     beside = swap(second, "ingroup", inner[-1])
-    across = swap(second, "group", outer[0])
-    last = swap(beside, "group", outer[0])
     for bit in outer[1:-1]:
         first = pack([first, swap(first, "group", bit)])
     first = [first, swap(first, "group", outer[-1])]
-    return first, [second, beside, across, last]
+    return first, [second, beside]
 
 
 def spread_end(parts, after):
-    bits = bits_of("group")[1:]
+    bits = bits_of("group")
     current = pack(parts, after)
     for bit in bits[:-1]:
         current = pack([current, swap(current, "group", bit)])
@@ -157,11 +156,19 @@
 
 
 def route_body(wide, topk, block, capacity, count, me, *refs):
-    parts, (gate_weight, up_weight, place_out, scale_out, part_out, sent_out) = (
-        refs[:count],
-        refs[count:],
-    )
-    features = gate_weight.shape[0]
+    parts, rest = refs[:count], refs[count:]
+    sources, (place_out, scale_out, part_out, sent_out, *held, sems) = rest[:2], rest[2:]
+    features, hidden = sources[0].shape
+    width = hidden // PIECES
+    copies = []
+    for i in range(2):
+        for j in range(PIECES):
+            piece = pl.ds(j * width, width)
+            copy = pltpu.make_async_copy(
+                sources[i].at[:, piece], held[i].at[:, piece], sems.at[i, j]
+            )
+            copy.start()
+            copies.append(copy)
     total, slots = place_out.shape
     routing = jnp.concatenate([p[:, wide : wide + LANES] for p in parts], axis=0)
     lane = lax.broadcasted_iota(jnp.int32, (total, LANES), 1)
@@ -192,10 +199,13 @@
     scale_out[...] = (high * 256.0 + low) / 65536.0
     values = jnp.concatenate([p[:, :features] for p in parts], axis=0)
     rows = dot(place, values, 0, 0).astype(BF16)
-    for i, weight in enumerate((gate_weight, up_weight)):
-        part = dot(rows, weight[...])
-        part_out[i * slots : (i + 1) * slots] = part
-        sent_out[i * slots : (i + 1) * slots] = part.astype(BF16)
+    for i in range(2):
+        for j in range(PIECES):
+            copies[i * PIECES + j].wait()
+            columns = slice(j * width, (j + 1) * width)
+            part = dot(rows, held[i][:, columns])
+            part_out[i * slots : (i + 1) * slots, columns] = part
+            sent_out[i * slots : (i + 1) * slots, columns] = part.astype(BF16)
 
 
 def back_body(count, *refs):
@@ -214,12 +224,13 @@
     return total
 
 
-def place_rows(place, rows, near_out, first_out, second_out):
-    half = near_out.shape[0]
-    middle = half + second_out.shape[0]
-    first_out[...] = dot(place[middle:], rows).astype(BF16)
-    second_out[...] = dot(place[half:middle], rows).astype(BF16)
-    near_out[...] = dot(place[:half], rows)
+def place_rows(place, rows, near_out, *far_outs):
+    end = place.shape[0]
+    for out in far_outs:
+        start = end - out.shape[0]
+        out[...] = dot(place[start:end], rows).astype(BF16)
+        end = start
+    near_out[...] = dot(place[:end], rows)
 
 
 def forward_sums(both, received):
@@ -229,11 +240,11 @@
 
 
 def out_body(peers, *refs):
-    scale, place, weight, _, near_out, first_out, second_out = refs[1 + peers :]
+    scale, place, weight, _, *outs = refs[1 + peers :]
     gate_pre, up_pre = forward_sums(refs[0], refs[1 : 1 + peers])
     hidden = (gate_pre / (1.0 + jnp.exp(-gate_pre)) * up_pre).astype(BF16)
     rows = (dot(hidden, weight[...]) * scale[:, :1]).astype(BF16)
-    place_rows(place, rows, near_out, first_out, second_out)
+    place_rows(place[...], rows, *outs)
 
 
 def factor_body(peers, *refs):
@@ -248,12 +259,12 @@
 def grad_body(peers, *refs):
     gate_factor, up_factor, back = refs[:3]
     back_in = refs[3 : 3 + peers]
-    place, gate_weight, up_weight, _, near_out, first_out, second_out = refs[3 + peers :]
+    place, gate_weight, up_weight, _, *outs = refs[3 + peers :]
     d_hidden = summed(back, back_in)
     d_gate = (d_hidden * gate_factor[...]).astype(BF16)
     d_up = (d_hidden * up_factor[...]).astype(BF16)
     rows = (dot(d_gate, gate_weight[...], 1, 1) + dot(d_up, up_weight[...], 1, 1)).astype(BF16)
-    place_rows(place, rows, near_out, first_out, second_out)
+    place_rows(place[...], rows, *outs)
 
 
 def add_body(count, at, parts, keep, *refs):
@@ -276,15 +287,14 @@
     )
 
 
-def collect_start(near, first, second):
+def collect_start(near, *pieces):
     for bit in reversed(bits_of("group")[2:]):
-        half, quarter = near.shape[0] // 2, near.shape[0] // 4
-        got_first, got_second = swap(first, "group", bit), swap(second, "group", bit)
-        (first,) = add(near, half + quarter, [(got_first, quarter)], [(quarter, BF16)])
-        (second,) = add(near, half, [(got_first, 0)], [(quarter, BF16)])
-        (near,) = add(near, 0, [(got_second, 0)], [(half, F32)])
-    bit = bits_of("group")[1]
-    return near, swap(first, "group", bit), swap(second, "group", bit)
+        half = near.shape[0] // 2
+        got = jnp.concatenate([swap(piece, "group", bit) for piece in pieces[::-1]], axis=0)
+        outs = [(piece.shape[0] // 2, BF16) for piece in pieces[::-1]]
+        pieces = add(near, half, [(got, half)], outs)[::-1]
+        (near,) = add(near, 0, [(got, 0)], [(half, F32)])
+    return near, *[swap(piece, "group", bits_of("group")[1]) for piece in pieces]
 
 
 def collect_end(near, far, bits):
@@ -296,21 +306,21 @@
         near, far = add(near, 0, [(received, 0)], [(half, F32), (half, BF16)])
 
 
-def collect_few(near, far, got_second):
-    inner, outer = bits_of("ingroup"), bits_of("group")
-    half = near.shape[0] // 2
+def collect_across(near, *got):
+    half, bit = near.shape[0] // 2, bits_of("group")[0]
     quarter = half // 2
-    received = swap(far, "group", outer[0])
-    near, far = add(near, 0, [(got_second, 0), (received, 0)], [(quarter, F32), (quarter, BF16)])
-    return collect_end(near, far, inner[::-1])
-
-
-def collect_early(near, got_first, got_second):
-    inner, outer = bits_of("ingroup"), bits_of("group")
+    if len(got) == 1:
+        low, high = add(near, half, [(got[0], 0)], [(quarter, BF16)] * 2)
+    else:
+        (high,) = add(near, half + quarter, [(got[0], 0)], [(quarter, BF16)])
+        (low,) = add(near, half, [(got[1], 0)], [(quarter, BF16)])
+    return swap(high, "group", bit), swap(low, "group", bit)
+
+
+def collect_rest(near, got_second, across, last):
+    inner = bits_of("ingroup")
     half = near.shape[0] // 2
     quarter, eighth = half // 2, half // 4
-    low, high = add(near, half, [(got_first, 0)], [(quarter, BF16), (quarter, BF16)])
-    across, last = swap(high, "group", outer[0]), swap(low, "group", outer[0])
     (far,) = add(near, quarter, [(got_second, quarter), (across, 0)], [(quarter, BF16)])
     beside = swap(far, "ingroup", inner[-1])
     near, far = add(
@@ -349,6 +359,10 @@
         [((total, slots), BF16), ((slots, LANES), F32), both, both_sent],
         [me] + x_parts + [w_gate, w_up],
         2 * product,
+        50,
+        hbm=(len(x_parts) + 1, len(x_parts) + 2),
+        scratch=[pltpu.VMEM((features, hidden), BF16)] * 2
+        + [pltpu.SemaphoreType.DMA((2, PIECES))],
     )
     both_in = from_peers(both_sent)
     d_parts = spread_end(d_parts, [both_sent])
@@ -357,37 +371,36 @@
         "back", functools.partial(back_body, len(d_parts)), sums, d_parts + [place, w_down], product
     )
     back_in = from_peers(back_sent)
-    placed = [((total // 2, features), F32)] + [((total // 4, features), BF16)] * 2
-    near, got_first, got_second = collect_start(
+    near = ((total // 2, features), F32)
+    fourth, eighth = ((total // 4, features), BF16), ((total // 8, features), BF16)
+    near_y, got_high, got_low, got_y = collect_start(
         *call(
             "out",
             functools.partial(out_body, peers),
-            placed,
+            [near, eighth, eighth, fourth],
             [both] + both_in + [scale, place, w_down, back_sent],
             product,
         )
     )
-    half = near.shape[0] // 2
-    (far,) = add(near, half, [(got_first, 0)], [(half, BF16)])
+    across, last = collect_across(near_y, got_high, got_low)
     factors = call(
         "factor",
         functools.partial(factor_body, peers),
         [((slots, hidden), F32)] * 2,
         [both] + both_in + [scale],
     )
-    grad = collect_early(
-        *collect_start(
-            *call(
-                "grad",
-                functools.partial(grad_body, peers),
-                placed,
-                list(factors) + [back] + back_in + [place, w_gate, w_up, far],
-                2 * product,
-                24,
-            )
+    near_dx, got_first, got_dx = collect_start(
+        *call(
+            "grad",
+            functools.partial(grad_body, peers),
+            [near, fourth, fourth],
+            list(factors) + [back] + back_in + [place, w_gate, w_up, across],
+            2 * product,
+            24,
         )
     )
-    return collect_few(near, far, got_second), grad
+    mixed = collect_rest(near_y, got_y, across, last)
+    return mixed, collect_rest(near_dx, got_dx, *collect_across(near_dx, got_first))
 
 
 def solution(mesh):

time: 81.1 us -> 75.4 us (0.930)
  waiting for transfers between devices: 41.9 us -> 32.7 us
  starting transfers between devices: 22.2 us -> 26.4 us
  local copies, waits for them, and re-layouts: 6.29 us -> 2.22 us
  Pallas kernels: 9.65 us -> 13.1 us
    ppermute x2, waiting for transfers between devices: 11.2 us -> 1.97 us  [from_peers(): lax.ppermute(sent, 'dp', [(i, (i + step) % count) for i in range(count)])]
    unnamed x18 -> x14, local copies, waits for them, and re-layouts: 6.29 us -> 2.22 us
    pallas_call x19 -> x21, Pallas kernels: 9.65 us -> 13.1 us  [call(): return kernel(*args, *passed)]
    ppermute x22 -> x23, starting transfers between devices: 20.1 us -> 23.3 us  [swap(): lax.ppermute(value, axis, [(i, i ^ offset) for i in range(lax.axis_size(a...]
    ppermute x2, starting transfers between devices: 2.16 us -> 3.05 us  [from_peers(): lax.ppermute(sent, 'dp', [(i, (i + step) % count) for i in range(count)])]
    ppermute x22 -> x23, waiting for transfers between devices: 30.6 us -> 30.7 us  [swap(): lax.ppermute(value, axis, [(i, i ^ offset) for i in range(lax.axis_size(a...]
  transfers between devices with their start and end apart: 24 -> 25, of which waited for: 14 -> 15; matrix products, arithmetic and copies ran while one was open for 0% -> 0% of each run, Pallas kernels for 7% -> 12%
where the time goes in v5:
time: 75.4 us; the launch traced here: 75.2 us
  waiting for transfers between devices  32.7 us (43%)
  starting transfers between devices  26.4 us (35%)
  Pallas kernels  13.1 us (17%)
  local copies, waits for them, and re-layouts  2.22 us (3%)
  between operations  0.81 us (1%)
    ppermute x23, waiting for transfers between devices, swap(): lax.ppermute(value, axis, [(i, i ^ offset) for i in range(lax.axis_size(a...  30.7 us
    ppermute x23, starting transfers between devices, swap(): lax.ppermute(value, axis, [(i, i ^ offset) for i in range(lax.axis_size(a...  23.3 us
    pallas_call x21, Pallas kernels, call(): return kernel(*args, *passed)  13.1 us
    ppermute x2, starting transfers between devices, from_peers(): lax.ppermute(sent, 'dp', [(i, (i + step) % count) for i in range(count)])  3.05 us
    unnamed x14, local copies, waits for them, and re-layouts  2.22 us
    ppermute x2, waiting for transfers between devices, from_peers(): lax.ppermute(sent, 'dp', [(i, (i + step) % count) for i in range(count)])  1.97 us
  transfers between devices with their start and end apart: 25, of which 15 were waited for; matrix products, arithmetic and copies ran while one was open for 0% of the time, Pallas kernels for 12%

profile of v5, /device:TPU:0, one launch (start us, length us, event | category | flops | bytes accessed | tf_op | source)
XLA Modules:
  0.0 75.2 jit_solution(12772501036062381181)
XLA Ops:
  0.6 4.1 %collective-permute-start = (bf16[16,1792]{1,0:T(8,128)(2,1)}, bf16[16,1792]{1,0:T(8,128)(2,1)S(1)}, u32[]{:S(2)}, u32[]{:S(2)}) collective-permute-start(bf16[16,1792]{1,0:T(8,128)(2,1)} %refs_0_.3), channel_id=1, source_target_pairs={{0,4},{2,6},{4,0},{6,2},{1,5},{3,7},{5,1},{7,3},{8,12},{10,14},{12... | collective-permute-start | bytes 172040 | tf_op jit(solution)/shard_map/ppermute | solution.py:57
  7.1 3.7 %collective-permute-done.1.refs_3_ = bf16[16,128]{1,0:T(8,128)(2,1)S(1)} collective-permute-done((bf16[16,128]{1,0:T(8,128)(2,1)S(1)}, bf16[16,128]{1,0:T(8,128)(2,1)S(1)}, u32[]{:S(2)}, u32[]{:S(2)}) %collective-permute-start.1) | collective-permute-done | bytes 4128 | tf_op jit(solution)/shard_map/ppermute | solution.py:57
  10.8 1.6 %collective-permute-start.2 = (bf16[32,1920]{1,0:T(8,128)(2,1)S(1)}, bf16[32,1920]{1,0:T(8,128)(2,1)S(1)}, u32[]{:S(2)}, u32[]{:S(2)}) collective-permute-start(bf16[32,1920]{1,0:T(8,128)(2,1)S(1)} %get-tuple-element.25.refs_0_), channel_id=1, source_target_pairs={{0,2},{2,0},{4,6},{6,4},{1,3},{3,1},{5,7},{7,5},{8,10},{10,8},{12,... | collective-permute-start | bytes 368648 | tf_op jit(solution)/shard_map/ppermute | solution.py:57
  12.4 1.5 %collective-permute-start.3 = (bf16[32,1920]{1,0:T(8,128)(2,1)S(1)}, bf16[32,1920]{1,0:T(8,128)(2,1)S(1)}, u32[]{:S(2)}, u32[]{:S(2)}) collective-permute-start(bf16[32,1920]{1,0:T(8,128)(2,1)S(1)} %get-tuple-element.25.refs_0_), channel_id=1, source_target_pairs={{0,16},{8,24},{16,0},{24,8},{1,17},{9,25},{17,1},{25,9},{2,18},{10... | collective-permute-start | bytes 368648 | tf_op jit(solution)/shard_map/ppermute | solution.py:57
  13.9 1.8 %collective-permute-done.2.refs_1_ = bf16[32,1920]{1,0:T(8,128)(2,1)S(1)} collective-permute-done((bf16[32,1920]{1,0:T(8,128)(2,1)S(1)}, bf16[32,1920]{1,0:T(8,128)(2,1)S(1)}, u32[]{:S(2)}, u32[]{:S(2)}) %collective-permute-start.2) | collective-permute-done | bytes 122912 | tf_op jit(solution)/shard_map/ppermute | solution.py:57
  15.7 1.5 %collective-permute-start.4 = (bf16[32,1920]{1,0:T(8,128)(2,1)S(1)}, bf16[32,1920]{1,0:T(8,128)(2,1)S(1)}, u32[]{:S(2)}, u32[]{:S(2)}) collective-permute-start(bf16[32,1920]{1,0:T(8,128)(2,1)S(1)} %collective-permute-done.2.refs_1_), channel_id=1, source_target_pairs={{0,16},{8,24},{16,0},{24,8},{1,17},{9,25},{17,1},{25,9},{2,18},{10... | collective-permute-start | bytes 368648 | tf_op jit(solution)/shard_map/ppermute | solution.py:57
  17.6 4.7 %collective-permute-done.5.refs_1_ = bf16[16,1792]{1,0:T(8,128)(2,1)S(1)} collective-permute-done((bf16[16,1792]{1,0:T(8,128)(2,1)S(1)}, bf16[16,1792]{1,0:T(8,128)(2,1)S(1)}, u32[]{:S(2)}, u32[]{:S(2)}) %collective-permute-start.5) | collective-permute-done | bytes 57376 | tf_op jit(solution)/shard_map/ppermute | solution.py:57
  22.5 2.2 %collective-permute-start.8 = (bf16[32,1792]{1,0:T(8,128)(2,1)S(1)}, bf16[32,1792]{1,0:T(8,128)(2,1)S(1)}, u32[]{:S(2)}, u32[]{:S(2)}) collective-permute-start(bf16[32,1792]{1,0:T(8,128)(2,1)S(1)} %pack.4.refs_4_.refs_0_), channel_id=1, source_target_pairs={{0,2},{2,0},{4,6},{6,4},{1,3},{3,1},{5,7},{7,5},{8,10},{10,8},{12,... | collective-permute-start | bytes 344072 | tf_op jit(solution)/shard_map/ppermute | solution.py:57
  24.7 5.1 %forward.1 = (bf16[256,128]{1,0:T(8,128)(2,1)S(1)}, f32[128,128]{1,0:T(8,128)S(1)}, f32[256,1024]{1,0:T(8,128)S(1)}, bf16[256,1024]{1,0:T(8,128)(2,1)S(1)}) custom-call(s32[1]{0:T(128)} %bitcast.refs_0_, bf16[128,1920]{1,0:T(8,128)(2,1)S(1)} %pack.5.refs_1_, bf16[128,1920]{1,0:T(8,128)(2,1)S(1)} %collective-permute-done.6.refs_2_, ...), custom_call_target="tpu_custom_call" | custom-call | flops 939524096 | bytes 10027012 | tf_op jit(solution)/shard_map/forward/forward/pallas_call | solution.py:53
  30.0 1.5 %collective-permute-start.7 = (bf16[256,1024]{1,0:T(8,128)(2,1)S(1)}, bf16[256,1024]{1,0:T(8,128)(2,1)S(1)}, u32[]{:S(2)}, u32[]{:S(2)}) collective-permute-start(bf16[256,1024]{1,0:T(8,128)(2,1)S(1)} %get-tuple-element.28.refs_2_), channel_id=1, source_target_pairs={{0,1},{1,0},{2,3},{3,2},{4,5},{5,4},{6,7},{7,6},{8,9},{9,8},{10,11... | collective-permute-start | bytes 1572872 | tf_op jit(solution)/shard_map/ppermute | solution.py:335
  31.5 6.1 %collective-permute-done.9.refs_1_ = bf16[64,1792]{1,0:T(8,128)(2,1)S(1)} collective-permute-done((bf16[64,1792]{1,0:T(8,128)(2,1)S(1)}, bf16[64,1792]{1,0:T(8,128)(2,1)S(1)}, u32[]{:S(2)}, u32[]{:S(2)}) %collective-permute-start.9) | collective-permute-done | bytes 229408 | tf_op jit(solution)/shard_map/ppermute | solution.py:57
  37.7 1.8 %collective-permute-done.10.refs_1_ = bf16[128,1792]{1,0:T(8,128)(2,1)S(1)} collective-permute-done((bf16[128,1792]{1,0:T(8,128)(2,1)S(1)}, bf16[128,1792]{1,0:T(8,128)(2,1)S(1)}, u32[]{:S(2)}, u32[]{:S(2)}) %collective-permute-start.10) | collective-permute-done | bytes 458784 | tf_op jit(solution)/shard_map/ppermute | solution.py:57
  40.8 1.6 %collective-permute-start.18 = (bf16[128,1024]{1,0:T(8,128)(2,1)S(1)}, bf16[128,1024]{1,0:T(8,128)(2,1)S(1)}, u32[]{:S(2)}, u32[]{:S(2)}) collective-permute-start(bf16[128,1024]{1,0:T(8,128)(2,1)S(1)} %get-tuple-element.31.refs_5_), channel_id=1, source_target_pairs={{0,1},{1,0},{2,3},{3,2},{4,5},{5,4},{6,7},{7,6},{8,9},{9,8},{10,11... | collective-permute-start | bytes 786440 | tf_op jit(solution)/shard_map/ppermute | solution.py:335
  42.4 2.0 %collective-permute-done.7.refs_1_ = bf16[256,1024]{1,0:T(8,128)(2,1)S(1)} collective-permute-done((bf16[256,1024]{1,0:T(8,128)(2,1)S(1)}, bf16[256,1024]{1,0:T(8,128)(2,1)S(1)}, u32[]{:S(2)}, u32[]{:S(2)}) %collective-permute-start.7) | collective-permute-done | bytes 524320 | tf_op jit(solution)/shard_map/ppermute | solution.py:335
  47.0 2.5 %collective-permute-start.15 = (bf16[32,1792]{1,0:T(8,128)(2,1)S(1)}, bf16[32,1792]{1,0:T(8,128)(2,1)S(1)}, u32[]{:S(2)}, u32[]{:S(2)}) collective-permute-start(bf16[32,1792]{1,0:T(8,128)(2,1)S(1)} %add.14), channel_id=1, source_target_pairs={{0,16},{8,24},{16,0},{24,8},{1,17},{9,25},{17,1},{25,9},{2,18},{10... | collective-permute-start | bytes 344072 | tf_op jit(solution)/shard_map/ppermute | solution.py:57
  49.9 3.0 %collective-permute-done.15.refs_2_.refs_7_ = bf16[32,1792]{1,0:T(8,128)(2,1)S(1)} collective-permute-done((bf16[32,1792]{1,0:T(8,128)(2,1)S(1)}, bf16[32,1792]{1,0:T(8,128)(2,1)S(1)}, u32[]{:S(2)}, u32[]{:S(2)}) %collective-permute-start.15) | collective-permute-done | bytes 114720 | tf_op jit(solution)/shard_map/ppermute | solution.py:57
  52.9 3.2 %grad.1 = (f32[128,1792]{1,0:T(8,128)S(1)}, bf16[64,1792]{1,0:T(8,128)(2,1)S(1)}, bf16[64,1792]{1,0:T(8,128)(2,1)S(1)}) custom-call(f32[128,1024]{1,0:T(8,128)S(1)} %get-tuple-element.38.refs_0_, f32[128,1024]{1,0:T(8,128)S(1)} %get-tuple-element.39.refs_1_, f32[128,1024]{1,0:T(8,128)S(1)} %get-tuple-element.40.refs_2_, ...), custom_call_target="tpu_custom_call" | custom-call | flops 939524096 | bytes 10731520 | tf_op jit(solution)/shard_map/grad/grad/pallas_call | solution.py:53
  57.8 1.8 %collective-permute-start.22 = (bf16[32,1792]{1,0:T(8,128)(2,1)S(1)}, bf16[32,1792]{1,0:T(8,128)(2,1)S(1)}, u32[]{:S(2)}, u32[]{:S(2)}) collective-permute-start(bf16[32,1792]{1,0:T(8,128)(2,1)S(1)} %get-tuple-element.45), channel_id=1, source_target_pairs={{0,16},{8,24},{16,0},{24,8},{1,17},{9,25},{17,1},{25,9},{2,18},{10... | collective-permute-start | bytes 344072 | tf_op jit(solution)/shard_map/ppermute | solution.py:57
  60.4 1.9 %collective-permute-start.16 = (bf16[32,1792]{1,0:T(8,128)(2,1)S(1)}, bf16[32,1792]{1,0:T(8,128)(2,1)S(1)}, u32[]{:S(2)}, u32[]{:S(2)}) collective-permute-start(bf16[32,1792]{1,0:T(8,128)(2,1)S(1)} %add.15), channel_id=1, source_target_pairs={{0,2},{2,0},{4,6},{6,4},{1,3},{3,1},{5,7},{7,5},{8,10},{10,8},{12,... | collective-permute-start | bytes 344072 | tf_op jit(solution)/shard_map/ppermute | solution.py:57
  62.3 1.3 %collective-permute-start.21 = (bf16[32,1792]{1,0:T(8,128)(2,1)S(1)}, bf16[32,1792]{1,0:T(8,128)(2,1)S(1)}, u32[]{:S(2)}, u32[]{:S(2)}) collective-permute-start(bf16[32,1792]{1,0:T(8,128)(2,1)S(1)} %get-tuple-element.44), channel_id=1, source_target_pairs={{0,16},{8,24},{16,0},{24,8},{1,17},{9,25},{17,1},{25,9},{2,18},{10... | collective-permute-start | bytes 344072 | tf_op jit(solution)/shard_map/ppermute | solution.py:57
  63.9 1.9 %collective-permute-start.23 = (bf16[32,1792]{1,0:T(8,128)(2,1)S(1)}, bf16[32,1792]{1,0:T(8,128)(2,1)S(1)}, u32[]{:S(2)}, u32[]{:S(2)}) collective-permute-start(bf16[32,1792]{1,0:T(8,128)(2,1)S(1)} %add.19), channel_id=1, source_target_pairs={{0,2},{2,0},{4,6},{6,4},{1,3},{3,1},{5,7},{7,5},{8,10},{10,8},{12,... | collective-permute-start | bytes 344072 | tf_op jit(solution)/shard_map/ppermute | solution.py:57
  67.9 1.4 %collective-permute-done.23.refs_3_ = bf16[32,1792]{1,0:T(8,128)(2,1)S(1)} collective-permute-done((bf16[32,1792]{1,0:T(8,128)(2,1)S(1)}, bf16[32,1792]{1,0:T(8,128)(2,1)S(1)}, u32[]{:S(2)}, u32[]{:S(2)}) %collective-permute-start.23) | collective-permute-done | bytes 114720 | tf_op jit(solution)/shard_map/ppermute | solution.py:57
  69.5 2.6 %collective-permute-done.17.refs_1_ = bf16[16,1792]{1,0:T(8,128)(2,1)S(1)} collective-permute-done((bf16[16,1792]{1,0:T(8,128)(2,1)S(1)}, bf16[16,1792]{1,0:T(8,128)(2,1)S(1)}, u32[]{:S(2)}, u32[]{:S(2)}) %collective-permute-start.17) | collective-permute-done | bytes 57376 | tf_op jit(solution)/shard_map/ppermute | solution.py:57
  72.7 1.8 %collective-permute-done.24.refs_1_ = bf16[16,1792]{1,0:T(8,128)(2,1)S(1)} collective-permute-done((bf16[16,1792]{1,0:T(8,128)(2,1)S(1)}, bf16[16,1792]{1,0:T(8,128)(2,1)S(1)}, u32[]{:S(2)}, u32[]{:S(2)}) %collective-permute-start.24) | collective-permute-done | bytes 57376 | tf_op jit(solution)/shard_map/ppermute | solution.py:57
  (61 shorter events, 13.8 us)
Async XLA Ops:
  0.6 10.1 %collective-permute-start = (bf16[16,1792]{1,0:T(8,128)(2,1)}, bf16[16,1792]{1,0:T(8,128)(2,1)S(1)}, u32[]{:S(2)}, u32[]{:S(2)}) collective-permute-start(bf16[16,1792]{1,0:T(8,128)(2,1)} %refs_0_.3), channel_id=1, source_target_pairs={{0,4},{2,6},{4,0},{6,2},{1,5},{3,7},{5,1},{7,3},{8,12},{10,14},{12... | collective-permute-start | bytes 172040 | tf_op jit(solution)/shard_map/ppermute | solution.py:57
  6.2 4.5 %collective-permute-start.1 = (bf16[16,128]{1,0:T(8,128)(2,1)S(1)}, bf16[16,128]{1,0:T(8,128)(2,1)S(1)}, u32[]{:S(2)}, u32[]{:S(2)}) collective-permute-start(bf16[16,128]{1,0:T(8,128)(2,1)S(1)} %routing.1.refs_1_.refs_2_), channel_id=1, source_target_pairs={{0,4},{2,6},{4,0},{6,2},{1,5},{3,7},{5,1},{7,3},{8,12},{10,14},{12... | collective-permute-start | bytes 12296 | tf_op jit(solution)/shard_map/ppermute | solution.py:57
  10.8 4.9 %collective-permute-start.2 = (bf16[32,1920]{1,0:T(8,128)(2,1)S(1)}, bf16[32,1920]{1,0:T(8,128)(2,1)S(1)}, u32[]{:S(2)}, u32[]{:S(2)}) collective-permute-start(bf16[32,1920]{1,0:T(8,128)(2,1)S(1)} %get-tuple-element.25.refs_0_), channel_id=1, source_target_pairs={{0,2},{2,0},{4,6},{6,4},{1,3},{3,1},{5,7},{7,5},{8,10},{10,8},{12,... | collective-permute-start | bytes 368648 | tf_op jit(solution)/shard_map/ppermute | solution.py:57
  12.4 9.9 %collective-permute-start.3 = (bf16[32,1920]{1,0:T(8,128)(2,1)S(1)}, bf16[32,1920]{1,0:T(8,128)(2,1)S(1)}, u32[]{:S(2)}, u32[]{:S(2)}) collective-permute-start(bf16[32,1920]{1,0:T(8,128)(2,1)S(1)} %get-tuple-element.25.refs_0_), channel_id=1, source_target_pairs={{0,16},{8,24},{16,0},{24,8},{1,17},{9,25},{17,1},{25,9},{2,18},{10... | collective-permute-start | bytes 368648 | tf_op jit(solution)/shard_map/ppermute | solution.py:57
  15.7 6.6 %collective-permute-start.4 = (bf16[32,1920]{1,0:T(8,128)(2,1)S(1)}, bf16[32,1920]{1,0:T(8,128)(2,1)S(1)}, u32[]{:S(2)}, u32[]{:S(2)}) collective-permute-start(bf16[32,1920]{1,0:T(8,128)(2,1)S(1)} %collective-permute-done.2.refs_1_), channel_id=1, source_target_pairs={{0,16},{8,24},{16,0},{24,8},{1,17},{9,25},{17,1},{25,9},{2,18},{10... | collective-permute-start | bytes 368648 | tf_op jit(solution)/shard_map/ppermute | solution.py:57
  17.2 5.1 %collective-permute-start.5 = (bf16[16,1792]{1,0:T(8,128)(2,1)S(1)}, bf16[16,1792]{1,0:T(8,128)(2,1)S(1)}, u32[]{:S(2)}, u32[]{:S(2)}) collective-permute-start(bf16[16,1792]{1,0:T(8,128)(2,1)S(1)} %get-tuple-element.26.refs_0_), channel_id=1, source_target_pairs={{0,4},{2,6},{4,0},{6,2},{1,5},{3,7},{5,1},{7,3},{8,12},{10,14},{12... | collective-permute-start | bytes 172040 | tf_op jit(solution)/shard_map/ppermute | solution.py:57
  22.4 2.3 %collective-permute-start.6 = (bf16[128,1920]{1,0:T(8,128)(2,1)S(1)}, bf16[128,1920]{1,0:T(8,128)(2,1)S(1)}, u32[]{:S(2)}, u32[]{:S(2)}) collective-permute-start(bf16[128,1920]{1,0:T(8,128)(2,1)S(1)} %pack.5.refs_1_), channel_id=1, source_target_pairs={{0,8},{8,0},{16,24},{24,16},{1,9},{9,1},{17,25},{25,17},{2,10},{10... | collective-permute-start | bytes 1474568 | tf_op jit(solution)/shard_map/ppermute | solution.py:57
  22.5 7.4 %collective-permute-start.8 = (bf16[32,1792]{1,0:T(8,128)(2,1)S(1)}, bf16[32,1792]{1,0:T(8,128)(2,1)S(1)}, u32[]{:S(2)}, u32[]{:S(2)}) collective-permute-start(bf16[32,1792]{1,0:T(8,128)(2,1)S(1)} %pack.4.refs_4_.refs_0_), channel_id=1, source_target_pairs={{0,2},{2,0},{4,6},{6,4},{1,3},{3,1},{5,7},{7,5},{8,10},{10,8},{12,... | collective-permute-start | bytes 344072 | tf_op jit(solution)/shard_map/ppermute | solution.py:57
  29.9 7.7 %collective-permute-start.9 = (bf16[64,1792]{1,0:T(8,128)(2,1)S(1)}, bf16[64,1792]{1,0:T(8,128)(2,1)S(1)}, u32[]{:S(2)}, u32[]{:S(2)}) collective-permute-start(bf16[64,1792]{1,0:T(8,128)(2,1)S(1)} %pack.6.refs_0_), channel_id=1, source_target_pairs={{0,16},{8,24},{16,0},{24,8},{1,17},{9,25},{17,1},{25,9},{2,18},{10... | collective-permute-start | bytes 688136 | tf_op jit(solution)/shard_map/ppermute | solution.py:57
  30.0 14.3 %collective-permute-start.7 = (bf16[256,1024]{1,0:T(8,128)(2,1)S(1)}, bf16[256,1024]{1,0:T(8,128)(2,1)S(1)}, u32[]{:S(2)}, u32[]{:S(2)}) collective-permute-start(bf16[256,1024]{1,0:T(8,128)(2,1)S(1)} %get-tuple-element.28.refs_2_), channel_id=1, source_target_pairs={{0,1},{1,0},{2,3},{3,2},{4,5},{5,4},{6,7},{7,6},{8,9},{9,8},{10,11... | collective-permute-start | bytes 1572872 | tf_op jit(solution)/shard_map/ppermute | solution.py:335
  37.6 1.9 %collective-permute-start.10 = (bf16[128,1792]{1,0:T(8,128)(2,1)S(1)}, bf16[128,1792]{1,0:T(8,128)(2,1)S(1)}, u32[]{:S(2)}, u32[]{:S(2)}) collective-permute-start(bf16[128,1792]{1,0:T(8,128)(2,1)S(1)} %pack.7.refs_0_), channel_id=1, source_target_pairs={{0,8},{8,0},{16,24},{24,16},{1,9},{9,1},{17,25},{25,17},{2,10},{10... | collective-permute-start | bytes 1376264 | tf_op jit(solution)/shard_map/ppermute | solution.py:57
  40.8 12.1 %collective-permute-start.18 = (bf16[128,1024]{1,0:T(8,128)(2,1)S(1)}, bf16[128,1024]{1,0:T(8,128)(2,1)S(1)}, u32[]{:S(2)}, u32[]{:S(2)}) collective-permute-start(bf16[128,1024]{1,0:T(8,128)(2,1)S(1)} %get-tuple-element.31.refs_5_), channel_id=1, source_target_pairs={{0,1},{1,0},{2,3},{3,2},{4,5},{5,4},{6,7},{7,6},{8,9},{9,8},{10,11... | collective-permute-start | bytes 786440 | tf_op jit(solution)/shard_map/ppermute | solution.py:335
  47.0 6.0 %collective-permute-start.15 = (bf16[32,1792]{1,0:T(8,128)(2,1)S(1)}, bf16[32,1792]{1,0:T(8,128)(2,1)S(1)}, u32[]{:S(2)}, u32[]{:S(2)}) collective-permute-start(bf16[32,1792]{1,0:T(8,128)(2,1)S(1)} %add.14), channel_id=1, source_target_pairs={{0,16},{8,24},{16,0},{24,8},{1,17},{9,25},{17,1},{25,9},{2,18},{10... | collective-permute-start | bytes 344072 | tf_op jit(solution)/shard_map/ppermute | solution.py:57
  56.2 1.6 %collective-permute-start.20 = (bf16[64,1792]{1,0:T(8,128)(2,1)S(1)}, bf16[64,1792]{1,0:T(8,128)(2,1)S(1)}, u32[]{:S(2)}, u32[]{:S(2)}) collective-permute-start(bf16[64,1792]{1,0:T(8,128)(2,1)S(1)} %get-tuple-element.43), channel_id=1, source_target_pairs={{0,8},{8,0},{16,24},{24,16},{1,9},{9,1},{17,25},{25,17},{2,10},{10... | collective-permute-start | bytes 688136 | tf_op jit(solution)/shard_map/ppermute | solution.py:57
  56.3 4.1 %collective-permute-start.11 = (bf16[64,1792]{1,0:T(8,128)(2,1)S(1)}, bf16[64,1792]{1,0:T(8,128)(2,1)S(1)}, u32[]{:S(2)}, u32[]{:S(2)}) collective-permute-start(bf16[64,1792]{1,0:T(8,128)(2,1)S(1)} %get-tuple-element.33), channel_id=1, source_target_pairs={{0,8},{8,0},{16,24},{24,16},{1,9},{9,1},{17,25},{25,17},{2,10},{10... | collective-permute-start | bytes 688136 | tf_op jit(solution)/shard_map/ppermute | solution.py:57
  56.8 6.8 %collective-permute-start.19 = (bf16[64,1792]{1,0:T(8,128)(2,1)S(1)}, bf16[64,1792]{1,0:T(8,128)(2,1)S(1)}, u32[]{:S(2)}, u32[]{:S(2)}) collective-permute-start(bf16[64,1792]{1,0:T(8,128)(2,1)S(1)} %get-tuple-element.42), channel_id=1, source_target_pairs={{0,8},{8,0},{16,24},{24,16},{1,9},{9,1},{17,25},{25,17},{2,10},{10... | collective-permute-start | bytes 688136 | tf_op jit(solution)/shard_map/ppermute | solution.py:57
  56.8 2.7 %collective-permute-start.12 = (bf16[32,1792]{1,0:T(8,128)(2,1)S(1)}, bf16[32,1792]{1,0:T(8,128)(2,1)S(1)}, u32[]{:S(2)}, u32[]{:S(2)}) collective-permute-start(bf16[32,1792]{1,0:T(8,128)(2,1)S(1)} %get-tuple-element.34), channel_id=1, source_target_pairs={{0,8},{8,0},{16,24},{24,16},{1,9},{9,1},{17,25},{25,17},{2,10},{10... | collective-permute-start | bytes 344072 | tf_op jit(solution)/shard_map/ppermute | solution.py:57
  57.8 6.1 %collective-permute-start.22 = (bf16[32,1792]{1,0:T(8,128)(2,1)S(1)}, bf16[32,1792]{1,0:T(8,128)(2,1)S(1)}, u32[]{:S(2)}, u32[]{:S(2)}) collective-permute-start(bf16[32,1792]{1,0:T(8,128)(2,1)S(1)} %get-tuple-element.45), channel_id=1, source_target_pairs={{0,16},{8,24},{16,0},{24,8},{1,17},{9,25},{17,1},{25,9},{2,18},{10... | collective-permute-start | bytes 344072 | tf_op jit(solution)/shard_map/ppermute | solution.py:57
  59.6 6.7 %collective-permute-start.13 = (bf16[32,1792]{1,0:T(8,128)(2,1)S(1)}, bf16[32,1792]{1,0:T(8,128)(2,1)S(1)}, u32[]{:S(2)}, u32[]{:S(2)}) collective-permute-start(bf16[32,1792]{1,0:T(8,128)(2,1)S(1)} %add.13), channel_id=1, source_target_pairs={{0,16},{8,24},{16,0},{24,8},{1,17},{9,25},{17,1},{25,9},{2,18},{10... | collective-permute-start | bytes 344072 | tf_op jit(solution)/shard_map/ppermute | solution.py:57
  60.4 5.9 %collective-permute-start.16 = (bf16[32,1792]{1,0:T(8,128)(2,1)S(1)}, bf16[32,1792]{1,0:T(8,128)(2,1)S(1)}, u32[]{:S(2)}, u32[]{:S(2)}) collective-permute-start(bf16[32,1792]{1,0:T(8,128)(2,1)S(1)} %add.15), channel_id=1, source_target_pairs={{0,2},{2,0},{4,6},{6,4},{1,3},{3,1},{5,7},{7,5},{8,10},{10,8},{12,... | collective-permute-start | bytes 344072 | tf_op jit(solution)/shard_map/ppermute | solution.py:57
  62.3 5.7 %collective-permute-start.21 = (bf16[32,1792]{1,0:T(8,128)(2,1)S(1)}, bf16[32,1792]{1,0:T(8,128)(2,1)S(1)}, u32[]{:S(2)}, u32[]{:S(2)}) collective-permute-start(bf16[32,1792]{1,0:T(8,128)(2,1)S(1)} %get-tuple-element.44), channel_id=1, source_target_pairs={{0,16},{8,24},{16,0},{24,8},{1,17},{9,25},{17,1},{25,9},{2,18},{10... | collective-permute-start | bytes 344072 | tf_op jit(solution)/shard_map/ppermute | solution.py:57
  63.9 5.5 %collective-permute-start.23 = (bf16[32,1792]{1,0:T(8,128)(2,1)S(1)}, bf16[32,1792]{1,0:T(8,128)(2,1)S(1)}, u32[]{:S(2)}, u32[]{:S(2)}) collective-permute-start(bf16[32,1792]{1,0:T(8,128)(2,1)S(1)} %add.19), channel_id=1, source_target_pairs={{0,2},{2,0},{4,6},{6,4},{1,3},{3,1},{5,7},{7,5},{8,10},{10,8},{12,... | collective-permute-start | bytes 344072 | tf_op jit(solution)/shard_map/ppermute | solution.py:57
  66.3 5.8 %collective-permute-start.17 = (bf16[16,1792]{1,0:T(8,128)(2,1)S(1)}, bf16[16,1792]{1,0:T(8,128)(2,1)S(1)}, u32[]{:S(2)}, u32[]{:S(2)}) collective-permute-start(bf16[16,1792]{1,0:T(8,128)(2,1)S(1)} %get-tuple-element.37), channel_id=1, source_target_pairs={{0,4},{2,6},{4,0},{6,2},{1,5},{3,7},{5,1},{7,3},{8,12},{10,14},{12... | collective-permute-start | bytes 172040 | tf_op jit(solution)/shard_map/ppermute | solution.py:57
  69.4 5.1 %collective-permute-start.24 = (bf16[16,1792]{1,0:T(8,128)(2,1)S(1)}, bf16[16,1792]{1,0:T(8,128)(2,1)S(1)}, u32[]{:S(2)}, u32[]{:S(2)}) collective-permute-start(bf16[16,1792]{1,0:T(8,128)(2,1)S(1)} %get-tuple-element.47), channel_id=1, source_target_pairs={{0,4},{2,6},{4,0},{6,2},{1,5},{3,7},{5,1},{7,3},{8,12},{10,14},{12... | collective-permute-start | bytes 172040 | tf_op jit(solution)/shard_map/ppermute | solution.py:57
  (8 other events, 35.0 us)

commit v6 on v5

--- a/solution.py
+++ b/solution.py
@@ -10,7 +10,7 @@
 PLANE = ("group", "ingroup")
 LANES = 128
 CHUNK = 256
-PIECES = 4
+FETCH = 50
 BF16 = jnp.bfloat16
 F32 = jnp.float32
 
@@ -65,32 +65,56 @@
     return bits
 
 
-def routing_body(ids, gate, out):
+def payload_body(tokens, ids, gate, out, tokens_held, ids_held, gate_held, sems):
+    copies = [
+        pltpu.make_async_copy(source, held, sems.at[i])
+        for i, (source, held) in enumerate(
+            ((ids, ids_held), (gate, gate_held), (tokens, tokens_held))
+        )
+    ]
+    for copy in copies:
+        copy.start()
     topk, block = ids.shape
+    features = tokens.shape[1]
+    wide = out.shape[1] - LANES
+    if wide != features:
+        out[...] = jnp.zeros_like(out)
+    eye = lax.broadcasted_iota(jnp.int32, (block, block), 0) == lax.broadcasted_iota(
+        jnp.int32, (block, block), 1
+    )
+    copies[0].wait()
+    copies[1].wait()
     rows = jnp.concatenate(
         [
-            ids[...].astype(F32),
-            (gate[...] >> 8).astype(F32),
-            (gate[...] & 255).astype(F32),
+            ids_held[...].astype(F32),
+            (gate_held[...] >> 8).astype(F32),
+            (gate_held[...] & 255).astype(F32),
             jnp.zeros((LANES - 3 * topk, block), F32),
         ],
         axis=0,
     ).astype(BF16)
-    eye = lax.broadcasted_iota(jnp.int32, (block, block), 0) == lax.broadcasted_iota(
-        jnp.int32, (block, block), 1
-    )
-    out[...] = dot(jnp.where(eye, 1.0, 0.0).astype(BF16), rows, 1, 1).astype(BF16)
-
-
-def merge_body(near_x, far_x, near_route, far_route, out):
-    block, features = near_x.shape
-    wide = out.shape[1] - LANES
-    if wide != features:
-        out[...] = jnp.zeros_like(out)
-    out[:block, :features] = near_x[...]
-    out[block:, :features] = far_x[...]
-    out[:block, wide:] = near_route[...]
-    out[block:, wide:] = far_route[...]
+    out[:, wide:] = dot(jnp.where(eye, 1.0, 0.0).astype(BF16), rows, 1, 1).astype(BF16)
+    copies[2].wait()
+    out[:, :features] = tokens_held[...]
+
+
+def fetch_body(source, after, out, token, sem):
+    copy = pltpu.make_async_copy(source, out, sem)
+    copy.start()
+    token[...] = jnp.zeros_like(token)
+    copy.wait()
+
+
+def fetch(source, after):
+    return call(
+        "fetch",
+        fetch_body,
+        [(source.shape, source.dtype), ((8, LANES), F32)],
+        [source, after],
+        limit=FETCH,
+        hbm=(0,),
+        scratch=[pltpu.SemaphoreType.DMA],
+    )
 
 
 def pack_body(count, *refs):
@@ -101,15 +125,17 @@
         at += part.shape[0]
 
 
-def pack(parts, after=()):
+def pack(parts, after=(), passed=()):
     shape = (sum(p.shape[0] for p in parts), parts[0].shape[1])
-    return call(
+    out = call(
         "pack",
         functools.partial(pack_body, len(parts)),
         [(shape, parts[0].dtype)],
         list(parts) + list(after),
         flops=1 << 29,
-    )[0]
+        passed=passed,
+    )
+    return out if passed else out[0]
 
 
 def copy_body(source, after, out):
@@ -120,31 +146,24 @@
     return call("copied", copy_body, [(source.shape, source.dtype)], [source, after], 1 << 31)[0]
 
 
-def spread(tokens, route, cotangent):
-    inner, outer = bits_of("ingroup"), bits_of("group")
-    block, features = tokens.shape
-    wide = -(-features // LANES) * LANES
-    first, second = None, copied(cotangent, route)
-    first, second = call(
-        "merge",
-        merge_body,
-        [((2 * block, wide + LANES), BF16)],
-        [tokens, swap(tokens, "ingroup", inner[0]), route, swap(route, "ingroup", inner[0])],
-        passed=[second],
-    )
-    for bit in inner[1:-1]:
-        first = pack([first, swap(first, "ingroup", bit)])
-    beside = swap(first, "ingroup", inner[-1])
-    across = swap(first, "group", outer[0])
-    last = swap(beside, "group", outer[0])
-    for bit in inner[:-1]:
+def spread(own, cotangent, w_gate, w_up):
+    outer, inner_count = bits_of("group"), lax.axis_size("ingroup")
+    second = copied(cotangent, own)
+    blocks = [own] + [swap(own, "ingroup", j) for j in range(1, inner_count)]
+    w_gate, token = fetch(w_gate, own)
+    early = pack(blocks[: inner_count // 2], [token])
+    w_up, token = fetch(w_up, early)
+    late, second = pack(blocks[inner_count // 2 :], passed=[second])
+    across = swap(early, "group", outer[0])
+    last = swap(late, "group", outer[0])
+    *bits, high = bits_of("ingroup")[::-1]
+    for bit in bits:
         second = pack([second, swap(second, "ingroup", bit)])
-    first = pack([first, beside, across, last], after=[second])
-    beside = swap(second, "ingroup", inner[-1])
+    first = pack([early, late, across, last], [token, second])
     for bit in outer[1:-1]:
         first = pack([first, swap(first, "group", bit)])
     first = [first, swap(first, "group", outer[-1])]
-    return first, [second, beside]
+    return first, [second, swap(second, "ingroup", high)], w_gate, w_up
 
 
 def spread_end(parts, after):
@@ -156,19 +175,11 @@
 
 
 def route_body(wide, topk, block, capacity, count, me, *refs):
-    parts, rest = refs[:count], refs[count:]
-    sources, (place_out, scale_out, part_out, sent_out, *held, sems) = rest[:2], rest[2:]
-    features, hidden = sources[0].shape
-    width = hidden // PIECES
-    copies = []
-    for i in range(2):
-        for j in range(PIECES):
-            piece = pl.ds(j * width, width)
-            copy = pltpu.make_async_copy(
-                sources[i].at[:, piece], held[i].at[:, piece], sems.at[i, j]
-            )
-            copy.start()
-            copies.append(copy)
+    parts, (gate_weight, up_weight, place_out, scale_out, part_out, sent_out) = (
+        refs[:count],
+        refs[count:],
+    )
+    features = gate_weight.shape[0]
     total, slots = place_out.shape
     routing = jnp.concatenate([p[:, wide : wide + LANES] for p in parts], axis=0)
     lane = lax.broadcasted_iota(jnp.int32, (total, LANES), 1)
@@ -199,13 +210,10 @@
     scale_out[...] = (high * 256.0 + low) / 65536.0
     values = jnp.concatenate([p[:, :features] for p in parts], axis=0)
     rows = dot(place, values, 0, 0).astype(BF16)
-    for i in range(2):
-        for j in range(PIECES):
-            copies[i * PIECES + j].wait()
-            columns = slice(j * width, (j + 1) * width)
-            part = dot(rows, held[i][:, columns])
-            part_out[i * slots : (i + 1) * slots, columns] = part
-            sent_out[i * slots : (i + 1) * slots, columns] = part.astype(BF16)
+    for i, weight in enumerate((gate_weight, up_weight)):
+        part = dot(rows, weight[...])
+        part_out[i * slots : (i + 1) * slots] = part
+        sent_out[i * slots : (i + 1) * slots] = part.astype(BF16)
 
 
 def back_body(count, *refs):
@@ -297,36 +305,29 @@
     return near, *[swap(piece, "group", bits_of("group")[1]) for piece in pieces]
 
 
-def collect_end(near, far, bits):
-    for bit in bits:
-        received = swap(far, "ingroup", bit)
-        half = near.shape[0] // 2
-        if bit == bits[-1]:
-            return add(near, 0, [(received, 0)], [(2 * half, BF16)])[0]
-        near, far = add(near, 0, [(received, 0)], [(half, F32), (half, BF16)])
-
-
-def collect_across(near, *got):
-    half, bit = near.shape[0] // 2, bits_of("group")[0]
-    quarter = half // 2
-    if len(got) == 1:
-        low, high = add(near, half, [(got[0], 0)], [(quarter, BF16)] * 2)
-    else:
-        (high,) = add(near, half + quarter, [(got[0], 0)], [(quarter, BF16)])
-        (low,) = add(near, half, [(got[1], 0)], [(quarter, BF16)])
-    return swap(high, "group", bit), swap(low, "group", bit)
-
-
-def collect_rest(near, got_second, across, last):
-    inner = bits_of("ingroup")
+def collect_few(near, far, got_stay):
     half = near.shape[0] // 2
-    quarter, eighth = half // 2, half // 4
-    (far,) = add(near, quarter, [(got_second, quarter), (across, 0)], [(quarter, BF16)])
-    beside = swap(far, "ingroup", inner[-1])
-    near, far = add(
-        near, 0, [(got_second, 0), (last, 0), (beside, 0)], [(eighth, F32), (eighth, BF16)]
-    )
-    return collect_end(near, far, inner[-2::-1])
+    received = [(got_stay, 0), (swap(far, "group", bits_of("group")[0]), 0)]
+    for bit in bits_of("ingroup"):
+        half //= 2
+        near, far = add(near, 0, received, [(half, F32), (half, BF16)])
+        received = [(swap(far, "ingroup", bit), 0)]
+    return add(near, 0, received, [(half, BF16)])[0]
+
+
+def collect_soon(near, got_go, got_stay):
+    count, bit = lax.axis_size("ingroup"), bits_of("group")[0]
+    half = near.shape[0] // 2
+    quarter, block = half // 2, half // count
+    low, high = add(near, half, [(got_go, 0)], [(quarter, BF16)] * 2)
+    across, last = swap(high, "group", bit), swap(low, "group", bit)
+    away = add(near, quarter, [(got_stay, quarter), (across, 0)], [(block, BF16)] * (count // 2))
+    sent = [swap(away[j], "ingroup", count // 2 + j) for j in range(count // 2)[::-1]]
+    own, *away = add(
+        near, 0, [(got_stay, 0), (last, 0)], [(block, F32)] + [(block, BF16)] * (count // 2 - 1)
+    )
+    sent += [swap(away[j], "ingroup", 1 + j) for j in range(count // 2 - 1)[::-1]]
+    return add(own, 0, [(s, 0) for s in sent], [(block, BF16)])[0]
 
 
 def from_peers(sent):
@@ -349,20 +350,27 @@
     w_gate, w_up, w_down = w_gate[0], w_up[0], w_down[0]
     product = 2 * slots * features * hidden
 
-    (route,) = call("routing", routing_body, [((block, LANES), BF16)], [expert_ids.T, gate_fixed.T])
-    x_parts, d_parts = spread(tokens, route, cotangent)
+    (own,) = call(
+        "payload",
+        payload_body,
+        [((block, wide + LANES), BF16)],
+        [tokens, expert_ids.T, gate_fixed.T],
+        limit=58,
+        hbm=(0, 1, 2),
+        scratch=[pltpu.VMEM(tokens.shape, BF16)]
+        + [pltpu.VMEM((topk, block), jnp.int32)] * 2
+        + [pltpu.SemaphoreType.DMA((3,))],
+    )
+    x_parts, d_parts, gate_held, up_held = spread(own, cotangent, w_gate, w_up)
     me = lax.axis_index(PLANE).astype(jnp.int32).reshape(1)
     both, both_sent = [((2 * slots, hidden), t) for t in (F32, BF16)]
     place, scale, both, both_sent = call(
         "forward",
         functools.partial(route_body, wide, topk, block, capacity, len(x_parts)),
         [((total, slots), BF16), ((slots, LANES), F32), both, both_sent],
-        [me] + x_parts + [w_gate, w_up],
+        [me] + x_parts + [gate_held, up_held],
         2 * product,
-        50,
-        hbm=(len(x_parts) + 1, len(x_parts) + 2),
-        scratch=[pltpu.VMEM((features, hidden), BF16)] * 2
-        + [pltpu.SemaphoreType.DMA((2, PIECES))],
+        16,
     )
     both_in = from_peers(both_sent)
     d_parts = spread_end(d_parts, [both_sent])
@@ -372,35 +380,34 @@
     )
     back_in = from_peers(back_sent)
     near = ((total // 2, features), F32)
-    fourth, eighth = ((total // 4, features), BF16), ((total // 8, features), BF16)
-    near_y, got_high, got_low, got_y = collect_start(
+    fourth = ((total // 4, features), BF16)
+    near_y, got_go, got_y = collect_start(
         *call(
             "out",
             functools.partial(out_body, peers),
-            [near, eighth, eighth, fourth],
+            [near, fourth, fourth],
             [both] + both_in + [scale, place, w_down, back_sent],
             product,
         )
     )
-    across, last = collect_across(near_y, got_high, got_low)
+    (far,) = add(near_y, near_y.shape[0] // 2, [(got_go, 0)], [(near_y.shape[0] // 2, BF16)])
     factors = call(
         "factor",
         functools.partial(factor_body, peers),
         [((slots, hidden), F32)] * 2,
         [both] + both_in + [scale],
     )
-    near_dx, got_first, got_dx = collect_start(
+    near_dx, got_go, got_dx = collect_start(
         *call(
             "grad",
             functools.partial(grad_body, peers),
             [near, fourth, fourth],
-            list(factors) + [back] + back_in + [place, w_gate, w_up, across],
+            list(factors) + [back] + back_in + [place, gate_held, up_held, far],
             2 * product,
             24,
         )
     )
-    mixed = collect_rest(near_y, got_y, across, last)
-    return mixed, collect_rest(near_dx, got_dx, *collect_across(near_dx, got_first))
+    return collect_few(near_y, far, got_y), collect_soon(near_dx, got_go, got_dx)
 
 
 def solution(mesh):

time: 75.4 us -> 75.8 us (level)
  waiting for transfers between devices: 32.7 us -> 22.9 us
  local copies, waits for them, and re-layouts: 2.22 us -> 10.2 us
  Pallas kernels: 13.1 us -> 15.1 us
    ppermute x23 -> x22, waiting for transfers between devices: 30.7 us -> 17.3 us  [swap(): lax.ppermute(value, axis, [(i, i ^ offset) for i in range(lax.axis_size(a...]
    unnamed x14 -> x20, local copies, waits for them, and re-layouts: 2.22 us -> 10.2 us
    ppermute x2, waiting for transfers between devices: 1.97 us -> 5.67 us  [from_peers(): lax.ppermute(sent, 'dp', [(i, (i + step) % count) for i in range(count)])]
    pallas_call x21 -> x23, Pallas kernels: 13.1 us -> 15.1 us  [call(): return kernel(*args, *passed)]
    ppermute x23 -> x22, starting transfers between devices: 23.3 us -> 23.2 us  [swap(): lax.ppermute(value, axis, [(i, i ^ offset) for i in range(lax.axis_size(a...]
  transfers between devices with their start and end apart: 25 -> 24, of which waited for: 15 -> 11; matrix products, arithmetic and copies ran while one was open for 0% -> 0% of each run, Pallas kernels for 12% -> 17%
where the time goes in v6:
time: 75.8 us; the launch traced here: 75.3 us
  starting transfers between devices  26.2 us (35%)
  waiting for transfers between devices  22.9 us (30%)
  Pallas kernels  15.1 us (20%)
  local copies, waits for them, and re-layouts  10.2 us (13%)
  between operations  0.84 us (1%)
    ppermute x22, starting transfers between devices, swap(): lax.ppermute(value, axis, [(i, i ^ offset) for i in range(lax.axis_size(a...  23.2 us
    ppermute x22, waiting for transfers between devices, swap(): lax.ppermute(value, axis, [(i, i ^ offset) for i in range(lax.axis_size(a...  17.3 us
    pallas_call x23, Pallas kernels, call(): return kernel(*args, *passed)  15.1 us
    unnamed x20, local copies, waits for them, and re-layouts  10.2 us
    ppermute x2, waiting for transfers between devices, from_peers(): lax.ppermute(sent, 'dp', [(i, (i + step) % count) for i in range(count)])  5.67 us
    ppermute x2, starting transfers between devices, from_peers(): lax.ppermute(sent, 'dp', [(i, (i + step) % count) for i in range(count)])  3.05 us
  transfers between devices with their start and end apart: 24, of which 11 were waited for; matrix products, arithmetic and copies ran while one was open for 0% of the time, Pallas kernels for 17%

profile of v6, /device:TPU:0, one launch (start us, length us, event | category | flops | bytes accessed | tf_op | source)
XLA Modules:
  0.0 75.3 jit_solution(12688308129310999476)
XLA Ops:
  0.6 1.5 %payload.1.refs_1_.refs_0_ = bf16[16,1920]{1,0:T(8,128)(2,1)} custom-call(bf16[16,1792]{1,0:T(8,128)(2,1)} %refs_0_.2, s32[8,16]{1,0:T(8,128)} %bitcast.10, s32[8,16]{1,0:T(8,128)} %bitcast.11), custom_call_target="tpu_custom_call" | custom-call | bytes 119808 | tf_op jit(solution)/shard_map/payload/payload/pallas_call | solution.py:53
  2.1 3.1 %collective-permute-start = (bf16[16,1920]{1,0:T(8,128)(2,1)}, bf16[16,1920]{1,0:T(8,128)(2,1)S(1)}, u32[]{:S(2)}, u32[]{:S(2)}) collective-permute-start(bf16[16,1920]{1,0:T(8,128)(2,1)} %payload.1.refs_1_.refs_0_), channel_id=1, source_target_pairs={{0,2},{2,0},{4,6},{6,4},{1,3},{3,1},{5,7},{7,5},{8,10},{10,8},{12,... | collective-permute-start | bytes 184328 | tf_op jit(solution)/shard_map/ppermute | solution.py:57
  5.2 2.6 %collective-permute-start.1 = (bf16[16,1920]{1,0:T(8,128)(2,1)}, bf16[16,1920]{1,0:T(8,128)(2,1)S(1)}, u32[]{:S(2)}, u32[]{:S(2)}) collective-permute-start(bf16[16,1920]{1,0:T(8,128)(2,1)} %payload.1.refs_1_.refs_0_), channel_id=1, source_target_pairs={{0,4},{2,6},{4,0},{6,2},{1,5},{3,7},{5,1},{7,3},{8,12},{10,14},{12... | collective-permute-start | bytes 184328 | tf_op jit(solution)/shard_map/ppermute | solution.py:57
  10.4 2.0 %fetch.2 = (bf16[1792,1024]{1,0:T(8,128)(2,1)S(1)}, f32[8,128]{1,0:T(8,128)S(1)}) custom-call(bf16[1792,1024]{1,0:T(8,128)(2,1)} %bitcast.8, bf16[16,1920]{1,0:T(8,128)(2,1)S(1)} %copy-done.8), custom_call_target="tpu_custom_call" | custom-call | bytes 7405568 | tf_op jit(solution)/shard_map/fetch/fetch/pallas_call | solution.py:53
  12.4 1.8 %copy-done = bf16[1792,1024]{1,0:T(8,128)(2,1)} copy-done((bf16[1792,1024]{1,0:T(8,128)(2,1)}, bf16[1792,1024]{1,0:T(8,128)(2,1)S(1)}, u32[]{:S(2)}) %copy-start) | copy-done | bytes 3670040
  14.2 1.8 %collective-permute-start.3 = (bf16[32,1920]{1,0:T(8,128)(2,1)S(1)}, bf16[32,1920]{1,0:T(8,128)(2,1)S(1)}, u32[]{:S(2)}, u32[]{:S(2)}) collective-permute-start(bf16[32,1920]{1,0:T(8,128)(2,1)S(1)} %pack.6.refs_1_.refs_0_), channel_id=1, source_target_pairs={{0,16},{8,24},{16,0},{24,8},{1,17},{9,25},{17,1},{25,9},{2,18},{10... | collective-permute-start | bytes 368648 | tf_op jit(solution)/shard_map/ppermute | solution.py:57
  17.3 2.0 %fetch.3 = (bf16[1792,1024]{1,0:T(8,128)(2,1)S(1)}, f32[8,128]{1,0:T(8,128)S(1)}) custom-call(bf16[1792,1024]{1,0:T(8,128)(2,1)} %bitcast.9, bf16[32,1920]{1,0:T(8,128)(2,1)S(1)} %pack.6.refs_1_.refs_0_), custom_call_target="tpu_custom_call" | custom-call | bytes 7467008 | tf_op jit(solution)/shard_map/fetch/fetch/pallas_call | solution.py:53
  19.3 1.8 %copy-done.3 = bf16[1792,1024]{1,0:T(8,128)(2,1)} copy-done((bf16[1792,1024]{1,0:T(8,128)(2,1)}, bf16[1792,1024]{1,0:T(8,128)(2,1)S(1)}, u32[]{:S(2)}) %copy-start.3) | copy-done | bytes 3670040
  21.5 3.3 %collective-permute-start.8 = (bf16[32,1792]{1,0:T(8,128)(2,1)S(1)}, bf16[32,1792]{1,0:T(8,128)(2,1)S(1)}, u32[]{:S(2)}, u32[]{:S(2)}) collective-permute-start(bf16[32,1792]{1,0:T(8,128)(2,1)S(1)} %pack.8.refs_5_.refs_0_), channel_id=1, source_target_pairs={{0,4},{2,6},{4,0},{6,2},{1,5},{3,7},{5,1},{7,3},{8,12},{10,14},{12... | collective-permute-start | bytes 344072 | tf_op jit(solution)/shard_map/ppermute | solution.py:57
  24.8 2.0 %copy-done.1 = bf16[1792,1024]{1,0:T(8,128)(2,1)S(1)} copy-done((bf16[1792,1024]{1,0:T(8,128)(2,1)S(1)}, bf16[1792,1024]{1,0:T(8,128)(2,1)}, u32[]{:S(2)}) %copy-start.1) | copy-done | bytes 3670040
  26.9 2.0 %copy-done.4 = bf16[1792,1024]{1,0:T(8,128)(2,1)S(1)} copy-done((bf16[1792,1024]{1,0:T(8,128)(2,1)S(1)}, bf16[1792,1024]{1,0:T(8,128)(2,1)}, u32[]{:S(2)}) %copy-start.4) | copy-done | bytes 3670040
  28.9 1.8 %forward.1 = (bf16[256,128]{1,0:T(8,128)(2,1)S(1)}, f32[128,128]{1,0:T(8,128)S(1)}, f32[256,1024]{1,0:T(8,128)S(1)}, bf16[256,1024]{1,0:T(8,128)(2,1)S(1)}) custom-call(s32[1]{0:T(128)} %bitcast.refs_0_, bf16[128,1920]{1,0:T(8,128)(2,1)S(1)} %pack.9.refs_1_, bf16[128,1920]{1,0:T(8,128)(2,1)S(1)} %collective-permute-done.6.refs_2_, ...), custom_call_target="tpu_custom_call" | custom-call | flops 939524096 | bytes 10027012 | tf_op jit(solution)/shard_map/forward/forward/pallas_call | solution.py:53
  31.0 1.6 %collective-permute-start.9 = (bf16[64,1792]{1,0:T(8,128)(2,1)S(1)}, bf16[64,1792]{1,0:T(8,128)(2,1)S(1)}, u32[]{:S(2)}, u32[]{:S(2)}) collective-permute-start(bf16[64,1792]{1,0:T(8,128)(2,1)S(1)} %pack.10.refs_0_), channel_id=1, source_target_pairs={{0,16},{8,24},{16,0},{24,8},{1,17},{9,25},{17,1},{25,9},{2,18},{10... | collective-permute-start | bytes 688136 | tf_op jit(solution)/shard_map/ppermute | solution.py:57
  34.1 4.4 %collective-permute-done.9.refs_1_ = bf16[64,1792]{1,0:T(8,128)(2,1)S(1)} collective-permute-done((bf16[64,1792]{1,0:T(8,128)(2,1)S(1)}, bf16[64,1792]{1,0:T(8,128)(2,1)S(1)}, u32[]{:S(2)}, u32[]{:S(2)}) %collective-permute-start.9) | collective-permute-done | bytes 229408 | tf_op jit(solution)/shard_map/ppermute | solution.py:57
  38.6 1.8 %collective-permute-done.10.refs_1_ = bf16[128,1792]{1,0:T(8,128)(2,1)S(1)} collective-permute-done((bf16[128,1792]{1,0:T(8,128)(2,1)S(1)}, bf16[128,1792]{1,0:T(8,128)(2,1)S(1)}, u32[]{:S(2)}, u32[]{:S(2)}) %collective-permute-start.10) | collective-permute-done | bytes 458784 | tf_op jit(solution)/shard_map/ppermute | solution.py:57
  41.7 1.6 %collective-permute-start.16 = (bf16[128,1024]{1,0:T(8,128)(2,1)S(1)}, bf16[128,1024]{1,0:T(8,128)(2,1)S(1)}, u32[]{:S(2)}, u32[]{:S(2)}) collective-permute-start(bf16[128,1024]{1,0:T(8,128)(2,1)S(1)} %get-tuple-element.42.refs_5_), channel_id=1, source_target_pairs={{0,1},{1,0},{2,3},{3,2},{4,5},{5,4},{6,7},{7,6},{8,9},{9,8},{10,11... | collective-permute-start | bytes 786440 | tf_op jit(solution)/shard_map/ppermute | solution.py:336
  43.3 4.2 %collective-permute-done.7.refs_1_ = bf16[256,1024]{1,0:T(8,128)(2,1)S(1)} collective-permute-done((bf16[256,1024]{1,0:T(8,128)(2,1)S(1)}, bf16[256,1024]{1,0:T(8,128)(2,1)S(1)}, u32[]{:S(2)}, u32[]{:S(2)}) %collective-permute-start.7) | collective-permute-done | bytes 524320 | tf_op jit(solution)/shard_map/ppermute | solution.py:336
  51.7 3.3 %grad.1 = (f32[128,1792]{1,0:T(8,128)S(1)}, bf16[64,1792]{1,0:T(8,128)(2,1)S(1)}, bf16[64,1792]{1,0:T(8,128)(2,1)S(1)}) custom-call(f32[128,1024]{1,0:T(8,128)S(1)} %get-tuple-element.50.refs_0_, f32[128,1024]{1,0:T(8,128)S(1)} %get-tuple-element.51.refs_1_, f32[128,1024]{1,0:T(8,128)S(1)} %get-tuple-element.52.refs_2_, ...), custom_call_target="tpu_custom_call" | custom-call | flops 939524096 | bytes 10846208 | tf_op jit(solution)/shard_map/grad/grad/pallas_call | solution.py:53
  55.5 2.3 %collective-permute-done.13.refs_2_ = bf16[64,1792]{1,0:T(8,128)(2,1)S(1)} collective-permute-done((bf16[64,1792]{1,0:T(8,128)(2,1)S(1)}, bf16[64,1792]{1,0:T(8,128)(2,1)S(1)}, u32[]{:S(2)}, u32[]{:S(2)}) %collective-permute-start.13) | collective-permute-done | bytes 229408 | tf_op jit(solution)/shard_map/ppermute | solution.py:57
  57.9 1.5 %collective-permute-start.14 = (bf16[32,1792]{1,0:T(8,128)(2,1)S(1)}, bf16[32,1792]{1,0:T(8,128)(2,1)S(1)}, u32[]{:S(2)}, u32[]{:S(2)}) collective-permute-start(bf16[32,1792]{1,0:T(8,128)(2,1)S(1)} %get-tuple-element.47), channel_id=1, source_target_pairs={{0,4},{2,6},{4,0},{6,2},{1,5},{3,7},{5,1},{7,3},{8,12},{10,14},{12... | collective-permute-start | bytes 344072 | tf_op jit(solution)/shard_map/ppermute | solution.py:57
  59.8 1.7 %collective-permute-start.19 = (bf16[32,1792]{1,0:T(8,128)(2,1)S(1)}, bf16[32,1792]{1,0:T(8,128)(2,1)S(1)}, u32[]{:S(2)}, u32[]{:S(2)}) collective-permute-start(bf16[32,1792]{1,0:T(8,128)(2,1)S(1)} %get-tuple-element.56), channel_id=1, source_target_pairs={{0,16},{8,24},{16,0},{24,8},{1,17},{9,25},{17,1},{25,9},{2,18},{10... | collective-permute-start | bytes 344072 | tf_op jit(solution)/shard_map/ppermute | solution.py:57
  61.6 4.1 %collective-permute-done.14.refs_1_ = bf16[32,1792]{1,0:T(8,128)(2,1)S(1)} collective-permute-done((bf16[32,1792]{1,0:T(8,128)(2,1)S(1)}, bf16[32,1792]{1,0:T(8,128)(2,1)S(1)}, u32[]{:S(2)}, u32[]{:S(2)}) %collective-permute-start.14) | collective-permute-done | bytes 114720 | tf_op jit(solution)/shard_map/ppermute | solution.py:57
  65.9 2.4 %collective-permute-start.21 = (bf16[16,1792]{1,0:T(8,128)(2,1)S(1)}, bf16[16,1792]{1,0:T(8,128)(2,1)S(1)}, u32[]{:S(2)}, u32[]{:S(2)}) collective-permute-start(bf16[16,1792]{1,0:T(8,128)(2,1)S(1)} %get-tuple-element.59), channel_id=1, source_target_pairs={{0,6},{2,4},{4,2},{6,0},{1,7},{3,5},{5,3},{7,1},{8,14},{10,12},{12... | collective-permute-start | bytes 172040 | tf_op jit(solution)/shard_map/ppermute | solution.py:57
  72.6 2.1 %collective-permute-done.22.refs_2_ = bf16[16,1792]{1,0:T(8,128)(2,1)S(1)} collective-permute-done((bf16[16,1792]{1,0:T(8,128)(2,1)S(1)}, bf16[16,1792]{1,0:T(8,128)(2,1)S(1)}, u32[]{:S(2)}, u32[]{:S(2)}) %collective-permute-start.22) | collective-permute-done | bytes 57376 | tf_op jit(solution)/shard_map/ppermute | solution.py:57
  (67 shorter events, 17.7 us)
Async XLA Ops:
  2.1 12.1 %collective-permute-start = (bf16[16,1920]{1,0:T(8,128)(2,1)}, bf16[16,1920]{1,0:T(8,128)(2,1)S(1)}, u32[]{:S(2)}, u32[]{:S(2)}) collective-permute-start(bf16[16,1920]{1,0:T(8,128)(2,1)} %payload.1.refs_1_.refs_0_), channel_id=1, source_target_pairs={{0,2},{2,0},{4,6},{6,4},{1,3},{3,1},{5,7},{7,5},{8,10},{10,8},{12,... | collective-permute-start | bytes 184328 | tf_op jit(solution)/shard_map/ppermute | solution.py:57
  5.2 10.8 %collective-permute-start.1 = (bf16[16,1920]{1,0:T(8,128)(2,1)}, bf16[16,1920]{1,0:T(8,128)(2,1)S(1)}, u32[]{:S(2)}, u32[]{:S(2)}) collective-permute-start(bf16[16,1920]{1,0:T(8,128)(2,1)} %payload.1.refs_1_.refs_0_), channel_id=1, source_target_pairs={{0,4},{2,6},{4,0},{6,2},{1,5},{3,7},{5,1},{7,3},{8,12},{10,14},{12... | collective-permute-start | bytes 184328 | tf_op jit(solution)/shard_map/ppermute | solution.py:57
  7.8 8.2 %collective-permute-start.2 = (bf16[16,1920]{1,0:T(8,128)(2,1)}, bf16[16,1920]{1,0:T(8,128)(2,1)S(1)}, u32[]{:S(2)}, u32[]{:S(2)}) collective-permute-start(bf16[16,1920]{1,0:T(8,128)(2,1)} %payload.1.refs_1_.refs_0_), channel_id=1, source_target_pairs={{0,6},{2,4},{4,2},{6,0},{1,7},{3,5},{5,3},{7,1},{8,14},{10,12},{12... | collective-permute-start | bytes 184328 | tf_op jit(solution)/shard_map/ppermute | solution.py:57
  14.2 6.9 %collective-permute-start.3 = (bf16[32,1920]{1,0:T(8,128)(2,1)S(1)}, bf16[32,1920]{1,0:T(8,128)(2,1)S(1)}, u32[]{:S(2)}, u32[]{:S(2)}) collective-permute-start(bf16[32,1920]{1,0:T(8,128)(2,1)S(1)} %pack.6.refs_1_.refs_0_), channel_id=1, source_target_pairs={{0,16},{8,24},{16,0},{24,8},{1,17},{9,25},{17,1},{25,9},{2,18},{10... | collective-permute-start | bytes 368648 | tf_op jit(solution)/shard_map/ppermute | solution.py:57
  16.0 5.4 %collective-permute-start.4 = (bf16[32,1920]{1,0:T(8,128)(2,1)S(1)}, bf16[32,1920]{1,0:T(8,128)(2,1)S(1)}, u32[]{:S(2)}, u32[]{:S(2)}) collective-permute-start(bf16[32,1920]{1,0:T(8,128)(2,1)S(1)} %get-tuple-element.33.refs_1_), channel_id=1, source_target_pairs={{0,16},{8,24},{16,0},{24,8},{1,17},{9,25},{17,1},{25,9},{2,18},{10... | collective-permute-start | bytes 368648 | tf_op jit(solution)/shard_map/ppermute | solution.py:57
  16.4 4.7 %collective-permute-start.5 = (bf16[16,1792]{1,0:T(8,128)(2,1)S(1)}, bf16[16,1792]{1,0:T(8,128)(2,1)S(1)}, u32[]{:S(2)}, u32[]{:S(2)}) collective-permute-start(bf16[16,1792]{1,0:T(8,128)(2,1)S(1)} %get-tuple-element.35.refs_0_), channel_id=1, source_target_pairs={{0,2},{2,0},{4,6},{6,4},{1,3},{3,1},{5,7},{7,5},{8,10},{10,8},{12,... | collective-permute-start | bytes 172040 | tf_op jit(solution)/shard_map/ppermute | solution.py:57
  21.5 3.4 %collective-permute-start.6 = (bf16[128,1920]{1,0:T(8,128)(2,1)S(1)}, bf16[128,1920]{1,0:T(8,128)(2,1)S(1)}, u32[]{:S(2)}, u32[]{:S(2)}) collective-permute-start(bf16[128,1920]{1,0:T(8,128)(2,1)S(1)} %pack.9.refs_1_), channel_id=1, source_target_pairs={{0,8},{8,0},{16,24},{24,16},{1,9},{9,1},{17,25},{25,17},{2,10},{10... | collective-permute-start | bytes 1474568 | tf_op jit(solution)/shard_map/ppermute | solution.py:57
  21.5 9.5 %collective-permute-start.8 = (bf16[32,1792]{1,0:T(8,128)(2,1)S(1)}, bf16[32,1792]{1,0:T(8,128)(2,1)S(1)}, u32[]{:S(2)}, u32[]{:S(2)}) collective-permute-start(bf16[32,1792]{1,0:T(8,128)(2,1)S(1)} %pack.8.refs_5_.refs_0_), channel_id=1, source_target_pairs={{0,4},{2,6},{4,0},{6,2},{1,5},{3,7},{5,1},{7,3},{8,12},{10,14},{12... | collective-permute-start | bytes 344072 | tf_op jit(solution)/shard_map/ppermute | solution.py:57
  31.0 7.5 %collective-permute-start.9 = (bf16[64,1792]{1,0:T(8,128)(2,1)S(1)}, bf16[64,1792]{1,0:T(8,128)(2,1)S(1)}, u32[]{:S(2)}, u32[]{:S(2)}) collective-permute-start(bf16[64,1792]{1,0:T(8,128)(2,1)S(1)} %pack.10.refs_0_), channel_id=1, source_target_pairs={{0,16},{8,24},{16,0},{24,8},{1,17},{9,25},{17,1},{25,9},{2,18},{10... | collective-permute-start | bytes 688136 | tf_op jit(solution)/shard_map/ppermute | solution.py:57
  32.6 14.8 %collective-permute-start.7 = (bf16[256,1024]{1,0:T(8,128)(2,1)S(1)}, bf16[256,1024]{1,0:T(8,128)(2,1)S(1)}, u32[]{:S(2)}, u32[]{:S(2)}) collective-permute-start(bf16[256,1024]{1,0:T(8,128)(2,1)S(1)} %get-tuple-element.39.refs_2_), channel_id=1, source_target_pairs={{0,1},{1,0},{2,3},{3,2},{4,5},{5,4},{6,7},{7,6},{8,9},{9,8},{10,11... | collective-permute-start | bytes 1572872 | tf_op jit(solution)/shard_map/ppermute | solution.py:336
  38.5 1.9 %collective-permute-start.10 = (bf16[128,1792]{1,0:T(8,128)(2,1)S(1)}, bf16[128,1792]{1,0:T(8,128)(2,1)S(1)}, u32[]{:S(2)}, u32[]{:S(2)}) collective-permute-start(bf16[128,1792]{1,0:T(8,128)(2,1)S(1)} %pack.11.refs_0_), channel_id=1, source_target_pairs={{0,8},{8,0},{16,24},{24,16},{1,9},{9,1},{17,25},{25,17},{2,10},{10... | collective-permute-start | bytes 1376264 | tf_op jit(solution)/shard_map/ppermute | solution.py:57
  41.7 10.0 %collective-permute-start.16 = (bf16[128,1024]{1,0:T(8,128)(2,1)S(1)}, bf16[128,1024]{1,0:T(8,128)(2,1)S(1)}, u32[]{:S(2)}, u32[]{:S(2)}) collective-permute-start(bf16[128,1024]{1,0:T(8,128)(2,1)S(1)} %get-tuple-element.42.refs_5_), channel_id=1, source_target_pairs={{0,1},{1,0},{2,3},{3,2},{4,5},{5,4},{6,7},{7,6},{8,9},{9,8},{10,11... | collective-permute-start | bytes 786440 | tf_op jit(solution)/shard_map/ppermute | solution.py:336
  48.5 1.6 %collective-permute-start.12 = (bf16[64,1792]{1,0:T(8,128)(2,1)S(1)}, bf16[64,1792]{1,0:T(8,128)(2,1)S(1)}, u32[]{:S(2)}, u32[]{:S(2)}) collective-permute-start(bf16[64,1792]{1,0:T(8,128)(2,1)S(1)} %get-tuple-element.45), channel_id=1, source_target_pairs={{0,8},{8,0},{16,24},{24,16},{1,9},{9,1},{17,25},{25,17},{2,10},{10... | collective-permute-start | bytes 688136 | tf_op jit(solution)/shard_map/ppermute | solution.py:57
  49.1 6.4 %collective-permute-start.11 = (bf16[64,1792]{1,0:T(8,128)(2,1)S(1)}, bf16[64,1792]{1,0:T(8,128)(2,1)S(1)}, u32[]{:S(2)}, u32[]{:S(2)}) collective-permute-start(bf16[64,1792]{1,0:T(8,128)(2,1)S(1)} %get-tuple-element.44), channel_id=1, source_target_pairs={{0,8},{8,0},{16,24},{24,16},{1,9},{9,1},{17,25},{25,17},{2,10},{10... | collective-permute-start | bytes 688136 | tf_op jit(solution)/shard_map/ppermute | solution.py:57
  50.1 7.7 %collective-permute-start.13 = (bf16[64,1792]{1,0:T(8,128)(2,1)S(1)}, bf16[64,1792]{1,0:T(8,128)(2,1)S(1)}, u32[]{:S(2)}, u32[]{:S(2)}) collective-permute-start(bf16[64,1792]{1,0:T(8,128)(2,1)S(1)} %add.12.refs_7_), channel_id=1, source_target_pairs={{0,16},{8,24},{16,0},{24,8},{1,17},{9,25},{17,1},{25,9},{2,18},{10... | collective-permute-start | bytes 688136 | tf_op jit(solution)/shard_map/ppermute | solution.py:57
  54.9 4.5 %collective-permute-start.18 = (bf16[64,1792]{1,0:T(8,128)(2,1)S(1)}, bf16[64,1792]{1,0:T(8,128)(2,1)S(1)}, u32[]{:S(2)}, u32[]{:S(2)}) collective-permute-start(bf16[64,1792]{1,0:T(8,128)(2,1)S(1)} %get-tuple-element.55), channel_id=1, source_target_pairs={{0,8},{8,0},{16,24},{24,16},{1,9},{9,1},{17,25},{25,17},{2,10},{10... | collective-permute-start | bytes 688136 | tf_op jit(solution)/shard_map/ppermute | solution.py:57
  55.0 10.8 %collective-permute-start.17 = (bf16[64,1792]{1,0:T(8,128)(2,1)S(1)}, bf16[64,1792]{1,0:T(8,128)(2,1)S(1)}, u32[]{:S(2)}, u32[]{:S(2)}) collective-permute-start(bf16[64,1792]{1,0:T(8,128)(2,1)S(1)} %get-tuple-element.54), channel_id=1, source_target_pairs={{0,8},{8,0},{16,24},{24,16},{1,9},{9,1},{17,25},{25,17},{2,10},{10... | collective-permute-start | bytes 688136 | tf_op jit(solution)/shard_map/ppermute | solution.py:57
  57.9 7.8 %collective-permute-start.14 = (bf16[32,1792]{1,0:T(8,128)(2,1)S(1)}, bf16[32,1792]{1,0:T(8,128)(2,1)S(1)}, u32[]{:S(2)}, u32[]{:S(2)}) collective-permute-start(bf16[32,1792]{1,0:T(8,128)(2,1)S(1)} %get-tuple-element.47), channel_id=1, source_target_pairs={{0,4},{2,6},{4,0},{6,2},{1,5},{3,7},{5,1},{7,3},{8,12},{10,14},{12... | collective-permute-start | bytes 344072 | tf_op jit(solution)/shard_map/ppermute | solution.py:57
  59.5 6.3 %collective-permute-start.20 = (bf16[32,1792]{1,0:T(8,128)(2,1)S(1)}, bf16[32,1792]{1,0:T(8,128)(2,1)S(1)}, u32[]{:S(2)}, u32[]{:S(2)}) collective-permute-start(bf16[32,1792]{1,0:T(8,128)(2,1)S(1)} %get-tuple-element.58), channel_id=1, source_target_pairs={{0,16},{8,24},{16,0},{24,8},{1,17},{9,25},{17,1},{25,9},{2,18},{10... | collective-permute-start | bytes 344072 | tf_op jit(solution)/shard_map/ppermute | solution.py:57
  59.8 9.6 %collective-permute-start.19 = (bf16[32,1792]{1,0:T(8,128)(2,1)S(1)}, bf16[32,1792]{1,0:T(8,128)(2,1)S(1)}, u32[]{:S(2)}, u32[]{:S(2)}) collective-permute-start(bf16[32,1792]{1,0:T(8,128)(2,1)S(1)} %get-tuple-element.56), channel_id=1, source_target_pairs={{0,16},{8,24},{16,0},{24,8},{1,17},{9,25},{17,1},{25,9},{2,18},{10... | collective-permute-start | bytes 344072 | tf_op jit(solution)/shard_map/ppermute | solution.py:57
  65.7 4.7 %collective-permute-start.15 = (bf16[16,1792]{1,0:T(8,128)(2,1)S(1)}, bf16[16,1792]{1,0:T(8,128)(2,1)S(1)}, u32[]{:S(2)}, u32[]{:S(2)}) collective-permute-start(bf16[16,1792]{1,0:T(8,128)(2,1)S(1)} %get-tuple-element.49), channel_id=1, source_target_pairs={{0,2},{2,0},{4,6},{6,4},{1,3},{3,1},{5,7},{7,5},{8,10},{10,8},{12,... | collective-permute-start | bytes 172040 | tf_op jit(solution)/shard_map/ppermute | solution.py:57
  65.9 6.7 %collective-permute-start.21 = (bf16[16,1792]{1,0:T(8,128)(2,1)S(1)}, bf16[16,1792]{1,0:T(8,128)(2,1)S(1)}, u32[]{:S(2)}, u32[]{:S(2)}) collective-permute-start(bf16[16,1792]{1,0:T(8,128)(2,1)S(1)} %get-tuple-element.59), channel_id=1, source_target_pairs={{0,6},{2,4},{4,2},{6,0},{1,7},{3,5},{5,3},{7,1},{8,14},{10,12},{12... | collective-permute-start | bytes 172040 | tf_op jit(solution)/shard_map/ppermute | solution.py:57
  68.3 6.3 %collective-permute-start.22 = (bf16[16,1792]{1,0:T(8,128)(2,1)S(1)}, bf16[16,1792]{1,0:T(8,128)(2,1)S(1)}, u32[]{:S(2)}, u32[]{:S(2)}) collective-permute-start(bf16[16,1792]{1,0:T(8,128)(2,1)S(1)} %get-tuple-element.60), channel_id=1, source_target_pairs={{0,4},{2,6},{4,0},{6,2},{1,5},{3,7},{5,1},{7,3},{8,12},{10,14},{12... | collective-permute-start | bytes 172040 | tf_op jit(solution)/shard_map/ppermute | solution.py:57
  69.5 5.2 %collective-permute-start.23 = (bf16[16,1792]{1,0:T(8,128)(2,1)S(1)}, bf16[16,1792]{1,0:T(8,128)(2,1)S(1)}, u32[]{:S(2)}, u32[]{:S(2)}) collective-permute-start(bf16[16,1792]{1,0:T(8,128)(2,1)S(1)} %get-tuple-element.61), channel_id=1, source_target_pairs={{0,2},{2,0},{4,6},{6,4},{1,3},{3,1},{5,7},{7,5},{8,10},{10,8},{12,... | collective-permute-start | bytes 172040 | tf_op jit(solution)/shard_map/ppermute | solution.py:57
  (10 other events, 28.3 us)

commit v7 on v6

--- a/solution.py
+++ b/solution.py
@@ -10,7 +10,6 @@
 PLANE = ("group", "ingroup")
 LANES = 128
 CHUNK = 256
-FETCH = 50
 BF16 = jnp.bfloat16
 F32 = jnp.float32
 
@@ -65,7 +64,7 @@
     return bits
 
 
-def payload_body(tokens, ids, gate, out, tokens_held, ids_held, gate_held, sems):
+def payload_body(me, tokens, ids, gate, out, tokens_held, ids_held, gate_held, sems):
     copies = [
         pltpu.make_async_copy(source, held, sems.at[i])
         for i, (source, held) in enumerate(
@@ -98,25 +97,6 @@
     out[:, :features] = tokens_held[...]
 
 
-def fetch_body(source, after, out, token, sem):
-    copy = pltpu.make_async_copy(source, out, sem)
-    copy.start()
-    token[...] = jnp.zeros_like(token)
-    copy.wait()
-
-
-def fetch(source, after):
-    return call(
-        "fetch",
-        fetch_body,
-        [(source.shape, source.dtype), ((8, LANES), F32)],
-        [source, after],
-        limit=FETCH,
-        hbm=(0,),
-        scratch=[pltpu.SemaphoreType.DMA],
-    )
-
-
 def pack_body(count, *refs):
     parts, out = refs[:count], refs[-1]
     at = 0
@@ -146,24 +126,24 @@
     return call("copied", copy_body, [(source.shape, source.dtype)], [source, after], 1 << 31)[0]
 
 
-def spread(own, cotangent, w_gate, w_up):
-    outer, inner_count = bits_of("group"), lax.axis_size("ingroup")
-    second = copied(cotangent, own)
-    blocks = [own] + [swap(own, "ingroup", j) for j in range(1, inner_count)]
-    w_gate, token = fetch(w_gate, own)
-    early = pack(blocks[: inner_count // 2], [token])
-    w_up, token = fetch(w_up, early)
-    late, second = pack(blocks[inner_count // 2 :], passed=[second])
+def exchange(own):
+    count = lax.axis_size("ingroup")
+    return [own] + [swap(own, "ingroup", j) for j in range(1, count)]
+
+
+def spread(own, cotangent):
+    outer = bits_of("group")
+    blocks = exchange(own)
+    half = len(blocks) // 2
+    early, second = pack(blocks[:half], passed=[copied(cotangent, own)])
+    second = exchange(second)
+    late = pack(blocks[half:])
     across = swap(early, "group", outer[0])
     last = swap(late, "group", outer[0])
-    *bits, high = bits_of("ingroup")[::-1]
-    for bit in bits:
-        second = pack([second, swap(second, "ingroup", bit)])
-    first = pack([early, late, across, last], [token, second])
+    first = pack([early, late, across, last], second)
     for bit in outer[1:-1]:
         first = pack([first, swap(first, "group", bit)])
-    first = [first, swap(first, "group", outer[-1])]
-    return first, [second, swap(second, "ingroup", high)], w_gate, w_up
+    return [first, swap(first, "group", outer[-1])], second
 
 
 def spread_end(parts, after):
@@ -275,23 +255,26 @@
     place_rows(place[...], rows, *outs)
 
 
-def add_body(count, at, parts, keep, *refs):
-    rows = sum(out.shape[0] for out in refs[count:])
+def add_body(count, after, at, parts, keep, *refs):
+    outs = refs[count + after :]
+    rows = sum(out.shape[0] for out in outs)
     total = keep[at : at + rows].astype(F32)
     for received, start in zip(refs[:count], parts):
         total = total + received[start : start + rows].astype(F32)
     start = 0
-    for out in refs[count:]:
+    for out in outs:
         out[...] = total[start : start + out.shape[0]].astype(out.dtype)
         start += out.shape[0]
 
 
-def add(keep, at, received, outs):
+def add(keep, at, received, outs, after=()):
     return call(
         "add",
-        functools.partial(add_body, len(received), at, [start for _, start in received]),
+        functools.partial(
+            add_body, len(received), len(after), at, [start for _, start in received]
+        ),
         [((rows, keep.shape[1]), dtype) for rows, dtype in outs],
-        [keep] + [r for r, _ in received],
+        [keep] + [r for r, _ in received] + list(after),
     )
 
 
@@ -305,12 +288,12 @@
     return near, *[swap(piece, "group", bits_of("group")[1]) for piece in pieces]
 
 
-def collect_few(near, far, got_stay):
+def collect_few(near, far, got_stay, ties):
     half = near.shape[0] // 2
     received = [(got_stay, 0), (swap(far, "group", bits_of("group")[0]), 0)]
-    for bit in bits_of("ingroup"):
+    for i, bit in enumerate(bits_of("ingroup")):
         half //= 2
-        near, far = add(near, 0, received, [(half, F32), (half, BF16)])
+        near, far = add(near, 0, received, [(half, F32), (half, BF16)], ties[i : i + 1])
         received = [(swap(far, "ingroup", bit), 0)]
     return add(near, 0, received, [(half, BF16)])[0]
 
@@ -323,11 +306,10 @@
     across, last = swap(high, "group", bit), swap(low, "group", bit)
     away = add(near, quarter, [(got_stay, quarter), (across, 0)], [(block, BF16)] * (count // 2))
     sent = [swap(away[j], "ingroup", count // 2 + j) for j in range(count // 2)[::-1]]
-    own, *away = add(
-        near, 0, [(got_stay, 0), (last, 0)], [(block, F32)] + [(block, BF16)] * (count // 2 - 1)
-    )
+    outs = [(block, F32)] + [(block, BF16)] * (count // 2 - 1)
+    own, *away = add(near, 0, [(got_stay, 0), (last, 0)], outs, away[:1])
     sent += [swap(away[j], "ingroup", 1 + j) for j in range(count // 2 - 1)[::-1]]
-    return add(own, 0, [(s, 0) for s in sent], [(block, BF16)])[0]
+    return add(own, 0, [(s, 0) for s in sent], [(block, BF16)])[0], [low, own]
 
 
 def from_peers(sent):
@@ -350,25 +332,25 @@
     w_gate, w_up, w_down = w_gate[0], w_up[0], w_down[0]
     product = 2 * slots * features * hidden
 
+    me = lax.axis_index(PLANE).astype(jnp.int32).reshape(1)
     (own,) = call(
         "payload",
         payload_body,
         [((block, wide + LANES), BF16)],
-        [tokens, expert_ids.T, gate_fixed.T],
+        [me, tokens, expert_ids.T, gate_fixed.T],
         limit=58,
-        hbm=(0, 1, 2),
+        hbm=(1, 2, 3),
         scratch=[pltpu.VMEM(tokens.shape, BF16)]
         + [pltpu.VMEM((topk, block), jnp.int32)] * 2
         + [pltpu.SemaphoreType.DMA((3,))],
     )
-    x_parts, d_parts, gate_held, up_held = spread(own, cotangent, w_gate, w_up)
-    me = lax.axis_index(PLANE).astype(jnp.int32).reshape(1)
+    x_parts, d_parts = spread(own, cotangent)
     both, both_sent = [((2 * slots, hidden), t) for t in (F32, BF16)]
     place, scale, both, both_sent = call(
         "forward",
         functools.partial(route_body, wide, topk, block, capacity, len(x_parts)),
         [((total, slots), BF16), ((slots, LANES), F32), both, both_sent],
-        [me] + x_parts + [gate_held, up_held],
+        [me] + x_parts + [w_gate, w_up],
         2 * product,
         16,
     )
@@ -402,12 +384,13 @@
             "grad",
             functools.partial(grad_body, peers),
             [near, fourth, fourth],
-            list(factors) + [back] + back_in + [place, gate_held, up_held, far],
+            list(factors) + [back] + back_in + [place, w_gate, w_up, far],
             2 * product,
             24,
         )
     )
-    return collect_few(near_y, far, got_y), collect_soon(near_dx, got_go, got_dx)
+    grad, ties = collect_soon(near_dx, got_go, got_dx)
+    return collect_few(near_y, far, got_y, ties), grad
 
 
 def solution(mesh):

time: 75.8 us -> 76.5 us (level)
  waiting for transfers between devices: 22.9 us -> 36.6 us
  local copies, waits for them, and re-layouts: 10.2 us -> 2.52 us
  Pallas kernels: 15.1 us -> 11 us
  starting transfers between devices: 26.2 us -> 25.3 us
    ppermute x22 -> x23, waiting for transfers between devices: 17.3 us -> 31.7 us  [swap(): lax.ppermute(value, axis, [(i, i ^ offset) for i in range(lax.axis_size(a...]
    unnamed x20 -> x12, local copies, waits for them, and re-layouts: 10.2 us -> 2.52 us
    pallas_call x23 -> x20, Pallas kernels: 15.1 us -> 11 us  [call(): return kernel(*args, *passed)]
    ppermute x22 -> x23, starting transfers between devices: 23.2 us -> 22.3 us  [swap(): lax.ppermute(value, axis, [(i, i ^ offset) for i in range(lax.axis_size(a...]
  transfers between devices with their start and end apart: 24 -> 25, of which waited for: 11 -> 17; matrix products, arithmetic and copies ran while one was open for 0% -> 0% of each run, Pallas kernels for 17% -> 5%
where the time goes in v7:
time: 76.5 us; the launch traced here: 76.2 us
  waiting for transfers between devices  36.6 us (48%)
  starting transfers between devices  25.3 us (33%)
  Pallas kernels  11 us (14%)
  local copies, waits for them, and re-layouts  2.52 us (3%)
  between operations  0.82 us (1%)
    ppermute x23, waiting for transfers between devices, swap(): lax.ppermute(value, axis, [(i, i ^ offset) for i in range(lax.axis_size(a...  31.7 us
    ppermute x23, starting transfers between devices, swap(): lax.ppermute(value, axis, [(i, i ^ offset) for i in range(lax.axis_size(a...  22.3 us
    pallas_call x20, Pallas kernels, call(): return kernel(*args, *passed)  11 us
    ppermute x2, waiting for transfers between devices, from_peers(): lax.ppermute(sent, 'dp', [(i, (i + step) % count) for i in range(count)])  4.93 us
    ppermute x2, starting transfers between devices, from_peers(): lax.ppermute(sent, 'dp', [(i, (i + step) % count) for i in range(count)])  3.05 us
    unnamed x12, local copies, waits for them, and re-layouts  2.52 us
  transfers between devices with their start and end apart: 25, of which 17 were waited for; matrix products, arithmetic and copies ran while one was open for 0% of the time, Pallas kernels for 5%

profile of v7, /device:TPU:0, one launch (start us, length us, event | category | flops | bytes accessed | tf_op | source)
XLA Modules:
  0.0 76.2 jit_solution(7227763242355855677)
XLA Ops:
  0.6 1.5 %payload.1.refs_1_.refs_0_ = bf16[16,1920]{1,0:T(8,128)(2,1)} custom-call(s32[1]{0:T(128)} %bitcast.refs_0_, bf16[16,1792]{1,0:T(8,128)(2,1)} %refs_1_.1, s32[8,16]{1,0:T(8,128)} %bitcast.12, s32[8,16]{1,0:T(8,128)} %bitcast.13), custom_call_target="tpu_custom_call" | custom-call | bytes 119812 | tf_op jit(solution)/shard_map/payload/payload/pallas_call | solution.py:52
  2.2 3.1 %collective-permute-start = (bf16[16,1920]{1,0:T(8,128)(2,1)}, bf16[16,1920]{1,0:T(8,128)(2,1)S(1)}, u32[]{:S(2)}, u32[]{:S(2)}) collective-permute-start(bf16[16,1920]{1,0:T(8,128)(2,1)} %payload.1.refs_1_.refs_0_), channel_id=1, source_target_pairs={{0,2},{2,0},{4,6},{6,4},{1,3},{3,1},{5,7},{7,5},{8,10},{10,8},{12,... | collective-permute-start | bytes 184328 | tf_op jit(solution)/shard_map/ppermute | solution.py:56
  5.2 2.6 %collective-permute-start.1 = (bf16[16,1920]{1,0:T(8,128)(2,1)}, bf16[16,1920]{1,0:T(8,128)(2,1)S(1)}, u32[]{:S(2)}, u32[]{:S(2)}) collective-permute-start(bf16[16,1920]{1,0:T(8,128)(2,1)} %payload.1.refs_1_.refs_0_), channel_id=1, source_target_pairs={{0,4},{2,6},{4,0},{6,2},{1,5},{3,7},{5,1},{7,3},{8,12},{10,14},{12... | collective-permute-start | bytes 184328 | tf_op jit(solution)/shard_map/ppermute | solution.py:56
  10.4 1.8 %collective-permute-start.3 = (bf16[32,1920]{1,0:T(8,128)(2,1)S(1)}, bf16[32,1920]{1,0:T(8,128)(2,1)S(1)}, u32[]{:S(2)}, u32[]{:S(2)}) collective-permute-start(bf16[32,1920]{1,0:T(8,128)(2,1)S(1)} %get-tuple-element.28.refs_0_), channel_id=1, source_target_pairs={{0,16},{8,24},{16,0},{24,8},{1,17},{9,25},{17,1},{25,9},{2,18},{10... | collective-permute-start | bytes 368648 | tf_op jit(solution)/shard_map/ppermute | solution.py:56
  12.2 1.9 %collective-permute-done.2.refs_1_ = bf16[16,1920]{1,0:T(8,128)(2,1)S(1)} collective-permute-done((bf16[16,1920]{1,0:T(8,128)(2,1)}, bf16[16,1920]{1,0:T(8,128)(2,1)S(1)}, u32[]{:S(2)}, u32[]{:S(2)}) %collective-permute-start.2) | collective-permute-done | bytes 61472 | tf_op jit(solution)/shard_map/ppermute | solution.py:56
  14.1 1.6 %collective-permute-start.4 = (bf16[32,1920]{1,0:T(8,128)(2,1)S(1)}, bf16[32,1920]{1,0:T(8,128)(2,1)S(1)}, u32[]{:S(2)}, u32[]{:S(2)}) collective-permute-start(bf16[32,1920]{1,0:T(8,128)(2,1)S(1)} %pack.6.refs_1_), channel_id=1, source_target_pairs={{0,16},{8,24},{16,0},{24,8},{1,17},{9,25},{17,1},{25,9},{2,18},{10... | collective-permute-start | bytes 368648 | tf_op jit(solution)/shard_map/ppermute | solution.py:56
  15.7 2.1 %collective-permute-start.6 = (bf16[16,1792]{1,0:T(8,128)(2,1)S(1)}, bf16[16,1792]{1,0:T(8,128)(2,1)S(1)}, u32[]{:S(2)}, u32[]{:S(2)}) collective-permute-start(bf16[16,1792]{1,0:T(8,128)(2,1)S(1)} %get-tuple-element.29.refs_4_.refs_0_), channel_id=1, source_target_pairs={{0,4},{2,6},{4,0},{6,2},{1,5},{3,7},{5,1},{7,3},{8,12},{10,14},{12... | collective-permute-start | bytes 172040 | tf_op jit(solution)/shard_map/ppermute | solution.py:56
  17.7 2.3 %collective-permute-start.7 = (bf16[16,1792]{1,0:T(8,128)(2,1)S(1)}, bf16[16,1792]{1,0:T(8,128)(2,1)S(1)}, u32[]{:S(2)}, u32[]{:S(2)}) collective-permute-start(bf16[16,1792]{1,0:T(8,128)(2,1)S(1)} %get-tuple-element.29.refs_4_.refs_0_), channel_id=1, source_target_pairs={{0,6},{2,4},{4,2},{6,0},{1,7},{3,5},{5,3},{7,1},{8,14},{10,12},{12... | collective-permute-start | bytes 172040 | tf_op jit(solution)/shard_map/ppermute | solution.py:56
  21.1 2.7 %collective-permute-done.7.refs_7_.refs_3_ = bf16[16,1792]{1,0:T(8,128)(2,1)S(1)} collective-permute-done((bf16[16,1792]{1,0:T(8,128)(2,1)S(1)}, bf16[16,1792]{1,0:T(8,128)(2,1)S(1)}, u32[]{:S(2)}, u32[]{:S(2)}) %collective-permute-start.7) | collective-permute-done | bytes 57376 | tf_op jit(solution)/shard_map/ppermute | solution.py:56
  23.9 1.9 %collective-permute-done.8.refs_2_ = bf16[128,1920]{1,0:T(8,128)(2,1)S(1)} collective-permute-done((bf16[128,1920]{1,0:T(8,128)(2,1)S(1)}, bf16[128,1920]{1,0:T(8,128)(2,1)S(1)}, u32[]{:S(2)}, u32[]{:S(2)}) %collective-permute-start.8) | collective-permute-done | bytes 491552 | tf_op jit(solution)/shard_map/ppermute | solution.py:56
  25.7 1.8 %forward.1 = (bf16[256,128]{1,0:T(8,128)(2,1)S(1)}, f32[128,128]{1,0:T(8,128)S(1)}, f32[256,1024]{1,0:T(8,128)S(1)}, bf16[256,1024]{1,0:T(8,128)(2,1)S(1)}) custom-call(s32[1]{0:T(128)} %bitcast.refs_0_, bf16[128,1920]{1,0:T(8,128)(2,1)S(1)} %pack.7.refs_1_, bf16[128,1920]{1,0:T(8,128)(2,1)S(1)} %collective-permute-done.8.refs_2_, ...), custom_call_target="tpu_custom_call" | custom-call | flops 939524096 | bytes 10027012 | tf_op jit(solution)/shard_map/forward/forward/pallas_call | solution.py:52
  29.8 5.5 %collective-permute-done.10.refs_1_ = bf16[64,1792]{1,0:T(8,128)(2,1)S(1)} collective-permute-done((bf16[64,1792]{1,0:T(8,128)(2,1)S(1)}, bf16[64,1792]{1,0:T(8,128)(2,1)S(1)}, u32[]{:S(2)}, u32[]{:S(2)}) %collective-permute-start.10) | collective-permute-done | bytes 229408 | tf_op jit(solution)/shard_map/ppermute | solution.py:56
  35.4 1.8 %collective-permute-done.11.refs_1_ = bf16[128,1792]{1,0:T(8,128)(2,1)S(1)} collective-permute-done((bf16[128,1792]{1,0:T(8,128)(2,1)S(1)}, bf16[128,1792]{1,0:T(8,128)(2,1)S(1)}, u32[]{:S(2)}, u32[]{:S(2)}) %collective-permute-start.11) | collective-permute-done | bytes 458784 | tf_op jit(solution)/shard_map/ppermute | solution.py:56
  38.5 1.6 %collective-permute-start.15 = (bf16[128,1024]{1,0:T(8,128)(2,1)S(1)}, bf16[128,1024]{1,0:T(8,128)(2,1)S(1)}, u32[]{:S(2)}, u32[]{:S(2)}) collective-permute-start(bf16[128,1024]{1,0:T(8,128)(2,1)S(1)} %get-tuple-element.34.refs_5_), channel_id=1, source_target_pairs={{0,1},{1,0},{2,3},{3,2},{4,5},{5,4},{6,7},{7,6},{8,9},{9,8},{10,11... | collective-permute-start | bytes 786440 | tf_op jit(solution)/shard_map/ppermute | solution.py:318
  40.0 2.6 %collective-permute-done.9.refs_1_ = bf16[256,1024]{1,0:T(8,128)(2,1)S(1)} collective-permute-done((bf16[256,1024]{1,0:T(8,128)(2,1)S(1)}, bf16[256,1024]{1,0:T(8,128)(2,1)S(1)}, u32[]{:S(2)}, u32[]{:S(2)}) %collective-permute-start.9) | collective-permute-done | bytes 524320 | tf_op jit(solution)/shard_map/ppermute | solution.py:318
  45.3 2.3 %collective-permute-done.15.refs_3_ = bf16[128,1024]{1,0:T(8,128)(2,1)S(1)} collective-permute-done((bf16[128,1024]{1,0:T(8,128)(2,1)S(1)}, bf16[128,1024]{1,0:T(8,128)(2,1)S(1)}, u32[]{:S(2)}, u32[]{:S(2)}) %collective-permute-start.15) | collective-permute-done | bytes 262176 | tf_op jit(solution)/shard_map/ppermute | solution.py:318
  47.6 3.2 %grad.1 = (f32[128,1792]{1,0:T(8,128)S(1)}, bf16[64,1792]{1,0:T(8,128)(2,1)S(1)}, bf16[64,1792]{1,0:T(8,128)(2,1)S(1)}) custom-call(f32[128,1024]{1,0:T(8,128)S(1)} %get-tuple-element.38.refs_0_, f32[128,1024]{1,0:T(8,128)S(1)} %get-tuple-element.39.refs_1_, f32[128,1024]{1,0:T(8,128)S(1)} %get-tuple-element.40.refs_2_, ...), custom_call_target="tpu_custom_call" | custom-call | flops 939524096 | bytes 10846208 | tf_op jit(solution)/shard_map/grad/grad/pallas_call | solution.py:52
  54.9 5.0 %collective-permute-done.14.refs_2_ = bf16[64,1792]{1,0:T(8,128)(2,1)S(1)} collective-permute-done((bf16[64,1792]{1,0:T(8,128)(2,1)S(1)}, bf16[64,1792]{1,0:T(8,128)(2,1)S(1)}, u32[]{:S(2)}, u32[]{:S(2)}) %collective-permute-start.14) | collective-permute-done | bytes 229408 | tf_op jit(solution)/shard_map/ppermute | solution.py:56
  60.1 2.3 %collective-permute-done.20.refs_2_ = bf16[32,1792]{1,0:T(8,128)(2,1)S(1)} collective-permute-done((bf16[32,1792]{1,0:T(8,128)(2,1)S(1)}, bf16[32,1792]{1,0:T(8,128)(2,1)S(1)}, u32[]{:S(2)}, u32[]{:S(2)}) %collective-permute-start.20) | collective-permute-done | bytes 114720 | tf_op jit(solution)/shard_map/ppermute | solution.py:56
  62.4 1.5 %collective-permute-done.19.refs_2_ = bf16[32,1792]{1,0:T(8,128)(2,1)S(1)} collective-permute-done((bf16[32,1792]{1,0:T(8,128)(2,1)S(1)}, bf16[32,1792]{1,0:T(8,128)(2,1)S(1)}, u32[]{:S(2)}, u32[]{:S(2)}) %collective-permute-start.19) | collective-permute-done | bytes 114720 | tf_op jit(solution)/shard_map/ppermute | solution.py:56
  64.0 2.3 %collective-permute-done.17.refs_1_ = bf16[32,1792]{1,0:T(8,128)(2,1)S(1)} collective-permute-done((bf16[32,1792]{1,0:T(8,128)(2,1)S(1)}, bf16[32,1792]{1,0:T(8,128)(2,1)S(1)}, u32[]{:S(2)}, u32[]{:S(2)}) %collective-permute-start.17) | collective-permute-done | bytes 114720 | tf_op jit(solution)/shard_map/ppermute | solution.py:56
  66.4 2.0 %collective-permute-start.24 = (bf16[16,1792]{1,0:T(8,128)(2,1)S(1)}, bf16[16,1792]{1,0:T(8,128)(2,1)S(1)}, u32[]{:S(2)}, u32[]{:S(2)}) collective-permute-start(bf16[16,1792]{1,0:T(8,128)(2,1)S(1)} %get-tuple-element.53), channel_id=1, source_target_pairs={{0,2},{2,0},{4,6},{6,4},{1,3},{3,1},{5,7},{7,5},{8,10},{10,8},{12,... | collective-permute-start | bytes 172040 | tf_op jit(solution)/shard_map/ppermute | solution.py:56
  68.4 1.7 %collective-permute-start.22 = (bf16[16,1792]{1,0:T(8,128)(2,1)S(1)}, bf16[16,1792]{1,0:T(8,128)(2,1)S(1)}, u32[]{:S(2)}, u32[]{:S(2)}) collective-permute-start(bf16[16,1792]{1,0:T(8,128)(2,1)S(1)} %get-tuple-element.52), channel_id=1, source_target_pairs={{0,6},{2,4},{4,2},{6,0},{1,7},{3,5},{5,3},{7,1},{8,14},{10,12},{12... | collective-permute-start | bytes 172040 | tf_op jit(solution)/shard_map/ppermute | solution.py:56
  71.8 2.5 %collective-permute-done.22.refs_1_ = bf16[16,1792]{1,0:T(8,128)(2,1)S(1)} collective-permute-done((bf16[16,1792]{1,0:T(8,128)(2,1)S(1)}, bf16[16,1792]{1,0:T(8,128)(2,1)S(1)}, u32[]{:S(2)}, u32[]{:S(2)}) %collective-permute-start.22) | collective-permute-done | bytes 57376 | tf_op jit(solution)/shard_map/ppermute | solution.py:56
  (58 shorter events, 17.9 us)
Async XLA Ops:
  2.2 7.4 %collective-permute-start = (bf16[16,1920]{1,0:T(8,128)(2,1)}, bf16[16,1920]{1,0:T(8,128)(2,1)S(1)}, u32[]{:S(2)}, u32[]{:S(2)}) collective-permute-start(bf16[16,1920]{1,0:T(8,128)(2,1)} %payload.1.refs_1_.refs_0_), channel_id=1, source_target_pairs={{0,2},{2,0},{4,6},{6,4},{1,3},{3,1},{5,7},{7,5},{8,10},{10,8},{12,... | collective-permute-start | bytes 184328 | tf_op jit(solution)/shard_map/ppermute | solution.py:56
  5.2 6.9 %collective-permute-start.1 = (bf16[16,1920]{1,0:T(8,128)(2,1)}, bf16[16,1920]{1,0:T(8,128)(2,1)S(1)}, u32[]{:S(2)}, u32[]{:S(2)}) collective-permute-start(bf16[16,1920]{1,0:T(8,128)(2,1)} %payload.1.refs_1_.refs_0_), channel_id=1, source_target_pairs={{0,4},{2,6},{4,0},{6,2},{1,5},{3,7},{5,1},{7,3},{8,12},{10,14},{12... | collective-permute-start | bytes 184328 | tf_op jit(solution)/shard_map/ppermute | solution.py:56
  7.8 6.2 %collective-permute-start.2 = (bf16[16,1920]{1,0:T(8,128)(2,1)}, bf16[16,1920]{1,0:T(8,128)(2,1)S(1)}, u32[]{:S(2)}, u32[]{:S(2)}) collective-permute-start(bf16[16,1920]{1,0:T(8,128)(2,1)} %payload.1.refs_1_.refs_0_), channel_id=1, source_target_pairs={{0,6},{2,4},{4,2},{6,0},{1,7},{3,5},{5,3},{7,1},{8,14},{10,12},{12... | collective-permute-start | bytes 184328 | tf_op jit(solution)/shard_map/ppermute | solution.py:56
  10.4 13.3 %collective-permute-start.3 = (bf16[32,1920]{1,0:T(8,128)(2,1)S(1)}, bf16[32,1920]{1,0:T(8,128)(2,1)S(1)}, u32[]{:S(2)}, u32[]{:S(2)}) collective-permute-start(bf16[32,1920]{1,0:T(8,128)(2,1)S(1)} %get-tuple-element.28.refs_0_), channel_id=1, source_target_pairs={{0,16},{8,24},{16,0},{24,8},{1,17},{9,25},{17,1},{25,9},{2,18},{10... | collective-permute-start | bytes 368648 | tf_op jit(solution)/shard_map/ppermute | solution.py:56
  14.1 9.7 %collective-permute-start.4 = (bf16[32,1920]{1,0:T(8,128)(2,1)S(1)}, bf16[32,1920]{1,0:T(8,128)(2,1)S(1)}, u32[]{:S(2)}, u32[]{:S(2)}) collective-permute-start(bf16[32,1920]{1,0:T(8,128)(2,1)S(1)} %pack.6.refs_1_), channel_id=1, source_target_pairs={{0,16},{8,24},{16,0},{24,8},{1,17},{9,25},{17,1},{25,9},{2,18},{10... | collective-permute-start | bytes 368648 | tf_op jit(solution)/shard_map/ppermute | solution.py:56
  15.7 5.4 %collective-permute-start.5 = (bf16[16,1792]{1,0:T(8,128)(2,1)S(1)}, bf16[16,1792]{1,0:T(8,128)(2,1)S(1)}, u32[]{:S(2)}, u32[]{:S(2)}) collective-permute-start(bf16[16,1792]{1,0:T(8,128)(2,1)S(1)} %get-tuple-element.29.refs_4_.refs_0_), channel_id=1, source_target_pairs={{0,2},{2,0},{4,6},{6,4},{1,3},{3,1},{5,7},{7,5},{8,10},{10,8},{12,... | collective-permute-start | bytes 172040 | tf_op jit(solution)/shard_map/ppermute | solution.py:56
  15.7 5.4 %collective-permute-start.6 = (bf16[16,1792]{1,0:T(8,128)(2,1)S(1)}, bf16[16,1792]{1,0:T(8,128)(2,1)S(1)}, u32[]{:S(2)}, u32[]{:S(2)}) collective-permute-start(bf16[16,1792]{1,0:T(8,128)(2,1)S(1)} %get-tuple-element.29.refs_4_.refs_0_), channel_id=1, source_target_pairs={{0,4},{2,6},{4,0},{6,2},{1,5},{3,7},{5,1},{7,3},{8,12},{10,14},{12... | collective-permute-start | bytes 172040 | tf_op jit(solution)/shard_map/ppermute | solution.py:56
  17.7 6.0 %collective-permute-start.7 = (bf16[16,1792]{1,0:T(8,128)(2,1)S(1)}, bf16[16,1792]{1,0:T(8,128)(2,1)S(1)}, u32[]{:S(2)}, u32[]{:S(2)}) collective-permute-start(bf16[16,1792]{1,0:T(8,128)(2,1)S(1)} %get-tuple-element.29.refs_4_.refs_0_), channel_id=1, source_target_pairs={{0,6},{2,4},{4,2},{6,0},{1,7},{3,5},{5,3},{7,1},{8,14},{10,12},{12... | collective-permute-start | bytes 172040 | tf_op jit(solution)/shard_map/ppermute | solution.py:56
  23.8 1.9 %collective-permute-start.8 = (bf16[128,1920]{1,0:T(8,128)(2,1)S(1)}, bf16[128,1920]{1,0:T(8,128)(2,1)S(1)}, u32[]{:S(2)}, u32[]{:S(2)}) collective-permute-start(bf16[128,1920]{1,0:T(8,128)(2,1)S(1)} %pack.7.refs_1_), channel_id=1, source_target_pairs={{0,8},{8,0},{16,24},{24,16},{1,9},{9,1},{17,25},{25,17},{2,10},{10... | collective-permute-start | bytes 1474568 | tf_op jit(solution)/shard_map/ppermute | solution.py:56
  27.5 7.7 %collective-permute-start.10 = (bf16[64,1792]{1,0:T(8,128)(2,1)S(1)}, bf16[64,1792]{1,0:T(8,128)(2,1)S(1)}, u32[]{:S(2)}, u32[]{:S(2)}) collective-permute-start(bf16[64,1792]{1,0:T(8,128)(2,1)S(1)} %pack.8.refs_0_), channel_id=1, source_target_pairs={{0,16},{8,24},{16,0},{24,8},{1,17},{9,25},{17,1},{25,9},{2,18},{10... | collective-permute-start | bytes 688136 | tf_op jit(solution)/shard_map/ppermute | solution.py:56
  28.3 14.3 %collective-permute-start.9 = (bf16[256,1024]{1,0:T(8,128)(2,1)S(1)}, bf16[256,1024]{1,0:T(8,128)(2,1)S(1)}, u32[]{:S(2)}, u32[]{:S(2)}) collective-permute-start(bf16[256,1024]{1,0:T(8,128)(2,1)S(1)} %get-tuple-element.31.refs_4_), channel_id=1, source_target_pairs={{0,1},{1,0},{2,3},{3,2},{4,5},{5,4},{6,7},{7,6},{8,9},{9,8},{10,11... | collective-permute-start | bytes 1572872 | tf_op jit(solution)/shard_map/ppermute | solution.py:318
  35.3 1.9 %collective-permute-start.11 = (bf16[128,1792]{1,0:T(8,128)(2,1)S(1)}, bf16[128,1792]{1,0:T(8,128)(2,1)S(1)}, u32[]{:S(2)}, u32[]{:S(2)}) collective-permute-start(bf16[128,1792]{1,0:T(8,128)(2,1)S(1)} %pack.9.refs_0_), channel_id=1, source_target_pairs={{0,8},{8,0},{16,24},{24,16},{1,9},{9,1},{17,25},{25,17},{2,10},{10... | collective-permute-start | bytes 1376264 | tf_op jit(solution)/shard_map/ppermute | solution.py:56
  38.5 9.1 %collective-permute-start.15 = (bf16[128,1024]{1,0:T(8,128)(2,1)S(1)}, bf16[128,1024]{1,0:T(8,128)(2,1)S(1)}, u32[]{:S(2)}, u32[]{:S(2)}) collective-permute-start(bf16[128,1024]{1,0:T(8,128)(2,1)S(1)} %get-tuple-element.34.refs_5_), channel_id=1, source_target_pairs={{0,1},{1,0},{2,3},{3,2},{4,5},{5,4},{6,7},{7,6},{8,9},{9,8},{10,11... | collective-permute-start | bytes 786440 | tf_op jit(solution)/shard_map/ppermute | solution.py:318
  50.9 1.9 %collective-permute-start.16 = (bf16[64,1792]{1,0:T(8,128)(2,1)S(1)}, bf16[64,1792]{1,0:T(8,128)(2,1)S(1)}, u32[]{:S(2)}, u32[]{:S(2)}) collective-permute-start(bf16[64,1792]{1,0:T(8,128)(2,1)S(1)} %get-tuple-element.42), channel_id=1, source_target_pairs={{0,8},{8,0},{16,24},{24,16},{1,9},{9,1},{17,25},{25,17},{2,10},{10... | collective-permute-start | bytes 688136 | tf_op jit(solution)/shard_map/ppermute | solution.py:56
  50.9 4.0 %collective-permute-start.12 = (bf16[64,1792]{1,0:T(8,128)(2,1)S(1)}, bf16[64,1792]{1,0:T(8,128)(2,1)S(1)}, u32[]{:S(2)}, u32[]{:S(2)}) collective-permute-start(bf16[64,1792]{1,0:T(8,128)(2,1)S(1)} %get-tuple-element.36), channel_id=1, source_target_pairs={{0,8},{8,0},{16,24},{24,16},{1,9},{9,1},{17,25},{25,17},{2,10},{10... | collective-permute-start | bytes 688136 | tf_op jit(solution)/shard_map/ppermute | solution.py:56
  51.4 8.5 %collective-permute-start.14 = (bf16[64,1792]{1,0:T(8,128)(2,1)S(1)}, bf16[64,1792]{1,0:T(8,128)(2,1)S(1)}, u32[]{:S(2)}, u32[]{:S(2)}) collective-permute-start(bf16[64,1792]{1,0:T(8,128)(2,1)S(1)} %add.12.refs_7_), channel_id=1, source_target_pairs={{0,16},{8,24},{16,0},{24,8},{1,17},{9,25},{17,1},{25,9},{2,18},{10... | collective-permute-start | bytes 688136 | tf_op jit(solution)/shard_map/ppermute | solution.py:56
  52.8 7.3 %collective-permute-start.18 = (bf16[64,1792]{1,0:T(8,128)(2,1)S(1)}, bf16[64,1792]{1,0:T(8,128)(2,1)S(1)}, u32[]{:S(2)}, u32[]{:S(2)}) collective-permute-start(bf16[64,1792]{1,0:T(8,128)(2,1)S(1)} %get-tuple-element.46), channel_id=1, source_target_pairs={{0,8},{8,0},{16,24},{24,16},{1,9},{9,1},{17,25},{25,17},{2,10},{10... | collective-permute-start | bytes 688136 | tf_op jit(solution)/shard_map/ppermute | solution.py:56
  52.8 9.5 %collective-permute-start.20 = (bf16[32,1792]{1,0:T(8,128)(2,1)S(1)}, bf16[32,1792]{1,0:T(8,128)(2,1)S(1)}, u32[]{:S(2)}, u32[]{:S(2)}) collective-permute-start(bf16[32,1792]{1,0:T(8,128)(2,1)S(1)} %get-tuple-element.47), channel_id=1, source_target_pairs={{0,16},{8,24},{16,0},{24,8},{1,17},{9,25},{17,1},{25,9},{2,18},{10... | collective-permute-start | bytes 344072 | tf_op jit(solution)/shard_map/ppermute | solution.py:56
  53.9 10.1 %collective-permute-start.19 = (bf16[32,1792]{1,0:T(8,128)(2,1)S(1)}, bf16[32,1792]{1,0:T(8,128)(2,1)S(1)}, u32[]{:S(2)}, u32[]{:S(2)}) collective-permute-start(bf16[32,1792]{1,0:T(8,128)(2,1)S(1)} %get-tuple-element.43.refs_3_), channel_id=1, source_target_pairs={{0,16},{8,24},{16,0},{24,8},{1,17},{9,25},{17,1},{25,9},{2,18},{10... | collective-permute-start | bytes 344072 | tf_op jit(solution)/shard_map/ppermute | solution.py:56
  60.0 6.3 %collective-permute-start.17 = (bf16[32,1792]{1,0:T(8,128)(2,1)S(1)}, bf16[32,1792]{1,0:T(8,128)(2,1)S(1)}, u32[]{:S(2)}, u32[]{:S(2)}) collective-permute-start(bf16[32,1792]{1,0:T(8,128)(2,1)S(1)} %get-tuple-element.45), channel_id=1, source_target_pairs={{0,4},{2,6},{4,0},{6,2},{1,5},{3,7},{5,1},{7,3},{8,12},{10,14},{12... | collective-permute-start | bytes 344072 | tf_op jit(solution)/shard_map/ppermute | solution.py:56
  66.3 4.2 %collective-permute-start.21 = (bf16[16,1792]{1,0:T(8,128)(2,1)S(1)}, bf16[16,1792]{1,0:T(8,128)(2,1)S(1)}, u32[]{:S(2)}, u32[]{:S(2)}) collective-permute-start(bf16[16,1792]{1,0:T(8,128)(2,1)S(1)} %get-tuple-element.51), channel_id=1, source_target_pairs={{0,2},{2,0},{4,6},{6,4},{1,3},{3,1},{5,7},{7,5},{8,10},{10,8},{12,... | collective-permute-start | bytes 172040 | tf_op jit(solution)/shard_map/ppermute | solution.py:56
  66.4 5.4 %collective-permute-start.24 = (bf16[16,1792]{1,0:T(8,128)(2,1)S(1)}, bf16[16,1792]{1,0:T(8,128)(2,1)S(1)}, u32[]{:S(2)}, u32[]{:S(2)}) collective-permute-start(bf16[16,1792]{1,0:T(8,128)(2,1)S(1)} %get-tuple-element.53), channel_id=1, source_target_pairs={{0,2},{2,0},{4,6},{6,4},{1,3},{3,1},{5,7},{7,5},{8,10},{10,8},{12,... | collective-permute-start | bytes 172040 | tf_op jit(solution)/shard_map/ppermute | solution.py:56
  68.4 6.0 %collective-permute-start.22 = (bf16[16,1792]{1,0:T(8,128)(2,1)S(1)}, bf16[16,1792]{1,0:T(8,128)(2,1)S(1)}, u32[]{:S(2)}, u32[]{:S(2)}) collective-permute-start(bf16[16,1792]{1,0:T(8,128)(2,1)S(1)} %get-tuple-element.52), channel_id=1, source_target_pairs={{0,6},{2,4},{4,2},{6,0},{1,7},{3,5},{5,3},{7,1},{8,14},{10,12},{12... | collective-permute-start | bytes 172040 | tf_op jit(solution)/shard_map/ppermute | solution.py:56
  70.1 5.5 %collective-permute-start.23 = (bf16[16,1792]{1,0:T(8,128)(2,1)S(1)}, bf16[16,1792]{1,0:T(8,128)(2,1)S(1)}, u32[]{:S(2)}, u32[]{:S(2)}) collective-permute-start(bf16[16,1792]{1,0:T(8,128)(2,1)S(1)} %get-tuple-element.48.refs_3_), channel_id=1, source_target_pairs={{0,4},{2,6},{4,0},{6,2},{1,5},{3,7},{5,1},{7,3},{8,12},{10,14},{12... | collective-permute-start | bytes 172040 | tf_op jit(solution)/shard_map/ppermute | solution.py:56
  (7 other events, 46.1 us)

commit v8 on v7

--- a/solution.py
+++ b/solution.py
@@ -126,24 +126,20 @@
     return call("copied", copy_body, [(source.shape, source.dtype)], [source, after], 1 << 31)[0]
 
 
-def exchange(own):
-    count = lax.axis_size("ingroup")
-    return [own] + [swap(own, "ingroup", j) for j in range(1, count)]
-
-
 def spread(own, cotangent):
-    outer = bits_of("group")
-    blocks = exchange(own)
-    half = len(blocks) // 2
-    early, second = pack(blocks[:half], passed=[copied(cotangent, own)])
-    second = exchange(second)
-    late = pack(blocks[half:])
+    outer, count = bits_of("group"), lax.axis_size("ingroup")
+    blocks = [own] + [swap(own, "ingroup", j) for j in range(1, count)]
+    early, second = pack(blocks[: count // 2], passed=[copied(cotangent, own)])
+    late = pack(blocks[count // 2 :])
     across = swap(early, "group", outer[0])
     last = swap(late, "group", outer[0])
-    first = pack([early, late, across, last], second)
+    for bit in bits_of("ingroup")[:0:-1]:
+        second = pack([second, swap(second, "ingroup", bit)])
+    first = pack([early, late, across, last], [second])
     for bit in outer[1:-1]:
         first = pack([first, swap(first, "group", bit)])
-    return [first, swap(first, "group", outer[-1])], second
+    first = [first, swap(first, "group", outer[-1])]
+    return first, [second, swap(second, "ingroup", bits_of("ingroup")[0])]
 
 
 def spread_end(parts, after):
@@ -228,31 +224,54 @@
 
 
 def out_body(peers, *refs):
-    scale, place, weight, _, *outs = refs[1 + peers :]
-    gate_pre, up_pre = forward_sums(refs[0], refs[1 : 1 + peers])
-    hidden = (gate_pre / (1.0 + jnp.exp(-gate_pre)) * up_pre).astype(BF16)
-    rows = (dot(hidden, weight[...]) * scale[:, :1]).astype(BF16)
-    place_rows(place[...], rows, *outs)
-
-
-def factor_body(peers, *refs):
-    scale, gate_out, up_out = refs[1 + peers :]
+    scale, place, weight, _, gate_out, up_out, *outs = refs[1 + peers :]
     gate_pre, up_pre = forward_sums(refs[0], refs[1 : 1 + peers])
     sigmoid = 1.0 / (1.0 + jnp.exp(-gate_pre))
+    silu = gate_pre * sigmoid
+    rows = (dot((silu * up_pre).astype(BF16), weight[...]) * scale[:, :1]).astype(BF16)
+    place_rows(place[...], rows, *outs)
     scaled = sigmoid * scale[:, :1]
     gate_out[...] = up_pre * scaled * (1.0 + gate_pre * (1.0 - sigmoid))
-    up_out[...] = gate_pre * scaled
+    up_out[...] = silu * scale[:, :1]
 
 
 def grad_body(peers, *refs):
     gate_factor, up_factor, back = refs[:3]
-    back_in = refs[3 : 3 + peers]
-    place, gate_weight, up_weight, _, *outs = refs[3 + peers :]
-    d_hidden = summed(back, back_in)
+    gate_weight, up_weight, _, rows_out = refs[3 + peers :]
+    d_hidden = summed(back, refs[3 : 3 + peers])
     d_gate = (d_hidden * gate_factor[...]).astype(BF16)
     d_up = (d_hidden * up_factor[...]).astype(BF16)
-    rows = (dot(d_gate, gate_weight[...], 1, 1) + dot(d_up, up_weight[...], 1, 1)).astype(BF16)
-    place_rows(place[...], rows, *outs)
+    rows_out[...] = (
+        dot(d_gate, gate_weight[...], 1, 1) + dot(d_up, up_weight[...], 1, 1)
+    ).astype(BF16)
+
+
+def place_body(place, rows, keep, stay, received, near_out, go_out, stay_out, keep_out, far_out):
+    place_rows(place[...], rows[...], near_out, go_out, stay_out)
+    half = keep_out.shape[0]
+    total = keep[: 2 * half] + stay[...].astype(F32) + received[...].astype(F32)
+    keep_out[...] = total[:half]
+    far_out[...] = total[half:].astype(BF16)
+
+
+def join_body(near, stay, last, keep, got, own_out, mixed_out, pair_out, *away_outs):
+    block = own_out.shape[0]
+    rows = last.shape[0]
+    total = near[:rows] + stay[:rows].astype(F32) + last[...].astype(F32)
+    mixed = keep[...] + got[...].astype(F32)
+    own_out[...] = total[:block]
+    mixed_out[...] = mixed[:block]
+    pair_out[:block] = mixed[block:].astype(BF16)
+    pair_out[block:] = total[block : 2 * block].astype(BF16)
+    for i, out in enumerate(away_outs):
+        out[...] = total[(2 + i) * block : (3 + i) * block].astype(BF16)
+
+
+def final_body(count, mixed, grad, pair, *refs):
+    block = mixed.shape[0]
+    mixed_out, grad_out = refs[count:]
+    mixed_out[...] = (mixed[...] + pair[:block].astype(F32)).astype(BF16)
+    grad_out[...] = (summed(grad, refs[:count]) + pair[block:].astype(F32)).astype(BF16)
 
 
 def add_body(count, after, at, parts, keep, *refs):
@@ -267,6 +286,13 @@
         start += out.shape[0]
 
 
+def far_body(keep, low, high, out):
+    half = out.shape[0]
+    middle = low.shape[0]
+    out[:middle] = (keep[half : half + middle] + low[...].astype(F32)).astype(BF16)
+    out[middle:] = (keep[half + middle :] + high[...].astype(F32)).astype(BF16)
+
+
 def add(keep, at, received, outs, after=()):
     return call(
         "add",
@@ -286,30 +312,6 @@
         pieces = add(near, half, [(got, half)], outs)[::-1]
         (near,) = add(near, 0, [(got, 0)], [(half, F32)])
     return near, *[swap(piece, "group", bits_of("group")[1]) for piece in pieces]
-
-
-def collect_few(near, far, got_stay, ties):
-    half = near.shape[0] // 2
-    received = [(got_stay, 0), (swap(far, "group", bits_of("group")[0]), 0)]
-    for i, bit in enumerate(bits_of("ingroup")):
-        half //= 2
-        near, far = add(near, 0, received, [(half, F32), (half, BF16)], ties[i : i + 1])
-        received = [(swap(far, "ingroup", bit), 0)]
-    return add(near, 0, received, [(half, BF16)])[0]
-
-
-def collect_soon(near, got_go, got_stay):
-    count, bit = lax.axis_size("ingroup"), bits_of("group")[0]
-    half = near.shape[0] // 2
-    quarter, block = half // 2, half // count
-    low, high = add(near, half, [(got_go, 0)], [(quarter, BF16)] * 2)
-    across, last = swap(high, "group", bit), swap(low, "group", bit)
-    away = add(near, quarter, [(got_stay, quarter), (across, 0)], [(block, BF16)] * (count // 2))
-    sent = [swap(away[j], "ingroup", count // 2 + j) for j in range(count // 2)[::-1]]
-    outs = [(block, F32)] + [(block, BF16)] * (count // 2 - 1)
-    own, *away = add(near, 0, [(got_stay, 0), (last, 0)], outs, away[:1])
-    sent += [swap(away[j], "ingroup", 1 + j) for j in range(count // 2 - 1)[::-1]]
-    return add(own, 0, [(s, 0) for s in sent], [(block, BF16)])[0], [low, own]
 
 
 def from_peers(sent):
@@ -362,35 +364,61 @@
     )
     back_in = from_peers(back_sent)
     near = ((total // 2, features), F32)
-    fourth = ((total // 4, features), BF16)
-    near_y, got_go, got_y = collect_start(
-        *call(
-            "out",
-            functools.partial(out_body, peers),
-            [near, fourth, fourth],
-            [both] + both_in + [scale, place, w_down, back_sent],
-            product,
-        )
-    )
-    (far,) = add(near_y, near_y.shape[0] // 2, [(got_go, 0)], [(near_y.shape[0] // 2, BF16)])
-    factors = call(
-        "factor",
-        functools.partial(factor_body, peers),
-        [((slots, hidden), F32)] * 2,
-        [both] + both_in + [scale],
-    )
-    near_dx, got_go, got_dx = collect_start(
-        *call(
-            "grad",
-            functools.partial(grad_body, peers),
-            [near, fourth, fourth],
-            list(factors) + [back] + back_in + [place, w_gate, w_up, far],
-            2 * product,
-            24,
-        )
-    )
-    grad, ties = collect_soon(near_dx, got_go, got_dx)
-    return collect_few(near_y, far, got_y, ties), grad
+    fourth, eighth = ((total // 4, features), BF16), ((total // 8, features), BF16)
+    gate_factor, up_factor, *placed = call(
+        "out",
+        functools.partial(out_body, peers),
+        [((slots, hidden), F32)] * 2 + [near, eighth, eighth, fourth],
+        [both] + both_in + [scale, place, w_down, back_sent],
+        product,
+    )
+    near_y, got_high, got_low, got_y = collect_start(*placed)
+    half = near_y.shape[0] // 2
+    (far,) = call(
+        "add",
+        far_body,
+        [((half, features), BF16)],
+        [near_y, got_low, got_high],
+    )
+    (rows,) = call(
+        "grad",
+        functools.partial(grad_body, peers),
+        [((slots, features), BF16)],
+        [gate_factor, up_factor, back] + back_in + [w_gate, w_up, far],
+        2 * product,
+        24,
+    )
+    axis, bits = "ingroup", bits_of("ingroup")
+    count, across_bit = lax.axis_size("ingroup"), bits_of("group")[0]
+    near_dx, go, stay, keep, far = call(
+        "place",
+        place_body,
+        [near, fourth, fourth] + [((half // 2, features), t) for t in (F32, BF16)],
+        [place, rows, near_y, got_y, swap(far, "group", across_bit)],
+    )
+    near_dx, got_go, got_dx = collect_start(near_dx, go, stay)
+    got = swap(far, axis, bits[0])
+    for bit in bits[1:-1]:
+        outs = [(keep.shape[0] // 2, t) for t in (F32, BF16)]
+        keep, far = add(keep, 0, [(got, 0)], outs)
+        got = swap(far, axis, bit)
+    (far,) = add(near_dx, half, [(got_go, 0)], [(half, BF16)])
+    own_dx, own_y, pair, *away = call(
+        "join",
+        join_body,
+        [((block, features), F32)] * 2
+        + [((2 * block, features), BF16)]
+        + [((block, features), BF16)] * (count - 2),
+        [near_dx, got_dx, swap(far, "group", across_bit), keep, got],
+    )
+    sent = [swap(part, axis, 2 + j) for j, part in enumerate(away)]
+    outs = [((block, features), BF16)] * 2
+    return call(
+        "final",
+        functools.partial(final_body, len(sent)),
+        outs,
+        [own_y, own_dx, swap(pair, axis, 1)] + sent,
+    )
 
 
 def solution(mesh):

time: 76.5 us -> 75.3 us (0.984)
  waiting for transfers between devices: 36.6 us -> 38.2 us
  starting transfers between devices: 25.3 us -> 23.8 us
  Pallas kernels: 11 us -> 9.65 us
    ppermute x23 -> x21, waiting for transfers between devices: 31.7 us -> 35.5 us  [swap(): lax.ppermute(value, axis, [(i, i ^ offset) for i in range(lax.axis_size(a...]
    ppermute x2, waiting for transfers between devices: 4.93 us -> 2.74 us  [from_peers(): lax.ppermute(sent, 'dp', [(i, (i + step) % count) for i in range(count)])]
    ppermute x23 -> x21, starting transfers between devices: 22.3 us -> 20.7 us  [swap(): lax.ppermute(value, axis, [(i, i ^ offset) for i in range(lax.axis_size(a...]
    pallas_call x20 -> x17, Pallas kernels: 11 us -> 9.65 us  [call(): return kernel(*args, *passed)]
  transfers between devices with their start and end apart: 25 -> 23, of which waited for: 17 -> 15; matrix products, arithmetic and copies ran while one was open for 0% -> 0% of each run, Pallas kernels for 5% -> 9%
where the time goes in v8:
time: 75.3 us; the launch traced here: 75 us
  waiting for transfers between devices  38.2 us (51%)
  starting transfers between devices  23.8 us (32%)
  Pallas kernels  9.65 us (13%)
  local copies, waits for them, and re-layouts  2.52 us (3%)
  between operations  0.83 us (1%)
    ppermute x21, waiting for transfers between devices, swap(): lax.ppermute(value, axis, [(i, i ^ offset) for i in range(lax.axis_size(a...  35.5 us
    ppermute x21, starting transfers between devices, swap(): lax.ppermute(value, axis, [(i, i ^ offset) for i in range(lax.axis_size(a...  20.7 us
    pallas_call x17, Pallas kernels, call(): return kernel(*args, *passed)  9.65 us
    ppermute x2, starting transfers between devices, from_peers(): lax.ppermute(sent, 'dp', [(i, (i + step) % count) for i in range(count)])  3.04 us
    ppermute x2, waiting for transfers between devices, from_peers(): lax.ppermute(sent, 'dp', [(i, (i + step) % count) for i in range(count)])  2.74 us
    unnamed x12, local copies, waits for them, and re-layouts  2.52 us
  transfers between devices with their start and end apart: 23, of which 15 were waited for; matrix products, arithmetic and copies ran while one was open for 0% of the time, Pallas kernels for 9%

profile of v8, /device:TPU:0, one launch (start us, length us, event | category | flops | bytes accessed | tf_op | source)
XLA Modules:
  0.0 75.0 jit_solution(16000177041718161561)
XLA Ops:
  0.6 1.5 %payload.1.refs_1_.refs_0_ = bf16[16,1920]{1,0:T(8,128)(2,1)} custom-call(s32[1]{0:T(128)} %bitcast.refs_0_, bf16[16,1792]{1,0:T(8,128)(2,1)} %refs_1_.1, s32[8,16]{1,0:T(8,128)} %bitcast.12, s32[8,16]{1,0:T(8,128)} %bitcast.13), custom_call_target="tpu_custom_call" | custom-call | bytes 119812 | tf_op jit(solution)/shard_map/payload/payload/pallas_call | solution.py:52
  2.1 3.1 %collective-permute-start = (bf16[16,1920]{1,0:T(8,128)(2,1)}, bf16[16,1920]{1,0:T(8,128)(2,1)S(1)}, u32[]{:S(2)}, u32[]{:S(2)}) collective-permute-start(bf16[16,1920]{1,0:T(8,128)(2,1)} %payload.1.refs_1_.refs_0_), channel_id=1, source_target_pairs={{0,2},{2,0},{4,6},{6,4},{1,3},{3,1},{5,7},{7,5},{8,10},{10,8},{12,... | collective-permute-start | bytes 184328 | tf_op jit(solution)/shard_map/ppermute | solution.py:56
  5.2 2.6 %collective-permute-start.1 = (bf16[16,1920]{1,0:T(8,128)(2,1)}, bf16[16,1920]{1,0:T(8,128)(2,1)S(1)}, u32[]{:S(2)}, u32[]{:S(2)}) collective-permute-start(bf16[16,1920]{1,0:T(8,128)(2,1)} %payload.1.refs_1_.refs_0_), channel_id=1, source_target_pairs={{0,4},{2,6},{4,0},{6,2},{1,5},{3,7},{5,1},{7,3},{8,12},{10,14},{12... | collective-permute-start | bytes 184328 | tf_op jit(solution)/shard_map/ppermute | solution.py:56
  10.4 1.8 %collective-permute-start.3 = (bf16[32,1920]{1,0:T(8,128)(2,1)S(1)}, bf16[32,1920]{1,0:T(8,128)(2,1)S(1)}, u32[]{:S(2)}, u32[]{:S(2)}) collective-permute-start(bf16[32,1920]{1,0:T(8,128)(2,1)S(1)} %get-tuple-element.26.refs_0_), channel_id=1, source_target_pairs={{0,16},{8,24},{16,0},{24,8},{1,17},{9,25},{17,1},{25,9},{2,18},{10... | collective-permute-start | bytes 368648 | tf_op jit(solution)/shard_map/ppermute | solution.py:56
  12.2 1.9 %collective-permute-done.2.refs_1_ = bf16[16,1920]{1,0:T(8,128)(2,1)S(1)} collective-permute-done((bf16[16,1920]{1,0:T(8,128)(2,1)}, bf16[16,1920]{1,0:T(8,128)(2,1)S(1)}, u32[]{:S(2)}, u32[]{:S(2)}) %collective-permute-start.2) | collective-permute-done | bytes 61472 | tf_op jit(solution)/shard_map/ppermute | solution.py:56
  14.1 1.6 %collective-permute-start.4 = (bf16[32,1920]{1,0:T(8,128)(2,1)S(1)}, bf16[32,1920]{1,0:T(8,128)(2,1)S(1)}, u32[]{:S(2)}, u32[]{:S(2)}) collective-permute-start(bf16[32,1920]{1,0:T(8,128)(2,1)S(1)} %pack.7.refs_1_), channel_id=1, source_target_pairs={{0,16},{8,24},{16,0},{24,8},{1,17},{9,25},{17,1},{25,9},{2,18},{10... | collective-permute-start | bytes 368648 | tf_op jit(solution)/shard_map/ppermute | solution.py:56
  15.7 4.2 %collective-permute-done.5.refs_1_ = bf16[16,1792]{1,0:T(8,128)(2,1)S(1)} collective-permute-done((bf16[16,1792]{1,0:T(8,128)(2,1)S(1)}, bf16[16,1792]{1,0:T(8,128)(2,1)S(1)}, u32[]{:S(2)}, u32[]{:S(2)}) %collective-permute-start.5) | collective-permute-done | bytes 57376 | tf_op jit(solution)/shard_map/ppermute | solution.py:56
  20.0 1.3 %collective-permute-start.8 = (bf16[32,1792]{1,0:T(8,128)(2,1)S(1)}, bf16[32,1792]{1,0:T(8,128)(2,1)S(1)}, u32[]{:S(2)}, u32[]{:S(2)}) collective-permute-start(bf16[32,1792]{1,0:T(8,128)(2,1)S(1)} %pack.8.refs_4_.refs_0_), channel_id=1, source_target_pairs={{0,4},{2,6},{4,0},{6,2},{1,5},{3,7},{5,1},{7,3},{8,12},{10,14},{12... | collective-permute-start | bytes 344072 | tf_op jit(solution)/shard_map/ppermute | solution.py:56
  21.8 1.8 %forward.1 = (bf16[256,128]{1,0:T(8,128)(2,1)S(1)}, f32[128,128]{1,0:T(8,128)S(1)}, f32[256,1024]{1,0:T(8,128)S(1)}, bf16[256,1024]{1,0:T(8,128)(2,1)S(1)}) custom-call(s32[1]{0:T(128)} %bitcast.refs_0_, bf16[128,1920]{1,0:T(8,128)(2,1)S(1)} %pack.9.refs_1_, bf16[128,1920]{1,0:T(8,128)(2,1)S(1)} %collective-permute-done.6.refs_2_, ...), custom_call_target="tpu_custom_call" | custom-call | flops 939524096 | bytes 10027012 | tf_op jit(solution)/shard_map/forward/forward/pallas_call | solution.py:52
  23.7 4.7 %collective-permute-done.8.refs_1_ = bf16[32,1792]{1,0:T(8,128)(2,1)S(1)} collective-permute-done((bf16[32,1792]{1,0:T(8,128)(2,1)S(1)}, bf16[32,1792]{1,0:T(8,128)(2,1)S(1)}, u32[]{:S(2)}, u32[]{:S(2)}) %collective-permute-start.8) | collective-permute-done | bytes 114720 | tf_op jit(solution)/shard_map/ppermute | solution.py:56
  29.1 1.5 %collective-permute-start.7 = (bf16[256,1024]{1,0:T(8,128)(2,1)S(1)}, bf16[256,1024]{1,0:T(8,128)(2,1)S(1)}, u32[]{:S(2)}, u32[]{:S(2)}) collective-permute-start(bf16[256,1024]{1,0:T(8,128)(2,1)S(1)} %get-tuple-element.30.refs_2_), channel_id=1, source_target_pairs={{0,1},{1,0},{2,3},{3,2},{4,5},{5,4},{6,7},{7,6},{8,9},{9,8},{10,11... | collective-permute-start | bytes 1572872 | tf_op jit(solution)/shard_map/ppermute | solution.py:320
  30.6 5.4 %collective-permute-done.9.refs_1_ = bf16[64,1792]{1,0:T(8,128)(2,1)S(1)} collective-permute-done((bf16[64,1792]{1,0:T(8,128)(2,1)S(1)}, bf16[64,1792]{1,0:T(8,128)(2,1)S(1)}, u32[]{:S(2)}, u32[]{:S(2)}) %collective-permute-start.9) | collective-permute-done | bytes 229408 | tf_op jit(solution)/shard_map/ppermute | solution.py:56
  36.1 1.8 %collective-permute-done.10.refs_1_ = bf16[128,1792]{1,0:T(8,128)(2,1)S(1)} collective-permute-done((bf16[128,1792]{1,0:T(8,128)(2,1)S(1)}, bf16[128,1792]{1,0:T(8,128)(2,1)S(1)}, u32[]{:S(2)}, u32[]{:S(2)}) %collective-permute-start.10) | collective-permute-done | bytes 458784 | tf_op jit(solution)/shard_map/ppermute | solution.py:56
  37.9 1.3 %back.1 = (f32[128,1024]{1,0:T(8,128)S(1)}, bf16[128,1024]{1,0:T(8,128)(2,1)S(1)}) custom-call(bf16[128,1792]{1,0:T(8,128)(2,1)S(1)} %pack.11.refs_0_, bf16[128,1792]{1,0:T(8,128)(2,1)S(1)} %collective-permute-done.10.refs_1_, bf16[256,128]{1,0:T(8,128)(2,1)S(1)} %get-tuple-element.28.refs_2_.refs_3_.refs_0_, bf16[1024,1792]{1,0:T(8,128)(2,1)S(1)} %bitcast.6), custom_call_target="tpu_custom_call" | custom-call | flops 469762048 | bytes 5439488 | tf_op jit(solution)/shard_map/back/back/pallas_call | solution.py:52
  39.2 1.6 %collective-permute-start.11 = (bf16[128,1024]{1,0:T(8,128)(2,1)S(1)}, bf16[128,1024]{1,0:T(8,128)(2,1)S(1)}, u32[]{:S(2)}, u32[]{:S(2)}) collective-permute-start(bf16[128,1024]{1,0:T(8,128)(2,1)S(1)} %get-tuple-element.32.refs_5_), channel_id=1, source_target_pairs={{0,1},{1,0},{2,3},{3,2},{4,5},{5,4},{6,7},{7,6},{8,9},{9,8},{10,11... | collective-permute-start | bytes 786440 | tf_op jit(solution)/shard_map/ppermute | solution.py:320
  40.8 2.5 %collective-permute-done.7.refs_1_ = bf16[256,1024]{1,0:T(8,128)(2,1)S(1)} collective-permute-done((bf16[256,1024]{1,0:T(8,128)(2,1)S(1)}, bf16[256,1024]{1,0:T(8,128)(2,1)S(1)}, u32[]{:S(2)}, u32[]{:S(2)}) %collective-permute-start.7) | collective-permute-done | bytes 524320 | tf_op jit(solution)/shard_map/ppermute | solution.py:320
  46.1 2.0 %collective-permute-start.15 = (bf16[64,1792]{1,0:T(8,128)(2,1)S(1)}, bf16[64,1792]{1,0:T(8,128)(2,1)S(1)}, u32[]{:S(2)}, u32[]{:S(2)}) collective-permute-start(bf16[64,1792]{1,0:T(8,128)(2,1)S(1)} %add.6.refs_6_), channel_id=1, source_target_pairs={{0,16},{8,24},{16,0},{24,8},{1,17},{9,25},{17,1},{25,9},{2,18},{10... | collective-permute-start | bytes 688136 | tf_op jit(solution)/shard_map/ppermute | solution.py:56
  48.3 2.5 %grad.1.refs_1_ = bf16[128,1792]{1,0:T(8,128)(2,1)S(1)} custom-call(f32[128,1024]{1,0:T(8,128)S(1)} %get-tuple-element.33.refs_0_, f32[128,1024]{1,0:T(8,128)S(1)} %get-tuple-element.34.refs_1_, f32[128,1024]{1,0:T(8,128)S(1)} %get-tuple-element.35.refs_2_, bf16[128,1024]{1,0:T(8,128)(2,1)S(1)} %collective-permute-done.11.refs_3_, ...), custom_call_target="tpu_custom_call" | custom-call | flops 939524096 | bytes 9863168 | tf_op jit(solution)/shard_map/grad/grad/pallas_call | solution.py:52
  50.8 3.4 %collective-permute-done.15.refs_4_ = bf16[64,1792]{1,0:T(8,128)(2,1)S(1)} collective-permute-done((bf16[64,1792]{1,0:T(8,128)(2,1)S(1)}, bf16[64,1792]{1,0:T(8,128)(2,1)S(1)}, u32[]{:S(2)}, u32[]{:S(2)}) %collective-permute-start.15) | collective-permute-done | bytes 229408 | tf_op jit(solution)/shard_map/ppermute | solution.py:56
  56.3 1.8 %collective-permute-start.18 = (bf16[64,1792]{1,0:T(8,128)(2,1)S(1)}, bf16[64,1792]{1,0:T(8,128)(2,1)S(1)}, u32[]{:S(2)}, u32[]{:S(2)}) collective-permute-start(bf16[64,1792]{1,0:T(8,128)(2,1)S(1)} %add.7), channel_id=1, source_target_pairs={{0,16},{8,24},{16,0},{24,8},{1,17},{9,25},{17,1},{25,9},{2,18},{10... | collective-permute-start | bytes 688136 | tf_op jit(solution)/shard_map/ppermute | solution.py:56
  58.1 7.3 %collective-permute-done.19.refs_4_ = bf16[32,1792]{1,0:T(8,128)(2,1)S(1)} collective-permute-done((bf16[32,1792]{1,0:T(8,128)(2,1)S(1)}, bf16[32,1792]{1,0:T(8,128)(2,1)S(1)}, u32[]{:S(2)}, u32[]{:S(2)}) %collective-permute-start.19) | collective-permute-done | bytes 114720 | tf_op jit(solution)/shard_map/ppermute | solution.py:56
  65.5 2.7 %collective-permute-start.21 = (bf16[16,1792]{1,0:T(8,128)(2,1)S(1)}, bf16[16,1792]{1,0:T(8,128)(2,1)S(1)}, u32[]{:S(2)}, u32[]{:S(2)}) collective-permute-start(bf16[16,1792]{1,0:T(8,128)(2,1)S(1)} %get-tuple-element.48), channel_id=1, source_target_pairs={{0,4},{2,6},{4,0},{6,2},{1,5},{3,7},{5,1},{7,3},{8,12},{10,14},{12... | collective-permute-start | bytes 172040 | tf_op jit(solution)/shard_map/ppermute | solution.py:56
  68.3 1.7 %collective-permute-start.22 = (bf16[16,1792]{1,0:T(8,128)(2,1)S(1)}, bf16[16,1792]{1,0:T(8,128)(2,1)S(1)}, u32[]{:S(2)}, u32[]{:S(2)}) collective-permute-start(bf16[16,1792]{1,0:T(8,128)(2,1)S(1)} %get-tuple-element.49), channel_id=1, source_target_pairs={{0,6},{2,4},{4,2},{6,0},{1,7},{3,5},{5,3},{7,1},{8,14},{10,12},{12... | collective-permute-start | bytes 172040 | tf_op jit(solution)/shard_map/ppermute | solution.py:56
  69.9 3.2 %collective-permute-done.21.refs_3_ = bf16[16,1792]{1,0:T(8,128)(2,1)S(1)} collective-permute-done((bf16[16,1792]{1,0:T(8,128)(2,1)S(1)}, bf16[16,1792]{1,0:T(8,128)(2,1)S(1)}, u32[]{:S(2)}, u32[]{:S(2)}) %collective-permute-start.21) | collective-permute-done | bytes 57376 | tf_op jit(solution)/shard_map/ppermute | solution.py:56
  (51 shorter events, 11.1 us)
Async XLA Ops:
  2.1 7.4 %collective-permute-start = (bf16[16,1920]{1,0:T(8,128)(2,1)}, bf16[16,1920]{1,0:T(8,128)(2,1)S(1)}, u32[]{:S(2)}, u32[]{:S(2)}) collective-permute-start(bf16[16,1920]{1,0:T(8,128)(2,1)} %payload.1.refs_1_.refs_0_), channel_id=1, source_target_pairs={{0,2},{2,0},{4,6},{6,4},{1,3},{3,1},{5,7},{7,5},{8,10},{10,8},{12,... | collective-permute-start | bytes 184328 | tf_op jit(solution)/shard_map/ppermute | solution.py:56
  5.2 6.9 %collective-permute-start.1 = (bf16[16,1920]{1,0:T(8,128)(2,1)}, bf16[16,1920]{1,0:T(8,128)(2,1)S(1)}, u32[]{:S(2)}, u32[]{:S(2)}) collective-permute-start(bf16[16,1920]{1,0:T(8,128)(2,1)} %payload.1.refs_1_.refs_0_), channel_id=1, source_target_pairs={{0,4},{2,6},{4,0},{6,2},{1,5},{3,7},{5,1},{7,3},{8,12},{10,14},{12... | collective-permute-start | bytes 184328 | tf_op jit(solution)/shard_map/ppermute | solution.py:56
  7.8 6.2 %collective-permute-start.2 = (bf16[16,1920]{1,0:T(8,128)(2,1)}, bf16[16,1920]{1,0:T(8,128)(2,1)S(1)}, u32[]{:S(2)}, u32[]{:S(2)}) collective-permute-start(bf16[16,1920]{1,0:T(8,128)(2,1)} %payload.1.refs_1_.refs_0_), channel_id=1, source_target_pairs={{0,6},{2,4},{4,2},{6,0},{1,7},{3,5},{5,3},{7,1},{8,14},{10,12},{12... | collective-permute-start | bytes 184328 | tf_op jit(solution)/shard_map/ppermute | solution.py:56
  10.4 9.5 %collective-permute-start.3 = (bf16[32,1920]{1,0:T(8,128)(2,1)S(1)}, bf16[32,1920]{1,0:T(8,128)(2,1)S(1)}, u32[]{:S(2)}, u32[]{:S(2)}) collective-permute-start(bf16[32,1920]{1,0:T(8,128)(2,1)S(1)} %get-tuple-element.26.refs_0_), channel_id=1, source_target_pairs={{0,16},{8,24},{16,0},{24,8},{1,17},{9,25},{17,1},{25,9},{2,18},{10... | collective-permute-start | bytes 368648 | tf_op jit(solution)/shard_map/ppermute | solution.py:56
  14.1 5.8 %collective-permute-start.4 = (bf16[32,1920]{1,0:T(8,128)(2,1)S(1)}, bf16[32,1920]{1,0:T(8,128)(2,1)S(1)}, u32[]{:S(2)}, u32[]{:S(2)}) collective-permute-start(bf16[32,1920]{1,0:T(8,128)(2,1)S(1)} %pack.7.refs_1_), channel_id=1, source_target_pairs={{0,16},{8,24},{16,0},{24,8},{1,17},{9,25},{17,1},{25,9},{2,18},{10... | collective-permute-start | bytes 368648 | tf_op jit(solution)/shard_map/ppermute | solution.py:56
  15.7 4.2 %collective-permute-start.5 = (bf16[16,1792]{1,0:T(8,128)(2,1)S(1)}, bf16[16,1792]{1,0:T(8,128)(2,1)S(1)}, u32[]{:S(2)}, u32[]{:S(2)}) collective-permute-start(bf16[16,1792]{1,0:T(8,128)(2,1)S(1)} %get-tuple-element.27.refs_0_), channel_id=1, source_target_pairs={{0,2},{2,0},{4,6},{6,4},{1,3},{3,1},{5,7},{7,5},{8,10},{10,8},{12,... | collective-permute-start | bytes 172040 | tf_op jit(solution)/shard_map/ppermute | solution.py:56
  19.9 1.9 %collective-permute-start.6 = (bf16[128,1920]{1,0:T(8,128)(2,1)S(1)}, bf16[128,1920]{1,0:T(8,128)(2,1)S(1)}, u32[]{:S(2)}, u32[]{:S(2)}) collective-permute-start(bf16[128,1920]{1,0:T(8,128)(2,1)S(1)} %pack.9.refs_1_), channel_id=1, source_target_pairs={{0,8},{8,0},{16,24},{24,16},{1,9},{9,1},{17,25},{25,17},{2,10},{10... | collective-permute-start | bytes 1474568 | tf_op jit(solution)/shard_map/ppermute | solution.py:56
  20.0 8.4 %collective-permute-start.8 = (bf16[32,1792]{1,0:T(8,128)(2,1)S(1)}, bf16[32,1792]{1,0:T(8,128)(2,1)S(1)}, u32[]{:S(2)}, u32[]{:S(2)}) collective-permute-start(bf16[32,1792]{1,0:T(8,128)(2,1)S(1)} %pack.8.refs_4_.refs_0_), channel_id=1, source_target_pairs={{0,4},{2,6},{4,0},{6,2},{1,5},{3,7},{5,1},{7,3},{8,12},{10,14},{12... | collective-permute-start | bytes 344072 | tf_op jit(solution)/shard_map/ppermute | solution.py:56
  23.7 14.3 %copy-start = (bf16[1,1024,1792]{2,1,0:T(8,128)(2,1)S(1)}, bf16[1,1024,1792]{2,1,0:T(8,128)(2,1)}, u32[]{:S(2)}) copy-start(bf16[1,1024,1792]{2,1,0:T(8,128)(2,1)} %param.13) | copy-start | bytes 11010052
  28.4 7.6 %collective-permute-start.9 = (bf16[64,1792]{1,0:T(8,128)(2,1)S(1)}, bf16[64,1792]{1,0:T(8,128)(2,1)S(1)}, u32[]{:S(2)}, u32[]{:S(2)}) collective-permute-start(bf16[64,1792]{1,0:T(8,128)(2,1)S(1)} %pack.10.refs_0_), channel_id=1, source_target_pairs={{0,16},{8,24},{16,0},{24,8},{1,17},{9,25},{17,1},{25,9},{2,18},{10... | collective-permute-start | bytes 688136 | tf_op jit(solution)/shard_map/ppermute | solution.py:56
  29.1 14.2 %collective-permute-start.7 = (bf16[256,1024]{1,0:T(8,128)(2,1)S(1)}, bf16[256,1024]{1,0:T(8,128)(2,1)S(1)}, u32[]{:S(2)}, u32[]{:S(2)}) collective-permute-start(bf16[256,1024]{1,0:T(8,128)(2,1)S(1)} %get-tuple-element.30.refs_2_), channel_id=1, source_target_pairs={{0,1},{1,0},{2,3},{3,2},{4,5},{5,4},{6,7},{7,6},{8,9},{9,8},{10,11... | collective-permute-start | bytes 1572872 | tf_op jit(solution)/shard_map/ppermute | solution.py:320
  36.0 1.9 %collective-permute-start.10 = (bf16[128,1792]{1,0:T(8,128)(2,1)S(1)}, bf16[128,1792]{1,0:T(8,128)(2,1)S(1)}, u32[]{:S(2)}, u32[]{:S(2)}) collective-permute-start(bf16[128,1792]{1,0:T(8,128)(2,1)S(1)} %pack.11.refs_0_), channel_id=1, source_target_pairs={{0,8},{8,0},{16,24},{24,16},{1,9},{9,1},{17,25},{25,17},{2,10},{10... | collective-permute-start | bytes 1376264 | tf_op jit(solution)/shard_map/ppermute | solution.py:56
  39.2 9.1 %collective-permute-start.11 = (bf16[128,1024]{1,0:T(8,128)(2,1)S(1)}, bf16[128,1024]{1,0:T(8,128)(2,1)S(1)}, u32[]{:S(2)}, u32[]{:S(2)}) collective-permute-start(bf16[128,1024]{1,0:T(8,128)(2,1)S(1)} %get-tuple-element.32.refs_5_), channel_id=1, source_target_pairs={{0,1},{1,0},{2,3},{3,2},{4,5},{5,4},{6,7},{7,6},{8,9},{9,8},{10,11... | collective-permute-start | bytes 786440 | tf_op jit(solution)/shard_map/ppermute | solution.py:320
  44.5 1.4 %collective-permute-start.12 = (bf16[32,1792]{1,0:T(8,128)(2,1)S(1)}, bf16[32,1792]{1,0:T(8,128)(2,1)S(1)}, u32[]{:S(2)}, u32[]{:S(2)}) collective-permute-start(bf16[32,1792]{1,0:T(8,128)(2,1)S(1)} %get-tuple-element.37), channel_id=1, source_target_pairs={{0,8},{8,0},{16,24},{24,16},{1,9},{9,1},{17,25},{25,17},{2,10},{10... | collective-permute-start | bytes 344072 | tf_op jit(solution)/shard_map/ppermute | solution.py:56
  44.6 1.5 %collective-permute-start.13 = (bf16[32,1792]{1,0:T(8,128)(2,1)S(1)}, bf16[32,1792]{1,0:T(8,128)(2,1)S(1)}, u32[]{:S(2)}, u32[]{:S(2)}) collective-permute-start(bf16[32,1792]{1,0:T(8,128)(2,1)S(1)} %get-tuple-element.38), channel_id=1, source_target_pairs={{0,8},{8,0},{16,24},{24,16},{1,9},{9,1},{17,25},{25,17},{2,10},{10... | collective-permute-start | bytes 344072 | tf_op jit(solution)/shard_map/ppermute | solution.py:56
  45.1 5.8 %collective-permute-start.14 = (bf16[64,1792]{1,0:T(8,128)(2,1)S(1)}, bf16[64,1792]{1,0:T(8,128)(2,1)S(1)}, u32[]{:S(2)}, u32[]{:S(2)}) collective-permute-start(bf16[64,1792]{1,0:T(8,128)(2,1)S(1)} %get-tuple-element.39), channel_id=1, source_target_pairs={{0,8},{8,0},{16,24},{24,16},{1,9},{9,1},{17,25},{25,17},{2,10},{10... | collective-permute-start | bytes 688136 | tf_op jit(solution)/shard_map/ppermute | solution.py:56
  46.1 8.1 %collective-permute-start.15 = (bf16[64,1792]{1,0:T(8,128)(2,1)S(1)}, bf16[64,1792]{1,0:T(8,128)(2,1)S(1)}, u32[]{:S(2)}, u32[]{:S(2)}) collective-permute-start(bf16[64,1792]{1,0:T(8,128)(2,1)S(1)} %add.6.refs_6_), channel_id=1, source_target_pairs={{0,16},{8,24},{16,0},{24,8},{1,17},{9,25},{17,1},{25,9},{2,18},{10... | collective-permute-start | bytes 688136 | tf_op jit(solution)/shard_map/ppermute | solution.py:56
  54.7 1.6 %collective-permute-start.17 = (bf16[64,1792]{1,0:T(8,128)(2,1)S(1)}, bf16[64,1792]{1,0:T(8,128)(2,1)S(1)}, u32[]{:S(2)}, u32[]{:S(2)}) collective-permute-start(bf16[64,1792]{1,0:T(8,128)(2,1)S(1)} %get-tuple-element.42), channel_id=1, source_target_pairs={{0,8},{8,0},{16,24},{24,16},{1,9},{9,1},{17,25},{25,17},{2,10},{10... | collective-permute-start | bytes 688136 | tf_op jit(solution)/shard_map/ppermute | solution.py:56
  54.8 10.6 %collective-permute-start.16 = (bf16[64,1792]{1,0:T(8,128)(2,1)S(1)}, bf16[64,1792]{1,0:T(8,128)(2,1)S(1)}, u32[]{:S(2)}, u32[]{:S(2)}) collective-permute-start(bf16[64,1792]{1,0:T(8,128)(2,1)S(1)} %get-tuple-element.41), channel_id=1, source_target_pairs={{0,8},{8,0},{16,24},{24,16},{1,9},{9,1},{17,25},{25,17},{2,10},{10... | collective-permute-start | bytes 688136 | tf_op jit(solution)/shard_map/ppermute | solution.py:56
  56.3 9.1 %collective-permute-start.18 = (bf16[64,1792]{1,0:T(8,128)(2,1)S(1)}, bf16[64,1792]{1,0:T(8,128)(2,1)S(1)}, u32[]{:S(2)}, u32[]{:S(2)}) collective-permute-start(bf16[64,1792]{1,0:T(8,128)(2,1)S(1)} %add.7), channel_id=1, source_target_pairs={{0,16},{8,24},{16,0},{24,8},{1,17},{9,25},{17,1},{25,9},{2,18},{10... | collective-permute-start | bytes 688136 | tf_op jit(solution)/shard_map/ppermute | solution.py:56
  58.1 7.3 %collective-permute-start.19 = (bf16[32,1792]{1,0:T(8,128)(2,1)S(1)}, bf16[32,1792]{1,0:T(8,128)(2,1)S(1)}, u32[]{:S(2)}, u32[]{:S(2)}) collective-permute-start(bf16[32,1792]{1,0:T(8,128)(2,1)S(1)} %get-tuple-element.44), channel_id=1, source_target_pairs={{0,4},{2,6},{4,0},{6,2},{1,5},{3,7},{5,1},{7,3},{8,12},{10,14},{12... | collective-permute-start | bytes 344072 | tf_op jit(solution)/shard_map/ppermute | solution.py:56
  65.5 8.9 %collective-permute-start.20 = (bf16[32,1792]{1,0:T(8,128)(2,1)S(1)}, bf16[32,1792]{1,0:T(8,128)(2,1)S(1)}, u32[]{:S(2)}, u32[]{:S(2)}) collective-permute-start(bf16[32,1792]{1,0:T(8,128)(2,1)S(1)} %get-tuple-element.47), channel_id=1, source_target_pairs={{0,2},{2,0},{4,6},{6,4},{1,3},{3,1},{5,7},{7,5},{8,10},{10,8},{12,... | collective-permute-start | bytes 344072 | tf_op jit(solution)/shard_map/ppermute | solution.py:56
  65.5 7.6 %collective-permute-start.21 = (bf16[16,1792]{1,0:T(8,128)(2,1)S(1)}, bf16[16,1792]{1,0:T(8,128)(2,1)S(1)}, u32[]{:S(2)}, u32[]{:S(2)}) collective-permute-start(bf16[16,1792]{1,0:T(8,128)(2,1)S(1)} %get-tuple-element.48), channel_id=1, source_target_pairs={{0,4},{2,6},{4,0},{6,2},{1,5},{3,7},{5,1},{7,3},{8,12},{10,14},{12... | collective-permute-start | bytes 172040 | tf_op jit(solution)/shard_map/ppermute | solution.py:56
  68.3 6.1 %collective-permute-start.22 = (bf16[16,1792]{1,0:T(8,128)(2,1)S(1)}, bf16[16,1792]{1,0:T(8,128)(2,1)S(1)}, u32[]{:S(2)}, u32[]{:S(2)}) collective-permute-start(bf16[16,1792]{1,0:T(8,128)(2,1)S(1)} %get-tuple-element.49), channel_id=1, source_target_pairs={{0,6},{2,4},{4,2},{6,0},{1,7},{3,5},{5,3},{7,1},{8,14},{10,12},{12... | collective-permute-start | bytes 172040 | tf_op jit(solution)/shard_map/ppermute | solution.py:56
  (5 other events, 27.1 us)

commit v9 on v8

--- a/solution.py
+++ b/solution.py
@@ -126,28 +126,37 @@
     return call("copied", copy_body, [(source.shape, source.dtype)], [source, after], 1 << 31)[0]
 
 
+def inner_order():
+    bits = bits_of("ingroup")
+    return [
+        sum(bit for i, bit in enumerate(bits) if k >> i & 1)
+        for k in range(lax.axis_size("ingroup"))
+    ]
+
+
 def spread(own, cotangent):
-    outer, count = bits_of("group"), lax.axis_size("ingroup")
-    blocks = [own] + [swap(own, "ingroup", j) for j in range(1, count)]
-    early, second = pack(blocks[: count // 2], passed=[copied(cotangent, own)])
-    late = pack(blocks[count // 2 :])
+    outer, inner = bits_of("group"), bits_of("ingroup")
+    blocks = [own] + [swap(own, "ingroup", j) for j in inner_order()[1:]]
+    half = len(blocks) // 2
+    second = copied(cotangent, blocks[half])
+    early = pack(blocks[:half])
+    for bit in inner[:-1]:
+        second = pack([second, swap(second, "ingroup", bit)])
+    late = pack(blocks[half:], [early])
     across = swap(early, "group", outer[0])
     last = swap(late, "group", outer[0])
-    for bit in bits_of("ingroup")[:0:-1]:
-        second = pack([second, swap(second, "ingroup", bit)])
     first = pack([early, late, across, last], [second])
     for bit in outer[1:-1]:
         first = pack([first, swap(first, "group", bit)])
     first = [first, swap(first, "group", outer[-1])]
-    return first, [second, swap(second, "ingroup", bits_of("ingroup")[0])]
+    return first, [second, swap(second, "ingroup", inner[-1])]
 
 
 def spread_end(parts, after):
-    bits = bits_of("group")
-    current = pack(parts, after)
-    for bit in bits[:-1]:
-        current = pack([current, swap(current, "group", bit)])
-    return [current, swap(current, "group", bits[-1])]
+    held = [pack(parts, after)]
+    for bit in bits_of("group"):
+        held = held + [swap(part, "group", bit) for part in held]
+    return held
 
 
 def route_body(wide, topk, block, capacity, count, me, *refs):
@@ -246,12 +255,15 @@
     ).astype(BF16)
 
 
-def place_body(place, rows, keep, stay, received, near_out, go_out, stay_out, keep_out, far_out):
+def place_body(
+    block, place, rows, keep, stay, received, near_out, go_out, stay_out, keep_out, far_out
+):
     place_rows(place[...], rows[...], near_out, go_out, stay_out)
     half = keep_out.shape[0]
     total = keep[: 2 * half] + stay[...].astype(F32) + received[...].astype(F32)
-    keep_out[...] = total[:half]
-    far_out[...] = total[half:].astype(BF16)
+    for at in range(0, half, block):
+        keep_out[at : at + block] = total[2 * at : 2 * at + block]
+        far_out[at : at + block] = total[2 * at + block : 2 * (at + block)].astype(BF16)
 
 
 def join_body(near, stay, last, keep, got, own_out, mixed_out, pair_out, *away_outs):
@@ -259,12 +271,14 @@
     rows = last.shape[0]
     total = near[:rows] + stay[:rows].astype(F32) + last[...].astype(F32)
     mixed = keep[...] + got[...].astype(F32)
+    middle = rows // 2
     own_out[...] = total[:block]
     mixed_out[...] = mixed[:block]
     pair_out[:block] = mixed[block:].astype(BF16)
-    pair_out[block:] = total[block : 2 * block].astype(BF16)
-    for i, out in enumerate(away_outs):
-        out[...] = total[(2 + i) * block : (3 + i) * block].astype(BF16)
+    pair_out[block:] = total[middle : middle + block].astype(BF16)
+    starts = [at for at in range(block, rows, block) if at != middle]
+    for at, out in zip(starts, away_outs):
+        out[...] = total[at : at + block].astype(BF16)
 
 
 def final_body(count, mixed, grad, pair, *refs):
@@ -392,16 +406,16 @@
     count, across_bit = lax.axis_size("ingroup"), bits_of("group")[0]
     near_dx, go, stay, keep, far = call(
         "place",
-        place_body,
+        functools.partial(place_body, block),
         [near, fourth, fourth] + [((half // 2, features), t) for t in (F32, BF16)],
         [place, rows, near_y, got_y, swap(far, "group", across_bit)],
     )
     near_dx, got_go, got_dx = collect_start(near_dx, go, stay)
     got = swap(far, axis, bits[0])
     for bit in bits[1:-1]:
-        outs = [(keep.shape[0] // 2, t) for t in (F32, BF16)]
-        keep, far = add(keep, 0, [(got, 0)], outs)
-        got = swap(far, axis, bit)
+        sums = (keep + got.astype(F32)).reshape(-1, 2, block, features)
+        keep = sums[:, 0].reshape(-1, features)
+        got = swap(sums[:, 1].reshape(-1, features).astype(BF16), axis, bit)
     (far,) = add(near_dx, half, [(got_go, 0)], [(half, BF16)])
     own_dx, own_y, pair, *away = call(
         "join",
@@ -411,7 +425,8 @@
         + [((block, features), BF16)] * (count - 2),
         [near_dx, got_dx, swap(far, "group", across_bit), keep, got],
     )
-    sent = [swap(part, axis, 2 + j) for j, part in enumerate(away)]
+    offsets = [j for j in inner_order() if j > 1]
+    sent = [swap(part, axis, j) for j, part in zip(offsets, away)]
     outs = [((block, features), BF16)] * 2
     return call(
         "final",

time: 75.3 us -> 71.1 us (0.944)
  local copies, waits for them, and re-layouts: 2.52 us -> 0.85 us
  waiting for transfers between devices: 38.2 us -> 37 us
  starting transfers between devices: 23.8 us -> 22.6 us
    ppermute x21 -> x22, waiting for transfers between devices: 35.5 us -> 33.3 us  [swap(): lax.ppermute(value, axis, [(i, i ^ offset) for i in range(lax.axis_size(a...]
    unnamed x12 -> x10, local copies, waits for them, and re-layouts: 2.52 us -> 0.85 us
    ppermute x21 -> x22, starting transfers between devices: 20.7 us -> 19.5 us  [swap(): lax.ppermute(value, axis, [(i, i ^ offset) for i in range(lax.axis_size(a...]
    ppermute x2, waiting for transfers between devices: 2.74 us -> 3.67 us  [from_peers(): lax.ppermute(sent, 'dp', [(i, (i + step) % count) for i in range(count)])]
    pallas_call x17 -> x16, Pallas kernels: 9.65 us -> 9.65 us  [call(): return kernel(*args, *passed)]
  transfers between devices with their start and end apart: 23 -> 24, of which waited for: 15 -> 16; matrix products, arithmetic and copies ran while one was open for 0% -> 0% of each run, Pallas kernels for 9% -> 10%
where the time goes in v9:
time: 71.1 us; the launch traced here: 70.9 us
  waiting for transfers between devices  37 us (52%)
  starting transfers between devices  22.6 us (32%)
  Pallas kernels  9.65 us (14%)
  local copies, waits for them, and re-layouts  0.85 us (1%)
  between operations  0.81 us (1%)
    ppermute x22, waiting for transfers between devices, swap(): lax.ppermute(value, axis, [(i, i ^ offset) for i in range(lax.axis_size(a...  33.3 us
    ppermute x22, starting transfers between devices, swap(): lax.ppermute(value, axis, [(i, i ^ offset) for i in range(lax.axis_size(a...  19.5 us
    pallas_call x16, Pallas kernels, call(): return kernel(*args, *passed)  9.65 us
    ppermute x2, waiting for transfers between devices, from_peers(): lax.ppermute(sent, 'dp', [(i, (i + step) % count) for i in range(count)])  3.67 us
    ppermute x2, starting transfers between devices, from_peers(): lax.ppermute(sent, 'dp', [(i, (i + step) % count) for i in range(count)])  3.11 us
  transfers between devices with their start and end apart: 24, of which 16 were waited for; matrix products, arithmetic and copies ran while one was open for 0% of the time, Pallas kernels for 10%

profile of v9, /device:TPU:0, one launch (start us, length us, event | category | flops | bytes accessed | tf_op | source)
XLA Modules:
  0.0 70.9 jit_solution(13491477761258849080)
XLA Ops:
  0.6 1.5 %payload.1.refs_0_ = bf16[16,1920]{1,0:T(8,128)(2,1)} custom-call(s32[1]{0:T(128)} %bitcast.refs_0_, bf16[16,1792]{1,0:T(8,128)(2,1)} %refs_1_.1, s32[8,16]{1,0:T(8,128)} %bitcast.12, s32[8,16]{1,0:T(8,128)} %bitcast.13), custom_call_target="tpu_custom_call" | custom-call | bytes 119812 | tf_op jit(solution)/shard_map/payload/payload/pallas_call | solution.py:52
  2.2 4.1 %collective-permute-start = (bf16[16,1920]{1,0:T(8,128)(2,1)}, bf16[16,1920]{1,0:T(8,128)(2,1)S(1)}, u32[]{:S(2)}, u32[]{:S(2)}) collective-permute-start(bf16[16,1920]{1,0:T(8,128)(2,1)} %payload.1.refs_0_), channel_id=1, source_target_pairs={{0,4},{2,6},{4,0},{6,2},{1,5},{3,7},{5,1},{7,3},{8,12},{10,14},{12... | collective-permute-start | bytes 184328 | tf_op jit(solution)/shard_map/ppermute | solution.py:56
  6.3 1.6 %collective-permute-start.1 = (bf16[16,1920]{1,0:T(8,128)(2,1)}, bf16[16,1920]{1,0:T(8,128)(2,1)S(1)}, u32[]{:S(2)}, u32[]{:S(2)}) collective-permute-start(bf16[16,1920]{1,0:T(8,128)(2,1)} %payload.1.refs_0_), channel_id=1, source_target_pairs={{0,2},{2,0},{4,6},{6,4},{1,3},{3,1},{5,7},{7,5},{8,10},{10,8},{12,... | collective-permute-start | bytes 184328 | tf_op jit(solution)/shard_map/ppermute | solution.py:56
  7.8 1.6 %collective-permute-done.refs_1_ = bf16[16,1920]{1,0:T(8,128)(2,1)S(1)} collective-permute-done((bf16[16,1920]{1,0:T(8,128)(2,1)}, bf16[16,1920]{1,0:T(8,128)(2,1)S(1)}, u32[]{:S(2)}, u32[]{:S(2)}) %collective-permute-start) | collective-permute-done | bytes 61472 | tf_op jit(solution)/shard_map/ppermute | solution.py:56
  10.3 1.9 %collective-permute-start.3 = (bf16[32,1920]{1,0:T(8,128)(2,1)S(1)}, bf16[32,1920]{1,0:T(8,128)(2,1)S(1)}, u32[]{:S(2)}, u32[]{:S(2)}) collective-permute-start(bf16[32,1920]{1,0:T(8,128)(2,1)S(1)} %pack.5.refs_2_.refs_0_), channel_id=1, source_target_pairs={{0,16},{8,24},{16,0},{24,8},{1,17},{9,25},{17,1},{25,9},{2,18},{10... | collective-permute-start | bytes 368648 | tf_op jit(solution)/shard_map/ppermute | solution.py:56
  12.1 1.9 %collective-permute-done.2.refs_1_ = bf16[16,1920]{1,0:T(8,128)(2,1)S(1)} collective-permute-done((bf16[16,1920]{1,0:T(8,128)(2,1)}, bf16[16,1920]{1,0:T(8,128)(2,1)S(1)}, u32[]{:S(2)}, u32[]{:S(2)}) %collective-permute-start.2) | collective-permute-done | bytes 61472 | tf_op jit(solution)/shard_map/ppermute | solution.py:56
  14.1 1.6 %collective-permute-start.4 = (bf16[32,1920]{1,0:T(8,128)(2,1)S(1)}, bf16[32,1920]{1,0:T(8,128)(2,1)S(1)}, u32[]{:S(2)}, u32[]{:S(2)}) collective-permute-start(bf16[32,1920]{1,0:T(8,128)(2,1)S(1)} %pack.6.refs_1_), channel_id=1, source_target_pairs={{0,16},{8,24},{16,0},{24,8},{1,17},{9,25},{17,1},{25,9},{2,18},{10... | collective-permute-start | bytes 368648 | tf_op jit(solution)/shard_map/ppermute | solution.py:56
  16.8 4.3 %collective-permute-done.5.refs_1_ = bf16[16,1792]{1,0:T(8,128)(2,1)S(1)} collective-permute-done((bf16[16,1792]{1,0:T(8,128)(2,1)S(1)}, bf16[16,1792]{1,0:T(8,128)(2,1)S(1)}, u32[]{:S(2)}, u32[]{:S(2)}) %collective-permute-start.5) | collective-permute-done | bytes 57376 | tf_op jit(solution)/shard_map/ppermute | solution.py:56
  21.3 1.8 %collective-permute-done.6.refs_2_ = bf16[128,1920]{1,0:T(8,128)(2,1)S(1)} collective-permute-done((bf16[128,1920]{1,0:T(8,128)(2,1)S(1)}, bf16[128,1920]{1,0:T(8,128)(2,1)S(1)}, u32[]{:S(2)}, u32[]{:S(2)}) %collective-permute-start.6) | collective-permute-done | bytes 491552 | tf_op jit(solution)/shard_map/ppermute | solution.py:56
  23.0 1.8 %forward.1 = (bf16[256,128]{1,0:T(8,128)(2,1)S(1)}, f32[128,128]{1,0:T(8,128)S(1)}, f32[256,1024]{1,0:T(8,128)S(1)}, bf16[256,1024]{1,0:T(8,128)(2,1)S(1)}) custom-call(s32[1]{0:T(128)} %bitcast.refs_0_, bf16[128,1920]{1,0:T(8,128)(2,1)S(1)} %pack.8.refs_1_, bf16[128,1920]{1,0:T(8,128)(2,1)S(1)} %collective-permute-done.6.refs_2_, ...), custom_call_target="tpu_custom_call" | custom-call | flops 939524096 | bytes 10027012 | tf_op jit(solution)/shard_map/forward/forward/pallas_call | solution.py:52
  24.8 1.6 %collective-permute-start.7 = (bf16[256,1024]{1,0:T(8,128)(2,1)S(1)}, bf16[256,1024]{1,0:T(8,128)(2,1)S(1)}, u32[]{:S(2)}, u32[]{:S(2)}) collective-permute-start(bf16[256,1024]{1,0:T(8,128)(2,1)S(1)} %get-tuple-element.26.refs_2_), channel_id=1, source_target_pairs={{0,1},{1,0},{2,3},{3,2},{4,5},{5,4},{6,7},{7,6},{8,9},{9,8},{10,11... | collective-permute-start | bytes 1572872 | tf_op jit(solution)/shard_map/ppermute | solution.py:334
  27.2 6.8 %collective-permute-done.9.refs_1_ = bf16[64,1792]{1,0:T(8,128)(2,1)S(1)} collective-permute-done((bf16[64,1792]{1,0:T(8,128)(2,1)S(1)}, bf16[64,1792]{1,0:T(8,128)(2,1)S(1)}, u32[]{:S(2)}, u32[]{:S(2)}) %collective-permute-start.9) | collective-permute-done | bytes 229408 | tf_op jit(solution)/shard_map/ppermute | solution.py:56
  34.0 1.5 %collective-permute-done.11.refs_3_ = bf16[64,1792]{1,0:T(8,128)(2,1)S(1)} collective-permute-done((bf16[64,1792]{1,0:T(8,128)(2,1)S(1)}, bf16[64,1792]{1,0:T(8,128)(2,1)S(1)}, u32[]{:S(2)}, u32[]{:S(2)}) %collective-permute-start.11) | collective-permute-done | bytes 229408 | tf_op jit(solution)/shard_map/ppermute | solution.py:56
  35.5 1.3 %back.1 = (f32[128,1024]{1,0:T(8,128)S(1)}, bf16[128,1024]{1,0:T(8,128)(2,1)S(1)}) custom-call(bf16[64,1792]{1,0:T(8,128)(2,1)S(1)} %pack.9.refs_0_, bf16[64,1792]{1,0:T(8,128)(2,1)S(1)} %collective-permute-done.9.refs_1_, bf16[64,1792]{1,0:T(8,128)(2,1)S(1)} %collective-permute-done.10.refs_2_, bf16[64,1792]{1,0:T(8,128)(2,1)S(1)} %collective-permute-done.11.refs_3_, ...), custom_call_target="tpu_custom_call" | custom-call | flops 469762048 | bytes 5439488 | tf_op jit(solution)/shard_map/back/back/pallas_call | solution.py:52
  36.8 1.6 %collective-permute-start.12 = (bf16[128,1024]{1,0:T(8,128)(2,1)S(1)}, bf16[128,1024]{1,0:T(8,128)(2,1)S(1)}, u32[]{:S(2)}, u32[]{:S(2)}) collective-permute-start(bf16[128,1024]{1,0:T(8,128)(2,1)S(1)} %get-tuple-element.28.refs_5_), channel_id=1, source_target_pairs={{0,1},{1,0},{2,3},{3,2},{4,5},{5,4},{6,7},{7,6},{8,9},{9,8},{10,11... | collective-permute-start | bytes 786440 | tf_op jit(solution)/shard_map/ppermute | solution.py:334
  38.9 1.2 %out.1 = (f32[128,1024]{1,0:T(8,128)S(1)}, f32[128,1024]{1,0:T(8,128)S(1)}, f32[128,1792]{1,0:T(8,128)S(1)}, bf16[32,1792]{1,0:T(8,128)(2,1)S(1)}, bf16[32,1792]...) custom-call(f32[256,1024]{1,0:T(8,128)S(1)} %get-tuple-element.25.refs_0_, ...), custom_call_target="tpu_custom_call" | custom-call | flops 469762048 | bytes 8060928 | tf_op jit(solution)/shard_map/out/out/pallas_call | solution.py:52
  42.1 3.1 %collective-permute-done.12.refs_3_ = bf16[128,1024]{1,0:T(8,128)(2,1)S(1)} collective-permute-done((bf16[128,1024]{1,0:T(8,128)(2,1)S(1)}, bf16[128,1024]{1,0:T(8,128)(2,1)S(1)}, u32[]{:S(2)}, u32[]{:S(2)}) %collective-permute-start.12) | collective-permute-done | bytes 262176 | tf_op jit(solution)/shard_map/ppermute | solution.py:334
  45.2 2.5 %grad.1.refs_1_ = bf16[128,1792]{1,0:T(8,128)(2,1)S(1)} custom-call(f32[128,1024]{1,0:T(8,128)S(1)} %get-tuple-element.29.refs_0_, f32[128,1024]{1,0:T(8,128)S(1)} %get-tuple-element.30.refs_1_, f32[128,1024]{1,0:T(8,128)S(1)} %get-tuple-element.31.refs_2_, bf16[128,1024]{1,0:T(8,128)(2,1)S(1)} %collective-permute-done.12.refs_3_, ...), custom_call_target="tpu_custom_call" | custom-call | flops 939524096 | bytes 9863168 | tf_op jit(solution)/shard_map/grad/grad/pallas_call | solution.py:52
  47.7 1.9 %collective-permute-done.16.refs_4_ = bf16[64,1792]{1,0:T(8,128)(2,1)S(1)} collective-permute-done((bf16[64,1792]{1,0:T(8,128)(2,1)S(1)}, bf16[64,1792]{1,0:T(8,128)(2,1)S(1)}, u32[]{:S(2)}, u32[]{:S(2)}) %collective-permute-start.16) | collective-permute-done | bytes 229408 | tf_op jit(solution)/shard_map/ppermute | solution.py:56
  52.0 2.3 %collective-permute-start.20 = (bf16[32,1792]{1,0:T(8,128)(2,1)S(1)}, bf16[32,1792]{1,0:T(8,128)(2,1)S(1)}, u32[]{:S(2)}, u32[]{:S(2)}) collective-permute-start(bf16[32,1792]{1,0:T(8,128)(2,1)S(1)} %get-tuple-element.40), channel_id=1, source_target_pairs={{0,4},{2,6},{4,0},{6,2},{1,5},{3,7},{5,1},{7,3},{8,12},{10,14},{12... | collective-permute-start | bytes 344072 | tf_op jit(solution)/shard_map/ppermute | solution.py:56
  54.3 6.0 %collective-permute-done.20.refs_4_ = bf16[32,1792]{1,0:T(8,128)(2,1)S(1)} collective-permute-done((bf16[32,1792]{1,0:T(8,128)(2,1)S(1)}, bf16[32,1792]{1,0:T(8,128)(2,1)S(1)}, u32[]{:S(2)}, u32[]{:S(2)}) %collective-permute-start.20) | collective-permute-done | bytes 114720 | tf_op jit(solution)/shard_map/ppermute | solution.py:56
  60.9 3.4 %collective-permute-start.22 = (bf16[16,1792]{1,0:T(8,128)(2,1)S(1)}, bf16[16,1792]{1,0:T(8,128)(2,1)S(1)}, u32[]{:S(2)}, u32[]{:S(2)}) collective-permute-start(bf16[16,1792]{1,0:T(8,128)(2,1)S(1)} %get-tuple-element.44), channel_id=1, source_target_pairs={{0,4},{2,6},{4,0},{6,2},{1,5},{3,7},{5,1},{7,3},{8,12},{10,14},{12... | collective-permute-start | bytes 172040 | tf_op jit(solution)/shard_map/ppermute | solution.py:56
  64.9 2.1 %collective-permute-done.22.refs_3_ = bf16[16,1792]{1,0:T(8,128)(2,1)S(1)} collective-permute-done((bf16[16,1792]{1,0:T(8,128)(2,1)S(1)}, bf16[16,1792]{1,0:T(8,128)(2,1)S(1)}, u32[]{:S(2)}, u32[]{:S(2)}) %collective-permute-start.22) | collective-permute-done | bytes 57376 | tf_op jit(solution)/shard_map/ppermute | solution.py:56
  67.0 3.2 %collective-permute-done.23.refs_4_ = bf16[16,1792]{1,0:T(8,128)(2,1)S(1)} collective-permute-done((bf16[16,1792]{1,0:T(8,128)(2,1)S(1)}, bf16[16,1792]{1,0:T(8,128)(2,1)S(1)}, u32[]{:S(2)}, u32[]{:S(2)}) %collective-permute-start.23) | collective-permute-done | bytes 57376 | tf_op jit(solution)/shard_map/ppermute | solution.py:56
  (50 shorter events, 9.7 us)
Async XLA Ops:
  2.2 7.3 %collective-permute-start = (bf16[16,1920]{1,0:T(8,128)(2,1)}, bf16[16,1920]{1,0:T(8,128)(2,1)S(1)}, u32[]{:S(2)}, u32[]{:S(2)}) collective-permute-start(bf16[16,1920]{1,0:T(8,128)(2,1)} %payload.1.refs_0_), channel_id=1, source_target_pairs={{0,4},{2,6},{4,0},{6,2},{1,5},{3,7},{5,1},{7,3},{8,12},{10,14},{12... | collective-permute-start | bytes 184328 | tf_op jit(solution)/shard_map/ppermute | solution.py:56
  6.3 5.9 %collective-permute-start.1 = (bf16[16,1920]{1,0:T(8,128)(2,1)}, bf16[16,1920]{1,0:T(8,128)(2,1)S(1)}, u32[]{:S(2)}, u32[]{:S(2)}) collective-permute-start(bf16[16,1920]{1,0:T(8,128)(2,1)} %payload.1.refs_0_), channel_id=1, source_target_pairs={{0,2},{2,0},{4,6},{6,4},{1,3},{3,1},{5,7},{7,5},{8,10},{10,8},{12,... | collective-permute-start | bytes 184328 | tf_op jit(solution)/shard_map/ppermute | solution.py:56
  7.8 6.2 %collective-permute-start.2 = (bf16[16,1920]{1,0:T(8,128)(2,1)}, bf16[16,1920]{1,0:T(8,128)(2,1)S(1)}, u32[]{:S(2)}, u32[]{:S(2)}) collective-permute-start(bf16[16,1920]{1,0:T(8,128)(2,1)} %payload.1.refs_0_), channel_id=1, source_target_pairs={{0,6},{2,4},{4,2},{6,0},{1,7},{3,5},{5,3},{7,1},{8,14},{10,12},{12... | collective-permute-start | bytes 184328 | tf_op jit(solution)/shard_map/ppermute | solution.py:56
  10.3 10.8 %collective-permute-start.3 = (bf16[32,1920]{1,0:T(8,128)(2,1)S(1)}, bf16[32,1920]{1,0:T(8,128)(2,1)S(1)}, u32[]{:S(2)}, u32[]{:S(2)}) collective-permute-start(bf16[32,1920]{1,0:T(8,128)(2,1)S(1)} %pack.5.refs_2_.refs_0_), channel_id=1, source_target_pairs={{0,16},{8,24},{16,0},{24,8},{1,17},{9,25},{17,1},{25,9},{2,18},{10... | collective-permute-start | bytes 368648 | tf_op jit(solution)/shard_map/ppermute | solution.py:56
  14.1 7.0 %collective-permute-start.4 = (bf16[32,1920]{1,0:T(8,128)(2,1)S(1)}, bf16[32,1920]{1,0:T(8,128)(2,1)S(1)}, u32[]{:S(2)}, u32[]{:S(2)}) collective-permute-start(bf16[32,1920]{1,0:T(8,128)(2,1)S(1)} %pack.6.refs_1_), channel_id=1, source_target_pairs={{0,16},{8,24},{16,0},{24,8},{1,17},{9,25},{17,1},{25,9},{2,18},{10... | collective-permute-start | bytes 368648 | tf_op jit(solution)/shard_map/ppermute | solution.py:56
  15.7 5.3 %collective-permute-start.5 = (bf16[16,1792]{1,0:T(8,128)(2,1)S(1)}, bf16[16,1792]{1,0:T(8,128)(2,1)S(1)}, u32[]{:S(2)}, u32[]{:S(2)}) collective-permute-start(bf16[16,1792]{1,0:T(8,128)(2,1)S(1)} %copied.1.refs_0_), channel_id=1, source_target_pairs={{0,4},{2,6},{4,0},{6,2},{1,5},{3,7},{5,1},{7,3},{8,12},{10,14},{12... | collective-permute-start | bytes 172040 | tf_op jit(solution)/shard_map/ppermute | solution.py:56
  21.1 1.9 %collective-permute-start.6 = (bf16[128,1920]{1,0:T(8,128)(2,1)S(1)}, bf16[128,1920]{1,0:T(8,128)(2,1)S(1)}, u32[]{:S(2)}, u32[]{:S(2)}) collective-permute-start(bf16[128,1920]{1,0:T(8,128)(2,1)S(1)} %pack.8.refs_1_), channel_id=1, source_target_pairs={{0,8},{8,0},{16,24},{24,16},{1,9},{9,1},{17,25},{25,17},{2,10},{10... | collective-permute-start | bytes 1474568 | tf_op jit(solution)/shard_map/ppermute | solution.py:56
  21.2 5.6 %collective-permute-start.8 = (bf16[32,1792]{1,0:T(8,128)(2,1)S(1)}, bf16[32,1792]{1,0:T(8,128)(2,1)S(1)}, u32[]{:S(2)}, u32[]{:S(2)}) collective-permute-start(bf16[32,1792]{1,0:T(8,128)(2,1)S(1)} %pack.7.refs_4_.refs_0_), channel_id=1, source_target_pairs={{0,2},{2,0},{4,6},{6,4},{1,3},{3,1},{5,7},{7,5},{8,10},{10,8},{12,... | collective-permute-start | bytes 344072 | tf_op jit(solution)/shard_map/ppermute | solution.py:56
  24.8 14.0 %collective-permute-start.7 = (bf16[256,1024]{1,0:T(8,128)(2,1)S(1)}, bf16[256,1024]{1,0:T(8,128)(2,1)S(1)}, u32[]{:S(2)}, u32[]{:S(2)}) collective-permute-start(bf16[256,1024]{1,0:T(8,128)(2,1)S(1)} %get-tuple-element.26.refs_2_), channel_id=1, source_target_pairs={{0,1},{1,0},{2,3},{3,2},{4,5},{5,4},{6,7},{7,6},{8,9},{9,8},{10,11... | collective-permute-start | bytes 1572872 | tf_op jit(solution)/shard_map/ppermute | solution.py:334
  26.8 7.2 %collective-permute-start.9 = (bf16[64,1792]{1,0:T(8,128)(2,1)S(1)}, bf16[64,1792]{1,0:T(8,128)(2,1)S(1)}, u32[]{:S(2)}, u32[]{:S(2)}) collective-permute-start(bf16[64,1792]{1,0:T(8,128)(2,1)S(1)} %pack.9.refs_0_), channel_id=1, source_target_pairs={{0,16},{8,24},{16,0},{24,8},{1,17},{9,25},{17,1},{25,9},{2,18},{10... | collective-permute-start | bytes 688136 | tf_op jit(solution)/shard_map/ppermute | solution.py:56
  27.2 6.8 %collective-permute-start.10 = (bf16[64,1792]{1,0:T(8,128)(2,1)S(1)}, bf16[64,1792]{1,0:T(8,128)(2,1)S(1)}, u32[]{:S(2)}, u32[]{:S(2)}) collective-permute-start(bf16[64,1792]{1,0:T(8,128)(2,1)S(1)} %pack.9.refs_0_), channel_id=1, source_target_pairs={{0,8},{8,0},{16,24},{24,16},{1,9},{9,1},{17,25},{25,17},{2,10},{10... | collective-permute-start | bytes 688136 | tf_op jit(solution)/shard_map/ppermute | solution.py:56
  34.0 1.5 %collective-permute-start.11 = (bf16[64,1792]{1,0:T(8,128)(2,1)S(1)}, bf16[64,1792]{1,0:T(8,128)(2,1)S(1)}, u32[]{:S(2)}, u32[]{:S(2)}) collective-permute-start(bf16[64,1792]{1,0:T(8,128)(2,1)S(1)} %collective-permute-done.9.refs_1_), channel_id=1, source_target_pairs={{0,8},{8,0},{16,24},{24,16},{1,9},{9,1},{17,25},{25,17},{2,10},{10... | collective-permute-start | bytes 688136 | tf_op jit(solution)/shard_map/ppermute | solution.py:56
  36.8 8.4 %collective-permute-start.12 = (bf16[128,1024]{1,0:T(8,128)(2,1)S(1)}, bf16[128,1024]{1,0:T(8,128)(2,1)S(1)}, u32[]{:S(2)}, u32[]{:S(2)}) collective-permute-start(bf16[128,1024]{1,0:T(8,128)(2,1)S(1)} %get-tuple-element.28.refs_5_), channel_id=1, source_target_pairs={{0,1},{1,0},{2,3},{3,2},{4,5},{5,4},{6,7},{7,6},{8,9},{9,8},{10,11... | collective-permute-start | bytes 786440 | tf_op jit(solution)/shard_map/ppermute | solution.py:334
  40.1 1.4 %collective-permute-start.13 = (bf16[32,1792]{1,0:T(8,128)(2,1)S(1)}, bf16[32,1792]{1,0:T(8,128)(2,1)S(1)}, u32[]{:S(2)}, u32[]{:S(2)}) collective-permute-start(bf16[32,1792]{1,0:T(8,128)(2,1)S(1)} %get-tuple-element.33), channel_id=1, source_target_pairs={{0,8},{8,0},{16,24},{24,16},{1,9},{9,1},{17,25},{25,17},{2,10},{10... | collective-permute-start | bytes 344072 | tf_op jit(solution)/shard_map/ppermute | solution.py:56
  40.1 1.5 %collective-permute-start.14 = (bf16[32,1792]{1,0:T(8,128)(2,1)S(1)}, bf16[32,1792]{1,0:T(8,128)(2,1)S(1)}, u32[]{:S(2)}, u32[]{:S(2)}) collective-permute-start(bf16[32,1792]{1,0:T(8,128)(2,1)S(1)} %get-tuple-element.34), channel_id=1, source_target_pairs={{0,8},{8,0},{16,24},{24,16},{1,9},{9,1},{17,25},{25,17},{2,10},{10... | collective-permute-start | bytes 344072 | tf_op jit(solution)/shard_map/ppermute | solution.py:56
  40.6 7.1 %collective-permute-start.15 = (bf16[64,1792]{1,0:T(8,128)(2,1)S(1)}, bf16[64,1792]{1,0:T(8,128)(2,1)S(1)}, u32[]{:S(2)}, u32[]{:S(2)}) collective-permute-start(bf16[64,1792]{1,0:T(8,128)(2,1)S(1)} %get-tuple-element.35), channel_id=1, source_target_pairs={{0,8},{8,0},{16,24},{24,16},{1,9},{9,1},{17,25},{25,17},{2,10},{10... | collective-permute-start | bytes 688136 | tf_op jit(solution)/shard_map/ppermute | solution.py:56
  41.7 7.9 %collective-permute-start.16 = (bf16[64,1792]{1,0:T(8,128)(2,1)S(1)}, bf16[64,1792]{1,0:T(8,128)(2,1)S(1)}, u32[]{:S(2)}, u32[]{:S(2)}) collective-permute-start(bf16[64,1792]{1,0:T(8,128)(2,1)S(1)} %add.6.refs_6_), channel_id=1, source_target_pairs={{0,16},{8,24},{16,0},{24,8},{1,17},{9,25},{17,1},{25,9},{2,18},{10... | collective-permute-start | bytes 688136 | tf_op jit(solution)/shard_map/ppermute | solution.py:56
  50.0 1.6 %collective-permute-start.18 = (bf16[64,1792]{1,0:T(8,128)(2,1)S(1)}, bf16[64,1792]{1,0:T(8,128)(2,1)S(1)}, u32[]{:S(2)}, u32[]{:S(2)}) collective-permute-start(bf16[64,1792]{1,0:T(8,128)(2,1)S(1)} %get-tuple-element.38), channel_id=1, source_target_pairs={{0,8},{8,0},{16,24},{24,16},{1,9},{9,1},{17,25},{25,17},{2,10},{10... | collective-permute-start | bytes 688136 | tf_op jit(solution)/shard_map/ppermute | solution.py:56
  50.1 10.2 %collective-permute-start.17 = (bf16[64,1792]{1,0:T(8,128)(2,1)S(1)}, bf16[64,1792]{1,0:T(8,128)(2,1)S(1)}, u32[]{:S(2)}, u32[]{:S(2)}) collective-permute-start(bf16[64,1792]{1,0:T(8,128)(2,1)S(1)} %get-tuple-element.37), channel_id=1, source_target_pairs={{0,8},{8,0},{16,24},{24,16},{1,9},{9,1},{17,25},{25,17},{2,10},{10... | collective-permute-start | bytes 688136 | tf_op jit(solution)/shard_map/ppermute | solution.py:56
  51.6 8.7 %collective-permute-start.19 = (bf16[64,1792]{1,0:T(8,128)(2,1)S(1)}, bf16[64,1792]{1,0:T(8,128)(2,1)S(1)}, u32[]{:S(2)}, u32[]{:S(2)}) collective-permute-start(bf16[64,1792]{1,0:T(8,128)(2,1)S(1)} %add.7), channel_id=1, source_target_pairs={{0,16},{8,24},{16,0},{24,8},{1,17},{9,25},{17,1},{25,9},{2,18},{10... | collective-permute-start | bytes 688136 | tf_op jit(solution)/shard_map/ppermute | solution.py:56
  52.0 8.3 %collective-permute-start.20 = (bf16[32,1792]{1,0:T(8,128)(2,1)S(1)}, bf16[32,1792]{1,0:T(8,128)(2,1)S(1)}, u32[]{:S(2)}, u32[]{:S(2)}) collective-permute-start(bf16[32,1792]{1,0:T(8,128)(2,1)S(1)} %get-tuple-element.40), channel_id=1, source_target_pairs={{0,4},{2,6},{4,0},{6,2},{1,5},{3,7},{5,1},{7,3},{8,12},{10,14},{12... | collective-permute-start | bytes 344072 | tf_op jit(solution)/shard_map/ppermute | solution.py:56
  60.4 9.8 %collective-permute-start.21 = (bf16[32,1792]{1,0:T(8,128)(2,1)S(1)}, bf16[32,1792]{1,0:T(8,128)(2,1)S(1)}, u32[]{:S(2)}, u32[]{:S(2)}) collective-permute-start(bf16[32,1792]{1,0:T(8,128)(2,1)S(1)} %get-tuple-element.43), channel_id=1, source_target_pairs={{0,2},{2,0},{4,6},{6,4},{1,3},{3,1},{5,7},{7,5},{8,10},{10,8},{12,... | collective-permute-start | bytes 344072 | tf_op jit(solution)/shard_map/ppermute | solution.py:56
  60.9 6.2 %collective-permute-start.22 = (bf16[16,1792]{1,0:T(8,128)(2,1)S(1)}, bf16[16,1792]{1,0:T(8,128)(2,1)S(1)}, u32[]{:S(2)}, u32[]{:S(2)}) collective-permute-start(bf16[16,1792]{1,0:T(8,128)(2,1)S(1)} %get-tuple-element.44), channel_id=1, source_target_pairs={{0,4},{2,6},{4,0},{6,2},{1,5},{3,7},{5,1},{7,3},{8,12},{10,14},{12... | collective-permute-start | bytes 172040 | tf_op jit(solution)/shard_map/ppermute | solution.py:56
  64.2 6.0 %collective-permute-start.23 = (bf16[16,1792]{1,0:T(8,128)(2,1)S(1)}, bf16[16,1792]{1,0:T(8,128)(2,1)S(1)}, u32[]{:S(2)}, u32[]{:S(2)}) collective-permute-start(bf16[16,1792]{1,0:T(8,128)(2,1)S(1)} %get-tuple-element.45), channel_id=1, source_target_pairs={{0,6},{2,4},{4,2},{6,0},{1,7},{3,5},{5,3},{7,1},{8,14},{10,12},{12... | collective-permute-start | bytes 172040 | tf_op jit(solution)/shard_map/ppermute | solution.py:56
  (5 other events, 43.0 us)

commit v10 on v9

--- a/solution.py
+++ b/solution.py
@@ -255,15 +255,18 @@
     ).astype(BF16)
 
 
-def place_body(
-    block, place, rows, keep, stay, received, near_out, go_out, stay_out, keep_out, far_out
-):
+def place_body(place, rows, near_out, go_out, stay_out):
     place_rows(place[...], rows[...], near_out, go_out, stay_out)
+
+
+def step_body(block, near, go, keep, stay, received, far_out, keep_out, away_out):
+    rows = far_out.shape[0]
+    far_out[...] = (near[rows:] + go[...].astype(F32)).astype(BF16)
     half = keep_out.shape[0]
     total = keep[: 2 * half] + stay[...].astype(F32) + received[...].astype(F32)
     for at in range(0, half, block):
         keep_out[at : at + block] = total[2 * at : 2 * at + block]
-        far_out[at : at + block] = total[2 * at + block : 2 * (at + block)].astype(BF16)
+        away_out[at : at + block] = total[2 * at + block : 2 * (at + block)].astype(BF16)
 
 
 def join_body(near, stay, last, keep, got, own_out, mixed_out, pair_out, *away_outs):
@@ -404,19 +407,20 @@
     )
     axis, bits = "ingroup", bits_of("ingroup")
     count, across_bit = lax.axis_size("ingroup"), bits_of("group")[0]
-    near_dx, go, stay, keep, far = call(
-        "place",
-        functools.partial(place_body, block),
-        [near, fourth, fourth] + [((half // 2, features), t) for t in (F32, BF16)],
-        [place, rows, near_y, got_y, swap(far, "group", across_bit)],
-    )
-    near_dx, got_go, got_dx = collect_start(near_dx, go, stay)
-    got = swap(far, axis, bits[0])
+    near_dx, got_go, got_dx = collect_start(
+        *call("place", place_body, [near, fourth, fourth], [place, rows])
+    )
+    far, keep, away = call(
+        "step",
+        functools.partial(step_body, block),
+        [((half, features), BF16)] + [((half // 2, features), t) for t in (F32, BF16)],
+        [near_dx, got_go, near_y, got_y, swap(far, "group", across_bit)],
+    )
+    got = swap(away, axis, bits[0])
     for bit in bits[1:-1]:
         sums = (keep + got.astype(F32)).reshape(-1, 2, block, features)
         keep = sums[:, 0].reshape(-1, features)
         got = swap(sums[:, 1].reshape(-1, features).astype(BF16), axis, bit)
-    (far,) = add(near_dx, half, [(got_go, 0)], [(half, BF16)])
     own_dx, own_y, pair, *away = call(
         "join",
         join_body,

time: 71.1 us -> 71.9 us (1.011)
  starting transfers between devices: 22.6 us -> 24.7 us
  waiting for transfers between devices: 37 us -> 35.6 us
    ppermute x22, starting transfers between devices: 19.5 us -> 21.7 us  [swap(): lax.ppermute(value, axis, [(i, i ^ offset) for i in range(lax.axis_size(a...]
    ppermute x2, waiting for transfers between devices: 3.67 us -> 2.83 us  [from_peers(): lax.ppermute(sent, 'dp', [(i, (i + step) % count) for i in range(count)])]
  transfers between devices with their start and end apart: 24 -> 24, of which waited for: 16 -> 14; matrix products, arithmetic and copies ran while one was open for 0% -> 0% of each run, Pallas kernels for 10% -> 10%
where the time goes in v10:
time: 71.9 us; the launch traced here: 71.6 us
  waiting for transfers between devices  35.6 us (50%)
  starting transfers between devices  24.7 us (34%)
  Pallas kernels  9.65 us (13%)
  local copies, waits for them, and re-layouts  0.85 us (1%)
  between operations  0.79 us (1%)
    ppermute x22, waiting for transfers between devices, swap(): lax.ppermute(value, axis, [(i, i ^ offset) for i in range(lax.axis_size(a...  32.8 us
    ppermute x22, starting transfers between devices, swap(): lax.ppermute(value, axis, [(i, i ^ offset) for i in range(lax.axis_size(a...  21.7 us
    pallas_call x16, Pallas kernels, call(): return kernel(*args, *passed)  9.65 us
    ppermute x2, starting transfers between devices, from_peers(): lax.ppermute(sent, 'dp', [(i, (i + step) % count) for i in range(count)])  3.05 us
    ppermute x2, waiting for transfers between devices, from_peers(): lax.ppermute(sent, 'dp', [(i, (i + step) % count) for i in range(count)])  2.83 us
  transfers between devices with their start and end apart: 24, of which 14 were waited for; matrix products, arithmetic and copies ran while one was open for 0% of the time, Pallas kernels for 10%

profile of v10, /device:TPU:0, one launch (start us, length us, event | category | flops | bytes accessed | tf_op | source)
XLA Modules:
  0.0 71.6 jit_solution(4621462245121927408)
XLA Ops:
  0.6 1.5 %payload.1.refs_0_ = bf16[16,1920]{1,0:T(8,128)(2,1)} custom-call(s32[1]{0:T(128)} %bitcast.refs_0_, bf16[16,1792]{1,0:T(8,128)(2,1)} %refs_1_.1, s32[8,16]{1,0:T(8,128)} %bitcast.12, s32[8,16]{1,0:T(8,128)} %bitcast.13), custom_call_target="tpu_custom_call" | custom-call | bytes 119812 | tf_op jit(solution)/shard_map/payload/payload/pallas_call | solution.py:52
  2.2 4.1 %collective-permute-start = (bf16[16,1920]{1,0:T(8,128)(2,1)}, bf16[16,1920]{1,0:T(8,128)(2,1)S(1)}, u32[]{:S(2)}, u32[]{:S(2)}) collective-permute-start(bf16[16,1920]{1,0:T(8,128)(2,1)} %payload.1.refs_0_), channel_id=1, source_target_pairs={{0,4},{2,6},{4,0},{6,2},{1,5},{3,7},{5,1},{7,3},{8,12},{10,14},{12... | collective-permute-start | bytes 184328 | tf_op jit(solution)/shard_map/ppermute | solution.py:56
  6.3 1.6 %collective-permute-start.1 = (bf16[16,1920]{1,0:T(8,128)(2,1)}, bf16[16,1920]{1,0:T(8,128)(2,1)S(1)}, u32[]{:S(2)}, u32[]{:S(2)}) collective-permute-start(bf16[16,1920]{1,0:T(8,128)(2,1)} %payload.1.refs_0_), channel_id=1, source_target_pairs={{0,2},{2,0},{4,6},{6,4},{1,3},{3,1},{5,7},{7,5},{8,10},{10,8},{12,... | collective-permute-start | bytes 184328 | tf_op jit(solution)/shard_map/ppermute | solution.py:56
  7.9 1.6 %collective-permute-done.refs_1_ = bf16[16,1920]{1,0:T(8,128)(2,1)S(1)} collective-permute-done((bf16[16,1920]{1,0:T(8,128)(2,1)}, bf16[16,1920]{1,0:T(8,128)(2,1)S(1)}, u32[]{:S(2)}, u32[]{:S(2)}) %collective-permute-start) | collective-permute-done | bytes 61472 | tf_op jit(solution)/shard_map/ppermute | solution.py:56
  10.3 1.9 %collective-permute-start.3 = (bf16[32,1920]{1,0:T(8,128)(2,1)S(1)}, bf16[32,1920]{1,0:T(8,128)(2,1)S(1)}, u32[]{:S(2)}, u32[]{:S(2)}) collective-permute-start(bf16[32,1920]{1,0:T(8,128)(2,1)S(1)} %pack.5.refs_2_.refs_0_), channel_id=1, source_target_pairs={{0,16},{8,24},{16,0},{24,8},{1,17},{9,25},{17,1},{25,9},{2,18},{10... | collective-permute-start | bytes 368648 | tf_op jit(solution)/shard_map/ppermute | solution.py:56
  12.1 1.9 %collective-permute-done.2.refs_1_ = bf16[16,1920]{1,0:T(8,128)(2,1)S(1)} collective-permute-done((bf16[16,1920]{1,0:T(8,128)(2,1)}, bf16[16,1920]{1,0:T(8,128)(2,1)S(1)}, u32[]{:S(2)}, u32[]{:S(2)}) %collective-permute-start.2) | collective-permute-done | bytes 61472 | tf_op jit(solution)/shard_map/ppermute | solution.py:56
  14.1 1.6 %collective-permute-start.4 = (bf16[32,1920]{1,0:T(8,128)(2,1)S(1)}, bf16[32,1920]{1,0:T(8,128)(2,1)S(1)}, u32[]{:S(2)}, u32[]{:S(2)}) collective-permute-start(bf16[32,1920]{1,0:T(8,128)(2,1)S(1)} %pack.6.refs_1_), channel_id=1, source_target_pairs={{0,16},{8,24},{16,0},{24,8},{1,17},{9,25},{17,1},{25,9},{2,18},{10... | collective-permute-start | bytes 368648 | tf_op jit(solution)/shard_map/ppermute | solution.py:56
  16.8 4.3 %collective-permute-done.5.refs_1_ = bf16[16,1792]{1,0:T(8,128)(2,1)S(1)} collective-permute-done((bf16[16,1792]{1,0:T(8,128)(2,1)S(1)}, bf16[16,1792]{1,0:T(8,128)(2,1)S(1)}, u32[]{:S(2)}, u32[]{:S(2)}) %collective-permute-start.5) | collective-permute-done | bytes 57376 | tf_op jit(solution)/shard_map/ppermute | solution.py:56
  21.3 1.8 %collective-permute-done.6.refs_2_ = bf16[128,1920]{1,0:T(8,128)(2,1)S(1)} collective-permute-done((bf16[128,1920]{1,0:T(8,128)(2,1)S(1)}, bf16[128,1920]{1,0:T(8,128)(2,1)S(1)}, u32[]{:S(2)}, u32[]{:S(2)}) %collective-permute-start.6) | collective-permute-done | bytes 491552 | tf_op jit(solution)/shard_map/ppermute | solution.py:56
  23.0 1.8 %forward.1 = (bf16[256,128]{1,0:T(8,128)(2,1)S(1)}, f32[128,128]{1,0:T(8,128)S(1)}, f32[256,1024]{1,0:T(8,128)S(1)}, bf16[256,1024]{1,0:T(8,128)(2,1)S(1)}) custom-call(s32[1]{0:T(128)} %bitcast.refs_0_, bf16[128,1920]{1,0:T(8,128)(2,1)S(1)} %pack.8.refs_1_, bf16[128,1920]{1,0:T(8,128)(2,1)S(1)} %collective-permute-done.6.refs_2_, ...), custom_call_target="tpu_custom_call" | custom-call | flops 939524096 | bytes 10027012 | tf_op jit(solution)/shard_map/forward/forward/pallas_call | solution.py:52
  24.8 1.9 %collective-permute-done.8.refs_1_ = bf16[32,1792]{1,0:T(8,128)(2,1)S(1)} collective-permute-done((bf16[32,1792]{1,0:T(8,128)(2,1)S(1)}, bf16[32,1792]{1,0:T(8,128)(2,1)S(1)}, u32[]{:S(2)}, u32[]{:S(2)}) %collective-permute-start.8) | collective-permute-done | bytes 114720 | tf_op jit(solution)/shard_map/ppermute | solution.py:56
  27.2 1.5 %collective-permute-start.7 = (bf16[256,1024]{1,0:T(8,128)(2,1)S(1)}, bf16[256,1024]{1,0:T(8,128)(2,1)S(1)}, u32[]{:S(2)}, u32[]{:S(2)}) collective-permute-start(bf16[256,1024]{1,0:T(8,128)(2,1)S(1)} %get-tuple-element.27.refs_2_), channel_id=1, source_target_pairs={{0,1},{1,0},{2,3},{3,2},{4,5},{5,4},{6,7},{7,6},{8,9},{9,8},{10,11... | collective-permute-start | bytes 1572872 | tf_op jit(solution)/shard_map/ppermute | solution.py:337
  28.7 5.3 %collective-permute-done.9.refs_1_ = bf16[64,1792]{1,0:T(8,128)(2,1)S(1)} collective-permute-done((bf16[64,1792]{1,0:T(8,128)(2,1)S(1)}, bf16[64,1792]{1,0:T(8,128)(2,1)S(1)}, u32[]{:S(2)}, u32[]{:S(2)}) %collective-permute-start.9) | collective-permute-done | bytes 229408 | tf_op jit(solution)/shard_map/ppermute | solution.py:56
  34.0 1.5 %collective-permute-done.11.refs_3_ = bf16[64,1792]{1,0:T(8,128)(2,1)S(1)} collective-permute-done((bf16[64,1792]{1,0:T(8,128)(2,1)S(1)}, bf16[64,1792]{1,0:T(8,128)(2,1)S(1)}, u32[]{:S(2)}, u32[]{:S(2)}) %collective-permute-start.11) | collective-permute-done | bytes 229408 | tf_op jit(solution)/shard_map/ppermute | solution.py:56
  36.8 1.6 %collective-permute-start.12 = (bf16[128,1024]{1,0:T(8,128)(2,1)S(1)}, bf16[128,1024]{1,0:T(8,128)(2,1)S(1)}, u32[]{:S(2)}, u32[]{:S(2)}) collective-permute-start(bf16[128,1024]{1,0:T(8,128)(2,1)S(1)} %get-tuple-element.29.refs_5_), channel_id=1, source_target_pairs={{0,1},{1,0},{2,3},{3,2},{4,5},{5,4},{6,7},{7,6},{8,9},{9,8},{10,11... | collective-permute-start | bytes 786440 | tf_op jit(solution)/shard_map/ppermute | solution.py:337
  38.3 2.8 %collective-permute-done.7.refs_1_ = bf16[256,1024]{1,0:T(8,128)(2,1)S(1)} collective-permute-done((bf16[256,1024]{1,0:T(8,128)(2,1)S(1)}, bf16[256,1024]{1,0:T(8,128)(2,1)S(1)}, u32[]{:S(2)}, u32[]{:S(2)}) %collective-permute-start.7) | collective-permute-done | bytes 524320 | tf_op jit(solution)/shard_map/ppermute | solution.py:337
  43.9 2.6 %collective-permute-start.18 = (bf16[64,1792]{1,0:T(8,128)(2,1)S(1)}, bf16[64,1792]{1,0:T(8,128)(2,1)S(1)}, u32[]{:S(2)}, u32[]{:S(2)}) collective-permute-start(bf16[64,1792]{1,0:T(8,128)(2,1)S(1)} %add.5.refs_6_), channel_id=1, source_target_pairs={{0,16},{8,24},{16,0},{24,8},{1,17},{9,25},{17,1},{25,9},{2,18},{10... | collective-permute-start | bytes 688136 | tf_op jit(solution)/shard_map/ppermute | solution.py:56
  46.6 2.5 %grad.1.refs_1_ = bf16[128,1792]{1,0:T(8,128)(2,1)S(1)} custom-call(f32[128,1024]{1,0:T(8,128)S(1)} %get-tuple-element.30.refs_0_, f32[128,1024]{1,0:T(8,128)S(1)} %get-tuple-element.31.refs_1_, f32[128,1024]{1,0:T(8,128)S(1)} %get-tuple-element.32.refs_2_, bf16[128,1024]{1,0:T(8,128)(2,1)S(1)} %collective-permute-done.12.refs_3_, ...), custom_call_target="tpu_custom_call" | custom-call | flops 939524096 | bytes 9863168 | tf_op jit(solution)/shard_map/grad/grad/pallas_call | solution.py:52
  50.1 2.6 %collective-permute-done.18.refs_4_ = bf16[64,1792]{1,0:T(8,128)(2,1)S(1)} collective-permute-done((bf16[64,1792]{1,0:T(8,128)(2,1)S(1)}, bf16[64,1792]{1,0:T(8,128)(2,1)S(1)}, u32[]{:S(2)}, u32[]{:S(2)}) %collective-permute-start.18) | collective-permute-done | bytes 229408 | tf_op jit(solution)/shard_map/ppermute | solution.py:56
  52.8 1.8 %collective-permute-start.19 = (bf16[64,1792]{1,0:T(8,128)(2,1)S(1)}, bf16[64,1792]{1,0:T(8,128)(2,1)S(1)}, u32[]{:S(2)}, u32[]{:S(2)}) collective-permute-start(bf16[64,1792]{1,0:T(8,128)(2,1)S(1)} %get-tuple-element.40), channel_id=1, source_target_pairs={{0,16},{8,24},{16,0},{24,8},{1,17},{9,25},{17,1},{25,9},{2,18},{10... | collective-permute-start | bytes 688136 | tf_op jit(solution)/shard_map/ppermute | solution.py:56
  55.5 6.5 %collective-permute-done.20.refs_4_ = bf16[32,1792]{1,0:T(8,128)(2,1)S(1)} collective-permute-done((bf16[32,1792]{1,0:T(8,128)(2,1)S(1)}, bf16[32,1792]{1,0:T(8,128)(2,1)S(1)}, u32[]{:S(2)}, u32[]{:S(2)}) %collective-permute-start.20) | collective-permute-done | bytes 114720 | tf_op jit(solution)/shard_map/ppermute | solution.py:56
  62.1 2.9 %collective-permute-start.22 = (bf16[16,1792]{1,0:T(8,128)(2,1)S(1)}, bf16[16,1792]{1,0:T(8,128)(2,1)S(1)}, u32[]{:S(2)}, u32[]{:S(2)}) collective-permute-start(bf16[16,1792]{1,0:T(8,128)(2,1)S(1)} %get-tuple-element.46), channel_id=1, source_target_pairs={{0,4},{2,6},{4,0},{6,2},{1,5},{3,7},{5,1},{7,3},{8,12},{10,14},{12... | collective-permute-start | bytes 172040 | tf_op jit(solution)/shard_map/ppermute | solution.py:56
  65.0 1.5 %collective-permute-start.23 = (bf16[16,1792]{1,0:T(8,128)(2,1)S(1)}, bf16[16,1792]{1,0:T(8,128)(2,1)S(1)}, u32[]{:S(2)}, u32[]{:S(2)}) collective-permute-start(bf16[16,1792]{1,0:T(8,128)(2,1)S(1)} %get-tuple-element.47), channel_id=1, source_target_pairs={{0,6},{2,4},{4,2},{6,0},{1,7},{3,5},{5,3},{7,1},{8,14},{10,12},{12... | collective-permute-start | bytes 172040 | tf_op jit(solution)/shard_map/ppermute | solution.py:56
  66.5 3.2 %collective-permute-done.22.refs_3_ = bf16[16,1792]{1,0:T(8,128)(2,1)S(1)} collective-permute-done((bf16[16,1792]{1,0:T(8,128)(2,1)S(1)}, bf16[16,1792]{1,0:T(8,128)(2,1)S(1)}, u32[]{:S(2)}, u32[]{:S(2)}) %collective-permute-start.22) | collective-permute-done | bytes 57376 | tf_op jit(solution)/shard_map/ppermute | solution.py:56
  (50 shorter events, 10.6 us)
Async XLA Ops:
  2.2 7.3 %collective-permute-start = (bf16[16,1920]{1,0:T(8,128)(2,1)}, bf16[16,1920]{1,0:T(8,128)(2,1)S(1)}, u32[]{:S(2)}, u32[]{:S(2)}) collective-permute-start(bf16[16,1920]{1,0:T(8,128)(2,1)} %payload.1.refs_0_), channel_id=1, source_target_pairs={{0,4},{2,6},{4,0},{6,2},{1,5},{3,7},{5,1},{7,3},{8,12},{10,14},{12... | collective-permute-start | bytes 184328 | tf_op jit(solution)/shard_map/ppermute | solution.py:56
  6.3 5.9 %collective-permute-start.1 = (bf16[16,1920]{1,0:T(8,128)(2,1)}, bf16[16,1920]{1,0:T(8,128)(2,1)S(1)}, u32[]{:S(2)}, u32[]{:S(2)}) collective-permute-start(bf16[16,1920]{1,0:T(8,128)(2,1)} %payload.1.refs_0_), channel_id=1, source_target_pairs={{0,2},{2,0},{4,6},{6,4},{1,3},{3,1},{5,7},{7,5},{8,10},{10,8},{12,... | collective-permute-start | bytes 184328 | tf_op jit(solution)/shard_map/ppermute | solution.py:56
  7.8 6.2 %collective-permute-start.2 = (bf16[16,1920]{1,0:T(8,128)(2,1)}, bf16[16,1920]{1,0:T(8,128)(2,1)S(1)}, u32[]{:S(2)}, u32[]{:S(2)}) collective-permute-start(bf16[16,1920]{1,0:T(8,128)(2,1)} %payload.1.refs_0_), channel_id=1, source_target_pairs={{0,6},{2,4},{4,2},{6,0},{1,7},{3,5},{5,3},{7,1},{8,14},{10,12},{12... | collective-permute-start | bytes 184328 | tf_op jit(solution)/shard_map/ppermute | solution.py:56
  10.3 10.8 %collective-permute-start.3 = (bf16[32,1920]{1,0:T(8,128)(2,1)S(1)}, bf16[32,1920]{1,0:T(8,128)(2,1)S(1)}, u32[]{:S(2)}, u32[]{:S(2)}) collective-permute-start(bf16[32,1920]{1,0:T(8,128)(2,1)S(1)} %pack.5.refs_2_.refs_0_), channel_id=1, source_target_pairs={{0,16},{8,24},{16,0},{24,8},{1,17},{9,25},{17,1},{25,9},{2,18},{10... | collective-permute-start | bytes 368648 | tf_op jit(solution)/shard_map/ppermute | solution.py:56
  14.1 7.0 %collective-permute-start.4 = (bf16[32,1920]{1,0:T(8,128)(2,1)S(1)}, bf16[32,1920]{1,0:T(8,128)(2,1)S(1)}, u32[]{:S(2)}, u32[]{:S(2)}) collective-permute-start(bf16[32,1920]{1,0:T(8,128)(2,1)S(1)} %pack.6.refs_1_), channel_id=1, source_target_pairs={{0,16},{8,24},{16,0},{24,8},{1,17},{9,25},{17,1},{25,9},{2,18},{10... | collective-permute-start | bytes 368648 | tf_op jit(solution)/shard_map/ppermute | solution.py:56
  15.7 5.3 %collective-permute-start.5 = (bf16[16,1792]{1,0:T(8,128)(2,1)S(1)}, bf16[16,1792]{1,0:T(8,128)(2,1)S(1)}, u32[]{:S(2)}, u32[]{:S(2)}) collective-permute-start(bf16[16,1792]{1,0:T(8,128)(2,1)S(1)} %copied.1.refs_0_), channel_id=1, source_target_pairs={{0,4},{2,6},{4,0},{6,2},{1,5},{3,7},{5,1},{7,3},{8,12},{10,14},{12... | collective-permute-start | bytes 172040 | tf_op jit(solution)/shard_map/ppermute | solution.py:56
  21.1 1.9 %collective-permute-start.6 = (bf16[128,1920]{1,0:T(8,128)(2,1)S(1)}, bf16[128,1920]{1,0:T(8,128)(2,1)S(1)}, u32[]{:S(2)}, u32[]{:S(2)}) collective-permute-start(bf16[128,1920]{1,0:T(8,128)(2,1)S(1)} %pack.8.refs_1_), channel_id=1, source_target_pairs={{0,8},{8,0},{16,24},{24,16},{1,9},{9,1},{17,25},{25,17},{2,10},{10... | collective-permute-start | bytes 1474568 | tf_op jit(solution)/shard_map/ppermute | solution.py:56
  21.2 5.6 %collective-permute-start.8 = (bf16[32,1792]{1,0:T(8,128)(2,1)S(1)}, bf16[32,1792]{1,0:T(8,128)(2,1)S(1)}, u32[]{:S(2)}, u32[]{:S(2)}) collective-permute-start(bf16[32,1792]{1,0:T(8,128)(2,1)S(1)} %pack.7.refs_4_.refs_0_), channel_id=1, source_target_pairs={{0,2},{2,0},{4,6},{6,4},{1,3},{3,1},{5,7},{7,5},{8,10},{10,8},{12,... | collective-permute-start | bytes 344072 | tf_op jit(solution)/shard_map/ppermute | solution.py:56
  26.8 7.2 %collective-permute-start.9 = (bf16[64,1792]{1,0:T(8,128)(2,1)S(1)}, bf16[64,1792]{1,0:T(8,128)(2,1)S(1)}, u32[]{:S(2)}, u32[]{:S(2)}) collective-permute-start(bf16[64,1792]{1,0:T(8,128)(2,1)S(1)} %pack.9.refs_0_), channel_id=1, source_target_pairs={{0,16},{8,24},{16,0},{24,8},{1,17},{9,25},{17,1},{25,9},{2,18},{10... | collective-permute-start | bytes 688136 | tf_op jit(solution)/shard_map/ppermute | solution.py:56
  27.2 14.0 %collective-permute-start.7 = (bf16[256,1024]{1,0:T(8,128)(2,1)S(1)}, bf16[256,1024]{1,0:T(8,128)(2,1)S(1)}, u32[]{:S(2)}, u32[]{:S(2)}) collective-permute-start(bf16[256,1024]{1,0:T(8,128)(2,1)S(1)} %get-tuple-element.27.refs_2_), channel_id=1, source_target_pairs={{0,1},{1,0},{2,3},{3,2},{4,5},{5,4},{6,7},{7,6},{8,9},{9,8},{10,11... | collective-permute-start | bytes 1572872 | tf_op jit(solution)/shard_map/ppermute | solution.py:337
  28.7 5.4 %collective-permute-start.10 = (bf16[64,1792]{1,0:T(8,128)(2,1)S(1)}, bf16[64,1792]{1,0:T(8,128)(2,1)S(1)}, u32[]{:S(2)}, u32[]{:S(2)}) collective-permute-start(bf16[64,1792]{1,0:T(8,128)(2,1)S(1)} %pack.9.refs_0_), channel_id=1, source_target_pairs={{0,8},{8,0},{16,24},{24,16},{1,9},{9,1},{17,25},{25,17},{2,10},{10... | collective-permute-start | bytes 688136 | tf_op jit(solution)/shard_map/ppermute | solution.py:56
  34.0 1.5 %collective-permute-start.11 = (bf16[64,1792]{1,0:T(8,128)(2,1)S(1)}, bf16[64,1792]{1,0:T(8,128)(2,1)S(1)}, u32[]{:S(2)}, u32[]{:S(2)}) collective-permute-start(bf16[64,1792]{1,0:T(8,128)(2,1)S(1)} %collective-permute-done.9.refs_1_), channel_id=1, source_target_pairs={{0,8},{8,0},{16,24},{24,16},{1,9},{9,1},{17,25},{25,17},{2,10},{10... | collective-permute-start | bytes 688136 | tf_op jit(solution)/shard_map/ppermute | solution.py:56
  36.8 9.8 %collective-permute-start.12 = (bf16[128,1024]{1,0:T(8,128)(2,1)S(1)}, bf16[128,1024]{1,0:T(8,128)(2,1)S(1)}, u32[]{:S(2)}, u32[]{:S(2)}) collective-permute-start(bf16[128,1024]{1,0:T(8,128)(2,1)S(1)} %get-tuple-element.29.refs_5_), channel_id=1, source_target_pairs={{0,1},{1,0},{2,3},{3,2},{4,5},{5,4},{6,7},{7,6},{8,9},{9,8},{10,11... | collective-permute-start | bytes 786440 | tf_op jit(solution)/shard_map/ppermute | solution.py:337
  42.3 1.4 %collective-permute-start.13 = (bf16[32,1792]{1,0:T(8,128)(2,1)S(1)}, bf16[32,1792]{1,0:T(8,128)(2,1)S(1)}, u32[]{:S(2)}, u32[]{:S(2)}) collective-permute-start(bf16[32,1792]{1,0:T(8,128)(2,1)S(1)} %get-tuple-element.34), channel_id=1, source_target_pairs={{0,8},{8,0},{16,24},{24,16},{1,9},{9,1},{17,25},{25,17},{2,10},{10... | collective-permute-start | bytes 344072 | tf_op jit(solution)/shard_map/ppermute | solution.py:56
  42.4 1.5 %collective-permute-start.14 = (bf16[32,1792]{1,0:T(8,128)(2,1)S(1)}, bf16[32,1792]{1,0:T(8,128)(2,1)S(1)}, u32[]{:S(2)}, u32[]{:S(2)}) collective-permute-start(bf16[32,1792]{1,0:T(8,128)(2,1)S(1)} %get-tuple-element.35), channel_id=1, source_target_pairs={{0,8},{8,0},{16,24},{24,16},{1,9},{9,1},{17,25},{25,17},{2,10},{10... | collective-permute-start | bytes 344072 | tf_op jit(solution)/shard_map/ppermute | solution.py:56
  42.9 7.1 %collective-permute-start.17 = (bf16[64,1792]{1,0:T(8,128)(2,1)S(1)}, bf16[64,1792]{1,0:T(8,128)(2,1)S(1)}, u32[]{:S(2)}, u32[]{:S(2)}) collective-permute-start(bf16[64,1792]{1,0:T(8,128)(2,1)S(1)} %get-tuple-element.39), channel_id=1, source_target_pairs={{0,8},{8,0},{16,24},{24,16},{1,9},{9,1},{17,25},{25,17},{2,10},{10... | collective-permute-start | bytes 688136 | tf_op jit(solution)/shard_map/ppermute | solution.py:56
  43.9 8.7 %collective-permute-start.18 = (bf16[64,1792]{1,0:T(8,128)(2,1)S(1)}, bf16[64,1792]{1,0:T(8,128)(2,1)S(1)}, u32[]{:S(2)}, u32[]{:S(2)}) collective-permute-start(bf16[64,1792]{1,0:T(8,128)(2,1)S(1)} %add.5.refs_6_), channel_id=1, source_target_pairs={{0,16},{8,24},{16,0},{24,8},{1,17},{9,25},{17,1},{25,9},{2,18},{10... | collective-permute-start | bytes 688136 | tf_op jit(solution)/shard_map/ppermute | solution.py:56
  49.5 3.2 %collective-permute-start.16 = (bf16[64,1792]{1,0:T(8,128)(2,1)S(1)}, bf16[64,1792]{1,0:T(8,128)(2,1)S(1)}, u32[]{:S(2)}, u32[]{:S(2)}) collective-permute-start(bf16[64,1792]{1,0:T(8,128)(2,1)S(1)} %get-tuple-element.38), channel_id=1, source_target_pairs={{0,8},{8,0},{16,24},{24,16},{1,9},{9,1},{17,25},{25,17},{2,10},{10... | collective-permute-start | bytes 688136 | tf_op jit(solution)/shard_map/ppermute | solution.py:56
  49.6 5.9 %collective-permute-start.15 = (bf16[64,1792]{1,0:T(8,128)(2,1)S(1)}, bf16[64,1792]{1,0:T(8,128)(2,1)S(1)}, u32[]{:S(2)}, u32[]{:S(2)}) collective-permute-start(bf16[64,1792]{1,0:T(8,128)(2,1)S(1)} %get-tuple-element.37), channel_id=1, source_target_pairs={{0,8},{8,0},{16,24},{24,16},{1,9},{9,1},{17,25},{25,17},{2,10},{10... | collective-permute-start | bytes 688136 | tf_op jit(solution)/shard_map/ppermute | solution.py:56
  52.8 9.2 %collective-permute-start.19 = (bf16[64,1792]{1,0:T(8,128)(2,1)S(1)}, bf16[64,1792]{1,0:T(8,128)(2,1)S(1)}, u32[]{:S(2)}, u32[]{:S(2)}) collective-permute-start(bf16[64,1792]{1,0:T(8,128)(2,1)S(1)} %get-tuple-element.40), channel_id=1, source_target_pairs={{0,16},{8,24},{16,0},{24,8},{1,17},{9,25},{17,1},{25,9},{2,18},{10... | collective-permute-start | bytes 688136 | tf_op jit(solution)/shard_map/ppermute | solution.py:56
  54.6 7.4 %collective-permute-start.20 = (bf16[32,1792]{1,0:T(8,128)(2,1)S(1)}, bf16[32,1792]{1,0:T(8,128)(2,1)S(1)}, u32[]{:S(2)}, u32[]{:S(2)}) collective-permute-start(bf16[32,1792]{1,0:T(8,128)(2,1)S(1)} %get-tuple-element.42), channel_id=1, source_target_pairs={{0,4},{2,6},{4,0},{6,2},{1,5},{3,7},{5,1},{7,3},{8,12},{10,14},{12... | collective-permute-start | bytes 344072 | tf_op jit(solution)/shard_map/ppermute | solution.py:56
  62.1 8.9 %collective-permute-start.21 = (bf16[32,1792]{1,0:T(8,128)(2,1)S(1)}, bf16[32,1792]{1,0:T(8,128)(2,1)S(1)}, u32[]{:S(2)}, u32[]{:S(2)}) collective-permute-start(bf16[32,1792]{1,0:T(8,128)(2,1)S(1)} %get-tuple-element.45), channel_id=1, source_target_pairs={{0,2},{2,0},{4,6},{6,4},{1,3},{3,1},{5,7},{7,5},{8,10},{10,8},{12,... | collective-permute-start | bytes 344072 | tf_op jit(solution)/shard_map/ppermute | solution.py:56
  62.1 7.6 %collective-permute-start.22 = (bf16[16,1792]{1,0:T(8,128)(2,1)S(1)}, bf16[16,1792]{1,0:T(8,128)(2,1)S(1)}, u32[]{:S(2)}, u32[]{:S(2)}) collective-permute-start(bf16[16,1792]{1,0:T(8,128)(2,1)S(1)} %get-tuple-element.46), channel_id=1, source_target_pairs={{0,4},{2,6},{4,0},{6,2},{1,5},{3,7},{5,1},{7,3},{8,12},{10,14},{12... | collective-permute-start | bytes 172040 | tf_op jit(solution)/shard_map/ppermute | solution.py:56
  65.0 6.0 %collective-permute-start.23 = (bf16[16,1792]{1,0:T(8,128)(2,1)S(1)}, bf16[16,1792]{1,0:T(8,128)(2,1)S(1)}, u32[]{:S(2)}, u32[]{:S(2)}) collective-permute-start(bf16[16,1792]{1,0:T(8,128)(2,1)S(1)} %get-tuple-element.47), channel_id=1, source_target_pairs={{0,6},{2,4},{4,2},{6,0},{1,7},{3,5},{5,3},{7,1},{8,14},{10,12},{12... | collective-permute-start | bytes 172040 | tf_op jit(solution)/shard_map/ppermute | solution.py:56
  (5 other events, 43.0 us)

commit v11 on v9

--- a/solution.py
+++ b/solution.py
@@ -255,15 +255,12 @@
     ).astype(BF16)
 
 
-def place_body(
-    block, place, rows, keep, stay, received, near_out, go_out, stay_out, keep_out, far_out
-):
+def place_body(place, rows, keep, stay, received, near_out, go_out, stay_out, keep_out, far_out):
     place_rows(place[...], rows[...], near_out, go_out, stay_out)
     half = keep_out.shape[0]
     total = keep[: 2 * half] + stay[...].astype(F32) + received[...].astype(F32)
-    for at in range(0, half, block):
-        keep_out[at : at + block] = total[2 * at : 2 * at + block]
-        far_out[at : at + block] = total[2 * at + block : 2 * (at + block)].astype(BF16)
+    keep_out[...] = total[:half]
+    far_out[...] = total[half:].astype(BF16)
 
 
 def join_body(near, stay, last, keep, got, own_out, mixed_out, pair_out, *away_outs):
@@ -271,13 +268,11 @@
     rows = last.shape[0]
     total = near[:rows] + stay[:rows].astype(F32) + last[...].astype(F32)
     mixed = keep[...] + got[...].astype(F32)
-    middle = rows // 2
     own_out[...] = total[:block]
     mixed_out[...] = mixed[:block]
     pair_out[:block] = mixed[block:].astype(BF16)
-    pair_out[block:] = total[middle : middle + block].astype(BF16)
-    starts = [at for at in range(block, rows, block) if at != middle]
-    for at, out in zip(starts, away_outs):
+    pair_out[block:] = total[block : 2 * block].astype(BF16)
+    for at, out in zip(range(2 * block, rows, block), away_outs):
         out[...] = total[at : at + block].astype(BF16)
 
 
@@ -406,16 +401,16 @@
     count, across_bit = lax.axis_size("ingroup"), bits_of("group")[0]
     near_dx, go, stay, keep, far = call(
         "place",
-        functools.partial(place_body, block),
+        place_body,
         [near, fourth, fourth] + [((half // 2, features), t) for t in (F32, BF16)],
         [place, rows, near_y, got_y, swap(far, "group", across_bit)],
     )
     near_dx, got_go, got_dx = collect_start(near_dx, go, stay)
-    got = swap(far, axis, bits[0])
-    for bit in bits[1:-1]:
-        sums = (keep + got.astype(F32)).reshape(-1, 2, block, features)
-        keep = sums[:, 0].reshape(-1, features)
-        got = swap(sums[:, 1].reshape(-1, features).astype(BF16), axis, bit)
+    got = swap(far, axis, bits[-1])
+    for bit in bits[-2:0:-1]:
+        outs = [(keep.shape[0] // 2, t) for t in (F32, BF16)]
+        keep, away = add(keep, 0, [(got, 0)], outs)
+        got = swap(away, axis, bit)
     (far,) = add(near_dx, half, [(got_go, 0)], [(half, BF16)])
     own_dx, own_y, pair, *away = call(
         "join",
@@ -425,14 +420,13 @@
         + [((block, features), BF16)] * (count - 2),
         [near_dx, got_dx, swap(far, "group", across_bit), keep, got],
     )
-    offsets = [j for j in inner_order() if j > 1]
-    sent = [swap(part, axis, j) for j, part in zip(offsets, away)]
+    sent = [swap(part, axis, j) for j, part in zip(inner_order()[2:], away)]
     outs = [((block, features), BF16)] * 2
     return call(
         "final",
         functools.partial(final_body, len(sent)),
         outs,
-        [own_y, own_dx, swap(pair, axis, 1)] + sent,
+        [own_y, own_dx, swap(pair, axis, bits[0])] + sent,
     )
 
 

time: 71.1 us -> 69.7 us (0.980)
  starting transfers between devices: 22.6 us -> 21.5 us
    ppermute x22, starting transfers between devices: 19.5 us -> 18.3 us  [swap(): lax.ppermute(value, axis, [(i, i ^ offset) for i in range(lax.axis_size(a...]
  transfers between devices with their start and end apart: 24 -> 24, of which waited for: 16 -> 18; matrix products, arithmetic and copies ran while one was open for 0% -> 0% of each run, Pallas kernels for 10% -> 10%
where the time goes in v11:
time: 69.7 us; the launch traced here: 69.4 us
  waiting for transfers between devices  36.7 us (53%)
  starting transfers between devices  21.5 us (31%)
  Pallas kernels  9.65 us (14%)
  local copies, waits for them, and re-layouts  0.85 us (1%)
  between operations  0.8 us (1%)
    ppermute x22, waiting for transfers between devices, swap(): lax.ppermute(value, axis, [(i, i ^ offset) for i in range(lax.axis_size(a...  33 us
    ppermute x22, starting transfers between devices, swap(): lax.ppermute(value, axis, [(i, i ^ offset) for i in range(lax.axis_size(a...  18.3 us
    pallas_call x16, Pallas kernels, call(): return kernel(*args, *passed)  9.65 us
    ppermute x2, waiting for transfers between devices, from_peers(): lax.ppermute(sent, 'dp', [(i, (i + step) % count) for i in range(count)])  3.67 us
    ppermute x2, starting transfers between devices, from_peers(): lax.ppermute(sent, 'dp', [(i, (i + step) % count) for i in range(count)])  3.11 us
  transfers between devices with their start and end apart: 24, of which 18 were waited for; matrix products, arithmetic and copies ran while one was open for 0% of the time, Pallas kernels for 10%

profile of v11, /device:TPU:0, one launch (start us, length us, event | category | flops | bytes accessed | tf_op | source)
XLA Modules:
  0.0 69.4 jit_solution(377861801344012161)
XLA Ops:
  0.6 1.5 %payload.1.refs_0_ = bf16[16,1920]{1,0:T(8,128)(2,1)} custom-call(s32[1]{0:T(128)} %bitcast.refs_0_, bf16[16,1792]{1,0:T(8,128)(2,1)} %refs_1_.1, s32[8,16]{1,0:T(8,128)} %bitcast.12, s32[8,16]{1,0:T(8,128)} %bitcast.13), custom_call_target="tpu_custom_call" | custom-call | bytes 119812 | tf_op jit(solution)/shard_map/payload/payload/pallas_call | solution.py:52
  2.2 4.1 %collective-permute-start = (bf16[16,1920]{1,0:T(8,128)(2,1)}, bf16[16,1920]{1,0:T(8,128)(2,1)S(1)}, u32[]{:S(2)}, u32[]{:S(2)}) collective-permute-start(bf16[16,1920]{1,0:T(8,128)(2,1)} %payload.1.refs_0_), channel_id=1, source_target_pairs={{0,4},{2,6},{4,0},{6,2},{1,5},{3,7},{5,1},{7,3},{8,12},{10,14},{12... | collective-permute-start | bytes 184328 | tf_op jit(solution)/shard_map/ppermute | solution.py:56
  6.3 1.6 %collective-permute-start.1 = (bf16[16,1920]{1,0:T(8,128)(2,1)}, bf16[16,1920]{1,0:T(8,128)(2,1)S(1)}, u32[]{:S(2)}, u32[]{:S(2)}) collective-permute-start(bf16[16,1920]{1,0:T(8,128)(2,1)} %payload.1.refs_0_), channel_id=1, source_target_pairs={{0,2},{2,0},{4,6},{6,4},{1,3},{3,1},{5,7},{7,5},{8,10},{10,8},{12,... | collective-permute-start | bytes 184328 | tf_op jit(solution)/shard_map/ppermute | solution.py:56
  7.8 1.6 %collective-permute-done.refs_1_ = bf16[16,1920]{1,0:T(8,128)(2,1)S(1)} collective-permute-done((bf16[16,1920]{1,0:T(8,128)(2,1)}, bf16[16,1920]{1,0:T(8,128)(2,1)S(1)}, u32[]{:S(2)}, u32[]{:S(2)}) %collective-permute-start) | collective-permute-done | bytes 61472 | tf_op jit(solution)/shard_map/ppermute | solution.py:56
  10.3 1.9 %collective-permute-start.3 = (bf16[32,1920]{1,0:T(8,128)(2,1)S(1)}, bf16[32,1920]{1,0:T(8,128)(2,1)S(1)}, u32[]{:S(2)}, u32[]{:S(2)}) collective-permute-start(bf16[32,1920]{1,0:T(8,128)(2,1)S(1)} %pack.5.refs_2_.refs_0_), channel_id=1, source_target_pairs={{0,16},{8,24},{16,0},{24,8},{1,17},{9,25},{17,1},{25,9},{2,18},{10... | collective-permute-start | bytes 368648 | tf_op jit(solution)/shard_map/ppermute | solution.py:56
  12.1 1.9 %collective-permute-done.2.refs_1_ = bf16[16,1920]{1,0:T(8,128)(2,1)S(1)} collective-permute-done((bf16[16,1920]{1,0:T(8,128)(2,1)}, bf16[16,1920]{1,0:T(8,128)(2,1)S(1)}, u32[]{:S(2)}, u32[]{:S(2)}) %collective-permute-start.2) | collective-permute-done | bytes 61472 | tf_op jit(solution)/shard_map/ppermute | solution.py:56
  14.1 1.6 %collective-permute-start.4 = (bf16[32,1920]{1,0:T(8,128)(2,1)S(1)}, bf16[32,1920]{1,0:T(8,128)(2,1)S(1)}, u32[]{:S(2)}, u32[]{:S(2)}) collective-permute-start(bf16[32,1920]{1,0:T(8,128)(2,1)S(1)} %pack.6.refs_1_), channel_id=1, source_target_pairs={{0,16},{8,24},{16,0},{24,8},{1,17},{9,25},{17,1},{25,9},{2,18},{10... | collective-permute-start | bytes 368648 | tf_op jit(solution)/shard_map/ppermute | solution.py:56
  16.8 4.3 %collective-permute-done.5.refs_1_ = bf16[16,1792]{1,0:T(8,128)(2,1)S(1)} collective-permute-done((bf16[16,1792]{1,0:T(8,128)(2,1)S(1)}, bf16[16,1792]{1,0:T(8,128)(2,1)S(1)}, u32[]{:S(2)}, u32[]{:S(2)}) %collective-permute-start.5) | collective-permute-done | bytes 57376 | tf_op jit(solution)/shard_map/ppermute | solution.py:56
  21.3 1.8 %collective-permute-done.6.refs_2_ = bf16[128,1920]{1,0:T(8,128)(2,1)S(1)} collective-permute-done((bf16[128,1920]{1,0:T(8,128)(2,1)S(1)}, bf16[128,1920]{1,0:T(8,128)(2,1)S(1)}, u32[]{:S(2)}, u32[]{:S(2)}) %collective-permute-start.6) | collective-permute-done | bytes 491552 | tf_op jit(solution)/shard_map/ppermute | solution.py:56
  23.0 1.8 %forward.1 = (bf16[256,128]{1,0:T(8,128)(2,1)S(1)}, f32[128,128]{1,0:T(8,128)S(1)}, f32[256,1024]{1,0:T(8,128)S(1)}, bf16[256,1024]{1,0:T(8,128)(2,1)S(1)}) custom-call(s32[1]{0:T(128)} %bitcast.refs_0_, bf16[128,1920]{1,0:T(8,128)(2,1)S(1)} %pack.8.refs_1_, bf16[128,1920]{1,0:T(8,128)(2,1)S(1)} %collective-permute-done.6.refs_2_, ...), custom_call_target="tpu_custom_call" | custom-call | flops 939524096 | bytes 10027012 | tf_op jit(solution)/shard_map/forward/forward/pallas_call | solution.py:52
  24.8 1.6 %collective-permute-start.7 = (bf16[256,1024]{1,0:T(8,128)(2,1)S(1)}, bf16[256,1024]{1,0:T(8,128)(2,1)S(1)}, u32[]{:S(2)}, u32[]{:S(2)}) collective-permute-start(bf16[256,1024]{1,0:T(8,128)(2,1)S(1)} %get-tuple-element.26.refs_2_), channel_id=1, source_target_pairs={{0,1},{1,0},{2,3},{3,2},{4,5},{5,4},{6,7},{7,6},{8,9},{9,8},{10,11... | collective-permute-start | bytes 1572872 | tf_op jit(solution)/shard_map/ppermute | solution.py:329
  27.2 6.8 %collective-permute-done.9.refs_1_ = bf16[64,1792]{1,0:T(8,128)(2,1)S(1)} collective-permute-done((bf16[64,1792]{1,0:T(8,128)(2,1)S(1)}, bf16[64,1792]{1,0:T(8,128)(2,1)S(1)}, u32[]{:S(2)}, u32[]{:S(2)}) %collective-permute-start.9) | collective-permute-done | bytes 229408 | tf_op jit(solution)/shard_map/ppermute | solution.py:56
  34.0 1.5 %collective-permute-done.11.refs_3_ = bf16[64,1792]{1,0:T(8,128)(2,1)S(1)} collective-permute-done((bf16[64,1792]{1,0:T(8,128)(2,1)S(1)}, bf16[64,1792]{1,0:T(8,128)(2,1)S(1)}, u32[]{:S(2)}, u32[]{:S(2)}) %collective-permute-start.11) | collective-permute-done | bytes 229408 | tf_op jit(solution)/shard_map/ppermute | solution.py:56
  35.5 1.3 %back.1 = (f32[128,1024]{1,0:T(8,128)S(1)}, bf16[128,1024]{1,0:T(8,128)(2,1)S(1)}) custom-call(bf16[64,1792]{1,0:T(8,128)(2,1)S(1)} %pack.9.refs_0_, bf16[64,1792]{1,0:T(8,128)(2,1)S(1)} %collective-permute-done.9.refs_1_, bf16[64,1792]{1,0:T(8,128)(2,1)S(1)} %collective-permute-done.10.refs_2_, bf16[64,1792]{1,0:T(8,128)(2,1)S(1)} %collective-permute-done.11.refs_3_, ...), custom_call_target="tpu_custom_call" | custom-call | flops 469762048 | bytes 5439488 | tf_op jit(solution)/shard_map/back/back/pallas_call | solution.py:52
  36.8 1.6 %collective-permute-start.12 = (bf16[128,1024]{1,0:T(8,128)(2,1)S(1)}, bf16[128,1024]{1,0:T(8,128)(2,1)S(1)}, u32[]{:S(2)}, u32[]{:S(2)}) collective-permute-start(bf16[128,1024]{1,0:T(8,128)(2,1)S(1)} %get-tuple-element.28.refs_5_), channel_id=1, source_target_pairs={{0,1},{1,0},{2,3},{3,2},{4,5},{5,4},{6,7},{7,6},{8,9},{9,8},{10,11... | collective-permute-start | bytes 786440 | tf_op jit(solution)/shard_map/ppermute | solution.py:329
  42.1 3.1 %collective-permute-done.12.refs_3_ = bf16[128,1024]{1,0:T(8,128)(2,1)S(1)} collective-permute-done((bf16[128,1024]{1,0:T(8,128)(2,1)S(1)}, bf16[128,1024]{1,0:T(8,128)(2,1)S(1)}, u32[]{:S(2)}, u32[]{:S(2)}) %collective-permute-start.12) | collective-permute-done | bytes 262176 | tf_op jit(solution)/shard_map/ppermute | solution.py:329
  45.2 2.5 %grad.1.refs_1_ = bf16[128,1792]{1,0:T(8,128)(2,1)S(1)} custom-call(f32[128,1024]{1,0:T(8,128)S(1)} %get-tuple-element.29.refs_0_, f32[128,1024]{1,0:T(8,128)S(1)} %get-tuple-element.30.refs_1_, f32[128,1024]{1,0:T(8,128)S(1)} %get-tuple-element.31.refs_2_, bf16[128,1024]{1,0:T(8,128)(2,1)S(1)} %collective-permute-done.12.refs_3_, ...), custom_call_target="tpu_custom_call" | custom-call | flops 939524096 | bytes 9863168 | tf_op jit(solution)/shard_map/grad/grad/pallas_call | solution.py:52
  47.7 1.9 %collective-permute-done.16.refs_4_ = bf16[64,1792]{1,0:T(8,128)(2,1)S(1)} collective-permute-done((bf16[64,1792]{1,0:T(8,128)(2,1)S(1)}, bf16[64,1792]{1,0:T(8,128)(2,1)S(1)}, u32[]{:S(2)}, u32[]{:S(2)}) %collective-permute-start.16) | collective-permute-done | bytes 229408 | tf_op jit(solution)/shard_map/ppermute | solution.py:56
  53.2 3.8 %collective-permute-done.20.refs_4_ = bf16[32,1792]{1,0:T(8,128)(2,1)S(1)} collective-permute-done((bf16[32,1792]{1,0:T(8,128)(2,1)S(1)}, bf16[32,1792]{1,0:T(8,128)(2,1)S(1)}, u32[]{:S(2)}, u32[]{:S(2)}) %collective-permute-start.20) | collective-permute-done | bytes 114720 | tf_op jit(solution)/shard_map/ppermute | solution.py:56
  57.0 2.4 %collective-permute-done.19.refs_2_ = bf16[64,1792]{1,0:T(8,128)(2,1)S(1)} collective-permute-done((bf16[64,1792]{1,0:T(8,128)(2,1)S(1)}, bf16[64,1792]{1,0:T(8,128)(2,1)S(1)}, u32[]{:S(2)}, u32[]{:S(2)}) %collective-permute-start.19) | collective-permute-done | bytes 229408 | tf_op jit(solution)/shard_map/ppermute | solution.py:56
  59.4 1.2 %collective-permute-start.21 = (bf16[32,1792]{1,0:T(8,128)(2,1)S(1)}, bf16[32,1792]{1,0:T(8,128)(2,1)S(1)}, u32[]{:S(2)}, u32[]{:S(2)}) collective-permute-start(bf16[32,1792]{1,0:T(8,128)(2,1)S(1)} %get-tuple-element.43), channel_id=1, source_target_pairs={{0,4},{2,6},{4,0},{6,2},{1,5},{3,7},{5,1},{7,3},{8,12},{10,14},{12... | collective-permute-start | bytes 344072 | tf_op jit(solution)/shard_map/ppermute | solution.py:56
  60.6 1.7 %collective-permute-start.22 = (bf16[16,1792]{1,0:T(8,128)(2,1)S(1)}, bf16[16,1792]{1,0:T(8,128)(2,1)S(1)}, u32[]{:S(2)}, u32[]{:S(2)}) collective-permute-start(bf16[16,1792]{1,0:T(8,128)(2,1)S(1)} %get-tuple-element.44), channel_id=1, source_target_pairs={{0,2},{2,0},{4,6},{6,4},{1,3},{3,1},{5,7},{7,5},{8,10},{10,8},{12,... | collective-permute-start | bytes 172040 | tf_op jit(solution)/shard_map/ppermute | solution.py:56
  62.4 1.5 %collective-permute-start.23 = (bf16[16,1792]{1,0:T(8,128)(2,1)S(1)}, bf16[16,1792]{1,0:T(8,128)(2,1)S(1)}, u32[]{:S(2)}, u32[]{:S(2)}) collective-permute-start(bf16[16,1792]{1,0:T(8,128)(2,1)S(1)} %get-tuple-element.45), channel_id=1, source_target_pairs={{0,6},{2,4},{4,2},{6,0},{1,7},{3,5},{5,3},{7,1},{8,14},{10,12},{12... | collective-permute-start | bytes 172040 | tf_op jit(solution)/shard_map/ppermute | solution.py:56
  65.0 3.5 %collective-permute-done.23.refs_4_ = bf16[16,1792]{1,0:T(8,128)(2,1)S(1)} collective-permute-done((bf16[16,1792]{1,0:T(8,128)(2,1)S(1)}, bf16[16,1792]{1,0:T(8,128)(2,1)S(1)}, u32[]{:S(2)}, u32[]{:S(2)}) %collective-permute-start.23) | collective-permute-done | bytes 57376 | tf_op jit(solution)/shard_map/ppermute | solution.py:56
  (50 shorter events, 12.3 us)
Async XLA Ops:
  2.2 7.3 %collective-permute-start = (bf16[16,1920]{1,0:T(8,128)(2,1)}, bf16[16,1920]{1,0:T(8,128)(2,1)S(1)}, u32[]{:S(2)}, u32[]{:S(2)}) collective-permute-start(bf16[16,1920]{1,0:T(8,128)(2,1)} %payload.1.refs_0_), channel_id=1, source_target_pairs={{0,4},{2,6},{4,0},{6,2},{1,5},{3,7},{5,1},{7,3},{8,12},{10,14},{12... | collective-permute-start | bytes 184328 | tf_op jit(solution)/shard_map/ppermute | solution.py:56
  6.3 5.9 %collective-permute-start.1 = (bf16[16,1920]{1,0:T(8,128)(2,1)}, bf16[16,1920]{1,0:T(8,128)(2,1)S(1)}, u32[]{:S(2)}, u32[]{:S(2)}) collective-permute-start(bf16[16,1920]{1,0:T(8,128)(2,1)} %payload.1.refs_0_), channel_id=1, source_target_pairs={{0,2},{2,0},{4,6},{6,4},{1,3},{3,1},{5,7},{7,5},{8,10},{10,8},{12,... | collective-permute-start | bytes 184328 | tf_op jit(solution)/shard_map/ppermute | solution.py:56
  7.8 6.2 %collective-permute-start.2 = (bf16[16,1920]{1,0:T(8,128)(2,1)}, bf16[16,1920]{1,0:T(8,128)(2,1)S(1)}, u32[]{:S(2)}, u32[]{:S(2)}) collective-permute-start(bf16[16,1920]{1,0:T(8,128)(2,1)} %payload.1.refs_0_), channel_id=1, source_target_pairs={{0,6},{2,4},{4,2},{6,0},{1,7},{3,5},{5,3},{7,1},{8,14},{10,12},{12... | collective-permute-start | bytes 184328 | tf_op jit(solution)/shard_map/ppermute | solution.py:56
  10.3 10.8 %collective-permute-start.3 = (bf16[32,1920]{1,0:T(8,128)(2,1)S(1)}, bf16[32,1920]{1,0:T(8,128)(2,1)S(1)}, u32[]{:S(2)}, u32[]{:S(2)}) collective-permute-start(bf16[32,1920]{1,0:T(8,128)(2,1)S(1)} %pack.5.refs_2_.refs_0_), channel_id=1, source_target_pairs={{0,16},{8,24},{16,0},{24,8},{1,17},{9,25},{17,1},{25,9},{2,18},{10... | collective-permute-start | bytes 368648 | tf_op jit(solution)/shard_map/ppermute | solution.py:56
  14.1 7.0 %collective-permute-start.4 = (bf16[32,1920]{1,0:T(8,128)(2,1)S(1)}, bf16[32,1920]{1,0:T(8,128)(2,1)S(1)}, u32[]{:S(2)}, u32[]{:S(2)}) collective-permute-start(bf16[32,1920]{1,0:T(8,128)(2,1)S(1)} %pack.6.refs_1_), channel_id=1, source_target_pairs={{0,16},{8,24},{16,0},{24,8},{1,17},{9,25},{17,1},{25,9},{2,18},{10... | collective-permute-start | bytes 368648 | tf_op jit(solution)/shard_map/ppermute | solution.py:56
  15.7 5.3 %collective-permute-start.5 = (bf16[16,1792]{1,0:T(8,128)(2,1)S(1)}, bf16[16,1792]{1,0:T(8,128)(2,1)S(1)}, u32[]{:S(2)}, u32[]{:S(2)}) collective-permute-start(bf16[16,1792]{1,0:T(8,128)(2,1)S(1)} %copied.1.refs_0_), channel_id=1, source_target_pairs={{0,4},{2,6},{4,0},{6,2},{1,5},{3,7},{5,1},{7,3},{8,12},{10,14},{12... | collective-permute-start | bytes 172040 | tf_op jit(solution)/shard_map/ppermute | solution.py:56
  21.1 1.9 %collective-permute-start.6 = (bf16[128,1920]{1,0:T(8,128)(2,1)S(1)}, bf16[128,1920]{1,0:T(8,128)(2,1)S(1)}, u32[]{:S(2)}, u32[]{:S(2)}) collective-permute-start(bf16[128,1920]{1,0:T(8,128)(2,1)S(1)} %pack.8.refs_1_), channel_id=1, source_target_pairs={{0,8},{8,0},{16,24},{24,16},{1,9},{9,1},{17,25},{25,17},{2,10},{10... | collective-permute-start | bytes 1474568 | tf_op jit(solution)/shard_map/ppermute | solution.py:56
  21.2 5.6 %collective-permute-start.8 = (bf16[32,1792]{1,0:T(8,128)(2,1)S(1)}, bf16[32,1792]{1,0:T(8,128)(2,1)S(1)}, u32[]{:S(2)}, u32[]{:S(2)}) collective-permute-start(bf16[32,1792]{1,0:T(8,128)(2,1)S(1)} %pack.7.refs_4_.refs_0_), channel_id=1, source_target_pairs={{0,2},{2,0},{4,6},{6,4},{1,3},{3,1},{5,7},{7,5},{8,10},{10,8},{12,... | collective-permute-start | bytes 344072 | tf_op jit(solution)/shard_map/ppermute | solution.py:56
  24.8 14.0 %collective-permute-start.7 = (bf16[256,1024]{1,0:T(8,128)(2,1)S(1)}, bf16[256,1024]{1,0:T(8,128)(2,1)S(1)}, u32[]{:S(2)}, u32[]{:S(2)}) collective-permute-start(bf16[256,1024]{1,0:T(8,128)(2,1)S(1)} %get-tuple-element.26.refs_2_), channel_id=1, source_target_pairs={{0,1},{1,0},{2,3},{3,2},{4,5},{5,4},{6,7},{7,6},{8,9},{9,8},{10,11... | collective-permute-start | bytes 1572872 | tf_op jit(solution)/shard_map/ppermute | solution.py:329
  26.8 7.2 %collective-permute-start.9 = (bf16[64,1792]{1,0:T(8,128)(2,1)S(1)}, bf16[64,1792]{1,0:T(8,128)(2,1)S(1)}, u32[]{:S(2)}, u32[]{:S(2)}) collective-permute-start(bf16[64,1792]{1,0:T(8,128)(2,1)S(1)} %pack.9.refs_0_), channel_id=1, source_target_pairs={{0,16},{8,24},{16,0},{24,8},{1,17},{9,25},{17,1},{25,9},{2,18},{10... | collective-permute-start | bytes 688136 | tf_op jit(solution)/shard_map/ppermute | solution.py:56
  27.2 6.8 %collective-permute-start.10 = (bf16[64,1792]{1,0:T(8,128)(2,1)S(1)}, bf16[64,1792]{1,0:T(8,128)(2,1)S(1)}, u32[]{:S(2)}, u32[]{:S(2)}) collective-permute-start(bf16[64,1792]{1,0:T(8,128)(2,1)S(1)} %pack.9.refs_0_), channel_id=1, source_target_pairs={{0,8},{8,0},{16,24},{24,16},{1,9},{9,1},{17,25},{25,17},{2,10},{10... | collective-permute-start | bytes 688136 | tf_op jit(solution)/shard_map/ppermute | solution.py:56
  34.0 1.5 %collective-permute-start.11 = (bf16[64,1792]{1,0:T(8,128)(2,1)S(1)}, bf16[64,1792]{1,0:T(8,128)(2,1)S(1)}, u32[]{:S(2)}, u32[]{:S(2)}) collective-permute-start(bf16[64,1792]{1,0:T(8,128)(2,1)S(1)} %collective-permute-done.9.refs_1_), channel_id=1, source_target_pairs={{0,8},{8,0},{16,24},{24,16},{1,9},{9,1},{17,25},{25,17},{2,10},{10... | collective-permute-start | bytes 688136 | tf_op jit(solution)/shard_map/ppermute | solution.py:56
  36.8 8.4 %collective-permute-start.12 = (bf16[128,1024]{1,0:T(8,128)(2,1)S(1)}, bf16[128,1024]{1,0:T(8,128)(2,1)S(1)}, u32[]{:S(2)}, u32[]{:S(2)}) collective-permute-start(bf16[128,1024]{1,0:T(8,128)(2,1)S(1)} %get-tuple-element.28.refs_5_), channel_id=1, source_target_pairs={{0,1},{1,0},{2,3},{3,2},{4,5},{5,4},{6,7},{7,6},{8,9},{9,8},{10,11... | collective-permute-start | bytes 786440 | tf_op jit(solution)/shard_map/ppermute | solution.py:329
  40.1 1.4 %collective-permute-start.13 = (bf16[32,1792]{1,0:T(8,128)(2,1)S(1)}, bf16[32,1792]{1,0:T(8,128)(2,1)S(1)}, u32[]{:S(2)}, u32[]{:S(2)}) collective-permute-start(bf16[32,1792]{1,0:T(8,128)(2,1)S(1)} %get-tuple-element.33), channel_id=1, source_target_pairs={{0,8},{8,0},{16,24},{24,16},{1,9},{9,1},{17,25},{25,17},{2,10},{10... | collective-permute-start | bytes 344072 | tf_op jit(solution)/shard_map/ppermute | solution.py:56
  40.1 1.5 %collective-permute-start.14 = (bf16[32,1792]{1,0:T(8,128)(2,1)S(1)}, bf16[32,1792]{1,0:T(8,128)(2,1)S(1)}, u32[]{:S(2)}, u32[]{:S(2)}) collective-permute-start(bf16[32,1792]{1,0:T(8,128)(2,1)S(1)} %get-tuple-element.34), channel_id=1, source_target_pairs={{0,8},{8,0},{16,24},{24,16},{1,9},{9,1},{17,25},{25,17},{2,10},{10... | collective-permute-start | bytes 344072 | tf_op jit(solution)/shard_map/ppermute | solution.py:56
  40.6 7.1 %collective-permute-start.15 = (bf16[64,1792]{1,0:T(8,128)(2,1)S(1)}, bf16[64,1792]{1,0:T(8,128)(2,1)S(1)}, u32[]{:S(2)}, u32[]{:S(2)}) collective-permute-start(bf16[64,1792]{1,0:T(8,128)(2,1)S(1)} %get-tuple-element.35), channel_id=1, source_target_pairs={{0,8},{8,0},{16,24},{24,16},{1,9},{9,1},{17,25},{25,17},{2,10},{10... | collective-permute-start | bytes 688136 | tf_op jit(solution)/shard_map/ppermute | solution.py:56
  41.7 7.9 %collective-permute-start.16 = (bf16[64,1792]{1,0:T(8,128)(2,1)S(1)}, bf16[64,1792]{1,0:T(8,128)(2,1)S(1)}, u32[]{:S(2)}, u32[]{:S(2)}) collective-permute-start(bf16[64,1792]{1,0:T(8,128)(2,1)S(1)} %add.6.refs_6_), channel_id=1, source_target_pairs={{0,16},{8,24},{16,0},{24,8},{1,17},{9,25},{17,1},{25,9},{2,18},{10... | collective-permute-start | bytes 688136 | tf_op jit(solution)/shard_map/ppermute | solution.py:56
  50.0 1.6 %collective-permute-start.18 = (bf16[64,1792]{1,0:T(8,128)(2,1)S(1)}, bf16[64,1792]{1,0:T(8,128)(2,1)S(1)}, u32[]{:S(2)}, u32[]{:S(2)}) collective-permute-start(bf16[64,1792]{1,0:T(8,128)(2,1)S(1)} %get-tuple-element.38), channel_id=1, source_target_pairs={{0,8},{8,0},{16,24},{24,16},{1,9},{9,1},{17,25},{25,17},{2,10},{10... | collective-permute-start | bytes 688136 | tf_op jit(solution)/shard_map/ppermute | solution.py:56
  50.1 6.9 %collective-permute-start.17 = (bf16[64,1792]{1,0:T(8,128)(2,1)S(1)}, bf16[64,1792]{1,0:T(8,128)(2,1)S(1)}, u32[]{:S(2)}, u32[]{:S(2)}) collective-permute-start(bf16[64,1792]{1,0:T(8,128)(2,1)S(1)} %get-tuple-element.37), channel_id=1, source_target_pairs={{0,8},{8,0},{16,24},{24,16},{1,9},{9,1},{17,25},{25,17},{2,10},{10... | collective-permute-start | bytes 688136 | tf_op jit(solution)/shard_map/ppermute | solution.py:56
  51.6 7.7 %collective-permute-start.19 = (bf16[64,1792]{1,0:T(8,128)(2,1)S(1)}, bf16[64,1792]{1,0:T(8,128)(2,1)S(1)}, u32[]{:S(2)}, u32[]{:S(2)}) collective-permute-start(bf16[64,1792]{1,0:T(8,128)(2,1)S(1)} %add.7), channel_id=1, source_target_pairs={{0,16},{8,24},{16,0},{24,8},{1,17},{9,25},{17,1},{25,9},{2,18},{10... | collective-permute-start | bytes 688136 | tf_op jit(solution)/shard_map/ppermute | solution.py:56
  52.0 4.9 %collective-permute-start.20 = (bf16[32,1792]{1,0:T(8,128)(2,1)S(1)}, bf16[32,1792]{1,0:T(8,128)(2,1)S(1)}, u32[]{:S(2)}, u32[]{:S(2)}) collective-permute-start(bf16[32,1792]{1,0:T(8,128)(2,1)S(1)} %get-tuple-element.40), channel_id=1, source_target_pairs={{0,2},{2,0},{4,6},{6,4},{1,3},{3,1},{5,7},{7,5},{8,10},{10,8},{12,... | collective-permute-start | bytes 344072 | tf_op jit(solution)/shard_map/ppermute | solution.py:56
  59.4 9.4 %collective-permute-start.21 = (bf16[32,1792]{1,0:T(8,128)(2,1)S(1)}, bf16[32,1792]{1,0:T(8,128)(2,1)S(1)}, u32[]{:S(2)}, u32[]{:S(2)}) collective-permute-start(bf16[32,1792]{1,0:T(8,128)(2,1)S(1)} %get-tuple-element.43), channel_id=1, source_target_pairs={{0,4},{2,6},{4,0},{6,2},{1,5},{3,7},{5,1},{7,3},{8,12},{10,14},{12... | collective-permute-start | bytes 344072 | tf_op jit(solution)/shard_map/ppermute | solution.py:56
  60.6 4.3 %collective-permute-start.22 = (bf16[16,1792]{1,0:T(8,128)(2,1)S(1)}, bf16[16,1792]{1,0:T(8,128)(2,1)S(1)}, u32[]{:S(2)}, u32[]{:S(2)}) collective-permute-start(bf16[16,1792]{1,0:T(8,128)(2,1)S(1)} %get-tuple-element.44), channel_id=1, source_target_pairs={{0,2},{2,0},{4,6},{6,4},{1,3},{3,1},{5,7},{7,5},{8,10},{10,8},{12,... | collective-permute-start | bytes 172040 | tf_op jit(solution)/shard_map/ppermute | solution.py:56
  62.4 6.1 %collective-permute-start.23 = (bf16[16,1792]{1,0:T(8,128)(2,1)S(1)}, bf16[16,1792]{1,0:T(8,128)(2,1)S(1)}, u32[]{:S(2)}, u32[]{:S(2)}) collective-permute-start(bf16[16,1792]{1,0:T(8,128)(2,1)S(1)} %get-tuple-element.45), channel_id=1, source_target_pairs={{0,6},{2,4},{4,2},{6,0},{1,7},{3,5},{5,3},{7,1},{8,14},{10,12},{12... | collective-permute-start | bytes 172040 | tf_op jit(solution)/shard_map/ppermute | solution.py:56
  (5 other events, 43.0 us)

commit v12 on v11

--- a/solution.py
+++ b/solution.py
@@ -65,17 +65,16 @@
 
 
 def payload_body(me, tokens, ids, gate, out, tokens_held, ids_held, gate_held, sems):
+    topk, block = ids.shape
+    features = tokens.shape[1]
+    wide = out.shape[1] - LANES
+    place = tokens_held if wide != features else out.at[:, pl.ds(0, features)]
     copies = [
         pltpu.make_async_copy(source, held, sems.at[i])
-        for i, (source, held) in enumerate(
-            ((ids, ids_held), (gate, gate_held), (tokens, tokens_held))
-        )
+        for i, (source, held) in enumerate(((ids, ids_held), (gate, gate_held), (tokens, place)))
     ]
     for copy in copies:
         copy.start()
-    topk, block = ids.shape
-    features = tokens.shape[1]
-    wide = out.shape[1] - LANES
     if wide != features:
         out[...] = jnp.zeros_like(out)
     eye = lax.broadcasted_iota(jnp.int32, (block, block), 0) == lax.broadcasted_iota(
@@ -94,7 +93,8 @@
     ).astype(BF16)
     out[:, wide:] = dot(jnp.where(eye, 1.0, 0.0).astype(BF16), rows, 1, 1).astype(BF16)
     copies[2].wait()
-    out[:, :features] = tokens_held[...]
+    if wide != features:
+        out[:, :features] = tokens_held[...]
 
 
 def pack_body(count, *refs):

time: 69.7 us -> 69.7 us (level)
  no operation moved by 1% of the time
where the time goes in v12:
time: 69.7 us; the launch traced here: 69.4 us
  waiting for transfers between devices  36.7 us (53%)
  starting transfers between devices  21.5 us (31%)
  Pallas kernels  9.63 us (14%)
  local copies, waits for them, and re-layouts  0.85 us (1%)
  between operations  0.8 us (1%)
    ppermute x22, waiting for transfers between devices, swap(): lax.ppermute(value, axis, [(i, i ^ offset) for i in range(lax.axis_size(a...  33 us
    ppermute x22, starting transfers between devices, swap(): lax.ppermute(value, axis, [(i, i ^ offset) for i in range(lax.axis_size(a...  18.4 us
    pallas_call x16, Pallas kernels, call(): return kernel(*args, *passed)  9.63 us
    ppermute x2, waiting for transfers between devices, from_peers(): lax.ppermute(sent, 'dp', [(i, (i + step) % count) for i in range(count)])  3.68 us
    ppermute x2, starting transfers between devices, from_peers(): lax.ppermute(sent, 'dp', [(i, (i + step) % count) for i in range(count)])  3.11 us
  transfers between devices with their start and end apart: 24, of which 18 were waited for; matrix products, arithmetic and copies ran while one was open for 0% of the time, Pallas kernels for 10%

profile of v12, /device:TPU:0, one launch (start us, length us, event | category | flops | bytes accessed | tf_op | source)
XLA Modules:
  0.0 69.4 jit_solution(15052451790594462877)
XLA Ops:
  0.6 1.5 %payload.1.refs_0_ = bf16[16,1920]{1,0:T(8,128)(2,1)} custom-call(s32[1]{0:T(128)} %bitcast.refs_0_, bf16[16,1792]{1,0:T(8,128)(2,1)} %refs_1_.1, s32[8,16]{1,0:T(8,128)} %bitcast.12, s32[8,16]{1,0:T(8,128)} %bitcast.13), custom_call_target="tpu_custom_call" | custom-call | bytes 119812 | tf_op jit(solution)/shard_map/payload/payload/pallas_call | solution.py:52
  2.2 4.1 %collective-permute-start = (bf16[16,1920]{1,0:T(8,128)(2,1)}, bf16[16,1920]{1,0:T(8,128)(2,1)S(1)}, u32[]{:S(2)}, u32[]{:S(2)}) collective-permute-start(bf16[16,1920]{1,0:T(8,128)(2,1)} %payload.1.refs_0_), channel_id=1, source_target_pairs={{0,4},{2,6},{4,0},{6,2},{1,5},{3,7},{5,1},{7,3},{8,12},{10,14},{12... | collective-permute-start | bytes 184328 | tf_op jit(solution)/shard_map/ppermute | solution.py:56
  6.3 1.6 %collective-permute-start.1 = (bf16[16,1920]{1,0:T(8,128)(2,1)}, bf16[16,1920]{1,0:T(8,128)(2,1)S(1)}, u32[]{:S(2)}, u32[]{:S(2)}) collective-permute-start(bf16[16,1920]{1,0:T(8,128)(2,1)} %payload.1.refs_0_), channel_id=1, source_target_pairs={{0,2},{2,0},{4,6},{6,4},{1,3},{3,1},{5,7},{7,5},{8,10},{10,8},{12,... | collective-permute-start | bytes 184328 | tf_op jit(solution)/shard_map/ppermute | solution.py:56
  7.8 1.6 %collective-permute-done.refs_1_ = bf16[16,1920]{1,0:T(8,128)(2,1)S(1)} collective-permute-done((bf16[16,1920]{1,0:T(8,128)(2,1)}, bf16[16,1920]{1,0:T(8,128)(2,1)S(1)}, u32[]{:S(2)}, u32[]{:S(2)}) %collective-permute-start) | collective-permute-done | bytes 61472 | tf_op jit(solution)/shard_map/ppermute | solution.py:56
  10.3 1.9 %collective-permute-start.3 = (bf16[32,1920]{1,0:T(8,128)(2,1)S(1)}, bf16[32,1920]{1,0:T(8,128)(2,1)S(1)}, u32[]{:S(2)}, u32[]{:S(2)}) collective-permute-start(bf16[32,1920]{1,0:T(8,128)(2,1)S(1)} %pack.5.refs_2_.refs_0_), channel_id=1, source_target_pairs={{0,16},{8,24},{16,0},{24,8},{1,17},{9,25},{17,1},{25,9},{2,18},{10... | collective-permute-start | bytes 368648 | tf_op jit(solution)/shard_map/ppermute | solution.py:56
  12.1 1.9 %collective-permute-done.2.refs_1_ = bf16[16,1920]{1,0:T(8,128)(2,1)S(1)} collective-permute-done((bf16[16,1920]{1,0:T(8,128)(2,1)}, bf16[16,1920]{1,0:T(8,128)(2,1)S(1)}, u32[]{:S(2)}, u32[]{:S(2)}) %collective-permute-start.2) | collective-permute-done | bytes 61472 | tf_op jit(solution)/shard_map/ppermute | solution.py:56
  14.1 1.6 %collective-permute-start.4 = (bf16[32,1920]{1,0:T(8,128)(2,1)S(1)}, bf16[32,1920]{1,0:T(8,128)(2,1)S(1)}, u32[]{:S(2)}, u32[]{:S(2)}) collective-permute-start(bf16[32,1920]{1,0:T(8,128)(2,1)S(1)} %pack.6.refs_1_), channel_id=1, source_target_pairs={{0,16},{8,24},{16,0},{24,8},{1,17},{9,25},{17,1},{25,9},{2,18},{10... | collective-permute-start | bytes 368648 | tf_op jit(solution)/shard_map/ppermute | solution.py:56
  16.8 4.3 %collective-permute-done.5.refs_1_ = bf16[16,1792]{1,0:T(8,128)(2,1)S(1)} collective-permute-done((bf16[16,1792]{1,0:T(8,128)(2,1)S(1)}, bf16[16,1792]{1,0:T(8,128)(2,1)S(1)}, u32[]{:S(2)}, u32[]{:S(2)}) %collective-permute-start.5) | collective-permute-done | bytes 57376 | tf_op jit(solution)/shard_map/ppermute | solution.py:56
  21.3 1.8 %collective-permute-done.6.refs_2_ = bf16[128,1920]{1,0:T(8,128)(2,1)S(1)} collective-permute-done((bf16[128,1920]{1,0:T(8,128)(2,1)S(1)}, bf16[128,1920]{1,0:T(8,128)(2,1)S(1)}, u32[]{:S(2)}, u32[]{:S(2)}) %collective-permute-start.6) | collective-permute-done | bytes 491552 | tf_op jit(solution)/shard_map/ppermute | solution.py:56
  23.0 1.8 %forward.1 = (bf16[256,128]{1,0:T(8,128)(2,1)S(1)}, f32[128,128]{1,0:T(8,128)S(1)}, f32[256,1024]{1,0:T(8,128)S(1)}, bf16[256,1024]{1,0:T(8,128)(2,1)S(1)}) custom-call(s32[1]{0:T(128)} %bitcast.refs_0_, bf16[128,1920]{1,0:T(8,128)(2,1)S(1)} %pack.8.refs_1_, bf16[128,1920]{1,0:T(8,128)(2,1)S(1)} %collective-permute-done.6.refs_2_, ...), custom_call_target="tpu_custom_call" | custom-call | flops 939524096 | bytes 10027012 | tf_op jit(solution)/shard_map/forward/forward/pallas_call | solution.py:52
  24.8 1.6 %collective-permute-start.7 = (bf16[256,1024]{1,0:T(8,128)(2,1)S(1)}, bf16[256,1024]{1,0:T(8,128)(2,1)S(1)}, u32[]{:S(2)}, u32[]{:S(2)}) collective-permute-start(bf16[256,1024]{1,0:T(8,128)(2,1)S(1)} %get-tuple-element.26.refs_2_), channel_id=1, source_target_pairs={{0,1},{1,0},{2,3},{3,2},{4,5},{5,4},{6,7},{7,6},{8,9},{9,8},{10,11... | collective-permute-start | bytes 1572872 | tf_op jit(solution)/shard_map/ppermute | solution.py:329
  27.2 6.8 %collective-permute-done.9.refs_1_ = bf16[64,1792]{1,0:T(8,128)(2,1)S(1)} collective-permute-done((bf16[64,1792]{1,0:T(8,128)(2,1)S(1)}, bf16[64,1792]{1,0:T(8,128)(2,1)S(1)}, u32[]{:S(2)}, u32[]{:S(2)}) %collective-permute-start.9) | collective-permute-done | bytes 229408 | tf_op jit(solution)/shard_map/ppermute | solution.py:56
  34.0 1.5 %collective-permute-done.11.refs_3_ = bf16[64,1792]{1,0:T(8,128)(2,1)S(1)} collective-permute-done((bf16[64,1792]{1,0:T(8,128)(2,1)S(1)}, bf16[64,1792]{1,0:T(8,128)(2,1)S(1)}, u32[]{:S(2)}, u32[]{:S(2)}) %collective-permute-start.11) | collective-permute-done | bytes 229408 | tf_op jit(solution)/shard_map/ppermute | solution.py:56
  35.5 1.3 %back.1 = (f32[128,1024]{1,0:T(8,128)S(1)}, bf16[128,1024]{1,0:T(8,128)(2,1)S(1)}) custom-call(bf16[64,1792]{1,0:T(8,128)(2,1)S(1)} %pack.9.refs_0_, bf16[64,1792]{1,0:T(8,128)(2,1)S(1)} %collective-permute-done.9.refs_1_, bf16[64,1792]{1,0:T(8,128)(2,1)S(1)} %collective-permute-done.10.refs_2_, bf16[64,1792]{1,0:T(8,128)(2,1)S(1)} %collective-permute-done.11.refs_3_, ...), custom_call_target="tpu_custom_call" | custom-call | flops 469762048 | bytes 5439488 | tf_op jit(solution)/shard_map/back/back/pallas_call | solution.py:52
  36.8 1.6 %collective-permute-start.12 = (bf16[128,1024]{1,0:T(8,128)(2,1)S(1)}, bf16[128,1024]{1,0:T(8,128)(2,1)S(1)}, u32[]{:S(2)}, u32[]{:S(2)}) collective-permute-start(bf16[128,1024]{1,0:T(8,128)(2,1)S(1)} %get-tuple-element.28.refs_5_), channel_id=1, source_target_pairs={{0,1},{1,0},{2,3},{3,2},{4,5},{5,4},{6,7},{7,6},{8,9},{9,8},{10,11... | collective-permute-start | bytes 786440 | tf_op jit(solution)/shard_map/ppermute | solution.py:329
  42.1 3.1 %collective-permute-done.12.refs_3_ = bf16[128,1024]{1,0:T(8,128)(2,1)S(1)} collective-permute-done((bf16[128,1024]{1,0:T(8,128)(2,1)S(1)}, bf16[128,1024]{1,0:T(8,128)(2,1)S(1)}, u32[]{:S(2)}, u32[]{:S(2)}) %collective-permute-start.12) | collective-permute-done | bytes 262176 | tf_op jit(solution)/shard_map/ppermute | solution.py:329
  45.2 2.5 %grad.1.refs_1_ = bf16[128,1792]{1,0:T(8,128)(2,1)S(1)} custom-call(f32[128,1024]{1,0:T(8,128)S(1)} %get-tuple-element.29.refs_0_, f32[128,1024]{1,0:T(8,128)S(1)} %get-tuple-element.30.refs_1_, f32[128,1024]{1,0:T(8,128)S(1)} %get-tuple-element.31.refs_2_, bf16[128,1024]{1,0:T(8,128)(2,1)S(1)} %collective-permute-done.12.refs_3_, ...), custom_call_target="tpu_custom_call" | custom-call | flops 939524096 | bytes 9863168 | tf_op jit(solution)/shard_map/grad/grad/pallas_call | solution.py:52
  47.7 1.9 %collective-permute-done.16.refs_4_ = bf16[64,1792]{1,0:T(8,128)(2,1)S(1)} collective-permute-done((bf16[64,1792]{1,0:T(8,128)(2,1)S(1)}, bf16[64,1792]{1,0:T(8,128)(2,1)S(1)}, u32[]{:S(2)}, u32[]{:S(2)}) %collective-permute-start.16) | collective-permute-done | bytes 229408 | tf_op jit(solution)/shard_map/ppermute | solution.py:56
  53.2 3.8 %collective-permute-done.20.refs_4_ = bf16[32,1792]{1,0:T(8,128)(2,1)S(1)} collective-permute-done((bf16[32,1792]{1,0:T(8,128)(2,1)S(1)}, bf16[32,1792]{1,0:T(8,128)(2,1)S(1)}, u32[]{:S(2)}, u32[]{:S(2)}) %collective-permute-start.20) | collective-permute-done | bytes 114720 | tf_op jit(solution)/shard_map/ppermute | solution.py:56
  57.0 2.4 %collective-permute-done.19.refs_2_ = bf16[64,1792]{1,0:T(8,128)(2,1)S(1)} collective-permute-done((bf16[64,1792]{1,0:T(8,128)(2,1)S(1)}, bf16[64,1792]{1,0:T(8,128)(2,1)S(1)}, u32[]{:S(2)}, u32[]{:S(2)}) %collective-permute-start.19) | collective-permute-done | bytes 229408 | tf_op jit(solution)/shard_map/ppermute | solution.py:56
  59.4 1.2 %collective-permute-start.21 = (bf16[32,1792]{1,0:T(8,128)(2,1)S(1)}, bf16[32,1792]{1,0:T(8,128)(2,1)S(1)}, u32[]{:S(2)}, u32[]{:S(2)}) collective-permute-start(bf16[32,1792]{1,0:T(8,128)(2,1)S(1)} %get-tuple-element.43), channel_id=1, source_target_pairs={{0,4},{2,6},{4,0},{6,2},{1,5},{3,7},{5,1},{7,3},{8,12},{10,14},{12... | collective-permute-start | bytes 344072 | tf_op jit(solution)/shard_map/ppermute | solution.py:56
  60.6 1.7 %collective-permute-start.22 = (bf16[16,1792]{1,0:T(8,128)(2,1)S(1)}, bf16[16,1792]{1,0:T(8,128)(2,1)S(1)}, u32[]{:S(2)}, u32[]{:S(2)}) collective-permute-start(bf16[16,1792]{1,0:T(8,128)(2,1)S(1)} %get-tuple-element.44), channel_id=1, source_target_pairs={{0,2},{2,0},{4,6},{6,4},{1,3},{3,1},{5,7},{7,5},{8,10},{10,8},{12,... | collective-permute-start | bytes 172040 | tf_op jit(solution)/shard_map/ppermute | solution.py:56
  62.4 1.5 %collective-permute-start.23 = (bf16[16,1792]{1,0:T(8,128)(2,1)S(1)}, bf16[16,1792]{1,0:T(8,128)(2,1)S(1)}, u32[]{:S(2)}, u32[]{:S(2)}) collective-permute-start(bf16[16,1792]{1,0:T(8,128)(2,1)S(1)} %get-tuple-element.45), channel_id=1, source_target_pairs={{0,6},{2,4},{4,2},{6,0},{1,7},{3,5},{5,3},{7,1},{8,14},{10,12},{12... | collective-permute-start | bytes 172040 | tf_op jit(solution)/shard_map/ppermute | solution.py:56
  65.0 3.5 %collective-permute-done.23.refs_4_ = bf16[16,1792]{1,0:T(8,128)(2,1)S(1)} collective-permute-done((bf16[16,1792]{1,0:T(8,128)(2,1)S(1)}, bf16[16,1792]{1,0:T(8,128)(2,1)S(1)}, u32[]{:S(2)}, u32[]{:S(2)}) %collective-permute-start.23) | collective-permute-done | bytes 57376 | tf_op jit(solution)/shard_map/ppermute | solution.py:56
  (50 shorter events, 12.4 us)
Async XLA Ops:
  2.2 7.3 %collective-permute-start = (bf16[16,1920]{1,0:T(8,128)(2,1)}, bf16[16,1920]{1,0:T(8,128)(2,1)S(1)}, u32[]{:S(2)}, u32[]{:S(2)}) collective-permute-start(bf16[16,1920]{1,0:T(8,128)(2,1)} %payload.1.refs_0_), channel_id=1, source_target_pairs={{0,4},{2,6},{4,0},{6,2},{1,5},{3,7},{5,1},{7,3},{8,12},{10,14},{12... | collective-permute-start | bytes 184328 | tf_op jit(solution)/shard_map/ppermute | solution.py:56
  6.3 5.9 %collective-permute-start.1 = (bf16[16,1920]{1,0:T(8,128)(2,1)}, bf16[16,1920]{1,0:T(8,128)(2,1)S(1)}, u32[]{:S(2)}, u32[]{:S(2)}) collective-permute-start(bf16[16,1920]{1,0:T(8,128)(2,1)} %payload.1.refs_0_), channel_id=1, source_target_pairs={{0,2},{2,0},{4,6},{6,4},{1,3},{3,1},{5,7},{7,5},{8,10},{10,8},{12,... | collective-permute-start | bytes 184328 | tf_op jit(solution)/shard_map/ppermute | solution.py:56
  7.8 6.2 %collective-permute-start.2 = (bf16[16,1920]{1,0:T(8,128)(2,1)}, bf16[16,1920]{1,0:T(8,128)(2,1)S(1)}, u32[]{:S(2)}, u32[]{:S(2)}) collective-permute-start(bf16[16,1920]{1,0:T(8,128)(2,1)} %payload.1.refs_0_), channel_id=1, source_target_pairs={{0,6},{2,4},{4,2},{6,0},{1,7},{3,5},{5,3},{7,1},{8,14},{10,12},{12... | collective-permute-start | bytes 184328 | tf_op jit(solution)/shard_map/ppermute | solution.py:56
  10.3 10.8 %collective-permute-start.3 = (bf16[32,1920]{1,0:T(8,128)(2,1)S(1)}, bf16[32,1920]{1,0:T(8,128)(2,1)S(1)}, u32[]{:S(2)}, u32[]{:S(2)}) collective-permute-start(bf16[32,1920]{1,0:T(8,128)(2,1)S(1)} %pack.5.refs_2_.refs_0_), channel_id=1, source_target_pairs={{0,16},{8,24},{16,0},{24,8},{1,17},{9,25},{17,1},{25,9},{2,18},{10... | collective-permute-start | bytes 368648 | tf_op jit(solution)/shard_map/ppermute | solution.py:56
  14.1 7.0 %collective-permute-start.4 = (bf16[32,1920]{1,0:T(8,128)(2,1)S(1)}, bf16[32,1920]{1,0:T(8,128)(2,1)S(1)}, u32[]{:S(2)}, u32[]{:S(2)}) collective-permute-start(bf16[32,1920]{1,0:T(8,128)(2,1)S(1)} %pack.6.refs_1_), channel_id=1, source_target_pairs={{0,16},{8,24},{16,0},{24,8},{1,17},{9,25},{17,1},{25,9},{2,18},{10... | collective-permute-start | bytes 368648 | tf_op jit(solution)/shard_map/ppermute | solution.py:56
  15.7 5.3 %collective-permute-start.5 = (bf16[16,1792]{1,0:T(8,128)(2,1)S(1)}, bf16[16,1792]{1,0:T(8,128)(2,1)S(1)}, u32[]{:S(2)}, u32[]{:S(2)}) collective-permute-start(bf16[16,1792]{1,0:T(8,128)(2,1)S(1)} %copied.1.refs_0_), channel_id=1, source_target_pairs={{0,4},{2,6},{4,0},{6,2},{1,5},{3,7},{5,1},{7,3},{8,12},{10,14},{12... | collective-permute-start | bytes 172040 | tf_op jit(solution)/shard_map/ppermute | solution.py:56
  21.1 1.9 %collective-permute-start.6 = (bf16[128,1920]{1,0:T(8,128)(2,1)S(1)}, bf16[128,1920]{1,0:T(8,128)(2,1)S(1)}, u32[]{:S(2)}, u32[]{:S(2)}) collective-permute-start(bf16[128,1920]{1,0:T(8,128)(2,1)S(1)} %pack.8.refs_1_), channel_id=1, source_target_pairs={{0,8},{8,0},{16,24},{24,16},{1,9},{9,1},{17,25},{25,17},{2,10},{10... | collective-permute-start | bytes 1474568 | tf_op jit(solution)/shard_map/ppermute | solution.py:56
  21.2 5.6 %collective-permute-start.8 = (bf16[32,1792]{1,0:T(8,128)(2,1)S(1)}, bf16[32,1792]{1,0:T(8,128)(2,1)S(1)}, u32[]{:S(2)}, u32[]{:S(2)}) collective-permute-start(bf16[32,1792]{1,0:T(8,128)(2,1)S(1)} %pack.7.refs_4_.refs_0_), channel_id=1, source_target_pairs={{0,2},{2,0},{4,6},{6,4},{1,3},{3,1},{5,7},{7,5},{8,10},{10,8},{12,... | collective-permute-start | bytes 344072 | tf_op jit(solution)/shard_map/ppermute | solution.py:56
  24.8 14.0 %collective-permute-start.7 = (bf16[256,1024]{1,0:T(8,128)(2,1)S(1)}, bf16[256,1024]{1,0:T(8,128)(2,1)S(1)}, u32[]{:S(2)}, u32[]{:S(2)}) collective-permute-start(bf16[256,1024]{1,0:T(8,128)(2,1)S(1)} %get-tuple-element.26.refs_2_), channel_id=1, source_target_pairs={{0,1},{1,0},{2,3},{3,2},{4,5},{5,4},{6,7},{7,6},{8,9},{9,8},{10,11... | collective-permute-start | bytes 1572872 | tf_op jit(solution)/shard_map/ppermute | solution.py:329
  26.8 7.2 %collective-permute-start.9 = (bf16[64,1792]{1,0:T(8,128)(2,1)S(1)}, bf16[64,1792]{1,0:T(8,128)(2,1)S(1)}, u32[]{:S(2)}, u32[]{:S(2)}) collective-permute-start(bf16[64,1792]{1,0:T(8,128)(2,1)S(1)} %pack.9.refs_0_), channel_id=1, source_target_pairs={{0,16},{8,24},{16,0},{24,8},{1,17},{9,25},{17,1},{25,9},{2,18},{10... | collective-permute-start | bytes 688136 | tf_op jit(solution)/shard_map/ppermute | solution.py:56
  27.2 6.8 %collective-permute-start.10 = (bf16[64,1792]{1,0:T(8,128)(2,1)S(1)}, bf16[64,1792]{1,0:T(8,128)(2,1)S(1)}, u32[]{:S(2)}, u32[]{:S(2)}) collective-permute-start(bf16[64,1792]{1,0:T(8,128)(2,1)S(1)} %pack.9.refs_0_), channel_id=1, source_target_pairs={{0,8},{8,0},{16,24},{24,16},{1,9},{9,1},{17,25},{25,17},{2,10},{10... | collective-permute-start | bytes 688136 | tf_op jit(solution)/shard_map/ppermute | solution.py:56
  34.0 1.5 %collective-permute-start.11 = (bf16[64,1792]{1,0:T(8,128)(2,1)S(1)}, bf16[64,1792]{1,0:T(8,128)(2,1)S(1)}, u32[]{:S(2)}, u32[]{:S(2)}) collective-permute-start(bf16[64,1792]{1,0:T(8,128)(2,1)S(1)} %collective-permute-done.9.refs_1_), channel_id=1, source_target_pairs={{0,8},{8,0},{16,24},{24,16},{1,9},{9,1},{17,25},{25,17},{2,10},{10... | collective-permute-start | bytes 688136 | tf_op jit(solution)/shard_map/ppermute | solution.py:56
  36.8 8.4 %collective-permute-start.12 = (bf16[128,1024]{1,0:T(8,128)(2,1)S(1)}, bf16[128,1024]{1,0:T(8,128)(2,1)S(1)}, u32[]{:S(2)}, u32[]{:S(2)}) collective-permute-start(bf16[128,1024]{1,0:T(8,128)(2,1)S(1)} %get-tuple-element.28.refs_5_), channel_id=1, source_target_pairs={{0,1},{1,0},{2,3},{3,2},{4,5},{5,4},{6,7},{7,6},{8,9},{9,8},{10,11... | collective-permute-start | bytes 786440 | tf_op jit(solution)/shard_map/ppermute | solution.py:329
  40.1 1.4 %collective-permute-start.13 = (bf16[32,1792]{1,0:T(8,128)(2,1)S(1)}, bf16[32,1792]{1,0:T(8,128)(2,1)S(1)}, u32[]{:S(2)}, u32[]{:S(2)}) collective-permute-start(bf16[32,1792]{1,0:T(8,128)(2,1)S(1)} %get-tuple-element.33), channel_id=1, source_target_pairs={{0,8},{8,0},{16,24},{24,16},{1,9},{9,1},{17,25},{25,17},{2,10},{10... | collective-permute-start | bytes 344072 | tf_op jit(solution)/shard_map/ppermute | solution.py:56
  40.1 1.5 %collective-permute-start.14 = (bf16[32,1792]{1,0:T(8,128)(2,1)S(1)}, bf16[32,1792]{1,0:T(8,128)(2,1)S(1)}, u32[]{:S(2)}, u32[]{:S(2)}) collective-permute-start(bf16[32,1792]{1,0:T(8,128)(2,1)S(1)} %get-tuple-element.34), channel_id=1, source_target_pairs={{0,8},{8,0},{16,24},{24,16},{1,9},{9,1},{17,25},{25,17},{2,10},{10... | collective-permute-start | bytes 344072 | tf_op jit(solution)/shard_map/ppermute | solution.py:56
  40.6 7.1 %collective-permute-start.15 = (bf16[64,1792]{1,0:T(8,128)(2,1)S(1)}, bf16[64,1792]{1,0:T(8,128)(2,1)S(1)}, u32[]{:S(2)}, u32[]{:S(2)}) collective-permute-start(bf16[64,1792]{1,0:T(8,128)(2,1)S(1)} %get-tuple-element.35), channel_id=1, source_target_pairs={{0,8},{8,0},{16,24},{24,16},{1,9},{9,1},{17,25},{25,17},{2,10},{10... | collective-permute-start | bytes 688136 | tf_op jit(solution)/shard_map/ppermute | solution.py:56
  41.7 7.9 %collective-permute-start.16 = (bf16[64,1792]{1,0:T(8,128)(2,1)S(1)}, bf16[64,1792]{1,0:T(8,128)(2,1)S(1)}, u32[]{:S(2)}, u32[]{:S(2)}) collective-permute-start(bf16[64,1792]{1,0:T(8,128)(2,1)S(1)} %add.6.refs_6_), channel_id=1, source_target_pairs={{0,16},{8,24},{16,0},{24,8},{1,17},{9,25},{17,1},{25,9},{2,18},{10... | collective-permute-start | bytes 688136 | tf_op jit(solution)/shard_map/ppermute | solution.py:56
  50.0 1.6 %collective-permute-start.18 = (bf16[64,1792]{1,0:T(8,128)(2,1)S(1)}, bf16[64,1792]{1,0:T(8,128)(2,1)S(1)}, u32[]{:S(2)}, u32[]{:S(2)}) collective-permute-start(bf16[64,1792]{1,0:T(8,128)(2,1)S(1)} %get-tuple-element.38), channel_id=1, source_target_pairs={{0,8},{8,0},{16,24},{24,16},{1,9},{9,1},{17,25},{25,17},{2,10},{10... | collective-permute-start | bytes 688136 | tf_op jit(solution)/shard_map/ppermute | solution.py:56
  50.1 6.9 %collective-permute-start.17 = (bf16[64,1792]{1,0:T(8,128)(2,1)S(1)}, bf16[64,1792]{1,0:T(8,128)(2,1)S(1)}, u32[]{:S(2)}, u32[]{:S(2)}) collective-permute-start(bf16[64,1792]{1,0:T(8,128)(2,1)S(1)} %get-tuple-element.37), channel_id=1, source_target_pairs={{0,8},{8,0},{16,24},{24,16},{1,9},{9,1},{17,25},{25,17},{2,10},{10... | collective-permute-start | bytes 688136 | tf_op jit(solution)/shard_map/ppermute | solution.py:56
  51.6 7.7 %collective-permute-start.19 = (bf16[64,1792]{1,0:T(8,128)(2,1)S(1)}, bf16[64,1792]{1,0:T(8,128)(2,1)S(1)}, u32[]{:S(2)}, u32[]{:S(2)}) collective-permute-start(bf16[64,1792]{1,0:T(8,128)(2,1)S(1)} %add.7), channel_id=1, source_target_pairs={{0,16},{8,24},{16,0},{24,8},{1,17},{9,25},{17,1},{25,9},{2,18},{10... | collective-permute-start | bytes 688136 | tf_op jit(solution)/shard_map/ppermute | solution.py:56
  52.0 4.9 %collective-permute-start.20 = (bf16[32,1792]{1,0:T(8,128)(2,1)S(1)}, bf16[32,1792]{1,0:T(8,128)(2,1)S(1)}, u32[]{:S(2)}, u32[]{:S(2)}) collective-permute-start(bf16[32,1792]{1,0:T(8,128)(2,1)S(1)} %get-tuple-element.40), channel_id=1, source_target_pairs={{0,2},{2,0},{4,6},{6,4},{1,3},{3,1},{5,7},{7,5},{8,10},{10,8},{12,... | collective-permute-start | bytes 344072 | tf_op jit(solution)/shard_map/ppermute | solution.py:56
  59.4 9.4 %collective-permute-start.21 = (bf16[32,1792]{1,0:T(8,128)(2,1)S(1)}, bf16[32,1792]{1,0:T(8,128)(2,1)S(1)}, u32[]{:S(2)}, u32[]{:S(2)}) collective-permute-start(bf16[32,1792]{1,0:T(8,128)(2,1)S(1)} %get-tuple-element.43), channel_id=1, source_target_pairs={{0,4},{2,6},{4,0},{6,2},{1,5},{3,7},{5,1},{7,3},{8,12},{10,14},{12... | collective-permute-start | bytes 344072 | tf_op jit(solution)/shard_map/ppermute | solution.py:56
  60.6 4.3 %collective-permute-start.22 = (bf16[16,1792]{1,0:T(8,128)(2,1)S(1)}, bf16[16,1792]{1,0:T(8,128)(2,1)S(1)}, u32[]{:S(2)}, u32[]{:S(2)}) collective-permute-start(bf16[16,1792]{1,0:T(8,128)(2,1)S(1)} %get-tuple-element.44), channel_id=1, source_target_pairs={{0,2},{2,0},{4,6},{6,4},{1,3},{3,1},{5,7},{7,5},{8,10},{10,8},{12,... | collective-permute-start | bytes 172040 | tf_op jit(solution)/shard_map/ppermute | solution.py:56
  62.4 6.1 %collective-permute-start.23 = (bf16[16,1792]{1,0:T(8,128)(2,1)S(1)}, bf16[16,1792]{1,0:T(8,128)(2,1)S(1)}, u32[]{:S(2)}, u32[]{:S(2)}) collective-permute-start(bf16[16,1792]{1,0:T(8,128)(2,1)S(1)} %get-tuple-element.45), channel_id=1, source_target_pairs={{0,6},{2,4},{4,2},{6,0},{1,7},{3,5},{5,3},{7,1},{8,14},{10,12},{12... | collective-permute-start | bytes 172040 | tf_op jit(solution)/shard_map/ppermute | solution.py:56
  (5 other events, 43.0 us)
